TPU v7x, 32 devices: a whole 2x2x4 slice. The times are simulated.
32 devices in a mesh: dp: 8 (over y, x, core), ctx: 4 (over z).
Axes of the slice: x: 2, y: 2, z: 4, core: 2. Of those that a mesh axis runs over, the one named last changes fastest.
Arguments:
- tokens: bfloat16 [8, 512, 2048], P('dp', 'ctx'), may hold values from -6 to 6
- segment_ids: int32 [8, 512], P('dp'), may hold values from 0 to 10, as said below
- out_grad: bfloat16 [8, 512, 2048], P('dp', 'ctx'), may hold values from -6 to 6
- gain_attn: bfloat16 [2048], P(('dp', 'ctx')), may hold values from 0.099609375 to 1.8984375
- w_query: bfloat16 [2048, 2048], P(('dp', 'ctx')), may hold values from -0.125 to 0.125
- key_weight: bfloat16 [2048, 256], P(('dp', 'ctx')), may hold values from -0.125 to 0.125
- value_weight: bfloat16 [2048, 256], P(('dp', 'ctx')), may hold values from -0.125 to 0.125
- w_out: bfloat16 [2048, 2048], P(('dp', 'ctx')), may hold values from -1 to 1
- gain_mlp: bfloat16 [2048], P(('dp', 'ctx')), may hold values from 0.099609375 to 1.8984375
- w_gate: bfloat16 [2048, 5632], P(('dp', 'ctx')), may hold values from -0.125 to 0.125
- w_up: bfloat16 [2048, 5632], P(('dp', 'ctx')), may hold values from -0.125 to 0.125
- w_down: bfloat16 [5632, 2048], P(('dp', 'ctx')), may hold values from -0.15625 to 0.15625
Outputs:
- result: bfloat16 [8, 512, 2048], P('dp', 'ctx')
- grad_input: float32 [8, 512, 2048], P('dp', 'ctx')
- grad_gain_attn: float32 [2048], P(('dp', 'ctx'))
- grad_query: float32 [2048, 2048], P(('dp', 'ctx'))
- grad_key: float32 [2048, 256], P(('dp', 'ctx'))
- grad_value: float32 [2048, 256], P(('dp', 'ctx'))
- grad_out: float32 [2048, 2048], P(('dp', 'ctx'))
- grad_gain_mlp: float32 [2048], P(('dp', 'ctx'))
- grad_gate: float32 [2048, 5632], P(('dp', 'ctx'))
- grad_up: float32 [2048, 5632], P(('dp', 'ctx'))
- grad_down: float32 [5632, 2048], P(('dp', 'ctx'))
Inputs may be any that keep to these rules, and one draw needn't show every extreme that they name: `segment_ids`: segment numbers start at 0 and rise by one at the first token of each new document; every document but the last of its sequence holds 50 to 500 tokens.
All inputs are finite; a program needn't handle non-finite values.
Results may differ from a plain program's by a relative error of at most 0.015.
Values may be sent and summed in bfloat16 or wider, within the bound.
No kernel may reach another device: no remote copies, remote signals or barrier semaphores. Data moves between devices by JAX's collectives and lax.ppermute only.
A program may use at most 384 MiB of HBM per device.

v0:
```python
import jax
import jax.numpy as jnp
from jax import lax
from jax.sharding import PartitionSpec as P

QUERY_HEADS = 32
KEY_VALUE_HEADS = 4
HEAD_SIZE = 64


EPS = 1e-05
NEG = -1e30


def apply_rotary(value_rows, cosine_table, sine_table):
    half = value_rows.shape[-1] // 2
    first = value_rows[..., :half]
    second = value_rows[..., half:]
    return jnp.concatenate(
        [first * cosine_table - second * sine_table, second * cosine_table + first * sine_table],
        axis=-1,
    )


def inverse_rotary(value_rows, cosine_table, sine_table):
    half = value_rows.shape[-1] // 2
    first = value_rows[..., :half]
    second = value_rows[..., half:]
    return jnp.concatenate(
        [first * cosine_table + second * sine_table, second * cosine_table - first * sine_table],
        axis=-1,
    )


def norm_back(grad_in, normed, inverse, gain):
    grad_normed = grad_in * gain
    grad_gain = jnp.sum(grad_in * normed, axis=0)
    grad_x = inverse * (
        grad_normed - normed * jnp.mean(grad_normed * normed, axis=-1, keepdims=True)
    )
    return (grad_x, grad_gain)


def per_device(
    tokens,
    segment_ids,
    out_grad,
    gain_attn,
    w_query,
    key_weight,
    value_weight,
    w_out,
    gain_mlp,
    w_gate,
    w_up,
    w_down,
):
    single_float = jnp.float32
    brain_float_half = jnp.bfloat16
    token_count = tokens.shape[1]
    sequence_length = segment_ids.shape[1]
    head_group = QUERY_HEADS // KEY_VALUE_HEADS
    scale = HEAD_SIZE ** (-0.5)
    everyone = segment_ids[0]
    offset = lax.axis_index("ctx") * token_count
    local_idx = offset + jnp.arange(token_count, dtype=jnp.int32)
    local_seg = lax.dynamic_slice_in_dim(everyone, offset, token_count)
    before = jnp.sum((everyone[None, :] < local_seg[:, None]).astype(jnp.int32), axis=1)
    place = (local_idx - before).astype(single_float)
    freq = 10000.0 ** (-jnp.arange(HEAD_SIZE // 2, dtype=single_float) / (HEAD_SIZE // 2))
    angle = place[:, None] * freq[None, :]
    cosine_table = jnp.cos(angle)[:, None, :]
    sine_table = jnp.sin(angle)[:, None, :]
    allowed = (jnp.arange(sequence_length, dtype=jnp.int32)[None, :] <= local_idx[:, None]) & (
        everyone[None, :] == local_seg[:, None]
    )
    attention_params = (
        lax.all_gather(gain_attn, ("dp", "ctx"), axis=0, tiled=True),
        lax.all_gather(w_query, ("dp", "ctx"), axis=0, tiled=True),
        lax.all_gather(key_weight, ("dp", "ctx"), axis=0, tiled=True),
        lax.all_gather(value_weight, ("dp", "ctx"), axis=0, tiled=True),
        lax.all_gather(w_out, ("dp", "ctx"), axis=0, tiled=True),
    )
    inputs = tokens[0].astype(single_float)
    inverse1 = lax.rsqrt(jnp.mean(inputs * inputs, axis=-1, keepdims=True) + EPS)
    normed1 = inputs * inverse1
    gain1 = attention_params[0].astype(single_float)
    first_input_rows = (normed1 * gain1).astype(brain_float_half)
    query_vector = jnp.dot(
        first_input_rows, attention_params[1], preferred_element_type=single_float
    ).reshape(token_count, QUERY_HEADS, HEAD_SIZE)
    key = jnp.dot(
        first_input_rows, attention_params[2], preferred_element_type=single_float
    ).reshape(token_count, KEY_VALUE_HEADS, HEAD_SIZE)
    value_vector = jnp.dot(
        first_input_rows, attention_params[3], preferred_element_type=single_float
    ).astype(brain_float_half)
    rotated_queries = apply_rotary(query_vector, cosine_table, sine_table).astype(brain_float_half)
    rotated_keys = (
        apply_rotary(key, cosine_table, sine_table)
        .astype(brain_float_half)
        .reshape(token_count, KEY_VALUE_HEADS * HEAD_SIZE)
    )
    complete_block = lax.all_gather(
        jnp.stack([rotated_keys, value_vector]), "ctx", axis=1, tiled=True
    )
    key_rows = (
        complete_block[0].reshape(sequence_length, KEY_VALUE_HEADS, HEAD_SIZE).transpose(1, 0, 2)
    )
    value_rows = (
        complete_block[1].reshape(sequence_length, KEY_VALUE_HEADS, HEAD_SIZE).transpose(1, 0, 2)
    )
    query_rows = rotated_queries.reshape(
        token_count, KEY_VALUE_HEADS, head_group, HEAD_SIZE
    ).transpose(1, 2, 0, 3)

    def attend(args):
        qg, kg, vg = args
        scores = jnp.einsum("gsd,jd->gsj", qg, kg, preferred_element_type=single_float) * scale
        scores = jnp.where(allowed[None], scores, NEG)
        top = jnp.max(scores, axis=-1, keepdims=True)
        expo = jnp.exp(scores - top)
        total = jnp.sum(expo, axis=-1, keepdims=True)
        probs = (expo / total).astype(brain_float_half)
        mixed = jnp.einsum("gsj,jd->gsd", probs, vg, preferred_element_type=single_float)
        return (mixed, top + jnp.log(total))

    mixed, logsum = lax.map(attend, (query_rows, key_rows, value_rows))
    attn_in = (
        mixed.transpose(2, 0, 1, 3)
        .reshape(token_count, QUERY_HEADS * HEAD_SIZE)
        .astype(brain_float_half)
    )
    resid = inputs + jnp.dot(attn_in, attention_params[4], preferred_element_type=single_float)
    mlp_ws = (
        lax.all_gather(gain_mlp, ("dp", "ctx"), axis=0, tiled=True),
        lax.all_gather(w_gate, ("dp", "ctx"), axis=0, tiled=True),
        lax.all_gather(w_up, ("dp", "ctx"), axis=0, tiled=True),
        lax.all_gather(w_down, ("dp", "ctx"), axis=0, tiled=True),
    )
    inverse2 = lax.rsqrt(jnp.mean(resid * resid, axis=-1, keepdims=True) + EPS)
    normed2 = resid * inverse2
    gain2 = mlp_ws[0].astype(single_float)
    second_in = (normed2 * gain2).astype(brain_float_half)
    gate = jnp.dot(second_in, mlp_ws[1], preferred_element_type=single_float)
    up = jnp.dot(second_in, mlp_ws[2], preferred_element_type=single_float)
    sig = jax.nn.sigmoid(gate)
    swish = gate * sig
    hidden = (swish * up).astype(brain_float_half)
    result = resid + jnp.dot(hidden, mlp_ws[3], preferred_element_type=single_float)
    back_mlp = (
        lax.all_gather(gain_mlp, ("dp", "ctx"), axis=0, tiled=True),
        lax.all_gather(w_gate, ("dp", "ctx"), axis=0, tiled=True),
        lax.all_gather(w_up, ("dp", "ctx"), axis=0, tiled=True),
        lax.all_gather(w_down, ("dp", "ctx"), axis=0, tiled=True),
    )
    grad_out = out_grad[0]
    grad_hidden = jnp.einsum(
        "td,fd->tf", grad_out, back_mlp[3], preferred_element_type=single_float
    )
    grad_gate = (grad_hidden * up * sig * (1.0 + gate * (1.0 - sig))).astype(brain_float_half)
    grad_up = (grad_hidden * swish).astype(brain_float_half)
    grad_second = jnp.einsum(
        "tf,df->td", grad_gate, back_mlp[1], preferred_element_type=single_float
    ) + jnp.einsum("tf,df->td", grad_up, back_mlp[2], preferred_element_type=single_float)
    grad_resid_norm, gain2_term = norm_back(
        grad_second, normed2, inverse2, back_mlp[0].astype(single_float)
    )
    mlp_terms = (
        gain2_term,
        jnp.einsum("td,tf->df", second_in, grad_gate, preferred_element_type=single_float),
        jnp.einsum("td,tf->df", second_in, grad_up, preferred_element_type=single_float),
        jnp.einsum("tf,td->fd", hidden, grad_out, preferred_element_type=single_float),
    )
    mlp_sums = (
        lax.psum_scatter(mlp_terms[0], ("dp", "ctx"), scatter_dimension=0, tiled=True),
        lax.psum_scatter(mlp_terms[1], ("dp", "ctx"), scatter_dimension=0, tiled=True),
        lax.psum_scatter(mlp_terms[2], ("dp", "ctx"), scatter_dimension=0, tiled=True),
        lax.psum_scatter(mlp_terms[3], ("dp", "ctx"), scatter_dimension=0, tiled=True),
    )
    grad_resid = grad_out.astype(single_float) + grad_resid_norm
    back_attn = (
        lax.all_gather(gain_attn, ("dp", "ctx"), axis=0, tiled=True),
        lax.all_gather(w_query, ("dp", "ctx"), axis=0, tiled=True),
        lax.all_gather(key_weight, ("dp", "ctx"), axis=0, tiled=True),
        lax.all_gather(value_weight, ("dp", "ctx"), axis=0, tiled=True),
        lax.all_gather(w_out, ("dp", "ctx"), axis=0, tiled=True),
    )
    grad_branch = grad_resid.astype(brain_float_half)
    grad_wout = jnp.einsum("tc,td->cd", attn_in, grad_branch, preferred_element_type=single_float)
    mixed_gradient = jnp.einsum(
        "td,cd->tc", grad_branch, back_attn[4], preferred_element_type=single_float
    ).astype(brain_float_half)
    head_gradient = mixed_gradient.reshape(
        token_count, KEY_VALUE_HEADS, head_group, HEAD_SIZE
    ).transpose(1, 2, 0, 3)

    def attend_back(args):
        qg, kg, vg, dg, lg = args
        scores = jnp.einsum("gsd,jd->gsj", qg, kg, preferred_element_type=single_float) * scale
        scores = jnp.where(allowed[None], scores, NEG)
        probs = jnp.exp(scores - lg)
        grad_vals = jnp.einsum(
            "gsj,gsd->jd", probs.astype(brain_float_half), dg, preferred_element_type=single_float
        )
        grad_probs = jnp.einsum("gsd,jd->gsj", dg, vg, preferred_element_type=single_float)
        inner = jnp.sum(probs * grad_probs, axis=-1, keepdims=True)
        grad_scores = (probs * (grad_probs - inner)).astype(brain_float_half)
        grad_qg = (
            jnp.einsum("gsj,jd->gsd", grad_scores, kg, preferred_element_type=single_float) * scale
        )
        grad_kg = (
            jnp.einsum("gsj,gsd->jd", grad_scores, qg, preferred_element_type=single_float) * scale
        )
        return (grad_qg, grad_kg, grad_vals)

    grad_q, key_gradient, value_gradient = lax.map(
        attend_back, (query_rows, key_rows, value_rows, head_gradient, logsum)
    )
    grad_query = inverse_rotary(
        grad_q.transpose(2, 0, 1, 3).reshape(token_count, QUERY_HEADS, HEAD_SIZE),
        cosine_table,
        sine_table,
    )
    grad_query = grad_query.reshape(token_count, QUERY_HEADS * HEAD_SIZE).astype(brain_float_half)
    key_terms = jnp.stack(
        [
            key_gradient.transpose(1, 0, 2).reshape(sequence_length, KEY_VALUE_HEADS * HEAD_SIZE),
            value_gradient.transpose(1, 0, 2).reshape(sequence_length, KEY_VALUE_HEADS * HEAD_SIZE),
        ]
    )
    key_partial_sums = lax.psum_scatter(key_terms, "ctx", scatter_dimension=1, tiled=True)
    grad_key = (
        inverse_rotary(
            key_partial_sums[0].reshape(token_count, KEY_VALUE_HEADS, HEAD_SIZE),
            cosine_table,
            sine_table,
        )
        .reshape(token_count, KEY_VALUE_HEADS * HEAD_SIZE)
        .astype(brain_float_half)
    )
    grad_value = key_partial_sums[1].astype(brain_float_half)
    grad_first = (
        jnp.einsum("tc,dc->td", grad_query, back_attn[1], preferred_element_type=single_float)
        + jnp.einsum("tc,dc->td", grad_key, back_attn[2], preferred_element_type=single_float)
        + jnp.einsum("tc,dc->td", grad_value, back_attn[3], preferred_element_type=single_float)
    )
    grad_input_norm, gain1_term = norm_back(
        grad_first, normed1, inverse1, back_attn[0].astype(single_float)
    )
    attn_terms = (
        gain1_term,
        jnp.einsum("td,tc->dc", first_input_rows, grad_query, preferred_element_type=single_float),
        jnp.einsum("td,tc->dc", first_input_rows, grad_key, preferred_element_type=single_float),
        jnp.einsum("td,tc->dc", first_input_rows, grad_value, preferred_element_type=single_float),
        grad_wout,
    )
    attn_sums = (
        lax.psum_scatter(attn_terms[0], ("dp", "ctx"), scatter_dimension=0, tiled=True),
        lax.psum_scatter(attn_terms[1], ("dp", "ctx"), scatter_dimension=0, tiled=True),
        lax.psum_scatter(attn_terms[2], ("dp", "ctx"), scatter_dimension=0, tiled=True),
        lax.psum_scatter(attn_terms[3], ("dp", "ctx"), scatter_dimension=0, tiled=True),
        lax.psum_scatter(attn_terms[4], ("dp", "ctx"), scatter_dimension=0, tiled=True),
    )
    grad_input = grad_resid + grad_input_norm
    return (
        result.astype(brain_float_half)[None],
        grad_input[None],
        attn_sums[0],
        attn_sums[1],
        attn_sums[2],
        attn_sums[3],
        attn_sums[4],
        mlp_sums[0],
        mlp_sums[1],
        mlp_sums[2],
        mlp_sums[3],
    )


def solution(mesh):
    placed = (
        P("dp", "ctx", None),
        P("dp", None),
        P("dp", "ctx", None),
        P(("dp", "ctx")),
        P(("dp", "ctx"), None),
        P(("dp", "ctx"), None),
        P(("dp", "ctx"), None),
        P(("dp", "ctx"), None),
        P(("dp", "ctx")),
        P(("dp", "ctx"), None),
        P(("dp", "ctx"), None),
        P(("dp", "ctx"), None),
    )
    return jax.shard_map(
        per_device,
        mesh=mesh,
        in_specs=placed,
        out_specs=(
            P("dp", "ctx", None),
            P("dp", "ctx", None),
            P(("dp", "ctx")),
            P(("dp", "ctx"), None),
            P(("dp", "ctx"), None),
            P(("dp", "ctx"), None),
            P(("dp", "ctx"), None),
            P(("dp", "ctx")),
            P(("dp", "ctx"), None),
            P(("dp", "ctx"), None),
            P(("dp", "ctx"), None),
        ),
        check_vma=False,
    )
```

profile of v0, /device:TPU:24, one launch (start us, length us, event | category | flops | bytes accessed | tf_op | source)
XLA Modules:
  0.0 4764.0 jit_solution(2991351565853898309)
XLA Ops:
  12.6 39.3 all-reduce.5
  52.6 12.3 all-gather.10.cloned.1.call-done
  64.8 1.5 copy.42
  67.0 53.6 %all-gather.12.cloned.1.call-done = bf16[2048,256]{1,0:T(8,128)(2,1)} async-done(((bf16[64,256]{1,0:T(8,128)(2,1)}), bf16[2048,256]{1,0:T(8,128)(2,1)}) %all-gather.12.cloned.1.call-update) | async-done | bytes 1048592 | tf_op jit(solution)/shard_map/all_gather | solution.py:81
  120.5 1.6 fusion.57
  122.2 16.4 all_gather.43
  138.9 61.5 %all-gather.8.cloned.1.call-done = bf16[2048,2048]{1,0:T(8,128)(2,1)} async-done(((bf16[64,2048]{1,0:T(8,128)(2,1)}), bf16[2048,2048]{1,0:T(8,128)(2,1)}) %all-gather.8.cloned.1.call-update) | async-done | bytes 8388624 | tf_op jit(solution)/shard_map/all_gather | solution.py:79
  200.4 12.3 copy.41
  212.7 5.8 fusion.75
  218.7 9.0 while.30
  227.7 51.5 %all-gather.14.cloned.1.call-done = bf16[2048,2048]{1,0:T(8,128)(2,1)} async-done(((bf16[64,2048]{1,0:T(8,128)(2,1)}), bf16[2048,2048]{1,0:T(8,128)(2,1)}) %all-gather.14.cloned.1.call-update) | async-done | bytes 8388624 | tf_op jit(solution)/shard_map/all_gather | solution.py:82
  279.2 4.7 multiply_reduce_fusion.3
  284.2 140.5 %all-gather.16.cloned.1.call-done = bf16[2048,5632]{1,0:T(8,128)(2,1)} async-done(((bf16[64,5632]{1,0:T(8,128)(2,1)}), bf16[2048,5632]{1,0:T(8,128)(2,1)}) %all-gather.16.cloned.1.call-update) | async-done | bytes 23068688 | tf_op jit(solution)/shard_map/all_gather | solution.py:137
  424.6 12.4 fusion.97
  437.0 133.1 %all-gather.18.cloned.1.call-done = bf16[2048,5632]{1,0:T(8,128)(2,1)} async-done(((bf16[64,5632]{1,0:T(8,128)(2,1)}), bf16[2048,5632]{1,0:T(8,128)(2,1)}) %all-gather.18.cloned.1.call-update) | async-done | bytes 23068688 | tf_op jit(solution)/shard_map/all_gather | solution.py:138
  570.1 12.3 fusion.98
  582.4 133.4 %all-gather.20.cloned.1.call-done = bf16[5632,2048]{1,0:T(8,128)(2,1)} async-done(((bf16[176,2048]{1,0:T(8,128)(2,1)}), bf16[5632,2048]{1,0:T(8,128)(2,1)}) %all-gather.20.cloned.1.call-update) | async-done | bytes 23068688 | tf_op jit(solution)/shard_map/all_gather | solution.py:139
  715.8 14.8 multiply_convert_fusion.1
  730.6 12.4 fusion.99
  743.0 13.9 multiply_reduce_fusion.1
  756.9 1.7 multiply_add_fusion
  758.6 7.1 convolution_convert_fusion
  765.6 2.0 copy.46
  767.7 27.0 while.31
  767.7 1.4 fusion.184
  769.3 0.9 multiply_reduce_fusion.6
  770.5 1.2 fusion.186
  771.6 1.0 fusion.187
  772.6 1.9 fusion.188
  774.4 1.4 fusion.184
  777.2 1.2 fusion.186
  778.4 1.0 fusion.187
  779.3 1.9 fusion.188
  781.2 1.4 fusion.184
  782.8 0.9 multiply_reduce_fusion.6
  784.0 1.2 fusion.186
  785.1 1.0 fusion.187
  786.1 1.9 fusion.188
  788.0 1.4 fusion.184
  790.7 1.2 fusion.186
  791.9 1.0 fusion.187
  792.8 1.9 fusion.188
  794.7 2.2 pad_maximum_fusion
  797.0 25.1 reduce-scatter.9.cloned.1.call-done
  823.1 1.9 fusion.81
  825.0 1.9 fusion.79
  827.0 1.4 multiply_add_fusion.1
  829.2 8.3 fusion.77
  837.8 9.2 fusion.85
  847.1 19.2 fusion.101
  866.4 19.2 fusion.102
  886.7 19.4 fusion.69
  906.1 1.0 copy-done.7
  907.2 6.4 fusion.100
  913.6 11.8 fusion.50
  926.6 1.5 fusion.64
  928.1 40.6 all-reduce.4
  969.9 2.6 fusion.63
  972.4 124.5 %reduce-scatter.15.cloned.1.call-done = f32[64,256]{1,0:T(8,128)} async-done(((f32[2048,256]{1,0:T(8,128)}), f32[64,256]{1,0:T(8,128)}) %reduce-scatter.15.cloned.1.call-update) | async-done | bytes 65552 | tf_op jit(solution)/shard_map/reduce_scatter | solution.py:262
  1096.9 368.7 %reduce-scatter.11.cloned.1.call-done = f32[64,2048]{1,0:T(8,128)} async-done(((f32[2048,2048]{1,0:T(8,128)}), f32[64,2048]{1,0:T(8,128)}) %reduce-scatter.11.cloned.1.call-update) | async-done | bytes 524304 | tf_op jit(solution)/shard_map/reduce_scatter | solution.py:260
  1465.6 365.0 %reduce-scatter.17.cloned.1.call-done = f32[64,2048]{1,0:T(8,128)} async-done(((f32[2048,2048]{1,0:T(8,128)}), f32[64,2048]{1,0:T(8,128)}) %reduce-scatter.17.cloned.1.call-update) | async-done | bytes 524304 | tf_op jit(solution)/shard_map/reduce_scatter | solution.py:263
  1830.6 975.2 %reduce-scatter.19.cloned.1.call-done = f32[64,5632]{1,0:T(8,128)} async-done(((f32[2048,5632]{1,0:T(8,128)}), f32[64,5632]{1,0:T(8,128)}) %reduce-scatter.19.cloned.1.call-update) | async-done | bytes 1441808 | tf_op jit(solution)/shard_map/reduce_scatter | solution.py:177
  2805.8 975.6 %reduce-scatter.21.cloned.1.call-done = f32[64,5632]{1,0:T(8,128)} async-done(((f32[2048,5632]{1,0:T(8,128)}), f32[64,5632]{1,0:T(8,128)}) %reduce-scatter.21.cloned.1.call-update) | async-done | bytes 1441808 | tf_op jit(solution)/shard_map/reduce_scatter | solution.py:178
  3781.4 975.6 %reduce-scatter.23.cloned.1.call-done = f32[176,2048]{1,0:T(8,128)} async-done(((f32[5632,2048]{1,0:T(8,128)}), f32[176,2048]{1,0:T(8,128)}) %reduce-scatter.23.cloned.1.call-update) | async-done | bytes 1441808 | tf_op jit(solution)/shard_map/reduce_scatter | solution.py:179
  (145 shorter events, 24.8 us)
Async XLA Ops:
  7.2 4.9 copy-start.16
  7.2 5.1 copy-start.17
  7.2 44.7 copy-start.14
  7.2 45.0 copy-start
  7.2 57.6 %all-gather.10.cloned.1.call-start = ((), (), s32[]{:S(2)}) async-start(), calls=%async_computation.9 | async-start | bytes 1081344 | tf_op jit(solution)/shard_map/all_gather | solution.py:80
  8.0 112.6 %all-gather.12.cloned.1.call-start = ((), (), s32[]{:S(2)}) async-start(), calls=%async_computation.10 | async-start | bytes 1081344 | tf_op jit(solution)/shard_map/all_gather | solution.py:81
  8.7 191.7 %all-gather.8.cloned.1.call-start = ((), (), s32[]{:S(2)}) async-start(), calls=%async_computation.8 | async-start | bytes 8650752 | tf_op jit(solution)/shard_map/all_gather | solution.py:79
  9.4 269.8 %all-gather.14.cloned.1.call-start = ((), (), s32[]{:S(2)}) async-start(), calls=%async_computation.11 | async-start | bytes 8650752 | tf_op jit(solution)/shard_map/all_gather | solution.py:82
  10.0 414.6 %all-gather.16.cloned.1.call-start = ((), (), s32[]{:S(2)}) async-start(), calls=%async_computation.12 | async-start | bytes 23789568 | tf_op jit(solution)/shard_map/all_gather | solution.py:137
  10.6 559.5 %all-gather.18.cloned.1.call-start = ((), (), s32[]{:S(2)}) async-start(), calls=%async_computation.13 | async-start | bytes 23789568 | tf_op jit(solution)/shard_map/all_gather | solution.py:138
  11.2 704.6 %all-gather.20.cloned.1.call-start = ((), (), s32[]{:S(2)}) async-start(), calls=%async_computation.14 | async-start | bytes 23789568 | tf_op jit(solution)/shard_map/all_gather | solution.py:139
  11.9 810.2 %reduce-scatter.9.cloned.1.call-start = ((), (), s32[]{:S(2)}) async-start(), calls=%async_computation.15 | async-start | bytes 1310720 | tf_op jit(solution)/shard_map/reduce_scatter | solution.py:232
  227.7 51.5 %copy-start.1 = (bf16[4,8,128,64]{2,3,1,0:T(8,128)(2,1)}, bf16[4,8,128,64]{2,3,1,0:T(8,128)(2,1)S(1)}, u32[]{:S(2)}) copy-start(bf16[4,8,128,64]{2,3,1,0:T(8,128)(2,1)S(1)} %get-tuple-element.514) | copy-start | bytes 1572868
  227.7 56.3 %copy-start.5 = (bf16[4,8,128,64]{2,3,1,0:T(8,128)(2,1)}, bf16[4,8,128,64]{2,3,1,0:T(8,128)(2,1)S(1)}, u32[]{:S(2)}) copy-start(bf16[4,8,128,64]{2,3,1,0:T(8,128)(2,1)S(1)} %get-tuple-element.103) | copy-start | bytes 1572868
  227.7 56.3 %copy-start.11 = (bf16[4,512,64]{1,2,0:T(8,128)(2,1)}, bf16[4,512,64]{1,2,0:T(8,128)(2,1)S(1)}, u32[]{:S(2)}) copy-start(bf16[4,512,64]{1,2,0:T(8,128)(2,1)S(1)} %get-tuple-element.523) | copy-start | bytes 786436
  437.0 278.8 %copy-start.9 = (bf16[1,128,2048]{2,1,0:T(8,128)(2,1)S(1)}, bf16[1,128,2048]{2,1,0:T(8,128)(2,1)}, u32[]{:S(2)}) copy-start(bf16[1,128,2048]{2,1,0:T(8,128)(2,1)} %param.18) | copy-start | bytes 1572868
  730.6 12.4 copy-start.3
  767.7 1.6 copy-start.2
  774.4 1.6 copy-start.2
  781.2 1.6 copy-start.2
  788.0 1.6 copy-start.2
  797.0 175.5 %reduce-scatter.13.cloned.1.call-start = ((), (), s32[]{:S(2)}) async-start(), calls=%async_computation.17 | async-start | bytes 2162688 | tf_op jit(solution)/shard_map/reduce_scatter | solution.py:261
  823.0 2.0 copy-start.13
  825.0 272.0 %reduce-scatter.15.cloned.1.call-start = ((), (), s32[]{:S(2)}) async-start(), calls=%async_computation.18 | async-start | bytes 2162688 | tf_op jit(solution)/shard_map/reduce_scatter | solution.py:262
  826.9 638.7 %reduce-scatter.11.cloned.1.call-start = ((), (), s32[]{:S(2)}) async-start(), calls=%async_computation.16 | async-start | bytes 17301504 | tf_op jit(solution)/shard_map/reduce_scatter | solution.py:260
  828.4 0.8 copy-start.6
  837.5 993.1 %reduce-scatter.17.cloned.1.call-start = ((), (), s32[]{:S(2)}) async-start(), calls=%async_computation.19 | async-start | bytes 17301504 | tf_op jit(solution)/shard_map/reduce_scatter | solution.py:263
  847.0 1958.7 %reduce-scatter.19.cloned.1.call-start = ((), (), s32[]{:S(2)}) async-start(), calls=%async_computation.20 | async-start | bytes 47579136 | tf_op jit(solution)/shard_map/reduce_scatter | solution.py:177
  866.4 2915.1 %reduce-scatter.21.cloned.1.call-start = ((), (), s32[]{:S(2)}) async-start(), calls=%async_computation.21 | async-start | bytes 47579136 | tf_op jit(solution)/shard_map/reduce_scatter | solution.py:178
  885.7 1.0 copy-start.10
  885.7 3871.4 %reduce-scatter.23.cloned.1.call-start = ((), (), s32[]{:S(2)}) async-start(), calls=%async_computation.22 | async-start | bytes 47579136 | tf_op jit(solution)/shard_map/reduce_scatter | solution.py:179
  906.1 1.0 copy-start.7
  907.2 6.4 copy-start.4
  913.6 11.8 copy-start.8
  925.4 1.2 copy-start.12
  926.6 1.5 copy-start.15
Sparse Core Ops, SparseCore 0:
  11.0 53.7 all-gather.9
  67.8 52.7 all-gather.11
  123.5 76.8 all-gather.7
  203.2 75.9 all-gather.13
  281.9 142.6 all-gather.15
  427.3 142.7 all-gather.17
  573.0 142.7 all-gather.19
  797.1 24.9 reduce-scatter.8
  825.1 133.0 reduce-scatter.12
  960.8 136.0 reduce-scatter.14
  1099.9 365.6 reduce-scatter.10
  1468.4 362.1 reduce-scatter.16
  1833.6 972.1 reduce-scatter.18
  2808.6 972.7 reduce-scatter.20
  3784.2 972.7 reduce-scatter.22
where the time goes:
time: 4770 us; the launch traced here: 4760 us
  waiting for transfers between devices  4400 us (92%)
  matrix products  215 us (5%)
  blocking collectives  96.3 us (2%)
    reduce_scatter x1, waiting for transfers between devices, per_device(): lax.psum_scatter(mlp_terms[2], ('dp', 'ctx'), scatter_dimension=0, tiled=...  976 us
    reduce_scatter x1, waiting for transfers between devices, per_device(): lax.psum_scatter(mlp_terms[3], ('dp', 'ctx'), scatter_dimension=0, tiled=...  976 us
    reduce_scatter x1, waiting for transfers between devices, per_device(): lax.psum_scatter(mlp_terms[1], ('dp', 'ctx'), scatter_dimension=0, tiled=...  975 us
    reduce_scatter x1, waiting for transfers between devices, per_device(): lax.psum_scatter(attn_terms[1], ('dp', 'ctx'), scatter_dimension=0, tiled...  369 us
    reduce_scatter x1, waiting for transfers between devices, per_device(): lax.psum_scatter(attn_terms[4], ('dp', 'ctx'), scatter_dimension=0, tiled...  365 us
    all_gather x1, waiting for transfers between devices, per_device(): lax.all_gather(w_gate, ('dp', 'ctx'), axis=0, tiled=True)  140 us
    all_gather x1, waiting for transfers between devices, per_device(): lax.all_gather(w_down, ('dp', 'ctx'), axis=0, tiled=True)  133 us
    all_gather x1, waiting for transfers between devices, per_device(): lax.all_gather(w_up, ('dp', 'ctx'), axis=0, tiled=True)  133 us
  transfers between devices with their start and end apart: 15, of which 14 were waited for; matrix products, arithmetic and copies ran while one was open for 3% of the time, Pallas kernels for 0%

commit v1 on v0

v1 whole, which is shorter than its diff:
```python
import functools

import jax
import jax.numpy as jnp
from jax import lax
from jax.sharding import PartitionSpec as P

QUERY_HEADS = 32
KEY_VALUE_HEADS = 4
HEAD_SIZE = 64
EPS = 1e-05
NEG = -1e30
F32 = jnp.float32
BF16 = jnp.bfloat16


def rotate(values, cosine, sine):
    half = values.shape[-1] // 2
    first, second = values[..., :half], values[..., half:]
    return jnp.concatenate(
        [first * cosine - second * sine, second * cosine + first * sine], axis=-1
    )


def dot(left, right):
    return jnp.dot(left, right, preferred_element_type=F32)


def dot_nt(left, right):
    return lax.dot_general(left, right, (((1,), (1,)), ((), ())), preferred_element_type=F32)


def dot_tn(left, right):
    return lax.dot_general(left, right, (((0,), (0,)), ((), ())), preferred_element_type=F32)


def swap(value, bit, size):
    return lax.ppermute(value, "dp", [(i, i ^ bit) for i in range(size)])


def swap_cores(value, size):
    paired = value.reshape(size // 2, 2, *value.shape[1:])
    return swap(paired[:, ::-1].reshape(value.shape), 1, size)


def row_parts(rows, parts):
    units = rows // 16
    edges = [units * j // parts * 16 for j in range(parts)] + [rows]
    return [(edges[j], edges[j + 1]) for j in range(parts)]


def gather_dp(rows, size):
    bits = [1 << j for j in range(1, size.bit_length() - 1)]
    cuts = row_parts(rows.shape[0], len(bits))
    held = [{0: rows[a:b]} for a, b in cuts]
    for step in range(len(bits)):
        for j, pieces in enumerate(held):
            bit = bits[(j + step) % len(bits)]
            for rel, piece in list(pieces.items()):
                pieces[rel ^ bit] = swap(piece, bit, size)
    for pieces in held:
        for rel, piece in list(pieces.items()):
            pieces[rel ^ 1] = swap(piece, 1, size)
    return [jnp.concatenate([pieces[rel] for pieces in held]) for rel in range(size)]


def scatter_dp(terms, size):
    bits = [1 << j for j in range(1, size.bit_length() - 1)]
    cuts = row_parts(terms.shape[1], len(bits))

    def add(own, came):
        return own.astype(F32) + came.astype(F32)

    summed = []
    for j, (a, b) in enumerate(cuts):
        acc = {
            rel: add(terms[rel, a:b], swap(terms[rel ^ 1, a:b], 1, size))
            for rel in range(0, size, 2)
        }
        for step in reversed(range(len(bits))):
            bit = bits[(j + step) % len(bits)]
            acc = {
                rel: add(acc[rel], swap(acc[rel ^ bit].astype(BF16), bit, size))
                for rel in acc
                if not rel & bit
            }
        summed.append(acc[0])
    return jnp.concatenate(summed)


def norm_back(grad_in, normed, inverse, gain):
    grad_normed = grad_in * gain
    return inverse * (
        grad_normed - normed * jnp.mean(grad_normed * normed, axis=-1, keepdims=True)
    )


def per_device(
    n,
    c,
    tokens,
    segment_ids,
    out_grad,
    gain_attn,
    w_query,
    key_weight,
    value_weight,
    w_out,
    gain_mlp,
    w_gate,
    w_up,
    w_down,
):
    t, width = tokens.shape[1:]
    length = segment_ids.shape[1]
    block = w_query.shape[0]
    ff = w_gate.shape[1]
    heads = QUERY_HEADS // n
    group = QUERY_HEADS // KEY_VALUE_HEADS
    q_cols, f_cols = heads * HEAD_SIZE, ff // n
    scale = HEAD_SIZE**-0.5
    me, place_z = lax.axis_index("dp"), lax.axis_index("ctx")
    core = me % 2

    def to_block_order(v):
        return v.reshape(t, n, c, block).transpose(0, 2, 1, 3).reshape(t, width)

    def from_block_order(v):
        return v.reshape(t, c, n, block).transpose(0, 2, 1, 3).reshape(t, width)

    pieces = []
    for d in range(n):
        g = d * heads // group
        kv = value_weight if d % 2 else key_weight
        pieces.append(
            jnp.concatenate(
                [
                    w_query[:, d * q_cols : (d + 1) * q_cols],
                    kv[:, g * HEAD_SIZE : (g + 1) * HEAD_SIZE],
                ],
                axis=1,
            )
        )
    w_attn = lax.all_to_all(jnp.stack(pieces), "dp", 0, 0).reshape(n * block, -1)
    w_attn = lax.all_gather(w_attn, "ctx", axis=0, tiled=True)
    wo = lax.all_gather(w_out, "ctx", axis=0, tiled=True)
    w_pair = jnp.concatenate(
        [w_gate.reshape(block, n, f_cols), w_up.reshape(block, n, f_cols)], axis=2
    ).transpose(1, 0, 2)
    w_pair = lax.all_to_all(w_pair, "dp", 0, 0).reshape(n * block, 2 * f_cols)
    w_pair = lax.all_gather(w_pair, "ctx", axis=0, tiled=True)
    wd = lax.all_gather(w_down, "ctx", axis=0, tiled=True)
    gains = lax.all_gather(
        jnp.stack([gain_attn, gain_mlp]), ("ctx", "dp"), axis=1, tiled=True
    ).astype(F32)
    gain1, gain2 = gains[0], gains[1]
    gain2_plain = gain2.reshape(c, n, block).transpose(1, 0, 2).reshape(width)

    segs = segment_ids
    for bit in [1 << j for j in range(n.bit_length() - 1)]:
        segs = jnp.concatenate([segs, swap(segs, bit, n)])
    local_idx = place_z * t + jnp.arange(t, dtype=jnp.int32)
    local_seg = lax.dynamic_slice_in_dim(segs, place_z * t, t, axis=1)
    before = jnp.sum((segs[:, None, :] < local_seg[:, :, None]).astype(jnp.int32), axis=2)
    place = (local_idx[None] - before).astype(F32)
    freq = 10000.0 ** (-jnp.arange(HEAD_SIZE // 2, dtype=F32) / (HEAD_SIZE // 2))
    angle = place.reshape(n * t)[:, None] * freq[None, :]
    cosine, sine = jnp.cos(angle), jnp.sin(angle)
    kv_cosine = jnp.where(core == 0, cosine, 1.0)
    kv_sine = jnp.where(core == 0, sine, 0.0)
    key_idx = (place_z * t + jnp.arange(length, dtype=jnp.int32)) % length
    key_seg = lax.dynamic_slice_in_dim(
        jnp.concatenate([segs, segs], axis=1), place_z * t, length, axis=1
    )
    allowed = (key_idx[None, None, :] <= local_idx[None, :, None]) & (
        key_seg[:, None, :] == local_seg[:, :, None]
    )

    rows = jnp.concatenate(gather_dp(to_block_order(tokens[0]), n)).astype(F32)
    inverse1 = lax.rsqrt(jnp.mean(rows * rows, axis=-1, keepdims=True) + EPS)
    first_in = (rows * inverse1 * gain1).astype(BF16)
    projected = dot(first_in, w_attn)
    queries = rotate(
        projected[:, :q_cols].reshape(n * t, heads, HEAD_SIZE), cosine[:, None], sine[:, None]
    ).astype(BF16)
    queries = queries.reshape(n, t, heads, HEAD_SIZE).transpose(0, 2, 1, 3)
    kv_own = rotate(projected[:, q_cols:], kv_cosine, kv_sine).astype(BF16).reshape(n, t, -1)
    kv_all = [kv_own] + [
        lax.ppermute(kv_own, "ctx", [(i, (i - j) % c) for i in range(c)]) for j in range(1, c)
    ]
    kv_all = jnp.concatenate(kv_all, axis=1)
    kv_other = swap_cores(kv_all, n)
    keys = jnp.where(core == 0, kv_all, kv_other)
    values = jnp.where(core == 0, kv_other, kv_all)

    scores = jnp.einsum("nhtd,nld->nhtl", queries, keys, preferred_element_type=F32) * scale
    scores = jnp.where(allowed[:, None], scores, NEG)
    top = jnp.max(scores, axis=-1, keepdims=True)
    expo = jnp.exp(scores - top)
    total = jnp.sum(expo, axis=-1, keepdims=True)
    probs = (expo / total).astype(BF16)
    logsum = top + jnp.log(total)
    mixed = jnp.einsum("nhtl,nld->nhtd", probs, values, preferred_element_type=F32)
    mixed = mixed.transpose(0, 2, 1, 3).reshape(n * t, q_cols).astype(BF16)
    x = tokens[0].astype(F32)
    resid = x + scatter_dp(dot(mixed, wo).astype(BF16).reshape(n, t, width), n)

    inverse2 = lax.rsqrt(jnp.mean(resid * resid, axis=-1, keepdims=True) + EPS)
    normed2 = resid * inverse2
    second_in = (normed2 * gain2_plain).astype(BF16)
    second_in = jnp.concatenate(gather_dp(to_block_order(second_in), n))
    dy_local = out_grad[0]
    dy = jnp.concatenate(gather_dp(dy_local, n))
    both = dot(second_in, w_pair)
    gate, up = both[:, :f_cols], both[:, f_cols:]
    sig = jax.nn.sigmoid(gate)
    swish = gate * sig
    hidden = (swish * up).astype(BF16)
    grad_hidden = dot_nt(dy, wd)
    grad_pair = jnp.concatenate(
        [
            (grad_hidden * up * sig * (1.0 + gate * (1.0 - sig))).astype(BF16),
            (grad_hidden * swish).astype(BF16),
        ],
        axis=1,
    )
    grad_second = from_block_order(
        scatter_dp(dot_nt(grad_pair, w_pair).astype(BF16).reshape(n, t, width), n)
    )
    result = resid + scatter_dp(dot(hidden, wd).astype(BF16).reshape(n, t, width), n)
    grad_down = lax.psum_scatter(
        dot_tn(hidden, dy).astype(BF16), "ctx", scatter_dimension=0, tiled=True
    )
    pair_sum = lax.psum_scatter(
        dot_tn(second_in, grad_pair).astype(BF16), "ctx", scatter_dimension=0, tiled=True
    )
    pair_sum = lax.all_to_all(pair_sum.reshape(n, block, 2 * f_cols), "dp", 0, 0).astype(F32)
    grad_gate = pair_sum[:, :, :f_cols].transpose(1, 0, 2).reshape(block, ff)
    grad_up = pair_sum[:, :, f_cols:].transpose(1, 0, 2).reshape(block, ff)
    grad_gain_mlp = jnp.sum(
        w_gate.astype(F32) * grad_gate + w_up.astype(F32) * grad_up, axis=1
    ) / gain_mlp.astype(F32)

    grad_resid = dy_local.astype(F32) + norm_back(grad_second, normed2, inverse2, gain2_plain)
    grad_branch = jnp.concatenate(gather_dp(grad_resid.astype(BF16), n))
    grad_wout = lax.psum_scatter(
        dot_tn(mixed, grad_branch).astype(BF16), "ctx", scatter_dimension=0, tiled=True
    )
    grad_mixed = dot_nt(grad_branch, wo).astype(BF16)
    grad_mixed = grad_mixed.reshape(n, t, heads, HEAD_SIZE).transpose(0, 2, 1, 3)
    probs = jnp.exp(scores - logsum)
    grad_values = jnp.einsum(
        "nhtl,nhtd->nld", probs.astype(BF16), grad_mixed, preferred_element_type=F32
    )
    grad_probs = jnp.einsum("nhtd,nld->nhtl", grad_mixed, values, preferred_element_type=F32)
    inner = jnp.sum(probs * grad_probs, axis=-1, keepdims=True)
    grad_scores = (probs * (grad_probs - inner)).astype(BF16)
    grad_q = jnp.einsum("nhtl,nld->nthd", grad_scores, keys, preferred_element_type=F32) * scale
    grad_keys = (
        jnp.einsum("nhtl,nhtd->nld", grad_scores, queries, preferred_element_type=F32) * scale
    )
    grad_q = rotate(
        grad_q.reshape(n * t, heads, HEAD_SIZE), cosine[:, None], -sine[:, None]
    ).reshape(n * t, q_cols)
    kept = jnp.where(core == 0, grad_keys, grad_values)
    sent = jnp.where(core == 0, grad_values, grad_keys)
    grad_kv = (kept + swap_cores(sent, n)).reshape(n, c, t, HEAD_SIZE)
    total_kv = grad_kv[:, 0]
    for j in range(1, c):
        total_kv = total_kv + lax.ppermute(
            grad_kv[:, j].astype(BF16), "ctx", [(i, (i + j) % c) for i in range(c)]
        ).astype(F32)
    grad_kv = rotate(total_kv.reshape(n * t, HEAD_SIZE), kv_cosine, -kv_sine)
    grad_attn = jnp.concatenate([grad_q, grad_kv], axis=1).astype(BF16)
    grad_first = scatter_dp(dot_nt(grad_attn, w_attn).astype(BF16).reshape(n, t, width), n)
    attn_sum = lax.psum_scatter(
        dot_tn(first_in, grad_attn).astype(BF16), "ctx", scatter_dimension=0, tiled=True
    )
    attn_sum = lax.all_to_all(attn_sum.reshape(n, block, -1), "dp", 0, 0).astype(F32)
    grad_query = attn_sum[:, :, :q_cols].transpose(1, 0, 2).reshape(block, -1)
    kv_sum = attn_sum[:, :, q_cols:].reshape(KEY_VALUE_HEADS, -1, 2, block, HEAD_SIZE).sum(axis=1)
    grad_key = kv_sum[:, 0].transpose(1, 0, 2).reshape(block, -1)
    grad_value = kv_sum[:, 1].transpose(1, 0, 2).reshape(block, -1)
    grad_gain_attn = (
        jnp.sum(w_query.astype(F32) * grad_query, axis=1)
        + jnp.sum(key_weight.astype(F32) * grad_key, axis=1)
        + jnp.sum(value_weight.astype(F32) * grad_value, axis=1)
    ) / gain_attn.astype(F32)
    grad_input = grad_resid + from_block_order(
        norm_back(grad_first, (rows * inverse1)[:t], inverse1[:t], gain1)
    )
    return (
        result.astype(BF16)[None],
        grad_input[None],
        grad_gain_attn,
        grad_query,
        grad_key,
        grad_value,
        grad_wout.astype(F32),
        grad_gain_mlp,
        grad_gate,
        grad_up,
        grad_down.astype(F32),
    )


def solution(mesh):
    n, c = mesh.shape["dp"], mesh.shape["ctx"]
    rows = P("dp", "ctx", None)
    weight, gain = P(("dp", "ctx"), None), P(("dp", "ctx"))
    return jax.shard_map(
        functools.partial(per_device, n, c),
        mesh=mesh,
        in_specs=(rows, P("dp", None), rows, gain, weight, weight, weight, weight, gain)
        + (weight,) * 3,
        out_specs=(rows, rows, gain, weight, weight, weight, weight, gain) + (weight,) * 3,
        check_vma=False,
    )
```

time: 4770 us -> 804 us (0.17)
  waiting for transfers between devices: 4400 us -> 245 us
  local copies, waits for them, and re-layouts: 22.2 us -> 205 us
  matrix products: 215 us -> 92.3 us
  starting transfers between devices: 1.06 us -> 95.5 us
  other arithmetic: 13.5 us -> 71.2 us
    reduce_scatter x8 -> x4, waiting for transfers between devices: 3810 us -> 30.9 us  [the longest x1 30.9 us: per_device(): lax.psum_scatter(dot_tn(hidden, dy).astype(BF16), 'ctx', scatter_dimensio...]
    all_gather x7 -> x4, waiting for transfers between devices: 586 us -> 0.05 us  [the longest x1 0.02 us: per_device(): wo = lax.all_gather(w_out, 'ctx', axis=0, tiled=True)]
    ppermute x0 -> x123, waiting for transfers between devices: none -> 212 us  [the longest x117 181 us: swap(): return lax.ppermute(value, 'dp', [(i, i ^ bit) for i in range(size)])]
    unnamed x40 -> x299, local copies, waits for them, and re-layouts: 4.98 us -> 134 us
    dot_general x49 -> x18, matrix products: 215 us -> 92.3 us  [the longest x4 26 us: dot_tn(): lax.dot_general(left, right, (((0,), (0,)), ((), ())), preferred_element_...]
    ppermute x0 -> x123, starting transfers between devices: none -> 87.4 us  [the longest x117 65.9 us: swap(): return lax.ppermute(value, 'dp', [(i, i ^ bit) for i in range(size)])]
    unnamed x2 -> x0, blocking collectives: 79.8 us -> none
  transfers between devices with their start and end apart: 15 -> 133, of which waited for: 14 -> 41; matrix products, arithmetic and copies ran while one was open for 3% -> 37% of each run, Pallas kernels for 0% -> 0%
where the time goes in v1:
time: 804 us; the launch traced here: 792 us
  waiting for transfers between devices  245 us (30%)
  local copies, waits for them, and re-layouts  205 us (25%)
  starting transfers between devices  95.5 us (12%)
  matrix products  92.3 us (11%)
  other arithmetic  71.2 us (9%)
  blocking collectives  66.2 us (8%)
  between operations  16.5 us (2%)
    ppermute x117, waiting for transfers between devices, swap(): return lax.ppermute(value, 'dp', [(i, i ^ bit) for i in range(size)])  181 us
    unnamed x299, local copies, waits for them, and re-layouts  134 us
    ppermute x117, starting transfers between devices, swap(): return lax.ppermute(value, 'dp', [(i, i ^ bit) for i in range(size)])  65.9 us
    all_gather x1, blocking collectives, per_device(): lax.all_gather(jnp.stack([gain_attn, gain_mlp]), ('ctx', 'dp'), axis=1, t...  31.6 us
    reduce_scatter x1, waiting for transfers between devices, per_device(): lax.psum_scatter(dot_tn(hidden, dy).astype(BF16), 'ctx', scatter_dimensio...  30.9 us
    dot_general x4, matrix products, dot_tn(): lax.dot_general(left, right, (((0,), (0,)), ((), ())), preferred_element_...  26 us
    dot_general x4, matrix products, dot_nt(): lax.dot_general(left, right, (((1,), (1,)), ((), ())), preferred_element_...  24.5 us
    all_to_all x1, blocking collectives, per_device(): w_pair = lax.all_to_all(w_pair, 'dp', 0, 0).reshape(n * block, 2 * f_cols)  22.7 us
  transfers between devices with their start and end apart: 133, of which 41 were waited for; matrix products, arithmetic and copies ran while one was open for 37% of the time, Pallas kernels for 0%

profile of v1, /device:TPU:24, one launch (start us, length us, event | category | flops | bytes accessed | tf_op | source)
XLA Modules:
  0.0 791.7 jit_solution(7876911905324241217)
XLA Ops:
  10.1 12.0 %all_to_all.20 = bf16[8,64,320]{2,1,0:T(8,128)(2,1)} all-to-all(bf16[8,64,320]{2,1,0:T(8,128)(2,1)S(1)} %constant_dynamic-update-slice_fusion.16), channel_id=1, replica_groups=mesh['dp'=8,'ctx'=4] {'dp'}, dimensions={0} | all-to-all | bytes 655360 | tf_op jit(solution)/shard_map/all_to_all | solution.py:144
  26.1 22.7 %all_to_all.21 = bf16[8,64,1408]{2,1,0:T(8,128)(2,1)} all-to-all(bf16[8,64,1408]{2,1,0:T(8,128)(2,1)S(1)} %copy.347), channel_id=1, replica_groups=mesh['dp'=8,'ctx'=4] {'dp'}, dimensions={0} | all-to-all | bytes 2883584 | tf_op jit(solution)/shard_map/all_to_all | solution.py:150
  57.5 31.6 %all-gather = bf16[32,64,2]{1,2,0:T(2,128)(2,1)S(1)} all-gather(bf16[1,64,2]{1,2,0:T(2,128)(2,1)S(1)} %maximum_bitcast_fusion.12), channel_id=1, replica_groups=mesh['dp'=8,'ctx'=4] {'ctx','dp'}, dimensions={0}, use_global_device_ids=true | all-gather | bytes 8448 | tf_op jit(solution)/shard_map/all_gather | solution.py:153
  93.7 3.5 collective-permute-start.2
  114.2 4.7 collective-permute-done.66
  145.6 3.2 fusion
  148.8 4.4 fusion.8
  154.6 7.0 collective-permute-start.18
  164.6 3.6 collective-permute-done.17
  168.3 8.9 %collective-permute-done.18 = bf16[8,128,64]{1,2,0:T(8,128)(2,1)S(1)} collective-permute-done((bf16[8,128,64]{1,2,0:T(8,128)(2,1)S(1)}, bf16[8,128,64]{1,2,0:T(8,128)(2,1)S(1)}, u32[]{:S(2)}, u32[]{:S(2)}) %collective-permute-start.18) | collective-permute-done | bytes 131104 | tf_op jit(solution)/shard_map/ppermute | solution.py:189
  179.4 2.8 rev.6
  185.8 3.2 fusion.118
  193.0 3.0 fusion.15
  196.4 2.7 convolution_convert_fusion.4
  236.0 12.5 %collective-permute-done.26 = bf16[64,2048]{0,1:T(8,128)(2,1)S(1)} collective-permute-done((bf16[64,2048]{0,1:T(8,128)(2,1)S(1)}, bf16[64,2048]{0,1:T(8,128)(2,1)S(1)}, u32[]{:S(2)}, u32[]{:S(2)}) %collective-permute-start.26) | collective-permute-done | bytes 262176 | tf_op jit(solution)/shard_map/ppermute | solution.py:38
  251.8 11.5 %collective-permute-done.33 = bf16[64,2048]{0,1:T(8,128)(2,1)S(1)} collective-permute-done((bf16[64,2048]{0,1:T(8,128)(2,1)S(1)}, bf16[64,2048]{0,1:T(8,128)(2,1)S(1)}, u32[]{:S(2)}, u32[]{:S(2)}) %collective-permute-start.33) | collective-permute-done | bytes 262176 | tf_op jit(solution)/shard_map/ppermute | solution.py:38
  264.6 19.5 %collective-permute-done.27 = bf16[64,2048]{0,1:T(8,128)(2,1)S(1)} collective-permute-done((bf16[64,2048]{0,1:T(8,128)(2,1)S(1)}, bf16[64,2048]{0,1:T(8,128)(2,1)S(1)}, u32[]{:S(2)}, u32[]{:S(2)}) %collective-permute-start.27) | collective-permute-done | bytes 262176 | tf_op jit(solution)/shard_map/ppermute | solution.py:38
  287.8 2.5 copy.345
  294.5 2.5 copy.346
  310.5 5.8 collective-permute-done.42
  327.6 11.7 %fusion.119 = f32[1024,1408]{1,0:T(8,128)} fusion(bf16[1024,2048]{1,0:T(8,128)(2,1)} %constant_dynamic-update-slice_fusion.26, bf16[2048,1408]{1,0:T(8,128)(2,1)} %all-gather.10.cloned.1.call-done), kind=kOutput, calls=%fused_computation.340 | convolution fusion | flops 5905580032 | bytes 15728640 | tf_op jit(solution)/shard_map/dot_general | solution.py:26
  339.4 10.3 %multiply_convert_fusion.3 = (bf16[1024,704]{1,0:T(8,128)(2,1)S(1)}, bf16[1024,704]{1,0:T(8,128)(2,1)S(1)}, bf16[1024,704]{1,0:T(8,128)(2,1)}) fusion(f32[1024,1408]{1,0:T(8,128)} %fusion.119, bf16[1024,2048]{1,0:T(8,128)(2,1)} %constant_dynamic-update-slice_fusion.42, bf16[704,2048]{1,0:T(8,128)(2,1)} %all-gather.12.cloned.1.call-done), kind=kOutput, calls=%fused_computation.22 | convolution fusion | flops 2963603456 | bytes 17170432 | tf_op jit(solution)/shard_map/dot_general | solution.py:30
  349.7 7.1 convolution_convert_fusion.2
  399.7 12.5 %collective-permute-done.82 = bf16[64,2048]{0,1:T(8,128)(2,1)S(1)} collective-permute-done((bf16[64,2048]{0,1:T(8,128)(2,1)S(1)}, bf16[64,2048]{0,1:T(8,128)(2,1)S(1)}, u32[]{:S(2)}, u32[]{:S(2)}) %collective-permute-start.82) | collective-permute-done | bytes 262176 | tf_op jit(solution)/shard_map/ppermute | solution.py:38
  415.6 11.5 %collective-permute-done.89 = bf16[64,2048]{0,1:T(8,128)(2,1)S(1)} collective-permute-done((bf16[64,2048]{0,1:T(8,128)(2,1)S(1)}, bf16[64,2048]{0,1:T(8,128)(2,1)S(1)}, u32[]{:S(2)}, u32[]{:S(2)}) %collective-permute-start.89) | collective-permute-done | bytes 262176 | tf_op jit(solution)/shard_map/ppermute | solution.py:38
  428.2 19.3 %collective-permute-done.83 = bf16[64,2048]{0,1:T(8,128)(2,1)S(1)} collective-permute-done((bf16[64,2048]{0,1:T(8,128)(2,1)S(1)}, bf16[64,2048]{0,1:T(8,128)(2,1)S(1)}, u32[]{:S(2)}, u32[]{:S(2)}) %collective-permute-start.83) | collective-permute-done | bytes 262176 | tf_op jit(solution)/shard_map/ppermute | solution.py:38
  456.2 10.8 %collective-permute-done.93 = bf16[64,2048]{0,1:T(8,128)(2,1)S(1)} collective-permute-done((bf16[64,2048]{0,1:T(8,128)(2,1)S(1)}, bf16[64,2048]{0,1:T(8,128)(2,1)S(1)}, u32[]{:S(2)}, u32[]{:S(2)}) %collective-permute-start.93) | collective-permute-done | bytes 262176 | tf_op jit(solution)/shard_map/ppermute | solution.py:38
  467.8 7.7 collective-permute-done.94
  475.8 2.8 collective-permute-done.97
  479.2 7.3 collective-permute-done.101
  490.8 9.8 %concatenate.178 = bf16[1024,2048]{0,1:T(8,128)(2,1)} concatenate(bf16[128,2048]{0,1:T(8,128)(2,1)S(1)} %fusion.19, bf16[64,2048]{0,1:T(8,128)(2,1)} %copy-done.47, bf16[64,2048]{0,1:T(8,128)(2,1)} %copy-done.48, bf16[64,2048]{0,1:T(8,128)(2,1)} %copy-done.43, bf16[64,2048]{0,1:T(8,128)(2,1)} %copy-done.45, bf16[64,2048]{0,1:T(8,128)(2,1)} %copy-done.52, ...), dimensions={0} | concatenate | bytes 8388608 | tf_op jit(solution)/shard_map/concatenate | solution.py:245
  500.6 4.6 convolution_convert_fusion.8
  506.6 5.8 multiply_reduce_fusion
  516.6 2.7 broadcast_select_fusion
  521.5 4.5 convolution_convert_fusion.7
  526.0 3.8 fusion.13
  531.0 2.6 select_add_fusion
  533.5 2.5 reshape.522
  538.1 8.1 %collective-permute-start.106 = (bf16[8,128,64]{1,0,2:T(8,128)(2,1)S(1)}, bf16[8,128,64]{1,0,2:T(8,128)(2,1)S(1)}, u32[]{:S(2)}, u32[]{:S(2)}) collective-permute-start(bf16[8,128,64]{1,0,2:T(8,128)(2,1)S(1)} %get-tuple-element.129), channel_id=1, source_target_pairs={{0,1},{1,2},{2,3},{3,0},{4,5},{5,6},{6,7},{7,4},{8,9},{9,10},{10,1... | collective-permute-start | bytes 393224 | tf_op jit(solution)/shard_map/ppermute | solution.py:270
  546.2 6.4 collective-permute-start.107
  554.6 4.2 collective-permute-done.106
  558.8 13.9 %collective-permute-done.107 = bf16[8,128,64]{1,0,2:T(8,128)(2,1)S(1)} collective-permute-done((bf16[8,128,64]{1,0,2:T(8,128)(2,1)S(1)}, bf16[8,128,64]{1,0,2:T(8,128)(2,1)S(1)}, u32[]{:S(2)}, u32[]{:S(2)}) %collective-permute-start.107) | collective-permute-done | bytes 131104 | tf_op jit(solution)/shard_map/ppermute | solution.py:270
  573.4 2.8 convolution_convert_fusion.6
  576.3 11.2 %convolution_convert_fusion = bf16[2048,1408]{1,0:T(8,128)(2,1)} fusion(bf16[1024,2048]{1,0:T(8,128)(2,1)} %constant_dynamic-update-slice_fusion.26, bf16[1024,704]{1,0:T(8,128)(2,1)} %copy-done.96, bf16[1024,704]{1,0:T(8,128)(2,1)} %copy-done.95), kind=kOutput, calls=%fused_computation.10 | convolution fusion | flops 5914230784 | bytes 12845056 | tf_op jit(solution)/shard_map/dot_general | solution.py:34
  587.6 6.3 convert_multiply_fusion
  593.8 3.8 convolution_convert_fusion.3
  601.4 7.6 convolution_convert_fusion.5
  642.3 2.4 convolution_convert_fusion.1
  645.5 2.5 fusion.36
  653.8 4.7 collective-permute-done.114
  659.2 2.3 collective-permute-done.61
  664.4 3.4 collective-permute-done.111
  671.8 7.3 collective-permute-done.51
  679.0 13.3 %collective-permute-done.55 = bf16[64,2048]{0,1:T(8,128)(2,1)S(1)} collective-permute-done((bf16[64,2048]{0,1:T(8,128)(2,1)S(1)}, bf16[64,2048]{0,1:T(8,128)(2,1)S(1)}, u32[]{:S(2)}, u32[]{:S(2)}) %collective-permute-start.55) | collective-permute-done | bytes 262176 | tf_op jit(solution)/shard_map/ppermute | solution.py:38
  694.1 5.0 collective-permute-done.121
  712.3 3.5 all-to-all-start.2
  715.7 2.6 subtract_multiply_fusion
  718.3 2.6 copy.391
  720.9 2.5 copy.392
  724.0 4.3 all-to-all-start.3
  728.3 4.2 fusion.17
  732.5 2.6 copy.400
  738.8 30.9 %reduce-scatter.11.cloned.1.call-done = bf16[176,2048]{1,0:T(8,128)(2,1)} async-done(((bf16[704,2048]{1,0:T(8,128)(2,1)}), bf16[176,2048]{1,0:T(8,128)(2,1)}) %reduce-scatter.11.cloned.1.call-update) | async-done | bytes 720912 | tf_op jit(solution)/shard_map/reduce_scatter | solution.py:231
  769.7 2.4 convert_element_type.796
  (684 shorter events, 310.1 us)
Async XLA Ops:
  7.2 141.6 %all-gather.6.cloned.1.call-start = ((), (), s32[]{:S(2)}) async-start(), calls=%async_computation.8 | async-start | bytes 1966080 | tf_op jit(solution)/shard_map/all_gather | solution.py:145
  22.1 174.3 %all-gather.8.cloned.1.call-start = ((), (), s32[]{:S(2)}) async-start(), calls=%async_computation.9 | async-start | bytes 1310720 | tf_op jit(solution)/shard_map/all_gather | solution.py:146
  22.9 304.8 %all-gather.10.cloned.1.call-start = ((), (), s32[]{:S(2)}) async-start(), calls=%async_computation.10 | async-start | bytes 7208960 | tf_op jit(solution)/shard_map/all_gather | solution.py:151
  48.8 290.5 %all-gather.12.cloned.1.call-start = ((), (), s32[]{:S(2)}) async-start(), calls=%async_computation.11 | async-start | bytes 3604480 | tf_op jit(solution)/shard_map/all_gather | solution.py:152
  50.7 51.9 %collective-permute-start.3 = (bf16[64,2048]{1,0:T(8,128)(2,1)S(1)}, bf16[64,2048]{1,0:T(8,128)(2,1)S(1)}, u32[]{:S(2)}, u32[]{:S(2)}) collective-permute-start(bf16[64,2048]{1,0:T(8,128)(2,1)S(1)} %slice.366), channel_id=1, source_target_pairs={{0,4},{4,0},{8,12},{12,8},{16,20},{20,16},{24,28},{28,24},{1,5},{5... | collective-permute-start | bytes 786440 | tf_op jit(solution)/shard_map/ppermute | solution.py:38
  50.7 53.4 %collective-permute-start.5 = (bf16[64,2048]{1,0:T(8,128)(2,1)S(1)}, bf16[64,2048]{1,0:T(8,128)(2,1)S(1)}, u32[]{:S(2)}, u32[]{:S(2)}) collective-permute-start(bf16[64,2048]{1,0:T(8,128)(2,1)S(1)} %slice.366), channel_id=1, source_target_pairs={{0,8},{4,12},{8,0},{12,4},{16,24},{20,28},{24,16},{28,20},{1,9},{5... | collective-permute-start | bytes 786440 | tf_op jit(solution)/shard_map/ppermute | solution.py:38
  52.6 50.8 %collective-permute-start.4 = (bf16[64,2048]{1,0:T(8,128)(2,1)S(1)}, bf16[64,2048]{1,0:T(8,128)(2,1)S(1)}, u32[]{:S(2)}, u32[]{:S(2)}) collective-permute-start(bf16[64,2048]{1,0:T(8,128)(2,1)S(1)} %slice.368), channel_id=1, source_target_pairs={{0,4},{4,0},{8,12},{12,8},{16,20},{20,16},{24,28},{28,24},{1,5},{5... | collective-permute-start | bytes 786440 | tf_op jit(solution)/shard_map/ppermute | solution.py:38
  52.8 54.0 %collective-permute-start.6 = (bf16[64,2048]{1,0:T(8,128)(2,1)S(1)}, bf16[64,2048]{1,0:T(8,128)(2,1)S(1)}, u32[]{:S(2)}, u32[]{:S(2)}) collective-permute-start(bf16[64,2048]{1,0:T(8,128)(2,1)S(1)} %slice.368), channel_id=1, source_target_pairs={{0,8},{4,12},{8,0},{12,4},{16,24},{20,28},{24,16},{28,20},{1,9},{5... | collective-permute-start | bytes 786440 | tf_op jit(solution)/shard_map/ppermute | solution.py:38
  54.3 35.7 %collective-permute-start = (s32[1,512]{1,0:T(1,128)S(1)}, s32[1,512]{1,0:T(1,128)S(1)}, u32[]{:S(2)}, u32[]{:S(2)}) collective-permute-start(s32[1,512]{1,0:T(1,128)S(1)} %copy-done.77), channel_id=1, source_target_pairs={{0,4},{4,0},{8,12},{12,8},{16,20},{20,16},{24,28},{28,24},{1,5},{5... | collective-permute-start | bytes 6152 | tf_op jit(solution)/shard_map/ppermute | solution.py:38
  54.4 649.1 %reduce-scatter.7.cloned.1.call-start = ((), (), s32[]{:S(2)}) async-start(), calls=%async_computation.13 | async-start | bytes 1310720 | tf_op jit(solution)/shard_map/reduce_scatter | solution.py:246
  98.8 23.7 %collective-permute-start.9 = (bf16[64,2048]{1,0:T(8,128)(2,1)S(1)}, bf16[64,2048]{1,0:T(8,128)(2,1)S(1)}, u32[]{:S(2)}, u32[]{:S(2)}) collective-permute-start(bf16[64,2048]{1,0:T(8,128)(2,1)S(1)} %slice.366), channel_id=1, source_target_pairs={{0,16},{4,20},{8,24},{12,28},{16,0},{20,4},{24,8},{28,12},{1,17},{... | collective-permute-start | bytes 786440 | tf_op jit(solution)/shard_map/ppermute | solution.py:38
  102.6 21.9 %collective-permute-start.10 = (bf16[64,2048]{1,0:T(8,128)(2,1)S(1)}, bf16[64,2048]{1,0:T(8,128)(2,1)S(1)}, u32[]{:S(2)}, u32[]{:S(2)}) collective-permute-start(bf16[64,2048]{1,0:T(8,128)(2,1)S(1)} %slice.368), channel_id=1, source_target_pairs={{0,16},{4,20},{8,24},{12,28},{16,0},{20,4},{24,8},{28,12},{1,17},{... | collective-permute-start | bytes 786440 | tf_op jit(solution)/shard_map/ppermute | solution.py:38
  108.8 18.4 %collective-permute-start.69 = (bf16[64,2048]{1,0:T(8,128)(2,1)}, bf16[64,2048]{1,0:T(8,128)(2,1)S(1)}, u32[]{:S(2)}, u32[]{:S(2)}) collective-permute-start(bf16[64,2048]{1,0:T(8,128)(2,1)} %get-tuple-element.135), channel_id=1, source_target_pairs={{0,16},{4,20},{8,24},{12,28},{16,0},{20,4},{24,8},{28,12},{1,17},{... | collective-permute-start | bytes 786440 | tf_op jit(solution)/shard_map/ppermute | solution.py:38
  140.6 61.6 %collective-permute-start.75 = (bf16[64,2048]{1,0:T(8,128)(2,1)}, bf16[64,2048]{1,0:T(8,128)(2,1)}, u32[]{:S(2)}, u32[]{:S(2)}) collective-permute-start(bf16[64,2048]{1,0:T(8,128)(2,1)} %collective-permute-done.73), channel_id=1, source_target_pairs={{0,4},{4,0},{8,12},{12,8},{16,20},{20,16},{24,28},{28,24},{1,5},{5... | collective-permute-start | bytes 786440 | tf_op jit(solution)/shard_map/ppermute | solution.py:38
  142.7 61.1 %collective-permute-start.76 = (bf16[64,2048]{1,0:T(8,128)(2,1)}, bf16[64,2048]{1,0:T(8,128)(2,1)}, u32[]{:S(2)}, u32[]{:S(2)}) collective-permute-start(bf16[64,2048]{1,0:T(8,128)(2,1)} %collective-permute-done.74), channel_id=1, source_target_pairs={{0,4},{4,0},{8,12},{12,8},{16,20},{20,16},{24,28},{28,24},{1,5},{5... | collective-permute-start | bytes 786440 | tf_op jit(solution)/shard_map/ppermute | solution.py:38
  154.6 22.6 %collective-permute-start.18 = (bf16[8,128,64]{1,2,0:T(8,128)(2,1)S(1)}, bf16[8,128,64]{1,2,0:T(8,128)(2,1)S(1)}, u32[]{:S(2)}, u32[]{:S(2)}) collective-permute-start(bf16[8,128,64]{1,2,0:T(8,128)(2,1)S(1)} %constant_dynamic-update-slice_fusion.24), channel_id=1, source_target_pairs={{0,2},{1,3},{2,0},{3,1},{4,6},{5,7},{6,4},{7,5},{8,10},{9,11},{10,... | collective-permute-start | bytes 393224 | tf_op jit(solution)/shard_map/ppermute | solution.py:189
  161.6 16.2 %collective-permute-start.19 = (bf16[8,128,64]{1,2,0:T(8,128)(2,1)S(1)}, bf16[8,128,64]{1,2,0:T(8,128)(2,1)S(1)}, u32[]{:S(2)}, u32[]{:S(2)}) collective-permute-start(bf16[8,128,64]{1,2,0:T(8,128)(2,1)S(1)} %constant_dynamic-update-slice_fusion.24), channel_id=1, source_target_pairs={{0,1},{1,2},{2,3},{3,0},{4,5},{5,6},{6,7},{7,4},{8,9},{9,10},{10,1... | collective-permute-start | bytes 393224 | tf_op jit(solution)/shard_map/ppermute | solution.py:189
  201.7 27.6 %collective-permute-start.22 = (bf16[64,2048]{0,1:T(8,128)(2,1)}, bf16[64,2048]{0,1:T(8,128)(2,1)}, u32[]{:S(2)}, u32[]{:S(2)}) collective-permute-start(bf16[64,2048]{0,1:T(8,128)(2,1)} %bitcast.34), channel_id=1, source_target_pairs={{0,4},{4,0},{8,12},{12,8},{16,20},{20,16},{24,28},{28,24},{1,5},{5... | collective-permute-start | bytes 786440 | tf_op jit(solution)/shard_map/ppermute | solution.py:38
  208.7 21.9 %collective-permute-start.25 = (bf16[64,2048]{0,1:T(8,128)(2,1)}, bf16[64,2048]{0,1:T(8,128)(2,1)}, u32[]{:S(2)}, u32[]{:S(2)}) collective-permute-start(bf16[64,2048]{0,1:T(8,128)(2,1)} %bitcast.38), channel_id=1, source_target_pairs={{0,4},{4,0},{8,12},{12,8},{16,20},{20,16},{24,28},{28,24},{1,5},{5... | collective-permute-start | bytes 786440 | tf_op jit(solution)/shard_map/ppermute | solution.py:38
  211.9 22.5 %collective-permute-start.24 = (bf16[64,2048]{0,1:T(8,128)(2,1)}, bf16[64,2048]{0,1:T(8,128)(2,1)}, u32[]{:S(2)}, u32[]{:S(2)}) collective-permute-start(bf16[64,2048]{0,1:T(8,128)(2,1)} %bitcast.472), channel_id=1, source_target_pairs={{0,4},{4,0},{8,12},{12,8},{16,20},{20,16},{24,28},{28,24},{1,5},{5... | collective-permute-start | bytes 786440 | tf_op jit(solution)/shard_map/ppermute | solution.py:38
  216.4 47.5 %collective-permute-start.21 = (bf16[64,2048]{0,1:T(8,128)(2,1)}, bf16[64,2048]{0,1:T(8,128)(2,1)}, u32[]{:S(2)}, u32[]{:S(2)}) collective-permute-start(bf16[64,2048]{0,1:T(8,128)(2,1)} %bitcast.468), channel_id=1, source_target_pairs={{0,4},{4,0},{8,12},{12,8},{16,20},{20,16},{24,28},{28,24},{1,5},{5... | collective-permute-start | bytes 786440 | tf_op jit(solution)/shard_map/ppermute | solution.py:38
  230.6 19.4 %collective-permute-start.31 = (bf16[64,2048]{0,1:T(8,128)(2,1)}, bf16[64,2048]{0,1:T(8,128)(2,1)S(1)}, u32[]{:S(2)}, u32[]{:S(2)}) collective-permute-start(bf16[64,2048]{0,1:T(8,128)(2,1)} %bitcast.474), channel_id=1, source_target_pairs={{0,4},{4,0},{8,12},{12,8},{16,20},{20,16},{24,28},{28,24},{1,5},{5... | collective-permute-start | bytes 786440 | tf_op jit(solution)/shard_map/ppermute | solution.py:38
  232.3 53.0 %collective-permute-start.28 = (bf16[64,2048]{0,1:T(8,128)(2,1)}, bf16[64,2048]{0,1:T(8,128)(2,1)S(1)}, u32[]{:S(2)}, u32[]{:S(2)}) collective-permute-start(bf16[64,2048]{0,1:T(8,128)(2,1)} %bitcast.470), channel_id=1, source_target_pairs={{0,4},{4,0},{8,12},{12,8},{16,20},{20,16},{24,28},{28,24},{1,5},{5... | collective-permute-start | bytes 786440 | tf_op jit(solution)/shard_map/ppermute | solution.py:38
  234.4 30.2 %collective-permute-start.23 = (bf16[64,2048]{0,1:T(8,128)(2,1)S(1)}, bf16[64,2048]{0,1:T(8,128)(2,1)S(1)}, u32[]{:S(2)}, u32[]{:S(2)}) collective-permute-start(bf16[64,2048]{0,1:T(8,128)(2,1)S(1)} %fusion.59), channel_id=1, source_target_pairs={{0,16},{4,20},{8,24},{12,28},{16,0},{20,4},{24,8},{28,12},{1,17},{... | collective-permute-start | bytes 786440 | tf_op jit(solution)/shard_map/ppermute | solution.py:38
  250.0 35.3 %collective-permute-start.30 = (bf16[64,2048]{0,1:T(8,128)(2,1)S(1)}, bf16[64,2048]{0,1:T(8,128)(2,1)S(1)}, u32[]{:S(2)}, u32[]{:S(2)}) collective-permute-start(bf16[64,2048]{0,1:T(8,128)(2,1)S(1)} %fusion.53), channel_id=1, source_target_pairs={{0,8},{4,12},{8,0},{12,4},{16,24},{20,28},{24,16},{28,20},{1,9},{5... | collective-permute-start | bytes 786440 | tf_op jit(solution)/shard_map/ppermute | solution.py:38
  263.3 20.7 %collective-permute-start.27 = (bf16[64,2048]{0,1:T(8,128)(2,1)S(1)}, bf16[64,2048]{0,1:T(8,128)(2,1)S(1)}, u32[]{:S(2)}, u32[]{:S(2)}) collective-permute-start(bf16[64,2048]{0,1:T(8,128)(2,1)S(1)} %fusion.58), channel_id=1, source_target_pairs={{0,8},{4,12},{8,0},{12,4},{16,24},{20,28},{24,16},{28,20},{1,9},{5... | collective-permute-start | bytes 786440 | tf_op jit(solution)/shard_map/ppermute | solution.py:38
  263.9 21.5 %collective-permute-start.34 = (bf16[64,2048]{0,1:T(8,128)(2,1)S(1)}, bf16[64,2048]{0,1:T(8,128)(2,1)S(1)}, u32[]{:S(2)}, u32[]{:S(2)}) collective-permute-start(bf16[64,2048]{0,1:T(8,128)(2,1)S(1)} %fusion.52), channel_id=1, source_target_pairs={{0,16},{4,20},{8,24},{12,28},{16,0},{20,4},{24,8},{28,12},{1,17},{... | collective-permute-start | bytes 786440 | tf_op jit(solution)/shard_map/ppermute | solution.py:38
  301.2 15.0 %collective-permute-start.41 = (bf16[64,2048]{1,0:T(8,128)(2,1)}, bf16[64,2048]{1,0:T(8,128)(2,1)S(1)}, u32[]{:S(2)}, u32[]{:S(2)}) collective-permute-start(bf16[64,2048]{1,0:T(8,128)(2,1)} %slice.409), channel_id=1, source_target_pairs={{0,16},{4,20},{8,24},{12,28},{16,0},{20,4},{24,8},{28,12},{1,17},{... | collective-permute-start | bytes 786440 | tf_op jit(solution)/shard_map/ppermute | solution.py:38
  360.9 31.7 %collective-permute-start.78 = (bf16[64,2048]{0,1:T(8,128)(2,1)}, bf16[64,2048]{0,1:T(8,128)(2,1)}, u32[]{:S(2)}, u32[]{:S(2)}) collective-permute-start(bf16[64,2048]{0,1:T(8,128)(2,1)} %bitcast.479), channel_id=1, source_target_pairs={{0,4},{4,0},{8,12},{12,8},{16,20},{20,16},{24,28},{28,24},{1,5},{5... | collective-permute-start | bytes 786440 | tf_op jit(solution)/shard_map/ppermute | solution.py:38
  366.9 27.3 %collective-permute-start.81 = (bf16[64,2048]{0,1:T(8,128)(2,1)}, bf16[64,2048]{0,1:T(8,128)(2,1)}, u32[]{:S(2)}, u32[]{:S(2)}) collective-permute-start(bf16[64,2048]{0,1:T(8,128)(2,1)} %bitcast.85), channel_id=1, source_target_pairs={{0,4},{4,0},{8,12},{12,8},{16,20},{20,16},{24,28},{28,24},{1,5},{5... | collective-permute-start | bytes 786440 | tf_op jit(solution)/shard_map/ppermute | solution.py:38
  370.2 28.0 %collective-permute-start.80 = (bf16[64,2048]{0,1:T(8,128)(2,1)}, bf16[64,2048]{0,1:T(8,128)(2,1)}, u32[]{:S(2)}, u32[]{:S(2)}) collective-permute-start(bf16[64,2048]{0,1:T(8,128)(2,1)} %bitcast.473), channel_id=1, source_target_pairs={{0,4},{4,0},{8,12},{12,8},{16,20},{20,16},{24,28},{28,24},{1,5},{5... | collective-permute-start | bytes 786440 | tf_op jit(solution)/shard_map/ppermute | solution.py:38
  374.5 53.1 %collective-permute-start.77 = (bf16[64,2048]{0,1:T(8,128)(2,1)}, bf16[64,2048]{0,1:T(8,128)(2,1)}, u32[]{:S(2)}, u32[]{:S(2)}) collective-permute-start(bf16[64,2048]{0,1:T(8,128)(2,1)} %bitcast.469), channel_id=1, source_target_pairs={{0,4},{4,0},{8,12},{12,8},{16,20},{20,16},{24,28},{28,24},{1,5},{5... | collective-permute-start | bytes 786440 | tf_op jit(solution)/shard_map/ppermute | solution.py:38
  378.5 17.3 %collective-permute-start.85 = (bf16[64,2048]{0,1:T(8,128)(2,1)}, bf16[64,2048]{0,1:T(8,128)(2,1)}, u32[]{:S(2)}, u32[]{:S(2)}) collective-permute-start(bf16[64,2048]{0,1:T(8,128)(2,1)} %bitcast.484), channel_id=1, source_target_pairs={{0,4},{4,0},{8,12},{12,8},{16,20},{20,16},{24,28},{28,24},{1,5},{5... | collective-permute-start | bytes 786440 | tf_op jit(solution)/shard_map/ppermute | solution.py:38
  394.2 19.6 %collective-permute-start.87 = (bf16[64,2048]{0,1:T(8,128)(2,1)}, bf16[64,2048]{0,1:T(8,128)(2,1)S(1)}, u32[]{:S(2)}, u32[]{:S(2)}) collective-permute-start(bf16[64,2048]{0,1:T(8,128)(2,1)} %bitcast.475), channel_id=1, source_target_pairs={{0,4},{4,0},{8,12},{12,8},{16,20},{20,16},{24,28},{28,24},{1,5},{5... | collective-permute-start | bytes 786440 | tf_op jit(solution)/shard_map/ppermute | solution.py:38
  395.8 52.9 %collective-permute-start.84 = (bf16[64,2048]{0,1:T(8,128)(2,1)}, bf16[64,2048]{0,1:T(8,128)(2,1)S(1)}, u32[]{:S(2)}, u32[]{:S(2)}) collective-permute-start(bf16[64,2048]{0,1:T(8,128)(2,1)} %bitcast.471), channel_id=1, source_target_pairs={{0,4},{4,0},{8,12},{12,8},{16,20},{20,16},{24,28},{28,24},{1,5},{5... | collective-permute-start | bytes 786440 | tf_op jit(solution)/shard_map/ppermute | solution.py:38
  398.2 30.0 %collective-permute-start.79 = (bf16[64,2048]{0,1:T(8,128)(2,1)S(1)}, bf16[64,2048]{0,1:T(8,128)(2,1)S(1)}, u32[]{:S(2)}, u32[]{:S(2)}) collective-permute-start(bf16[64,2048]{0,1:T(8,128)(2,1)S(1)} %fusion.33), channel_id=1, source_target_pairs={{0,16},{4,20},{8,24},{12,28},{16,0},{20,4},{24,8},{28,12},{1,17},{... | collective-permute-start | bytes 786440 | tf_op jit(solution)/shard_map/ppermute | solution.py:38
  413.8 35.0 %collective-permute-start.86 = (bf16[64,2048]{0,1:T(8,128)(2,1)S(1)}, bf16[64,2048]{0,1:T(8,128)(2,1)S(1)}, u32[]{:S(2)}, u32[]{:S(2)}) collective-permute-start(bf16[64,2048]{0,1:T(8,128)(2,1)S(1)} %fusion.27), channel_id=1, source_target_pairs={{0,8},{4,12},{8,0},{12,4},{16,24},{20,28},{24,16},{28,20},{1,9},{5... | collective-permute-start | bytes 786440 | tf_op jit(solution)/shard_map/ppermute | solution.py:38
  427.1 20.4 %collective-permute-start.83 = (bf16[64,2048]{0,1:T(8,128)(2,1)S(1)}, bf16[64,2048]{0,1:T(8,128)(2,1)S(1)}, u32[]{:S(2)}, u32[]{:S(2)}) collective-permute-start(bf16[64,2048]{0,1:T(8,128)(2,1)S(1)} %fusion.32), channel_id=1, source_target_pairs={{0,8},{4,12},{8,0},{12,4},{16,24},{20,28},{24,16},{28,20},{1,9},{5... | collective-permute-start | bytes 786440 | tf_op jit(solution)/shard_map/ppermute | solution.py:38
  427.6 21.1 %collective-permute-start.90 = (bf16[64,2048]{0,1:T(8,128)(2,1)S(1)}, bf16[64,2048]{0,1:T(8,128)(2,1)S(1)}, u32[]{:S(2)}, u32[]{:S(2)}) collective-permute-start(bf16[64,2048]{0,1:T(8,128)(2,1)S(1)} %fusion.26), channel_id=1, source_target_pairs={{0,16},{4,20},{8,24},{12,28},{16,0},{20,4},{24,8},{28,12},{1,17},{... | collective-permute-start | bytes 786440 | tf_op jit(solution)/shard_map/ppermute | solution.py:38
  452.1 14.9 %collective-permute-start.93 = (bf16[64,2048]{0,1:T(8,128)(2,1)S(1)}, bf16[64,2048]{0,1:T(8,128)(2,1)S(1)}, u32[]{:S(2)}, u32[]{:S(2)}) collective-permute-start(bf16[64,2048]{0,1:T(8,128)(2,1)S(1)} %get-tuple-element.133), channel_id=1, source_target_pairs={{0,8},{4,12},{8,0},{12,4},{16,24},{20,28},{24,16},{28,20},{1,9},{5... | collective-permute-start | bytes 786440 | tf_op jit(solution)/shard_map/ppermute | solution.py:38
  452.4 14.9 %collective-permute-start.98 = (bf16[64,2048]{0,1:T(8,128)(2,1)S(1)}, bf16[64,2048]{0,1:T(8,128)(2,1)S(1)}, u32[]{:S(2)}, u32[]{:S(2)}) collective-permute-start(bf16[64,2048]{0,1:T(8,128)(2,1)S(1)} %get-tuple-element.132), channel_id=1, source_target_pairs={{0,16},{4,20},{8,24},{12,28},{16,0},{20,4},{24,8},{28,12},{1,17},{... | collective-permute-start | bytes 786440 | tf_op jit(solution)/shard_map/ppermute | solution.py:38
  453.0 22.5 %collective-permute-start.94 = (bf16[64,2048]{0,1:T(8,128)(2,1)S(1)}, bf16[64,2048]{0,1:T(8,128)(2,1)S(1)}, u32[]{:S(2)}, u32[]{:S(2)}) collective-permute-start(bf16[64,2048]{0,1:T(8,128)(2,1)S(1)} %get-tuple-element.132), channel_id=1, source_target_pairs={{0,8},{4,12},{8,0},{12,4},{16,24},{20,28},{24,16},{28,20},{1,9},{5... | collective-permute-start | bytes 786440 | tf_op jit(solution)/shard_map/ppermute | solution.py:38
  454.7 23.8 %collective-permute-start.97 = (bf16[64,2048]{0,1:T(8,128)(2,1)S(1)}, bf16[64,2048]{0,1:T(8,128)(2,1)S(1)}, u32[]{:S(2)}, u32[]{:S(2)}) collective-permute-start(bf16[64,2048]{0,1:T(8,128)(2,1)S(1)} %get-tuple-element.133), channel_id=1, source_target_pairs={{0,16},{4,20},{8,24},{12,28},{16,0},{20,4},{24,8},{28,12},{1,17},{... | collective-permute-start | bytes 786440 | tf_op jit(solution)/shard_map/ppermute | solution.py:38
  456.2 22.3 %collective-permute-start.91 = (bf16[64,2048]{0,1:T(8,128)(2,1)S(1)}, bf16[64,2048]{0,1:T(8,128)(2,1)S(1)}, u32[]{:S(2)}, u32[]{:S(2)}) collective-permute-start(bf16[64,2048]{0,1:T(8,128)(2,1)S(1)} %get-tuple-element.133), channel_id=1, source_target_pairs={{0,4},{4,0},{8,12},{12,8},{16,20},{20,16},{24,28},{28,24},{1,5},{5... | collective-permute-start | bytes 786440 | tf_op jit(solution)/shard_map/ppermute | solution.py:38
  467.3 19.3 %collective-permute-start.101 = (bf16[64,2048]{0,1:T(8,128)(2,1)S(1)}, bf16[64,2048]{0,1:T(8,128)(2,1)S(1)}, u32[]{:S(2)}, u32[]{:S(2)}) collective-permute-start(bf16[64,2048]{0,1:T(8,128)(2,1)S(1)} %collective-permute-done.93), channel_id=1, source_target_pairs={{0,16},{4,20},{8,24},{12,28},{16,0},{20,4},{24,8},{28,12},{1,17},{... | collective-permute-start | bytes 786440 | tf_op jit(solution)/shard_map/ppermute | solution.py:38
  526.0 184.4 %reduce-scatter.5.cloned.1.call-start = ((), (), s32[]{:S(2)}) async-start(), calls=%async_computation.12 | async-start | bytes 1638400 | tf_op jit(solution)/shard_map/reduce_scatter | solution.py:276
  538.1 20.7 %collective-permute-start.106 = (bf16[8,128,64]{1,0,2:T(8,128)(2,1)S(1)}, bf16[8,128,64]{1,0,2:T(8,128)(2,1)S(1)}, u32[]{:S(2)}, u32[]{:S(2)}) collective-permute-start(bf16[8,128,64]{1,0,2:T(8,128)(2,1)S(1)} %get-tuple-element.129), channel_id=1, source_target_pairs={{0,1},{1,2},{2,3},{3,0},{4,5},{5,6},{6,7},{7,4},{8,9},{9,10},{10,1... | collective-permute-start | bytes 393224 | tf_op jit(solution)/shard_map/ppermute | solution.py:270
  546.2 26.5 %collective-permute-start.107 = (bf16[8,128,64]{1,0,2:T(8,128)(2,1)S(1)}, bf16[8,128,64]{1,0,2:T(8,128)(2,1)S(1)}, u32[]{:S(2)}, u32[]{:S(2)}) collective-permute-start(bf16[8,128,64]{1,0,2:T(8,128)(2,1)S(1)} %get-tuple-element.131), channel_id=1, source_target_pairs={{0,2},{1,3},{2,0},{3,1},{4,6},{5,7},{6,4},{7,5},{8,10},{9,11},{10,... | collective-permute-start | bytes 393224 | tf_op jit(solution)/shard_map/ppermute | solution.py:270
  552.5 20.1 %collective-permute-start.108 = (bf16[8,128,64]{1,0,2:T(8,128)(2,1)S(1)}, bf16[8,128,64]{1,0,2:T(8,128)(2,1)S(1)}, u32[]{:S(2)}, u32[]{:S(2)}) collective-permute-start(bf16[8,128,64]{1,0,2:T(8,128)(2,1)S(1)} %get-tuple-element.130), channel_id=1, source_target_pairs={{0,3},{1,0},{2,1},{3,2},{4,7},{5,4},{6,5},{7,6},{8,11},{9,8},{10,9... | collective-permute-start | bytes 393224 | tf_op jit(solution)/shard_map/ppermute | solution.py:270
  576.2 147.8 %reduce-scatter.9.cloned.1.call-start = ((), (), s32[]{:S(2)}) async-start(), calls=%async_computation.14 | async-start | bytes 7208960 | tf_op jit(solution)/shard_map/reduce_scatter | solution.py:234
  587.5 182.2 %reduce-scatter.11.cloned.1.call-start = ((), (), s32[]{:S(2)}) async-start(), calls=%async_computation.15 | async-start | bytes 3604480 | tf_op jit(solution)/shard_map/reduce_scatter | solution.py:231
  601.4 34.7 %collective-permute-start.53 = (bf16[64,2048]{0,1:T(8,128)(2,1)}, bf16[64,2048]{0,1:T(8,128)(2,1)}, u32[]{:S(2)}, u32[]{:S(2)}) collective-permute-start(bf16[64,2048]{0,1:T(8,128)(2,1)} %bitcast.477), channel_id=1, source_target_pairs={{0,4},{4,0},{8,12},{12,8},{16,20},{20,16},{24,28},{28,24},{1,5},{5... | collective-permute-start | bytes 786440 | tf_op jit(solution)/shard_map/ppermute | solution.py:38
  611.0 27.0 %collective-permute-start.50 = (bf16[64,2048]{0,1:T(8,128)(2,1)}, bf16[64,2048]{0,1:T(8,128)(2,1)}, u32[]{:S(2)}, u32[]{:S(2)}) collective-permute-start(bf16[64,2048]{0,1:T(8,128)(2,1)} %bitcast.478), channel_id=1, source_target_pairs={{0,4},{4,0},{8,12},{12,8},{16,20},{20,16},{24,28},{28,24},{1,5},{5... | collective-permute-start | bytes 786440 | tf_op jit(solution)/shard_map/ppermute | solution.py:38
  617.3 32.4 %collective-permute-start.52 = (bf16[64,2048]{0,1:T(8,128)(2,1)}, bf16[64,2048]{0,1:T(8,128)(2,1)}, u32[]{:S(2)}, u32[]{:S(2)}) collective-permute-start(bf16[64,2048]{0,1:T(8,128)(2,1)} %bitcast.467), channel_id=1, source_target_pairs={{0,4},{4,0},{8,12},{12,8},{16,20},{20,16},{24,28},{28,24},{1,5},{5... | collective-permute-start | bytes 786440 | tf_op jit(solution)/shard_map/ppermute | solution.py:38
  625.3 15.6 %collective-permute-start.57 = (bf16[64,2048]{0,1:T(8,128)(2,1)}, bf16[64,2048]{0,1:T(8,128)(2,1)}, u32[]{:S(2)}, u32[]{:S(2)}) collective-permute-start(bf16[64,2048]{0,1:T(8,128)(2,1)} %bitcast.480), channel_id=1, source_target_pairs={{0,4},{4,0},{8,12},{12,8},{16,20},{20,16},{24,28},{28,24},{1,5},{5... | collective-permute-start | bytes 786440 | tf_op jit(solution)/shard_map/ppermute | solution.py:38
  627.7 17.3 %collective-permute-start.60 = (bf16[64,2048]{0,1:T(8,128)(2,1)}, bf16[64,2048]{0,1:T(8,128)(2,1)}, u32[]{:S(2)}, u32[]{:S(2)}) collective-permute-start(bf16[64,2048]{0,1:T(8,128)(2,1)} %bitcast.476), channel_id=1, source_target_pairs={{0,4},{4,0},{8,12},{12,8},{16,20},{20,16},{24,28},{28,24},{1,5},{5... | collective-permute-start | bytes 786440 | tf_op jit(solution)/shard_map/ppermute | solution.py:38
  636.0 22.6 %collective-permute-start.59 = (bf16[64,2048]{0,1:T(8,128)(2,1)}, bf16[64,2048]{0,1:T(8,128)(2,1)S(1)}, u32[]{:S(2)}, u32[]{:S(2)}) collective-permute-start(bf16[64,2048]{0,1:T(8,128)(2,1)} %bitcast.466), channel_id=1, source_target_pairs={{0,4},{4,0},{8,12},{12,8},{16,20},{20,16},{24,28},{28,24},{1,5},{5... | collective-permute-start | bytes 786440 | tf_op jit(solution)/shard_map/ppermute | solution.py:38
  663.4 37.1 %collective-permute-start.56 = (bf16[64,2048]{0,1:T(8,128)(2,1)S(1)}, bf16[64,2048]{0,1:T(8,128)(2,1)S(1)}, u32[]{:S(2)}, u32[]{:S(2)}) collective-permute-start(bf16[64,2048]{0,1:T(8,128)(2,1)S(1)} %bitcast.464), channel_id=1, source_target_pairs={{0,4},{4,0},{8,12},{12,8},{16,20},{20,16},{24,28},{28,24},{1,5},{5... | collective-permute-start | bytes 786440 | tf_op jit(solution)/shard_map/ppermute | solution.py:38
  663.9 15.2 %collective-permute-start.51 = (bf16[64,2048]{0,1:T(8,128)(2,1)S(1)}, bf16[64,2048]{0,1:T(8,128)(2,1)S(1)}, u32[]{:S(2)}, u32[]{:S(2)}) collective-permute-start(bf16[64,2048]{0,1:T(8,128)(2,1)S(1)} %fusion.46), channel_id=1, source_target_pairs={{0,16},{4,20},{8,24},{12,28},{16,0},{20,4},{24,8},{28,12},{1,17},{... | collective-permute-start | bytes 786440 | tf_op jit(solution)/shard_map/ppermute | solution.py:38
  667.8 34.4 %collective-permute-start.58 = (bf16[64,2048]{0,1:T(8,128)(2,1)S(1)}, bf16[64,2048]{0,1:T(8,128)(2,1)S(1)}, u32[]{:S(2)}, u32[]{:S(2)}) collective-permute-start(bf16[64,2048]{0,1:T(8,128)(2,1)S(1)} %fusion.39), channel_id=1, source_target_pairs={{0,8},{4,12},{8,0},{12,4},{16,24},{20,28},{24,16},{28,20},{1,9},{5... | collective-permute-start | bytes 786440 | tf_op jit(solution)/shard_map/ppermute | solution.py:38
  668.7 23.6 %collective-permute-start.55 = (bf16[64,2048]{0,1:T(8,128)(2,1)S(1)}, bf16[64,2048]{0,1:T(8,128)(2,1)S(1)}, u32[]{:S(2)}, u32[]{:S(2)}) collective-permute-start(bf16[64,2048]{0,1:T(8,128)(2,1)S(1)} %fusion.45), channel_id=1, source_target_pairs={{0,8},{4,12},{8,0},{12,4},{16,24},{20,28},{24,16},{28,20},{1,9},{5... | collective-permute-start | bytes 786440 | tf_op jit(solution)/shard_map/ppermute | solution.py:38
  671.3 30.9 %collective-permute-start.62 = (bf16[64,2048]{0,1:T(8,128)(2,1)S(1)}, bf16[64,2048]{0,1:T(8,128)(2,1)S(1)}, u32[]{:S(2)}, u32[]{:S(2)}) collective-permute-start(bf16[64,2048]{0,1:T(8,128)(2,1)S(1)} %fusion.38), channel_id=1, source_target_pairs={{0,16},{4,20},{8,24},{12,28},{16,0},{20,4},{24,8},{28,12},{1,17},{... | collective-permute-start | bytes 786440 | tf_op jit(solution)/shard_map/ppermute | solution.py:38
  679.0 15.1 %collective-permute-start.119 = (bf16[64,2048]{1,0:T(8,128)(2,1)S(1)}, bf16[64,2048]{1,0:T(8,128)(2,1)S(1)}, u32[]{:S(2)}, u32[]{:S(2)}) collective-permute-start(bf16[64,2048]{1,0:T(8,128)(2,1)S(1)} %get-tuple-element.63), channel_id=1, source_target_pairs={{0,4},{4,0},{8,12},{12,8},{16,20},{20,16},{24,28},{28,24},{1,5},{5... | collective-permute-start | bytes 786440 | tf_op jit(solution)/shard_map/ppermute | solution.py:38
  724.0 48.0 %all-to-all-start.3 = ((bf16[8,64,1408]{2,1,0:T(8,128)(2,1)}), bf16[8,64,1408]{2,1,0:T(8,128)(2,1)}, u32[]{:S(2)}, u32[]{:S(2)}) async-start(bf16[8,64,1408]{2,1,0:T(8,128)(2,1)} %bitcast.456), calls=%async_computation.6 | async-start | bytes 2883584 | tf_op jit(solution)/shard_map/all_to_all | solution.py:237
  (169 other events, 2233.4 us)
Sparse Core Ops, SparseCore 0:
  22.2 34.1 all-gather.5
  58.0 27.4 all-gather.7
  87.1 115.7 all-gather.9
  204.3 57.7 all-gather.11
  526.1 44.9 reduce-scatter.6
  576.3 29.9 reduce-scatter.4
  608.7 102.4 reduce-scatter.8
  713.6 56.0 reduce-scatter.10

commit v2 on v1

v2 whole, which is shorter than its diff:
```python
import functools

import jax
import jax.numpy as jnp
from jax import lax
from jax.experimental import pallas as pl
from jax.experimental.pallas import tpu as pltpu
from jax.sharding import Mesh
from jax.sharding import PartitionSpec as P

QUERY_HEADS = 32
KEY_VALUE_HEADS = 4
HEAD_SIZE = 64
EPS = 1e-05
NEG = -1e30
F32 = jnp.float32
BF16 = jnp.bfloat16


def dot(left, right):
    return jnp.dot(left, right, preferred_element_type=F32)


def dot_nt(left, right):
    return lax.dot_general(left, right, (((1,), (1,)), ((), ())), preferred_element_type=F32)


def dot_tn(left, right):
    return lax.dot_general(left, right, (((0,), (0,)), ((), ())), preferred_element_type=F32)


def swap(value, rel):
    size = lax.axis_size(("plane", "core"))
    return lax.ppermute(value, ("plane", "core"), [(i, i ^ rel) for i in range(size)])


def shift(value, step, size):
    return lax.ppermute(value, "ctx", [(i, (i - step) % size) for i in range(size)])


def shifts(value, size):
    return [shift(value, j, size) for j in range(1, size)]


def together(*values):
    return lax.optimization_barrier(values)


def after(value, *earlier):
    return together(value, *earlier)[0]


def dp_same(rows, size):
    return [swap(rows, rel) for rel in range(2, size, 2)]


def kernel_params(mib=48):
    return pltpu.CompilerParams(vmem_limit_bytes=mib * 2**20)

LIGHT = pl.CostEstimate(flops=1024, bytes_accessed=1024, transcendentals=0)


def transposed_dot(lefts, rights):
    tokens, rows = lefts[0].shape
    columns, count = rights[0].shape[1], len(lefts)
    by_rows = rows % 256 == 0 and rows > columns
    row_tile = 256 if by_rows else rows
    column_tile = columns if by_rows or columns % 512 else 512
    moving = pl.BlockSpec((tokens, row_tile if by_rows else column_tile), lambda i: (0, i))
    resting = pl.BlockSpec((tokens, column_tile if by_rows else row_tile), lambda i: (0, 0))

    def body(*refs):
        total = 0.0
        for left, right in zip(refs[:count], refs[count:-1]):
            total += lax.dot_general(
                left[...], right[...], (((0,), (0,)), ((), ())), preferred_element_type=F32
            )
        refs[-1][...] = total.astype(BF16)

    return pl.pallas_call(
        body,
        grid=(rows // row_tile if by_rows else columns // column_tile,),
        in_specs=[moving if by_rows else resting] * count + [resting if by_rows else moving] * count,
        out_specs=pl.BlockSpec(
            (row_tile, column_tile), (lambda i: (i, 0)) if by_rows else (lambda i: (0, i))
        ),
        out_shape=jax.ShapeDtypeStruct((rows, columns), BF16),
        compiler_params=kernel_params(),
        cost_estimate=LIGHT,
    )(*lefts, *rights)


def turn(values, cosine, sine):
    half = HEAD_SIZE // 2
    width = values.shape[1]
    lane = lax.broadcasted_iota(jnp.int32, values.shape, 1)
    up = jnp.concatenate([values[:, half:], values[:, :half]], axis=1)
    down = jnp.concatenate([values[:, width - half :], values[:, : width - half]], axis=1)
    return values * cosine + jnp.where(lane % HEAD_SIZE < half, up, down) * sine


def widen(table, columns):
    return jnp.concatenate([table] * (columns // table.shape[1]), axis=1)


def pack(rows):
    half = rows.shape[0] // 2
    return jnp.concatenate([rows[:half], rows[half:]], axis=1)


def unpack(rows):
    half = rows.shape[1] // 2
    return jnp.concatenate([rows[:, :half], rows[:, half:]], axis=0)


def project(where, even, odd, gain, weights, cosine, sine, q_cols, part):
    half, width = even.shape
    columns = q_cols + HEAD_SIZE
    tile = 256
    steps = half // tile

    def body(at, e, o, gn, w, cs, sn, first, queries, kv):
        x = jnp.where(pl.program_id(0) < steps, e[...], o[...]).astype(F32)
        normed = x * lax.rsqrt(jnp.mean(x * x, axis=-1, keepdims=True) + EPS)
        rows = (normed * gn[...]).astype(BF16)
        first[...] = rows
        raw = dot(rows, w[...])
        queries[...] = turn(
            raw[:, :q_cols], widen(cs[...], q_cols), widen(sn[...], q_cols)
        ).astype(BF16)
        plain = raw[:, q_cols:columns]
        turned = turn(plain, cs[:, :HEAD_SIZE], sn[:, :HEAD_SIZE])
        chosen = jnp.where(at[1] == 0, turned, plain)
        for p in range(tile // part):
            kv[p] = pack(chosen[p * part : (p + 1) * part]).astype(BF16)

    def rows(size):
        return pl.BlockSpec((tile, size), lambda i: (i, 0))

    return pl.pallas_call(
        body,
        grid=(2 * steps,),
        in_specs=[
            pl.BlockSpec(memory_space=pltpu.SMEM),
            pl.BlockSpec((tile, width), lambda i: (jnp.minimum(i, steps - 1), 0)),
            pl.BlockSpec((tile, width), lambda i: (jnp.maximum(i - steps, 0), 0)),
            pl.BlockSpec((1, width), lambda i: (0, 0)),
            pl.BlockSpec(weights.shape, lambda i: (0, 0)),
            rows(cosine.shape[1]),
            rows(cosine.shape[1]),
        ],
        out_specs=(
            rows(width),
            rows(q_cols),
            pl.BlockSpec((tile // part, part // 2, 2 * HEAD_SIZE), lambda i: (i, 0, 0)),
        ),
        out_shape=(
            jax.ShapeDtypeStruct((2 * half, width), BF16),
            jax.ShapeDtypeStruct((2 * half, q_cols), BF16),
            jax.ShapeDtypeStruct((2 * half // part, part // 2, 2 * HEAD_SIZE), BF16),
        ),
        compiler_params=kernel_params(),
        cost_estimate=LIGHT,
    )(where, even, odd, gain, weights, cosine, sine)


def stacked(values, heads):
    return jnp.concatenate(
        [values[:, h * HEAD_SIZE : (h + 1) * HEAD_SIZE] for h in range(heads)], axis=0
    )


def side_by_side(values, heads):
    rows = values.shape[0] // heads
    return jnp.concatenate([values[h * rows : (h + 1) * rows] for h in range(heads)], axis=1)


def probabilities(queries, keys, mine, theirs, place, parts, heads):
    rows, length = queries.shape[0] // heads, keys.shape[0]
    part = length // parts
    scores = dot_nt(queries, keys) * HEAD_SIZE**-0.5
    query_at = place * part + lax.broadcasted_iota(jnp.int32, (rows, length), 0)
    key_at = place * part + lax.broadcasted_iota(jnp.int32, (rows, length), 1)
    key_at = jnp.where(key_at >= length, key_at - length, key_at)
    allowed = (key_at <= query_at) & (mine == theirs)
    allowed = jnp.concatenate([allowed] * heads, axis=0)
    scores = jnp.where(allowed, scores, NEG)
    expo = jnp.exp(scores - jnp.max(scores, axis=-1, keepdims=True))
    return expo / jnp.sum(expo, axis=-1, keepdims=True)


def sequence_specs(sequences, part, parts):
    half = sequences // 2
    shape = (1, part // 2, 2 * HEAD_SIZE)
    own = pl.BlockSpec(shape, lambda i: (i, 0, 0))
    came = pl.BlockSpec(shape, lambda i: (lax.rem(i + half, sequences), 0, 0))
    return [own] * parts + [came] * parts


def keys_values(first, refs):
    parts = len(refs) // 2
    own, came = (
        jnp.concatenate([unpack(ref[0]) for ref in half], axis=0) for half in (refs[:parts], refs[parts:])
    )
    return jnp.where(first, own, came), jnp.where(first, came, own)


def attend(where, queries, own, came, mine, theirs):
    parts = len(own)
    sequences, part = own[0].shape[0], 2 * own[0].shape[1]
    rows, columns = queries.shape[0] // sequences, queries.shape[1]
    heads = columns // HEAD_SIZE

    def body(at, q, m, th, *refs):
        keys, values = keys_values(at[1] == 0, refs[:-1])
        probs = probabilities(stacked(q[...], heads), keys, m[0], th[0], at[0], parts, heads)
        refs[-1][...] = side_by_side(dot(probs.astype(BF16), values), heads).astype(BF16)

    return pl.pallas_call(
        body,
        grid=(sequences,),
        in_specs=[
            pl.BlockSpec(memory_space=pltpu.SMEM),
            pl.BlockSpec((rows, columns), lambda i: (i, 0)),
            pl.BlockSpec((1, rows, 1), lambda i: (i, 0, 0)),
            pl.BlockSpec((1, 1, parts * part), lambda i: (i, 0, 0)),
            *sequence_specs(sequences, part, parts),
        ],
        out_specs=pl.BlockSpec((rows, columns), lambda i: (i, 0)),
        out_shape=jax.ShapeDtypeStruct(queries.shape, BF16),
        compiler_params=kernel_params(),
        cost_estimate=LIGHT,
    )(where, queries, mine, theirs, *own, *came)


def attend_back(where, same, other, w_out, queries, own, came, mine, theirs, cosine, sine):
    parts = len(own)
    sequences, part = own[0].shape[0], 2 * own[0].shape[1]
    length = parts * part
    rows, columns = queries.shape[0] // sequences, queries.shape[1]
    heads, half, width = columns // HEAD_SIZE, sequences // 2, same.shape[1]
    packed = parts, part // 2, 2 * HEAD_SIZE
    scale = HEAD_SIZE**-0.5

    def body(at, s, o, w, q, m, th, cs, sn, *refs):
        dq, down, dcame = refs[-3:]
        first = at[1] == 0
        keys, values = keys_values(first, refs[:-3])
        branch = jnp.where(pl.program_id(0) < half, s[...], o[...])
        mixed = stacked(dot_nt(branch, w[...]).astype(BF16), heads)
        stack = stacked(q[...], heads)
        probs = probabilities(stack, keys, m[0], th[0], at[0], parts, heads)
        grad = dot_nt(mixed, values)
        inner = jnp.sum(probs * grad, axis=-1, keepdims=True)
        scores = (probs * (grad - inner)).astype(BF16)
        grad_q = side_by_side(dot(scores, keys) * scale, heads)
        dq[...] = turn(grad_q, widen(cs[...], columns), -widen(sn[...], columns)).astype(BF16)
        grad_k = dot_tn(scores, stack) * scale
        grad_v = dot_tn(probs.astype(BF16), mixed)
        kept, sent = jnp.where(first, grad_k, grad_v), jnp.where(first, grad_v, grad_k)
        for j in range(parts):
            at_rows = slice(j * part, (j + 1) * part)
            down[0, j] = pack(kept[at_rows])
            dcame[0, j] = pack(sent[at_rows]).astype(BF16)

    def strip(size):
        return pl.BlockSpec((rows, size), lambda i: (i, 0))

    return pl.pallas_call(
        body,
        grid=(sequences,),
        in_specs=[
            pl.BlockSpec(memory_space=pltpu.SMEM),
            pl.BlockSpec((rows, width), lambda i: (jnp.minimum(i, half - 1), 0)),
            pl.BlockSpec((rows, width), lambda i: (jnp.maximum(i - half, 0), 0)),
            pl.BlockSpec(w_out.shape, lambda i: (0, 0)),
            strip(columns),
            pl.BlockSpec((1, rows, 1), lambda i: (i, 0, 0)),
            pl.BlockSpec((1, 1, length), lambda i: (i, 0, 0)),
            strip(cosine.shape[1]),
            strip(cosine.shape[1]),
            *sequence_specs(sequences, part, parts),
        ],
        out_specs=(
            strip(columns),
            pl.BlockSpec((1, *packed), lambda i: (i, 0, 0, 0)),
            pl.BlockSpec((1, *packed), lambda i: (lax.rem(i + half, sequences), 0, 0, 0)),
        ),
        out_shape=(
            jax.ShapeDtypeStruct(queries.shape, BF16),
            jax.ShapeDtypeStruct((sequences, *packed), F32),
            jax.ShapeDtypeStruct((sequences, *packed), BF16),
        ),
        compiler_params=kernel_params(),
        cost_estimate=LIGHT,
    )(where, same, other, w_out, queries, mine, theirs, cosine, sine, *own, *came)


def add_parts(kept, came):
    sequences, parts, rows, columns = kept.shape

    def body(a, b, *outs):
        for j, out in enumerate(outs):
            out[...] = (a[:, j] + b[:, j].astype(F32)).astype(out.dtype)

    return pl.pallas_call(
        body,
        out_shape=[
            jax.ShapeDtypeStruct((sequences, rows, columns), BF16 if j else F32)
            for j in range(parts)
        ],
        compiler_params=kernel_params(),
        cost_estimate=LIGHT,
    )(kept, came)


def sum_keys(where, own, came, cosine, sine):
    sequences, rows, _ = own.shape
    count = len(came)

    def body(at, a, cs, sn, *refs):
        total = a[...]
        for ref in refs[:count]:
            total += ref[...].astype(F32)
        out = refs[count]
        for i in range(sequences):
            at_rows = slice(2 * i * rows, 2 * (i + 1) * rows)
            plain = unpack(total[i])
            turned = turn(plain, cs[at_rows, :HEAD_SIZE], -sn[at_rows, :HEAD_SIZE])
            out[at_rows, :] = jnp.where(at[1] == 0, turned, plain).astype(BF16)

    whole = pl.BlockSpec(memory_space=pltpu.VMEM)
    return pl.pallas_call(
        body,
        in_specs=[pl.BlockSpec(memory_space=pltpu.SMEM)] + [whole] * (3 + count),
        out_shape=jax.ShapeDtypeStruct((2 * sequences * rows, HEAD_SIZE), BF16),
        compiler_params=kernel_params(),
        cost_estimate=LIGHT,
    )(where, own, cosine, sine, *came)


def attention_weight_terms(where, first_in, grad_attn, mixed, grad_branch, used, members, parts):
    tokens, width = first_in.shape
    columns, half = mixed.shape[1], mixed.shape[0] // 2
    block, strip = width // (members * parts), width // members
    lanes = used + strip + -(used + strip) % 128

    def body(at, x, g, m, ba, bb, *refs):
        outs, (left, right) = refs[:parts], refs[parts:]
        left[...] = dot_tn(x[...], g[:, : left.shape[1]])
        right[...] = dot_tn(m[:half, :], ba[...]) + dot_tn(m[half:, :], bb[...])
        unused = jnp.zeros((block, lanes - used - strip), F32)
        for j, out in enumerate(outs):
            place = lax.rem(at[0] + j, parts)
            own = right[pl.ds(pl.multiple_of(place * block, block), block), :]
            for d in range(members):
                rows = pl.ds(pl.multiple_of((d * parts + place) * block, block), block)
                out[d * block : (d + 1) * block, :] = jnp.concatenate(
                    [left[rows, :][:, :used], own[:, d * strip : (d + 1) * strip], unused], axis=1
                ).astype(BF16)

    whole = pl.BlockSpec(memory_space=pltpu.VMEM)
    return pl.pallas_call(
        body,
        in_specs=[pl.BlockSpec(memory_space=pltpu.SMEM)] + [whole] * 5,
        out_shape=[jax.ShapeDtypeStruct((members * block, lanes), BF16)] * parts,
        scratch_shapes=[
            pltpu.VMEM((width, grad_attn.shape[1]), F32),
            pltpu.VMEM((columns, width), F32),
        ],
        compiler_params=kernel_params(),
        cost_estimate=LIGHT,
    )(where, first_in, grad_attn, mixed, *grad_branch)


def feed_forward(second_in, grad_hidden, w_pair, w_down):
    tokens, width = second_in.shape
    ff = w_down.shape[0]
    tile = 512

    def body(x, dh, w, wd, hidden, grads, back, forth):
        both = dot(x[...], w[...])
        gate, up = both[:, :ff], both[:, ff:]
        sig = jax.nn.sigmoid(gate)
        swish = gate * sig
        inner = (swish * up).astype(BF16)
        hidden[...] = inner
        forth[...] = dot(inner, wd[...]).astype(BF16)
        dh_sig = dh[...] * sig
        grad = jnp.concatenate(
            [dh_sig * up * (1.0 + gate * (1.0 - sig)), dh_sig * gate], axis=1
        ).astype(BF16)
        grads[...] = grad
        back[...] = dot_nt(grad, w[...]).astype(BF16)

    def rows(columns):
        return pl.BlockSpec((tile, columns), lambda i: (i, 0))

    def whole(array):
        return pl.BlockSpec(array.shape, lambda i: (0, 0))

    return pl.pallas_call(
        body,
        grid=(tokens // tile,),
        in_specs=[rows(width), rows(ff), whole(w_pair), whole(w_down)],
        out_specs=(rows(ff), rows(2 * ff), rows(width), rows(width)),
        out_shape=(
            jax.ShapeDtypeStruct((tokens, ff), BF16),
            jax.ShapeDtypeStruct((tokens, 2 * ff), BF16),
            jax.ShapeDtypeStruct((tokens, width), BF16),
            jax.ShapeDtypeStruct((tokens, width), BF16),
        ),
        compiler_params=kernel_params(),
        cost_estimate=LIGHT,
    )(second_in, grad_hidden, w_pair, w_down)


def add_blocks(own, came, blocks):
    tokens, columns = own.shape[0] // blocks, own.shape[1]

    def body(a, b, *outs):
        for j, out in enumerate(outs):
            rows = pl.ds(j * tokens, tokens)
            out[...] = (a[rows, :].astype(F32) + b[rows, :].astype(F32)).astype(out.dtype)

    return pl.pallas_call(
        body,
        out_shape=[
            jax.ShapeDtypeStruct((tokens, columns), BF16 if j else F32) for j in range(blocks)
        ],
        compiler_params=kernel_params(),
        cost_estimate=LIGHT,
    )(own, came)


def regroup(values, outer, inner):
    part = values.shape[1] // (outer * inner)
    return jnp.concatenate(
        [
            values[:, (o * inner + i) * part : (o * inner + i + 1) * part]
            for i in range(inner)
            for o in range(outer)
        ],
        axis=1,
    )


def second_norm(x, own, sent, gain, outer, inner):
    count = len(sent)

    def body(x, own, gain, *refs):
        resid = x[...].astype(F32) + own[...]
        for ref in refs[:count]:
            resid += ref[...].astype(F32)
        refs[count][...] = resid
        normed = resid * lax.rsqrt(jnp.mean(resid * resid, axis=-1, keepdims=True) + EPS)
        refs[count + 1][...] = regroup((normed * gain[...]).astype(BF16), outer, inner)

    return pl.pallas_call(
        body,
        out_shape=(
            jax.ShapeDtypeStruct(x.shape, F32),
            jax.ShapeDtypeStruct(x.shape, BF16),
        ),
        compiler_params=kernel_params(),
        cost_estimate=LIGHT,
    )(x, own, gain, *sent)


def second_norm_back(resid, own, sent, gain, grad_out, outer, inner):
    count = len(sent)

    def body(resid, own, gain, grad_out, *refs):
        grad = own[...]
        for ref in refs[:count]:
            grad += ref[...].astype(F32)
        grad = regroup(grad, inner, outer)
        rows = resid[...]
        inverse = lax.rsqrt(jnp.mean(rows * rows, axis=-1, keepdims=True) + EPS)
        total = grad_out[...].astype(F32) + norm_back(grad, rows * inverse, inverse, gain[...])
        refs[count][...] = total
        refs[count + 1][...] = total.astype(BF16)

    return pl.pallas_call(
        body,
        out_shape=(
            jax.ShapeDtypeStruct(resid.shape, F32),
            jax.ShapeDtypeStruct(resid.shape, BF16),
        ),
        compiler_params=kernel_params(),
        cost_estimate=LIGHT,
    )(resid, own, gain, grad_out, *sent)


def dot_blocks(left, right, came, blocks, product):
    tokens, columns = came.shape[0] // blocks, came.shape[1]

    def body(a, b, c, *outs):
        for j, out in enumerate(outs):
            rows = pl.ds(j * tokens, tokens)
            out[...] = (product(a[rows, :], b[...]) + c[rows, :].astype(F32)).astype(out.dtype)

    return pl.pallas_call(
        body,
        out_shape=[
            jax.ShapeDtypeStruct((tokens, columns), BF16 if j else F32) for j in range(blocks)
        ],
        compiler_params=kernel_params(),
        cost_estimate=LIGHT,
    )(left, right, came)


def columns_out(gate, up, planes, members):
    rows, ff = gate.shape
    part = ff // (planes * members)

    def body(g, u, o):
        both = g[...], u[...]
        for s in range(members):
            o[s] = jnp.concatenate(
                [
                    v[:, (p * members + s) * part : (p * members + s + 1) * part]
                    for v in both
                    for p in range(planes)
                ],
                axis=1,
            )

    return pl.pallas_call(
        body,
        out_shape=jax.ShapeDtypeStruct((members, rows, 2 * planes * part), gate.dtype),
        compiler_params=kernel_params(),
        cost_estimate=LIGHT,
    )(gate, up)


def columns_back(blocks, gate, up, gain, planes):
    members, rows, both = blocks.shape
    part = both // (2 * planes)
    ff = planes * members * part

    def body(x, g, u, gn, og, ou, ogn):
        total = 0.0
        for m, (w, o) in enumerate(((g, og), (u, ou))):
            grad = jnp.concatenate(
                [
                    x[s, :, (m * planes + p) * part : (m * planes + p + 1) * part]
                    for p in range(planes)
                    for s in range(members)
                ],
                axis=1,
            ).astype(F32)
            o[...] = grad
            total += jnp.sum(w[...].astype(F32) * grad, axis=1, keepdims=True)
        ogn[...] = total / gn[...].astype(F32)

    shape = jax.ShapeDtypeStruct((rows, ff), F32)
    out = pl.pallas_call(
        body,
        out_shape=(shape, shape, jax.ShapeDtypeStruct((rows, 1), F32)),
        compiler_params=kernel_params(),
        cost_estimate=LIGHT,
    )(blocks, gate, up, gain[:, None])
    return out[0], out[1], out[2][:, 0]


def scatter_dp(left, right, size, product):
    came = swap(product(left[left.shape[0] // 2 :], right).astype(BF16), 1)
    return dot_blocks(left, right, came, size // 2, product)


def attention_weights(parts, place, at_gains):
    size = len(parts)
    a, b, m = parts[0].shape
    lanes = at_gains // 128 * 128

    def body(at, *refs):
        out, gains = refs[-2:]
        for j in range(size):
            out[:, pl.ds(lax.rem(at[0] + j, size), 1)] = refs[j][...][:, None]
        strip = out[:, :, :, lanes : lanes + 128].reshape(a * size * b, 128).astype(F32)
        gains[...] = strip.T[at_gains - lanes : at_gains - lanes + 2]

    return pl.pallas_call(
        body,
        in_specs=[pl.BlockSpec(memory_space=pltpu.SMEM)]
        + [pl.BlockSpec(memory_space=pltpu.VMEM)] * size,
        out_shape=(
            jax.ShapeDtypeStruct((a, size, b, m), parts[0].dtype),
            jax.ShapeDtypeStruct((2, a * size * b), F32),
        ),
        compiler_params=kernel_params(),
        cost_estimate=LIGHT,
    )(jnp.full((1,), place, jnp.int32), *parts)


def norm_back(grad_in, normed, inverse, gain):
    grad_normed = grad_in * gain
    return inverse * (
        grad_normed - normed * jnp.mean(grad_normed * normed, axis=-1, keepdims=True)
    )


def per_device(
    n,
    c,
    tokens,
    segment_ids,
    out_grad,
    gain_attn,
    w_query,
    key_weight,
    value_weight,
    w_out,
    gain_mlp,
    w_gate,
    w_up,
    w_down,
):
    t, width = tokens.shape[1:]
    length = segment_ids.shape[1]
    block = w_query.shape[0]
    ff = w_gate.shape[1]
    heads = QUERY_HEADS // n
    group = QUERY_HEADS // KEY_VALUE_HEADS
    q_cols, f_cols = heads * HEAD_SIZE, ff // n
    every_dp = ("plane", "core")
    plane, core, place_z = (lax.axis_index(axis) for axis in ("plane", "core", "ctx"))
    me = 2 * plane + core

    pieces = []
    used = q_cols + HEAD_SIZE
    extras = jnp.concatenate(
        [gain_attn[:, None], gain_mlp[:, None], segment_ids.astype(BF16).reshape(block, -1)], axis=1
    )
    extras = jnp.pad(extras, ((0, 0), (0, -(used + extras.shape[1]) % 128)))
    for d in range(n):
        g = d * heads // group
        kv = value_weight if d % 2 else key_weight
        pieces += [
            w_query[:, d * q_cols : (d + 1) * q_cols],
            kv[:, g * HEAD_SIZE : (g + 1) * HEAD_SIZE],
            extras,
        ]
    w_attn = jnp.concatenate(pieces, axis=1).reshape(block, n, -1).transpose(1, 0, 2)
    w_attn = lax.all_to_all(w_attn, every_dp, 0, 0)
    x16, dy_local = tokens[0], out_grad[0]
    wd = lax.all_gather(w_down, "ctx", axis=0, tiled=True)
    wo = lax.all_gather(w_out, "ctx", axis=0, tiled=True)
    seg_rows = w_attn[:, :, used + 2 : used + 2 + length // block].reshape(n, length)

    order = me ^ jnp.array([*range(0, n, 2), *range(1, n, 2)], jnp.int32)
    pick = (order[:, None] == jnp.arange(n, dtype=jnp.int32)[None]).astype(BF16)
    segs = dot(pick, seg_rows)
    local_idx = place_z * t + jnp.arange(t, dtype=jnp.int32)
    local_seg = lax.dynamic_slice_in_dim(segs, place_z * t, t, axis=1)
    before = jnp.sum((segs[:, None, :] < local_seg[:, :, None]).astype(jnp.int32), axis=2)
    place = (local_idx[None] - before).astype(F32)
    freq = 10000.0 ** (-jnp.arange(HEAD_SIZE // 2, dtype=F32) / (HEAD_SIZE // 2))
    angle = place.reshape(n * t)[:, None] * freq[None, :]
    cosine, sine = jnp.cos(angle), jnp.sin(angle)
    cosine = jnp.concatenate([cosine] * 4, axis=1)
    sine = jnp.concatenate([-sine, sine] * 2, axis=1)
    w_pair = columns_out(*after((w_gate, w_up), w_attn), 1, n)
    w_pair = lax.all_to_all(w_pair, every_dp, 0, 0).reshape(n * block, 2 * f_cols)
    w_pair = lax.all_gather(w_pair, "ctx", axis=0, tiled=True)
    w_parts, same, cosine, sine = together(
        shifts(w_attn, c), dp_same(after(x16, w_attn), n), cosine, sine
    )
    even = jnp.concatenate([x16, *same])
    odd = swap(even, 1)

    w_attn, gains = attention_weights([w_attn, *w_parts], place_z, used)
    w_attn = w_attn.reshape(width, -1)
    gain1, gain2 = gains[:1], gains[1:]
    where = jnp.stack([place_z, core]).astype(jnp.int32)
    key_seg = lax.dynamic_slice_in_dim(
        jnp.concatenate([segs, segs], axis=1), place_z * t, length, axis=1
    )
    sides = local_seg[:, :, None], key_seg[:, None, :]

    first_in, queries, kv_own = project(where, even, odd, gain1, w_attn, cosine, sine, q_cols, t)

    kv_parts, dy_same = together(shifts(kv_own, c), dp_same(after(dy_local, first_in), n))
    dy_same = jnp.concatenate([dy_local, *dy_same])
    dy = dy_same, swap(dy_same, 1)
    kv_all = [kv_own, *kv_parts]
    kv_other = [swap(v, 1) for v in kv_all]
    mixed = attend(where, queries, kv_all, kv_other, *sides)
    attn_own, *sends = scatter_dp(mixed, wo, n, dot)
    sent = together(*[swap(v, 2 * j) for j, v in enumerate(sends, 1)])
    resid, second_in = second_norm(x16, attn_own, sent, gain2, n, c)

    in_parts, grad_hidden = together(
        dp_same(second_in, n), [dot_nt(half, wd).astype(BF16) for half in dy]
    )
    second_in = jnp.concatenate([second_in, *in_parts])
    second_in = second_in, swap(second_in, 1)
    same = feed_forward(second_in[0], grad_hidden[0], w_pair, wd)
    other = feed_forward(second_in[1], after(grad_hidden[1], same[2]), w_pair, wd)
    hidden, grad_pair = (same[0], other[0]), (same[1], other[1])
    back_came = swap(other[2], 1)
    down_term = transposed_dot(hidden, dy)
    grad_down = lax.psum_scatter(down_term, "ctx", scatter_dimension=0, tiled=True)
    back, *sends = add_blocks(same[2], after(back_came, down_term), n // 2)
    forth = swap(after(other[3], sends), 1)
    pair_term = transposed_dot(after(second_in, forth, down_term), grad_pair)
    forth, *forth_sends = add_blocks(same[3], forth, n // 2)
    sent, pair_term, forth_sends = together(
        [swap(v, 2 * j) for j, v in enumerate(sends, 1)], pair_term, forth_sends
    )
    grad_resid, branch = second_norm_back(resid, back, sent, gain2, dy_local, n, c)

    same, grad_down, pair_term = together(dp_same(branch, n), grad_down, pair_term)
    pair_sum = lax.psum_scatter(pair_term, "ctx", scatter_dimension=0, tiled=True)
    same = jnp.concatenate([branch, *same])
    grad_branch = same, swap(same, 1)
    grad_q, kept, sent = attend_back(
        where, *grad_branch, wo, queries, kv_all, kv_other, *sides, cosine, sine
    )
    result_parts = [swap(v, 2 * j) for j, v in enumerate(forth_sends, 1)]
    kept, sent, result_parts = together(kept, sent, result_parts)
    own_kv, *kv_sends = add_parts(kept, swap(sent, 1))
    kv_parts = together(*[shift(v, -j, c) for j, v in enumerate(kv_sends, 1)])
    result = resid + forth + sum(v.astype(F32) for v in result_parts)
    grad_kv = sum_keys(where, own_kv, kv_parts, cosine, sine)
    unused = jnp.zeros((n * t, w_attn.shape[1] - used), BF16)
    grad_attn = jnp.concatenate([grad_q, grad_kv, unused], axis=1)
    first_own, *sends = scatter_dp(grad_attn, w_attn, n, dot_nt)
    own_terms, *terms = attention_weight_terms(
        where, first_in, grad_attn, mixed, grad_branch, used, n, c
    )
    sent, terms = together(
        [swap(v, 2 * j) for j, v in enumerate(sends, 1)],
        [shift(v, -j, c) for j, v in enumerate(terms, 1)],
    )
    pair_sum = after(pair_sum, terms).reshape(n, block, 2 * f_cols)
    pair_sum = lax.all_to_all(pair_sum, every_dp, 0, 0)
    terms = (own_terms.astype(F32) + sum(v.astype(F32) for v in terms)).reshape(n, block, -1)
    grad_wout = terms[:, :, used : used + width // n].transpose(1, 0, 2).reshape(block, width)
    attn_sum = lax.all_to_all(terms[:, :, :used].astype(BF16), every_dp, 0, 0).astype(F32)
    grad_first = first_own + sum(v.astype(F32) for v in sent)
    grad_down = after(grad_down, attn_sum).astype(F32)

    grad_gate, grad_up, grad_gain_mlp = columns_back(pair_sum, w_gate, w_up, gain_mlp, 1)
    grad_query = attn_sum[:, :, :q_cols].transpose(1, 0, 2).reshape(block, -1)
    kv_sum = attn_sum[:, :, q_cols:].reshape(KEY_VALUE_HEADS, -1, 2, block, HEAD_SIZE).sum(axis=1)
    grad_key = kv_sum[:, 0].transpose(1, 0, 2).reshape(block, -1)
    grad_value = kv_sum[:, 1].transpose(1, 0, 2).reshape(block, -1)
    grad_gain_attn = (
        jnp.sum(w_query.astype(F32) * grad_query, axis=1)
        + jnp.sum(key_weight.astype(F32) * grad_key, axis=1)
        + jnp.sum(value_weight.astype(F32) * grad_value, axis=1)
    ) / gain_attn.astype(F32)
    x = x16.astype(F32)
    inverse1 = lax.rsqrt(jnp.mean(x * x, axis=-1, keepdims=True) + EPS)
    grad_input = grad_resid + norm_back(grad_first, x * inverse1, inverse1, gain1)
    return (
        result.astype(BF16)[None],
        grad_input[None],
        grad_gain_attn,
        grad_query,
        grad_key,
        grad_value,
        grad_wout,
        grad_gain_mlp,
        grad_gate,
        grad_up,
        grad_down,
    )


def solution(mesh):
    n, c = mesh.shape["dp"], mesh.shape["ctx"]
    split = Mesh(mesh.devices.reshape(n // 2, 2, c), ("plane", "core", "ctx"))
    dp, every = ("plane", "core"), ("plane", "core", "ctx")
    rows = P(dp, "ctx", None)
    weight, gain = P(every, None), P(every)
    return jax.shard_map(
        functools.partial(per_device, n, c),
        mesh=split,
        in_specs=(rows, P(dp, None), rows, gain, weight, weight, weight, weight, gain)
        + (weight,) * 3,
        out_specs=(rows, rows, gain, weight, weight, weight, weight, gain) + (weight,) * 3,
        check_vma=False,
    )
```

time: 804 us -> 585 us (0.73)
  local copies, waits for them, and re-layouts: 205 us -> 59.3 us
  Pallas kernels: 0 us -> 109 us
  matrix products: 92.3 us -> 14.5 us
  blocking collectives: 66.2 us -> 0 us
  other arithmetic: 71.2 us -> 22.5 us
  waiting for transfers between devices: 245 us -> 265 us
    pallas_call x0 -> x19, Pallas kernels: none -> 109 us  [the longest x2 26.3 us: feed_forward(): pl.pallas_call(body, grid=(tokens // tile,), in_specs=[rows(width), rows(...]
    unnamed x299 -> x231, local copies, waits for them, and re-layouts: 134 us -> 47.2 us
    dot_general x10 -> x0, matrix products: 45.2 us -> none  [the longest x4 26 us: dot_tn(): lax.dot_general(left, right, (((0,), (0,)), ((), ())), preferred_element_...]
    all_to_all x2 -> x0, blocking collectives: 34.7 us -> none  [the longest x1 22.7 us: per_device(): w_pair = lax.all_to_all(w_pair, 'dp', 0, 0).reshape(n * block, 2 * f_cols)]
    all_gather x1 -> x0, blocking collectives: 31.6 us -> none  [per_device(): lax.all_gather(jnp.stack([gain_attn, gain_mlp]), ('ctx', 'dp'), axis=1, t...]
    reduce_scatter x4 -> x2, waiting for transfers between devices: 30.9 us -> 0.01 us  [the longest x1 0.01 us: per_device(): lax.psum_scatter(down_term, 'ctx', scatter_dimension=0, tiled=True)]
    ppermute x123 -> x49, waiting for transfers between devices: 212 us -> 240 us  [the longest x12 169 us: shift(): lax.ppermute(value, 'ctx', [(i, (i - step) % size) for i in range(size)])]
    convert_element_type x28 -> x3, other arithmetic: 28.2 us -> 3.18 us  [the longest x1 2.42 us: per_device(): grad_down = after(grad_down, attn_sum).astype(F32)]
  transfers between devices with their start and end apart: 133 -> 58, of which waited for: 41 -> 26; matrix products, arithmetic and copies ran while one was open for 37% -> 10% of each run, Pallas kernels for 0% -> 15%
where the time goes in v2:
time: 585 us; the launch traced here: 576 us
  waiting for transfers between devices  265 us (45%)
  Pallas kernels  109 us (19%)
  starting transfers between devices  89.8 us (15%)
  local copies, waits for them, and re-layouts  59.3 us (10%)
  other arithmetic  22.5 us (4%)
  between operations  15.2 us (3%)
  matrix products  14.5 us (2%)
    ppermute x12, waiting for transfers between devices, shift(): lax.ppermute(value, 'ctx', [(i, (i - step) % size) for i in range(size)])  169 us
    ppermute x37, waiting for transfers between devices, swap(): lax.ppermute(value, ('plane', 'core'), [(i, i ^ rel) for i in range(size)])  70.9 us
    unnamed x231, local copies, waits for them, and re-layouts  47.2 us
    ppermute x12, starting transfers between devices, shift(): lax.ppermute(value, 'ctx', [(i, (i - step) % size) for i in range(size)])  42.2 us
    ppermute x37, starting transfers between devices, swap(): lax.ppermute(value, ('plane', 'core'), [(i, i ^ rel) for i in range(size)])  32.7 us
    pallas_call x2, Pallas kernels, feed_forward(): pl.pallas_call(body, grid=(tokens // tile,), in_specs=[rows(width), rows(...  26.3 us
    pallas_call x1, Pallas kernels, attend_back(): pl.pallas_call(body, grid=(sequences,), in_specs=[pl.BlockSpec(memory_spa...  17.8 us
    pallas_call x2, Pallas kernels, transposed_dot(): pl.pallas_call(body, grid=(rows // row_tile if by_rows else columns // co...  17.7 us
  transfers between devices with their start and end apart: 58, of which 26 were waited for; matrix products, arithmetic and copies ran while one was open for 10% of the time, Pallas kernels for 15%

profile of v2, /device:TPU:24, one launch (start us, length us, event | category | flops | bytes accessed | tf_op | source)
XLA Modules:
  0.0 575.6 jit_solution(11796666392001590731)
XLA Ops:
  13.2 3.7 all-to-all-start
  17.0 8.3 %all-to-all-done.refs_0_ = bf16[8,64,384]{2,1,0:T(8,128)(2,1)S(1)} async-done(((bf16[8,64,384]{2,1,0:T(8,128)(2,1)}), bf16[8,64,384]{2,1,0:T(8,128)(2,1)S(1)}, u32[]{:S(2)}, u32[]{:S(2)}) %all-to-all-start) | async-done | bytes 393248 | tf_op jit(solution)/shard_map/all_to_all | solution.py:646
  26.4 2.4 collective-permute-start.5
  30.4 3.6 all-to-all-start.1
  35.6 12.4 %collective-permute-done.refs_1_ = bf16[8,64,384]{2,1,0:T(8,128)(2,1)S(1)} collective-permute-done((bf16[8,64,384]{2,1,0:T(8,128)(2,1)S(1)}, bf16[8,64,384]{2,1,0:T(8,128)(2,1)S(1)}, u32[]{:S(2)}, u32[]{:S(2)}) %collective-permute-start) | collective-permute-done | bytes 393248 | tf_op jit(solution)/shard_map/ppermute | solution.py:38
  48.0 1.9 fusion.11
  50.8 31.4 %collective-permute-done.1.refs_2_ = bf16[8,64,384]{2,1,0:T(8,128)(2,1)S(1)} collective-permute-done((bf16[8,64,384]{2,1,0:T(8,128)(2,1)S(1)}, bf16[8,64,384]{2,1,0:T(8,128)(2,1)S(1)}, u32[]{:S(2)}, u32[]{:S(2)}) %collective-permute-start.1) | collective-permute-done | bytes 393248 | tf_op jit(solution)/shard_map/ppermute | solution.py:38
  83.0 1.7 collective-permute-done.2.refs_3_
  85.5 2.9 pad_maximum_fusion.e
  93.6 7.8 %shard_map.213 = (bf16[1024,2048]{1,0:T(8,128)(2,1)}, bf16[1024,256]{1,0:T(8,128)(2,1)S(1)}, bf16[8,64,128]{2,1,0:T(8,128)(2,1)S(1)}) custom-call(s32[2]{0:T(128)S(1)} %pad_add_fusion.at, bf16[512,2048]{1,0:T(8,128)(2,1)} %pad_maximum_fusion.e, bf16[512,2048]{1,0:T(8,128)(2,1)} %collective-permute-done.6.o, f32[1,2048]{1,0:T(1,128)S(1)} %get-tuple-element.242.gn, ...), custom_call_target="tpu_custom_call" | custom-call | flops 1024 | bytes 1024 | tf_op jit(solution)/shard_map/pallas_call | solution.py:140
  102.2 1.8 collective-permute-start.10
  105.7 26.4 %collective-permute-start.7 = (bf16[8,64,128]{2,1,0:T(8,128)(2,1)S(1)}, bf16[8,64,128]{2,1,0:T(8,128)(2,1)S(1)}, u32[]{:S(2)}, u32[]{:S(2)}) collective-permute-start(bf16[8,64,128]{2,1,0:T(8,128)(2,1)S(1)} %get-tuple-element.129.refs_0_), channel_id=1, source_target_pairs={{0,3},{1,0},{2,1},{3,2},{4,7},{5,4},{6,5},{7,6},{8,11},{9,8},{10,9... | collective-permute-start | bytes 393224 | tf_op jit(solution)/shard_map/ppermute | solution.py:38
  132.1 5.1 collective-permute-done.7.refs_1_
  137.1 13.4 %collective-permute-done.8.refs_2_ = bf16[8,64,128]{2,1,0:T(8,128)(2,1)S(1)} collective-permute-done((bf16[8,64,128]{2,1,0:T(8,128)(2,1)S(1)}, bf16[8,64,128]{2,1,0:T(8,128)(2,1)S(1)}, u32[]{:S(2)}, u32[]{:S(2)}) %collective-permute-start.8) | collective-permute-done | bytes 131104 | tf_op jit(solution)/shard_map/ppermute | solution.py:38
  161.3 10.0 %shard_map.214.a.m = bf16[1024,256]{1,0:T(8,128)(2,1)S(1)} custom-call(s32[2]{0:T(128)S(1)} %copy-done.70, bf16[1024,256]{1,0:T(8,128)(2,1)S(1)} %copy-done.25, f32[8,128,1]{2,1,0:T(8,128)S(1)} %copy.94.m, f32[8,1,512]{2,1,0:T(1,128)S(1)} %broadcast_in_dim.34.th, bf16[8,64,128]{2,1,0:T(8,128)(2,1)S(1)} %get-tuple-element.129.refs_0_, ...), custom_call_target="tpu_custom_call" | custom-call | flops 1024 | bytes 1024 | tf_op jit(solution)/shard_map/pallas_call | solution.py:219
  171.4 2.0 convolution_convert_fusion
  174.2 3.0 pad_maximum_fusion.1.refs_2_
  179.7 3.2 shard_map.215
  183.9 1.6 collective-permute-start.18
  187.4 5.3 convolution_convert_fusion.3.dh
  192.8 6.1 %collective-permute-done.18.refs_0_ = bf16[128,2048]{1,0:T(8,128)(2,1)S(1)} collective-permute-done((bf16[128,2048]{1,0:T(8,128)(2,1)}, bf16[128,2048]{1,0:T(8,128)(2,1)S(1)}, u32[]{:S(2)}, u32[]{:S(2)}) %collective-permute-start.18) | collective-permute-done | bytes 524320 | tf_op jit(solution)/shard_map/ppermute | solution.py:34
  199.7 11.0 %collective-permute-done.19.refs_1_ = bf16[128,2048]{1,0:T(8,128)(2,1)S(1)} collective-permute-done((bf16[128,2048]{1,0:T(8,128)(2,1)}, bf16[128,2048]{1,0:T(8,128)(2,1)S(1)}, u32[]{:S(2)}, u32[]{:S(2)}) %collective-permute-start.19) | collective-permute-done | bytes 524320 | tf_op jit(solution)/shard_map/ppermute | solution.py:34
  214.8 1.7 shard_map.216
  220.0 4.3 convolution_convert_fusion.2.dh
  225.2 6.2 %collective-permute-done.21 = bf16[128,2048]{1,0:T(8,128)(2,1)S(1)} collective-permute-done((bf16[128,2048]{1,0:T(8,128)(2,1)S(1)}, bf16[128,2048]{1,0:T(8,128)(2,1)S(1)}, u32[]{:S(2)}, u32[]{:S(2)}) %collective-permute-start.21) | collective-permute-done | bytes 524320 | tf_op jit(solution)/shard_map/ppermute | solution.py:34
  231.4 8.3 %collective-permute-done.22 = bf16[128,2048]{1,0:T(8,128)(2,1)S(1)} collective-permute-done((bf16[128,2048]{1,0:T(8,128)(2,1)S(1)}, bf16[128,2048]{1,0:T(8,128)(2,1)S(1)}, u32[]{:S(2)}, u32[]{:S(2)}) %collective-permute-start.22) | collective-permute-done | bytes 524320 | tf_op jit(solution)/shard_map/ppermute | solution.py:34
  239.8 1.8 collective-permute-done.23
  245.3 13.5 %shard_map.218 = (bf16[512,704]{1,0:T(8,128)(2,1)S(1)}, bf16[512,1408]{1,0:T(8,128)(2,1)S(1)}, bf16[512,2048]{1,0:T(8,128)(2,1)S(1)}, bf16[512,2048]{1,0:T(8,128)(2,1)}) custom-call(bf16[512,2048]{1,0:T(8,128)(2,1)} %constant_dynamic-update-slice_fusion.x.refs_0_, bf16[512,704]{1,0:T(8,128)(2,1)S(1)} %copy-done.39, ...), custom_call_target="tpu_custom_call" | custom-call | flops 1024 | bytes 1024 | tf_op jit(solution)/shard_map/pallas_call | solution.py:402
  261.2 12.9 %shard_map.219 = (bf16[512,704]{1,0:T(8,128)(2,1)S(1)}, bf16[512,1408]{1,0:T(8,128)(2,1)S(1)}, bf16[512,2048]{1,0:T(8,128)(2,1)S(1)}, bf16[512,2048]{1,0:T(8,128)(2,1)}) custom-call(bf16[512,2048]{1,0:T(8,128)(2,1)} %collective-permute-done.25.x.refs_1_, bf16[512,704]{1,0:T(8,128)(2,1)S(1)} %copy-done.40, bf16[2048,1408]{1,0:T(8,128)(2,1)} %all-gather.8.cloned.1.call-done.w, ...), custom_call_target="tpu_custom_call" | custom-call | flops 1024 | bytes 1024 | tf_op jit(solution)/shard_map/pallas_call | solution.py:402
  276.5 6.5 %shard_map.220 = bf16[704,2048]{1,0:T(8,128)(2,1)} custom-call(bf16[512,704]{1,0:T(8,128)(2,1)S(1)} %get-tuple-element.159.refs_0_, bf16[512,704]{1,0:T(8,128)(2,1)S(1)} %get-tuple-element.160.refs_1_, bf16[512,2048]{1,0:T(8,128)(2,1)} %pad_maximum_fusion.1.refs_2_, bf16[512,2048]{1,0:T(8,128)(2,1)} %collective-permute-done.24.refs_3_), custom_call_target="tpu_custom_call" | custom-call | flops 1024 | bytes 1024 | tf_op jit(solution)/shard_map/pallas_call | solution.py:80
  283.7 4.0 collective-permute-done.26.b
  289.0 1.6 copy-done.23
  290.6 3.0 shard_map.221
  295.5 1.7 collective-permute-start.29
  299.1 11.2 %shard_map.223 = bf16[2048,1408]{1,0:T(8,128)(2,1)} custom-call(bf16[512,2048]{1,0:T(8,128)(2,1)} %constant_dynamic-update-slice_fusion.x.refs_0_, bf16[512,2048]{1,0:T(8,128)(2,1)} %collective-permute-done.25.x.refs_1_, bf16[512,1408]{1,0:T(8,128)(2,1)S(1)} %copy-done.28, bf16[512,1408]{1,0:T(8,128)(2,1)S(1)} %copy-done.30), custom_call_target="tpu_custom_call" | custom-call | flops 1024 | bytes 1024 | tf_op jit(solution)/shard_map/pallas_call | solution.py:80
  311.9 2.2 shard_map.222
  315.7 5.1 collective-permute-done.29.refs_1_
  320.8 2.4 shard_map.224
  327.7 11.4 %collective-permute-done.31 = bf16[128,2048]{1,0:T(8,128)(2,1)S(1)} collective-permute-done((bf16[128,2048]{1,0:T(8,128)(2,1)S(1)}, bf16[128,2048]{1,0:T(8,128)(2,1)S(1)}, u32[]{:S(2)}, u32[]{:S(2)}) %collective-permute-start.31) | collective-permute-done | bytes 524320 | tf_op jit(solution)/shard_map/ppermute | solution.py:34
  339.1 10.7 %collective-permute-done.32 = bf16[128,2048]{1,0:T(8,128)(2,1)S(1)} collective-permute-done((bf16[128,2048]{1,0:T(8,128)(2,1)S(1)}, bf16[128,2048]{1,0:T(8,128)(2,1)S(1)}, u32[]{:S(2)}, u32[]{:S(2)}) %collective-permute-start.32) | collective-permute-done | bytes 524320 | tf_op jit(solution)/shard_map/ppermute | solution.py:34
  355.4 2.4 collective-permute-start.37
  359.8 17.8 %shard_map.225 = (bf16[1024,256]{1,0:T(8,128)(2,1)S(1)}, f32[8,4,64,128]{3,2,1,0:T(8,128)S(1)}, bf16[8,4,64,128]{3,2,1,0:T(8,128)(2,1)S(1)}) custom-call(s32[2]{0:T(128)S(1)} %copy-done.71, bf16[512,2048]{1,0:T(8,128)(2,1)} %copy-done.1, bf16[512,2048]{1,0:T(8,128)(2,1)} %copy-done.79, bf16[256,2048]{1,0:T(8,128)(2,1)} %all-gather.4.cloned.1.call-done.b.w, ...), custom_call_target="tpu_custom_call" | custom-call | flops 1024 | bytes 1024 | tf_op jit(solution)/shard_map/pallas_call | solution.py:269
  377.6 2.4 collective-permute-done.36
  380.1 1.9 collective-permute-done.38.b
  382.1 6.9 %collective-permute-start.39 = (bf16[8,64,128]{2,1,0:T(8,128)(2,1)S(1)}, bf16[8,64,128]{2,1,0:T(8,128)(2,1)S(1)}, u32[]{:S(2)}, u32[]{:S(2)}) collective-permute-start(bf16[8,64,128]{2,1,0:T(8,128)(2,1)S(1)} %get-tuple-element.196), channel_id=1, source_target_pairs={{0,1},{1,2},{2,3},{3,0},{4,5},{5,6},{6,7},{7,4},{8,9},{9,10},{10,1... | collective-permute-start | bytes 393224 | tf_op jit(solution)/shard_map/ppermute | solution.py:38
  389.0 5.6 collective-permute-start.40
  394.7 8.3 %collective-permute-done.39.refs_0_ = bf16[8,64,128]{2,1,0:T(8,128)(2,1)S(1)} collective-permute-done((bf16[8,64,128]{2,1,0:T(8,128)(2,1)S(1)}, bf16[8,64,128]{2,1,0:T(8,128)(2,1)S(1)}, u32[]{:S(2)}, u32[]{:S(2)}) %collective-permute-start.39) | collective-permute-done | bytes 131104 | tf_op jit(solution)/shard_map/ppermute | solution.py:38
  403.0 19.7 %collective-permute-done.40.refs_1_ = bf16[8,64,128]{2,1,0:T(8,128)(2,1)S(1)} collective-permute-done((bf16[8,64,128]{2,1,0:T(8,128)(2,1)S(1)}, bf16[8,64,128]{2,1,0:T(8,128)(2,1)S(1)}, u32[]{:S(2)}, u32[]{:S(2)}) %collective-permute-start.40) | collective-permute-done | bytes 131104 | tf_op jit(solution)/shard_map/ppermute | solution.py:38
  424.2 2.6 convolution_convert_fusion.1
  426.8 8.3 %shard_map.229 = (bf16[512,640]{1,0:T(8,128)(2,1)S(1)}, bf16[512,640]{1,0:T(8,128)(2,1)}, bf16[512,640]{1,0:T(8,128)(2,1)}, bf16[512,640]{1,0:T(8,128)(2,1)}) custom-call(s32[2]{0:T(128)S(1)} %copy-done.71, bf16[1024,2048]{1,0:T(8,128)(2,1)} %get-tuple-element.130.x, bf16[1024,384]{1,0:T(8,128)(2,1)S(1)} %maximum_maximum_fusion.a.g, ...), custom_call_target="tpu_custom_call" | custom-call | flops 1024 | bytes 1024 | tf_op jit(solution)/shard_map/pallas_call | solution.py:363
  435.4 2.3 collective-permute-start.48
  439.0 3.8 shard_map.228
  442.8 1.8 collective-permute-start.43
  446.0 28.0 %collective-permute-done.46 = bf16[512,640]{1,0:T(8,128)(2,1)} collective-permute-done((bf16[512,640]{1,0:T(8,128)(2,1)}, bf16[512,640]{1,0:T(8,128)(2,1)}, u32[]{:S(2)}, u32[]{:S(2)}) %collective-permute-start.46) | collective-permute-done | bytes 655392 | tf_op jit(solution)/shard_map/ppermute | solution.py:38
  474.0 2.4 collective-permute-start.45
  477.5 49.1 %collective-permute-done.47 = bf16[512,640]{1,0:T(8,128)(2,1)} collective-permute-done((bf16[512,640]{1,0:T(8,128)(2,1)}, bf16[512,640]{1,0:T(8,128)(2,1)}, u32[]{:S(2)}, u32[]{:S(2)}) %collective-permute-start.47) | collective-permute-done | bytes 655392 | tf_op jit(solution)/shard_map/ppermute | solution.py:38
  526.7 2.3 add_add_fusion
  530.9 3.8 all-to-all-start.2
  534.7 1.9 fusion.2
  538.3 4.8 all-to-all-done.2
  543.0 3.6 all-to-all-start.3
  552.2 2.4 convert_element_type.111
  555.5 10.7 %all-to-all-done.3.x = bf16[8,64,1408]{2,1,0:T(8,128)(2,1)S(1)} async-done(((bf16[8,64,1408]{2,1,0:T(8,128)(2,1)}), bf16[8,64,1408]{2,1,0:T(8,128)(2,1)S(1)}, u32[]{:S(2)}, u32[]{:S(2)}) %all-to-all-start.3) | async-done | bytes 1441824 | tf_op jit(solution)/shard_map/all_to_all | solution.py:738
  566.2 2.1 shard_map.230
  (367 shorter events, 92.2 us)
Async XLA Ops:
  7.2 164.2 %all-gather.4.cloned.1.call-start = ((), (), s32[]{:S(2)}) async-start(), calls=%async_computation.6 | async-start | bytes 1310720 | tf_op jit(solution)/shard_map/all_gather | solution.py:649
  8.0 179.5 %all-gather.6.cloned.1.call-start = ((), (), s32[]{:S(2)}) async-start(), calls=%async_computation.7 | async-start | bytes 3604480 | tf_op jit(solution)/shard_map/all_gather | solution.py:648
  13.2 12.1 %all-to-all-start = ((bf16[8,64,384]{2,1,0:T(8,128)(2,1)}), bf16[8,64,384]{2,1,0:T(8,128)(2,1)S(1)}, u32[]{:S(2)}, u32[]{:S(2)}) async-start(bf16[8,64,384]{2,1,0:T(8,128)(2,1)} %bitcast.51), calls=%async_computation | async-start | bytes 786432 | tf_op jit(solution)/shard_map/all_to_all | solution.py:646
  25.3 60.2 %collective-permute-start.3 = (bf16[128,2048]{1,0:T(8,128)(2,1)S(1)}, bf16[128,2048]{1,0:T(8,128)(2,1)}, u32[]{:S(2)}, u32[]{:S(2)}) collective-permute-start(bf16[128,2048]{1,0:T(8,128)(2,1)S(1)} %bitcast.57), channel_id=1, source_target_pairs={{0,8},{4,12},{8,0},{12,4},{16,24},{20,28},{24,16},{28,20},{1,9},{5... | collective-permute-start | bytes 1572872 | tf_op jit(solution)/shard_map/ppermute | solution.py:34
  25.8 59.6 %collective-permute-start.4 = (bf16[128,2048]{1,0:T(8,128)(2,1)S(1)}, bf16[128,2048]{1,0:T(8,128)(2,1)}, u32[]{:S(2)}, u32[]{:S(2)}) collective-permute-start(bf16[128,2048]{1,0:T(8,128)(2,1)S(1)} %bitcast.58), channel_id=1, source_target_pairs={{0,16},{4,20},{8,24},{12,28},{16,0},{20,4},{24,8},{28,12},{1,17},{... | collective-permute-start | bytes 1572872 | tf_op jit(solution)/shard_map/ppermute | solution.py:34
  26.4 59.1 %collective-permute-start.5 = (bf16[128,2048]{1,0:T(8,128)(2,1)S(1)}, bf16[128,2048]{1,0:T(8,128)(2,1)}, u32[]{:S(2)}, u32[]{:S(2)}) collective-permute-start(bf16[128,2048]{1,0:T(8,128)(2,1)S(1)} %bitcast.59), channel_id=1, source_target_pairs={{0,24},{4,28},{8,16},{12,20},{16,8},{20,12},{24,0},{28,4},{1,25},{... | collective-permute-start | bytes 1572872 | tf_op jit(solution)/shard_map/ppermute | solution.py:34
  30.4 58.0 %all-to-all-start.1 = ((bf16[8,64,1408]{2,1,0:T(8,128)(2,1)}), bf16[8,64,1408]{2,1,0:T(8,128)(2,1)S(1)}, u32[]{:S(2)}, u32[]{:S(2)}) async-start(bf16[8,64,1408]{2,1,0:T(8,128)(2,1)} %shard_map.217), calls=%async_computation.1 | async-start | bytes 2883584 | tf_op jit(solution)/shard_map/all_to_all | solution.py:665
  34.0 210.2 %all-gather.8.cloned.1.call-start = ((), (), s32[]{:S(2)}) async-start(), calls=%async_computation.8 | async-start | bytes 7208960 | tf_op jit(solution)/shard_map/all_gather | solution.py:666
  34.1 13.9 %collective-permute-start = (bf16[8,64,384]{2,1,0:T(8,128)(2,1)S(1)}, bf16[8,64,384]{2,1,0:T(8,128)(2,1)S(1)}, u32[]{:S(2)}, u32[]{:S(2)}) collective-permute-start(bf16[8,64,384]{2,1,0:T(8,128)(2,1)S(1)} %all-to-all-done.refs_0_), channel_id=1, source_target_pairs={{0,3},{1,0},{2,1},{3,2},{4,7},{5,4},{6,5},{7,6},{8,11},{9,8},{10,9... | collective-permute-start | bytes 1179656 | tf_op jit(solution)/shard_map/ppermute | solution.py:38
  35.2 47.1 %collective-permute-start.1 = (bf16[8,64,384]{2,1,0:T(8,128)(2,1)S(1)}, bf16[8,64,384]{2,1,0:T(8,128)(2,1)S(1)}, u32[]{:S(2)}, u32[]{:S(2)}) collective-permute-start(bf16[8,64,384]{2,1,0:T(8,128)(2,1)S(1)} %all-to-all-done.refs_0_), channel_id=1, source_target_pairs={{0,2},{1,3},{2,0},{3,1},{4,6},{5,7},{6,4},{7,5},{8,10},{9,11},{10,... | collective-permute-start | bytes 1179656 | tf_op jit(solution)/shard_map/ppermute | solution.py:38
  48.0 36.8 %collective-permute-start.2 = (bf16[8,64,384]{2,1,0:T(8,128)(2,1)S(1)}, bf16[8,64,384]{2,1,0:T(8,128)(2,1)S(1)}, u32[]{:S(2)}, u32[]{:S(2)}) collective-permute-start(bf16[8,64,384]{2,1,0:T(8,128)(2,1)S(1)} %all-to-all-done.refs_0_), channel_id=1, source_target_pairs={{0,1},{1,2},{2,3},{3,0},{4,5},{5,6},{6,7},{7,4},{8,9},{9,10},{10,1... | collective-permute-start | bytes 1179656 | tf_op jit(solution)/shard_map/ppermute | solution.py:38
  50.3 43.3 %copy-start.4 = (f32[1024,128]{1,0:T(8,128)}, f32[1024,128]{1,0:T(8,128)S(1)}, u32[]{:S(2)}) copy-start(f32[1024,128]{1,0:T(8,128)S(1)} %pad_maximum_fusion.2.cs) | copy-start | bytes 1572868
  50.8 42.8 %copy-start.6 = (f32[1024,128]{1,0:T(8,128)}, f32[1024,128]{1,0:T(8,128)S(1)}, u32[]{:S(2)}) copy-start(f32[1024,128]{1,0:T(8,128)S(1)} %pad_maximum_fusion.3.sn) | copy-start | bytes 1572868
  88.4 5.2 collective-permute-start.6
  89.5 261.1 %reduce-scatter.3.cloned.1.call-start = ((), (), s32[]{:S(2)}) async-start(), calls=%async_computation.9 | async-start | bytes 3604480 | tf_op jit(solution)/shard_map/reduce_scatter | solution.py:704
  102.2 48.3 %collective-permute-start.10 = (bf16[128,2048]{1,0:T(8,128)(2,1)}, bf16[128,2048]{1,0:T(8,128)(2,1)S(1)}, u32[]{:S(2)}, u32[]{:S(2)}) collective-permute-start(bf16[128,2048]{1,0:T(8,128)(2,1)} %bitcast.9.grad_out), channel_id=1, source_target_pairs={{0,8},{4,12},{8,0},{12,4},{16,24},{20,28},{24,16},{28,20},{1,9},{5... | collective-permute-start | bytes 1572872 | tf_op jit(solution)/shard_map/ppermute | solution.py:34
  104.0 46.6 %collective-permute-start.11 = (bf16[128,2048]{1,0:T(8,128)(2,1)}, bf16[128,2048]{1,0:T(8,128)(2,1)}, u32[]{:S(2)}, u32[]{:S(2)}) collective-permute-start(bf16[128,2048]{1,0:T(8,128)(2,1)} %bitcast.9.grad_out), channel_id=1, source_target_pairs={{0,16},{4,20},{8,24},{12,28},{16,0},{20,4},{24,8},{28,12},{1,17},{... | collective-permute-start | bytes 1572872 | tf_op jit(solution)/shard_map/ppermute | solution.py:34
  105.5 45.9 %collective-permute-start.12 = (bf16[128,2048]{1,0:T(8,128)(2,1)}, bf16[128,2048]{1,0:T(8,128)(2,1)}, u32[]{:S(2)}, u32[]{:S(2)}) collective-permute-start(bf16[128,2048]{1,0:T(8,128)(2,1)} %bitcast.9.grad_out), channel_id=1, source_target_pairs={{0,24},{4,28},{8,16},{12,20},{16,8},{20,12},{24,0},{28,4},{1,25},{... | collective-permute-start | bytes 1572872 | tf_op jit(solution)/shard_map/ppermute | solution.py:34
  105.7 31.4 %collective-permute-start.7 = (bf16[8,64,128]{2,1,0:T(8,128)(2,1)S(1)}, bf16[8,64,128]{2,1,0:T(8,128)(2,1)S(1)}, u32[]{:S(2)}, u32[]{:S(2)}) collective-permute-start(bf16[8,64,128]{2,1,0:T(8,128)(2,1)S(1)} %get-tuple-element.129.refs_0_), channel_id=1, source_target_pairs={{0,3},{1,0},{2,1},{3,2},{4,7},{5,4},{6,5},{7,6},{8,11},{9,8},{10,9... | collective-permute-start | bytes 393224 | tf_op jit(solution)/shard_map/ppermute | solution.py:38
  132.1 18.4 %collective-permute-start.8 = (bf16[8,64,128]{2,1,0:T(8,128)(2,1)S(1)}, bf16[8,64,128]{2,1,0:T(8,128)(2,1)S(1)}, u32[]{:S(2)}, u32[]{:S(2)}) collective-permute-start(bf16[8,64,128]{2,1,0:T(8,128)(2,1)S(1)} %get-tuple-element.129.refs_0_), channel_id=1, source_target_pairs={{0,2},{1,3},{2,0},{3,1},{4,6},{5,7},{6,4},{7,5},{8,10},{9,11},{10,... | collective-permute-start | bytes 393224 | tf_op jit(solution)/shard_map/ppermute | solution.py:38
  137.1 13.4 %collective-permute-start.9 = (bf16[8,64,128]{2,1,0:T(8,128)(2,1)S(1)}, bf16[8,64,128]{2,1,0:T(8,128)(2,1)S(1)}, u32[]{:S(2)}, u32[]{:S(2)}) collective-permute-start(bf16[8,64,128]{2,1,0:T(8,128)(2,1)S(1)} %get-tuple-element.129.refs_0_), channel_id=1, source_target_pairs={{0,1},{1,2},{2,3},{3,0},{4,5},{5,6},{6,7},{7,4},{8,9},{9,10},{10,1... | collective-permute-start | bytes 393224 | tf_op jit(solution)/shard_map/ppermute | solution.py:38
  150.5 3.4 collective-permute-start.13
  151.4 3.3 collective-permute-start.14
  151.9 3.5 collective-permute-start.15
  151.9 4.1 collective-permute-start.16
  174.2 4.2 collective-permute-start.17
  177.2 42.8 %collective-permute-start.24 = (bf16[512,2048]{1,0:T(8,128)(2,1)}, bf16[512,2048]{1,0:T(8,128)(2,1)}, u32[]{:S(2)}, u32[]{:S(2)}) collective-permute-start(bf16[512,2048]{1,0:T(8,128)(2,1)} %pad_maximum_fusion.1.refs_2_), channel_id=1, source_target_pairs={{0,4},{4,0},{8,12},{12,8},{16,20},{20,16},{24,28},{28,24},{1,5},{5... | collective-permute-start | bytes 6291464 | tf_op jit(solution)/shard_map/ppermute | solution.py:34
  183.9 15.0 %collective-permute-start.18 = (bf16[128,2048]{1,0:T(8,128)(2,1)}, bf16[128,2048]{1,0:T(8,128)(2,1)S(1)}, u32[]{:S(2)}, u32[]{:S(2)}) collective-permute-start(bf16[128,2048]{1,0:T(8,128)(2,1)} %get-tuple-element.136), channel_id=1, source_target_pairs={{0,8},{4,12},{8,0},{12,4},{16,24},{20,28},{24,16},{28,20},{1,9},{5... | collective-permute-start | bytes 1572872 | tf_op jit(solution)/shard_map/ppermute | solution.py:34
  185.6 25.1 %collective-permute-start.19 = (bf16[128,2048]{1,0:T(8,128)(2,1)}, bf16[128,2048]{1,0:T(8,128)(2,1)S(1)}, u32[]{:S(2)}, u32[]{:S(2)}) collective-permute-start(bf16[128,2048]{1,0:T(8,128)(2,1)} %get-tuple-element.137), channel_id=1, source_target_pairs={{0,16},{4,20},{8,24},{12,28},{16,0},{20,4},{24,8},{28,12},{1,17},{... | collective-permute-start | bytes 1572872 | tf_op jit(solution)/shard_map/ppermute | solution.py:34
  187.0 24.5 %collective-permute-start.20 = (bf16[128,2048]{1,0:T(8,128)(2,1)}, bf16[128,2048]{1,0:T(8,128)(2,1)}, u32[]{:S(2)}, u32[]{:S(2)}) collective-permute-start(bf16[128,2048]{1,0:T(8,128)(2,1)} %get-tuple-element.138), channel_id=1, source_target_pairs={{0,24},{4,28},{8,16},{12,20},{16,8},{20,12},{24,0},{28,4},{1,25},{... | collective-permute-start | bytes 1572872 | tf_op jit(solution)/shard_map/ppermute | solution.py:34
  216.5 104.3 %copy-start.15 = (f32[128,2048]{1,0:T(8,128)}, f32[128,2048]{1,0:T(8,128)S(1)}, u32[]{:S(2)}) copy-start(f32[128,2048]{1,0:T(8,128)S(1)} %get-tuple-element.142.resid) | copy-start | bytes 3145732
  216.5 14.9 %collective-permute-start.21 = (bf16[128,2048]{1,0:T(8,128)(2,1)S(1)}, bf16[128,2048]{1,0:T(8,128)(2,1)S(1)}, u32[]{:S(2)}, u32[]{:S(2)}) collective-permute-start(bf16[128,2048]{1,0:T(8,128)(2,1)S(1)} %get-tuple-element.143), channel_id=1, source_target_pairs={{0,8},{4,12},{8,0},{12,4},{16,24},{20,28},{24,16},{28,20},{1,9},{5... | collective-permute-start | bytes 1572872 | tf_op jit(solution)/shard_map/ppermute | solution.py:34
  217.0 22.7 %collective-permute-start.22 = (bf16[128,2048]{1,0:T(8,128)(2,1)S(1)}, bf16[128,2048]{1,0:T(8,128)(2,1)S(1)}, u32[]{:S(2)}, u32[]{:S(2)}) collective-permute-start(bf16[128,2048]{1,0:T(8,128)(2,1)S(1)} %get-tuple-element.143), channel_id=1, source_target_pairs={{0,16},{4,20},{8,24},{12,28},{16,0},{20,4},{24,8},{28,12},{1,17},{... | collective-permute-start | bytes 1572872 | tf_op jit(solution)/shard_map/ppermute | solution.py:34
  218.5 23.1 %collective-permute-start.23 = (bf16[128,2048]{1,0:T(8,128)(2,1)S(1)}, bf16[128,2048]{1,0:T(8,128)(2,1)S(1)}, u32[]{:S(2)}, u32[]{:S(2)}) collective-permute-start(bf16[128,2048]{1,0:T(8,128)(2,1)S(1)} %get-tuple-element.143), channel_id=1, source_target_pairs={{0,24},{4,28},{8,16},{12,20},{16,8},{20,12},{24,0},{28,4},{1,25},{... | collective-permute-start | bytes 1572872 | tf_op jit(solution)/shard_map/ppermute | solution.py:34
  244.2 17.0 %collective-permute-start.25 = (bf16[512,2048]{1,0:T(8,128)(2,1)}, bf16[512,2048]{1,0:T(8,128)(2,1)}, u32[]{:S(2)}, u32[]{:S(2)}) collective-permute-start(bf16[512,2048]{1,0:T(8,128)(2,1)} %constant_dynamic-update-slice_fusion.x.refs_0_), channel_id=1, source_target_pairs={{0,4},{4,0},{8,12},{12,8},{16,20},{20,16},{24,28},{28,24},{1,5},{5... | collective-permute-start | bytes 6291464 | tf_op jit(solution)/shard_map/ppermute | solution.py:34
  283.0 255.2 %reduce-scatter.5.cloned.1.call-start = ((), (), s32[]{:S(2)}) async-start(), calls=%async_computation.10 | async-start | bytes 7208960 | tf_op jit(solution)/shard_map/reduce_scatter | solution.py:715
  283.1 4.6 collective-permute-start.26
  294.6 4.5 collective-permute-start.27
  294.9 20.7 %collective-permute-start.28 = (bf16[128,2048]{1,0:T(8,128)(2,1)}, bf16[128,2048]{1,0:T(8,128)(2,1)}, u32[]{:S(2)}, u32[]{:S(2)}) collective-permute-start(bf16[128,2048]{1,0:T(8,128)(2,1)} %get-tuple-element.162), channel_id=1, source_target_pairs={{0,8},{4,12},{8,0},{12,4},{16,24},{20,28},{24,16},{28,20},{1,9},{5... | collective-permute-start | bytes 1572872 | tf_op jit(solution)/shard_map/ppermute | solution.py:34
  295.5 25.2 %collective-permute-start.29 = (bf16[128,2048]{1,0:T(8,128)(2,1)}, bf16[128,2048]{1,0:T(8,128)(2,1)}, u32[]{:S(2)}, u32[]{:S(2)}) collective-permute-start(bf16[128,2048]{1,0:T(8,128)(2,1)} %get-tuple-element.163), channel_id=1, source_target_pairs={{0,16},{4,20},{8,24},{12,28},{16,0},{20,4},{24,8},{28,12},{1,17},{... | collective-permute-start | bytes 1572872 | tf_op jit(solution)/shard_map/ppermute | solution.py:34
  297.2 23.5 %collective-permute-start.30 = (bf16[128,2048]{1,0:T(8,128)(2,1)}, bf16[128,2048]{1,0:T(8,128)(2,1)}, u32[]{:S(2)}, u32[]{:S(2)}) collective-permute-start(bf16[128,2048]{1,0:T(8,128)(2,1)} %get-tuple-element.164), channel_id=1, source_target_pairs={{0,24},{4,28},{8,16},{12,20},{16,8},{20,12},{24,0},{28,4},{1,25},{... | collective-permute-start | bytes 1572872 | tf_op jit(solution)/shard_map/ppermute | solution.py:34
  324.2 14.9 %collective-permute-start.31 = (bf16[128,2048]{1,0:T(8,128)(2,1)S(1)}, bf16[128,2048]{1,0:T(8,128)(2,1)S(1)}, u32[]{:S(2)}, u32[]{:S(2)}) collective-permute-start(bf16[128,2048]{1,0:T(8,128)(2,1)S(1)} %get-tuple-element.178), channel_id=1, source_target_pairs={{0,8},{4,12},{8,0},{12,4},{16,24},{20,28},{24,16},{28,20},{1,9},{5... | collective-permute-start | bytes 1572872 | tf_op jit(solution)/shard_map/ppermute | solution.py:34
  325.6 24.1 %collective-permute-start.32 = (bf16[128,2048]{1,0:T(8,128)(2,1)S(1)}, bf16[128,2048]{1,0:T(8,128)(2,1)S(1)}, u32[]{:S(2)}, u32[]{:S(2)}) collective-permute-start(bf16[128,2048]{1,0:T(8,128)(2,1)S(1)} %get-tuple-element.178), channel_id=1, source_target_pairs={{0,16},{4,20},{8,24},{12,28},{16,0},{20,4},{24,8},{28,12},{1,17},{... | collective-permute-start | bytes 1572872 | tf_op jit(solution)/shard_map/ppermute | solution.py:34
  326.3 24.3 %collective-permute-start.33 = (bf16[128,2048]{1,0:T(8,128)(2,1)S(1)}, bf16[128,2048]{1,0:T(8,128)(2,1)}, u32[]{:S(2)}, u32[]{:S(2)}) collective-permute-start(bf16[128,2048]{1,0:T(8,128)(2,1)S(1)} %get-tuple-element.178), channel_id=1, source_target_pairs={{0,24},{4,28},{8,16},{12,20},{16,8},{20,12},{24,0},{28,4},{1,25},{... | collective-permute-start | bytes 1572872 | tf_op jit(solution)/shard_map/ppermute | solution.py:34
  354.2 4.2 collective-permute-start.34
  354.3 23.3 %collective-permute-start.35 = (bf16[128,2048]{1,0:T(8,128)(2,1)}, bf16[128,2048]{1,0:T(8,128)(2,1)S(1)}, u32[]{:S(2)}, u32[]{:S(2)}) collective-permute-start(bf16[128,2048]{1,0:T(8,128)(2,1)} %copy-done.77), channel_id=1, source_target_pairs={{0,8},{4,12},{8,0},{12,4},{16,24},{20,28},{24,16},{28,20},{1,9},{5... | collective-permute-start | bytes 1572872 | tf_op jit(solution)/shard_map/ppermute | solution.py:34
  354.8 25.2 %collective-permute-start.36 = (bf16[128,2048]{1,0:T(8,128)(2,1)S(1)}, bf16[128,2048]{1,0:T(8,128)(2,1)S(1)}, u32[]{:S(2)}, u32[]{:S(2)}) collective-permute-start(bf16[128,2048]{1,0:T(8,128)(2,1)S(1)} %copy-done.76), channel_id=1, source_target_pairs={{0,16},{4,20},{8,24},{12,28},{16,0},{20,4},{24,8},{28,12},{1,17},{... | collective-permute-start | bytes 1572872 | tf_op jit(solution)/shard_map/ppermute | solution.py:34
  355.4 24.6 %collective-permute-start.37 = (bf16[128,2048]{1,0:T(8,128)(2,1)S(1)}, bf16[128,2048]{1,0:T(8,128)(2,1)S(1)}, u32[]{:S(2)}, u32[]{:S(2)}) collective-permute-start(bf16[128,2048]{1,0:T(8,128)(2,1)S(1)} %copy-done.74), channel_id=1, source_target_pairs={{0,24},{4,28},{8,16},{12,20},{16,8},{20,12},{24,0},{28,4},{1,25},{... | collective-permute-start | bytes 1572872 | tf_op jit(solution)/shard_map/ppermute | solution.py:34
  380.0 44.0 %copy-start.97 = (bf16[128,2048]{1,0:T(8,128)(2,1)}, bf16[128,2048]{1,0:T(8,128)(2,1)S(1)}, u32[]{:S(2)}) copy-start(bf16[128,2048]{1,0:T(8,128)(2,1)S(1)} %collective-permute-done.36) | copy-start | bytes 1572868
  380.0 44.1 %copy-start.99 = (bf16[128,2048]{1,0:T(8,128)(2,1)}, bf16[128,2048]{1,0:T(8,128)(2,1)S(1)}, u32[]{:S(2)}) copy-start(bf16[128,2048]{1,0:T(8,128)(2,1)S(1)} %collective-permute-done.37) | copy-start | bytes 1572868
  380.0 2.0 collective-permute-start.38
  382.1 20.9 %collective-permute-start.39 = (bf16[8,64,128]{2,1,0:T(8,128)(2,1)S(1)}, bf16[8,64,128]{2,1,0:T(8,128)(2,1)S(1)}, u32[]{:S(2)}, u32[]{:S(2)}) collective-permute-start(bf16[8,64,128]{2,1,0:T(8,128)(2,1)S(1)} %get-tuple-element.196), channel_id=1, source_target_pairs={{0,1},{1,2},{2,3},{3,0},{4,5},{5,6},{6,7},{7,4},{8,9},{9,10},{10,1... | collective-permute-start | bytes 393224 | tf_op jit(solution)/shard_map/ppermute | solution.py:38
  389.0 33.7 %collective-permute-start.40 = (bf16[8,64,128]{2,1,0:T(8,128)(2,1)S(1)}, bf16[8,64,128]{2,1,0:T(8,128)(2,1)S(1)}, u32[]{:S(2)}, u32[]{:S(2)}) collective-permute-start(bf16[8,64,128]{2,1,0:T(8,128)(2,1)S(1)} %get-tuple-element.197), channel_id=1, source_target_pairs={{0,2},{1,3},{2,0},{3,1},{4,6},{5,7},{6,4},{7,5},{8,10},{9,11},{10,... | collective-permute-start | bytes 393224 | tf_op jit(solution)/shard_map/ppermute | solution.py:38
  394.7 28.1 %collective-permute-start.41 = (bf16[8,64,128]{2,1,0:T(8,128)(2,1)S(1)}, bf16[8,64,128]{2,1,0:T(8,128)(2,1)S(1)}, u32[]{:S(2)}, u32[]{:S(2)}) collective-permute-start(bf16[8,64,128]{2,1,0:T(8,128)(2,1)S(1)} %get-tuple-element.198), channel_id=1, source_target_pairs={{0,3},{1,0},{2,1},{3,2},{4,7},{5,4},{6,5},{7,6},{8,11},{9,8},{10,9... | collective-permute-start | bytes 393224 | tf_op jit(solution)/shard_map/ppermute | solution.py:38
  426.8 12.2 %collective-permute-start.42 = (bf16[512,2048]{1,0:T(8,128)(2,1)}, bf16[512,2048]{1,0:T(8,128)(2,1)}, u32[]{:S(2)}, u32[]{:S(2)}) collective-permute-start(bf16[512,2048]{1,0:T(8,128)(2,1)} %convolution_convert_fusion.1), channel_id=1, source_target_pairs={{0,4},{4,0},{8,12},{12,8},{16,20},{20,16},{24,28},{28,24},{1,5},{5... | collective-permute-start | bytes 6291464 | tf_op jit(solution)/shard_map/ppermute | solution.py:34
  435.1 38.9 %collective-permute-start.46 = (bf16[512,640]{1,0:T(8,128)(2,1)}, bf16[512,640]{1,0:T(8,128)(2,1)}, u32[]{:S(2)}, u32[]{:S(2)}) collective-permute-start(bf16[512,640]{1,0:T(8,128)(2,1)} %get-tuple-element.206), channel_id=1, source_target_pairs={{0,1},{1,2},{2,3},{3,0},{4,5},{5,6},{6,7},{7,4},{8,9},{9,10},{10,1... | collective-permute-start | bytes 1966088 | tf_op jit(solution)/shard_map/ppermute | solution.py:38
  435.3 91.3 %collective-permute-start.47 = (bf16[512,640]{1,0:T(8,128)(2,1)}, bf16[512,640]{1,0:T(8,128)(2,1)}, u32[]{:S(2)}, u32[]{:S(2)}) collective-permute-start(bf16[512,640]{1,0:T(8,128)(2,1)} %get-tuple-element.207), channel_id=1, source_target_pairs={{0,2},{1,3},{2,0},{3,1},{4,6},{5,7},{6,4},{7,5},{8,10},{9,11},{10,... | collective-permute-start | bytes 1966088 | tf_op jit(solution)/shard_map/ppermute | solution.py:38
  435.4 91.3 %collective-permute-start.48 = (bf16[512,640]{1,0:T(8,128)(2,1)}, bf16[512,640]{1,0:T(8,128)(2,1)}, u32[]{:S(2)}, u32[]{:S(2)}) collective-permute-start(bf16[512,640]{1,0:T(8,128)(2,1)} %get-tuple-element.208), channel_id=1, source_target_pairs={{0,3},{1,0},{2,1},{3,2},{4,7},{5,4},{6,5},{7,6},{8,11},{9,8},{10,9... | collective-permute-start | bytes 1966088 | tf_op jit(solution)/shard_map/ppermute | solution.py:38
  438.9 37.4 %copy-start.16 = (f32[128,2048]{1,0:T(8,128)S(1)}, f32[128,2048]{1,0:T(8,128)}, u32[]{:S(2)}) copy-start(f32[128,2048]{1,0:T(8,128)} %copy-done.15) | copy-start | bytes 3145732
  442.8 83.8 %collective-permute-start.43 = (bf16[128,2048]{1,0:T(8,128)(2,1)S(1)}, bf16[128,2048]{1,0:T(8,128)(2,1)S(1)}, u32[]{:S(2)}, u32[]{:S(2)}) collective-permute-start(bf16[128,2048]{1,0:T(8,128)(2,1)S(1)} %get-tuple-element.203), channel_id=1, source_target_pairs={{0,8},{4,12},{8,0},{12,4},{16,24},{20,28},{24,16},{28,20},{1,9},{5... | collective-permute-start | bytes 1572872 | tf_op jit(solution)/shard_map/ppermute | solution.py:34
  444.6 82.0 %collective-permute-start.44 = (bf16[128,2048]{1,0:T(8,128)(2,1)S(1)}, bf16[128,2048]{1,0:T(8,128)(2,1)S(1)}, u32[]{:S(2)}, u32[]{:S(2)}) collective-permute-start(bf16[128,2048]{1,0:T(8,128)(2,1)S(1)} %get-tuple-element.204), channel_id=1, source_target_pairs={{0,16},{4,20},{8,24},{12,28},{16,0},{20,4},{24,8},{28,12},{1,17},{... | collective-permute-start | bytes 1572872 | tf_op jit(solution)/shard_map/ppermute | solution.py:34
  474.0 52.7 %collective-permute-start.45 = (bf16[128,2048]{1,0:T(8,128)(2,1)S(1)}, bf16[128,2048]{1,0:T(8,128)(2,1)S(1)}, u32[]{:S(2)}, u32[]{:S(2)}) collective-permute-start(bf16[128,2048]{1,0:T(8,128)(2,1)S(1)} %get-tuple-element.205), channel_id=1, source_target_pairs={{0,24},{4,28},{8,16},{12,20},{16,8},{20,12},{24,0},{28,4},{1,25},{... | collective-permute-start | bytes 1572872 | tf_op jit(solution)/shard_map/ppermute | solution.py:34
  530.9 12.1 %all-to-all-start.2 = ((bf16[8,64,320]{2,1,0:T(8,128)(2,1)}), bf16[8,64,320]{2,1,0:T(8,128)(2,1)S(1)}, u32[]{:S(2)}, u32[]{:S(2)}) async-start(bf16[8,64,320]{2,1,0:T(8,128)(2,1)} %slice.125), calls=%async_computation.3 | async-start | bytes 786432 | tf_op jit(solution)/shard_map/all_to_all | solution.py:741
  543.0 23.1 %all-to-all-start.3 = ((bf16[8,64,1408]{2,1,0:T(8,128)(2,1)}), bf16[8,64,1408]{2,1,0:T(8,128)(2,1)S(1)}, u32[]{:S(2)}, u32[]{:S(2)}) async-start(bf16[8,64,1408]{2,1,0:T(8,128)(2,1)} %bitcast.70), calls=%async_computation.5 | async-start | bytes 2883584 | tf_op jit(solution)/shard_map/all_to_all | solution.py:738
  (104 other events, 713.3 us)
Sparse Core Ops, SparseCore 0:
  9.6 27.4 all-gather.3
  38.7 83.2 all-gather.5
  124.1 112.4 all-gather.7
  283.2 64.2 reduce-scatter.2
  350.7 148.3 reduce-scatter.4

commit v3 on v2

--- a/solution.py
+++ b/solution.py
@@ -54,7 +54,7 @@
     return [swap(rows, rel) for rel in range(2, size, 2)]
 
 
-def kernel_params(mib=48):
+def kernel_params(mib=32):
     return pltpu.CompilerParams(vmem_limit_bytes=mib * 2**20)
 
 LIGHT = pl.CostEstimate(flops=1024, bytes_accessed=1024, transcendentals=0)
@@ -343,27 +343,30 @@
     tokens, width = first_in.shape
     columns, half = mixed.shape[1], mixed.shape[0] // 2
     block, strip = width // (members * parts), width // members
-    lanes = used + strip + -(used + strip) % 128
+    upper = members // 2
 
     def body(at, x, g, m, ba, bb, *refs):
         outs, (left, right) = refs[:parts], refs[parts:]
         left[...] = dot_tn(x[...], g[:, : left.shape[1]])
         right[...] = dot_tn(m[:half, :], ba[...]) + dot_tn(m[half:, :], bb[...])
-        unused = jnp.zeros((block, lanes - used - strip), F32)
         for j, out in enumerate(outs):
             place = lax.rem(at[0] + j, parts)
             own = right[pl.ds(pl.multiple_of(place * block, block), block), :]
-            for d in range(members):
+
+            def both(d):
                 rows = pl.ds(pl.multiple_of((d * parts + place) * block, block), block)
+                return [left[rows, :][:, :used], own[:, d * strip : (d + 1) * strip]]
+
+            for d in range(upper):
                 out[d * block : (d + 1) * block, :] = jnp.concatenate(
-                    [left[rows, :][:, :used], own[:, d * strip : (d + 1) * strip], unused], axis=1
+                    both(d) + both(d + upper), axis=1
                 ).astype(BF16)
 
     whole = pl.BlockSpec(memory_space=pltpu.VMEM)
     return pl.pallas_call(
         body,
         in_specs=[pl.BlockSpec(memory_space=pltpu.SMEM)] + [whole] * 5,
-        out_shape=[jax.ShapeDtypeStruct((members * block, lanes), BF16)] * parts,
+        out_shape=[jax.ShapeDtypeStruct((upper * block, 2 * (used + strip)), BF16)] * parts,
         scratch_shapes=[
             pltpu.VMEM((width, grad_attn.shape[1]), F32),
             pltpu.VMEM((columns, width), F32),
@@ -373,20 +376,44 @@
     )(where, first_in, grad_attn, mixed, *grad_branch)
 
 
-def feed_forward(second_in, grad_hidden, w_pair, w_down):
+def hidden_units(second_in, w_pair):
     tokens, width = second_in.shape
-    ff = w_down.shape[0]
-    tile = 512
-
-    def body(x, dh, w, wd, hidden, grads, back, forth):
-        both = dot(x[...], w[...])
+    ff = w_pair.shape[1] // 2
+    tile = 256
+
+    def body(x, w, both, hidden):
+        product = dot(x[...], w[...])
+        gate, up = product[:, :ff], product[:, ff:]
+        both[...] = product
+        hidden[...] = (gate * jax.nn.sigmoid(gate) * up).astype(BF16)
+
+    def rows(columns):
+        return pl.BlockSpec((tile, columns), lambda i: (i, 0))
+
+    return pl.pallas_call(
+        body,
+        grid=(tokens // tile,),
+        in_specs=[rows(width), pl.BlockSpec(w_pair.shape, lambda i: (0, 0), pipeline_mode=pl.Buffered(1))],
+        out_specs=(rows(2 * ff), rows(ff)),
+        out_shape=(
+            jax.ShapeDtypeStruct((tokens, 2 * ff), F32),
+            jax.ShapeDtypeStruct((tokens, ff), BF16),
+        ),
+        compiler_params=kernel_params(),
+        cost_estimate=LIGHT,
+    )(second_in, w_pair)
+
+
+def feed_forward_back(both, hidden, grad_out, w_pair, w_down):
+    tokens, width = grad_out.shape
+    ff = hidden.shape[1]
+    tile = 256
+
+    def body(both, h, dy, w, wd, grads, back, forth):
         gate, up = both[:, :ff], both[:, ff:]
         sig = jax.nn.sigmoid(gate)
-        swish = gate * sig
-        inner = (swish * up).astype(BF16)
-        hidden[...] = inner
-        forth[...] = dot(inner, wd[...]).astype(BF16)
-        dh_sig = dh[...] * sig
+        forth[...] = dot(h[...], wd[...]).astype(BF16)
+        dh_sig = dot_nt(dy[...], wd[...]) * sig
         grad = jnp.concatenate(
             [dh_sig * up * (1.0 + gate * (1.0 - sig)), dh_sig * gate], axis=1
         ).astype(BF16)
@@ -397,22 +424,21 @@
         return pl.BlockSpec((tile, columns), lambda i: (i, 0))
 
     def whole(array):
-        return pl.BlockSpec(array.shape, lambda i: (0, 0))
+        return pl.BlockSpec(array.shape, lambda i: (0, 0), pipeline_mode=pl.Buffered(1))
 
     return pl.pallas_call(
         body,
         grid=(tokens // tile,),
-        in_specs=[rows(width), rows(ff), whole(w_pair), whole(w_down)],
-        out_specs=(rows(ff), rows(2 * ff), rows(width), rows(width)),
+        in_specs=[rows(2 * ff), rows(ff), rows(width), whole(w_pair), whole(w_down)],
+        out_specs=(rows(2 * ff), rows(width), rows(width)),
         out_shape=(
-            jax.ShapeDtypeStruct((tokens, ff), BF16),
             jax.ShapeDtypeStruct((tokens, 2 * ff), BF16),
             jax.ShapeDtypeStruct((tokens, width), BF16),
             jax.ShapeDtypeStruct((tokens, width), BF16),
         ),
         compiler_params=kernel_params(),
         cost_estimate=LIGHT,
-    )(second_in, grad_hidden, w_pair, w_down)
+    )(both, hidden, grad_out, w_pair, w_down)
 
 
 def add_blocks(own, came, blocks):
@@ -534,39 +560,91 @@
     )(gate, up)
 
 
-def columns_back(blocks, gate, up, gain, planes):
-    members, rows, both = blocks.shape
-    part = both // (2 * planes)
-    ff = planes * members * part
-
-    def body(x, g, u, gn, og, ou, ogn):
-        total = 0.0
-        for m, (w, o) in enumerate(((g, og), (u, ou))):
-            grad = jnp.concatenate(
-                [
-                    x[s, :, (m * planes + p) * part : (m * planes + p + 1) * part]
-                    for p in range(planes)
-                    for s in range(members)
-                ],
-                axis=1,
-            ).astype(F32)
-            o[...] = grad
-            total += jnp.sum(w[...].astype(F32) * grad, axis=1, keepdims=True)
-        ogn[...] = total / gn[...].astype(F32)
-
-    shape = jax.ShapeDtypeStruct((rows, ff), F32)
-    out = pl.pallas_call(
-        body,
-        out_shape=(shape, shape, jax.ShapeDtypeStruct((rows, 1), F32)),
-        compiler_params=kernel_params(),
-        cost_estimate=LIGHT,
-    )(blocks, gate, up, gain[:, None])
-    return out[0], out[1], out[2][:, 0]
+def gather_terms(own, sums, members, used, width):
+    block, count, strip = 2 * own.shape[0] // members, len(sums), width // members
+
+    def body(a, *refs):
+        total = a[...].astype(F32)
+        for ref in refs[:count]:
+            total += ref[...].astype(F32)
+        out, payload = refs[count:]
+        strips = []
+        for d in range(members):
+            side, row = divmod(d, members // 2)
+            start = side * (used + strip)
+            rows = total[row * block : (row + 1) * block]
+            payload[d] = rows[:, start : start + used].astype(BF16)
+            strips.append(rows[:, start + used : start + used + strip])
+        out[...] = jnp.concatenate(strips, axis=1)
+
+    return pl.pallas_call(
+        body,
+        out_shape=(
+            jax.ShapeDtypeStruct((block, width), F32),
+            jax.ShapeDtypeStruct((members, block, used), BF16),
+        ),
+        compiler_params=kernel_params(),
+        cost_estimate=LIGHT,
+    )(own, *sums)
+
+
+def weight_gradients(pairs, blocks, weights, gains, q_cols):
+    members, rows, _ = blocks.shape
+    part, shared = pairs.shape[2] // 2, members // (2 * KEY_VALUE_HEADS)
+
+    def body(pair, x, g, u, q, k, v, gains, og, ou, oq, ok, ov, ogain):
+        def side(start, size, chosen, x=x):
+            return [x[d, :, start : start + size].astype(F32) for d in chosen]
+
+        def heads(core):
+            found = side(q_cols, HEAD_SIZE, range(core, members, 2))
+            return jnp.concatenate(
+                [sum(found[h * shared : (h + 1) * shared]) for h in range(KEY_VALUE_HEADS)], axis=1
+            )
+
+        og[...] = jnp.concatenate(side(0, part, range(members), pair), axis=1)
+        ou[...] = jnp.concatenate(side(part, part, range(members), pair), axis=1)
+        oq[...] = jnp.concatenate(side(0, q_cols, range(members)), axis=1)
+        ok[...] = heads(0)
+        ov[...] = heads(1)
+
+        def gain(both):
+            return sum(jnp.sum(w[...].astype(F32) * o[...], axis=1, keepdims=True) for w, o in both)
+
+        total = jnp.concatenate([gain(((q, oq), (k, ok), (v, ov))), gain(((g, og), (u, ou)))], axis=1)
+        ogain[...] = total / gains[...].astype(F32)
+
+    return pl.pallas_call(
+        body,
+        out_shape=[jax.ShapeDtypeStruct(w.shape, F32) for w in weights]
+        + [jax.ShapeDtypeStruct((rows, 2), F32)],
+        compiler_params=kernel_params(),
+        cost_estimate=LIGHT,
+    )(pairs, blocks, *weights, gains)
 
 
 def scatter_dp(left, right, size, product):
     came = swap(product(left[left.shape[0] // 2 :], right).astype(BF16), 1)
     return dot_blocks(left, right, came, size // 2, product)
+
+
+def in_order(parts, place):
+    size = len(parts)
+    rows, columns = parts[0].shape
+
+    def body(at, *refs):
+        for j in range(size):
+            refs[-1][pl.ds(lax.rem(at[0] + j, size), 1)] = refs[j][...][None]
+
+    out = pl.pallas_call(
+        body,
+        in_specs=[pl.BlockSpec(memory_space=pltpu.SMEM)]
+        + [pl.BlockSpec(memory_space=pltpu.VMEM)] * size,
+        out_shape=jax.ShapeDtypeStruct((size, rows, columns), parts[0].dtype),
+        compiler_params=kernel_params(),
+        cost_estimate=LIGHT,
+    )(jnp.full((1,), place, jnp.int32), *parts)
+    return out.reshape(size * rows, columns)
 
 
 def attention_weights(parts, place, at_gains):
@@ -645,8 +723,7 @@
     w_attn = jnp.concatenate(pieces, axis=1).reshape(block, n, -1).transpose(1, 0, 2)
     w_attn = lax.all_to_all(w_attn, every_dp, 0, 0)
     x16, dy_local = tokens[0], out_grad[0]
-    wd = lax.all_gather(w_down, "ctx", axis=0, tiled=True)
-    wo = lax.all_gather(w_out, "ctx", axis=0, tiled=True)
+    w_attn, wo_parts = together(w_attn, shifts(w_out, c))
     seg_rows = w_attn[:, :, used + 2 : used + 2 + length // block].reshape(n, length)
 
     order = me ^ jnp.array([*range(0, n, 2), *range(1, n, 2)], jnp.int32)
@@ -663,16 +740,17 @@
     sine = jnp.concatenate([-sine, sine] * 2, axis=1)
     w_pair = columns_out(*after((w_gate, w_up), w_attn), 1, n)
     w_pair = lax.all_to_all(w_pair, every_dp, 0, 0).reshape(n * block, 2 * f_cols)
+    w_parts, same, cosine, sine, w_pair = together(
+        shifts(w_attn, c), dp_same(after(x16, w_attn), n), cosine, sine, w_pair
+    )
     w_pair = lax.all_gather(w_pair, "ctx", axis=0, tiled=True)
-    w_parts, same, cosine, sine = together(
-        shifts(w_attn, c), dp_same(after(x16, w_attn), n), cosine, sine
-    )
     even = jnp.concatenate([x16, *same])
     odd = swap(even, 1)
 
     w_attn, gains = attention_weights([w_attn, *w_parts], place_z, used)
     w_attn = w_attn.reshape(width, -1)
     gain1, gain2 = gains[:1], gains[1:]
+    wo = in_order([w_out, *wo_parts], place_z)
     where = jnp.stack([place_z, core]).astype(jnp.int32)
     key_seg = lax.dynamic_slice_in_dim(
         jnp.concatenate([segs, segs], axis=1), place_z * t, length, axis=1
@@ -688,31 +766,31 @@
     kv_other = [swap(v, 1) for v in kv_all]
     mixed = attend(where, queries, kv_all, kv_other, *sides)
     attn_own, *sends = scatter_dp(mixed, wo, n, dot)
-    sent = together(*[swap(v, 2 * j) for j, v in enumerate(sends, 1)])
+    sent, w_pair = together([swap(v, 2 * j) for j, v in enumerate(sends, 1)], w_pair)
+    wd = lax.all_gather(after(w_down, w_pair), "ctx", axis=0, tiled=True)
     resid, second_in = second_norm(x16, attn_own, sent, gain2, n, c)
 
-    in_parts, grad_hidden = together(
-        dp_same(second_in, n), [dot_nt(half, wd).astype(BF16) for half in dy]
-    )
-    second_in = jnp.concatenate([second_in, *in_parts])
+    second_in = jnp.concatenate([second_in, *together(*dp_same(second_in, n))])
     second_in = second_in, swap(second_in, 1)
-    same = feed_forward(second_in[0], grad_hidden[0], w_pair, wd)
-    other = feed_forward(second_in[1], after(grad_hidden[1], same[2]), w_pair, wd)
-    hidden, grad_pair = (same[0], other[0]), (same[1], other[1])
-    back_came = swap(other[2], 1)
+    units = hidden_units(second_in[0], w_pair)
+    units = units, hidden_units(after(second_in[1], units), w_pair)
+    hidden = [half[1] for half in units]
     down_term = transposed_dot(hidden, dy)
-    grad_down = lax.psum_scatter(down_term, "ctx", scatter_dimension=0, tiled=True)
-    back, *sends = add_blocks(same[2], after(back_came, down_term), n // 2)
-    forth = swap(after(other[3], sends), 1)
-    pair_term = transposed_dot(after(second_in, forth, down_term), grad_pair)
-    forth, *forth_sends = add_blocks(same[3], forth, n // 2)
-    sent, pair_term, forth_sends = together(
-        [swap(v, 2 * j) for j, v in enumerate(sends, 1)], pair_term, forth_sends
-    )
+    grad_down = lax.psum_scatter(after(down_term, wd), "ctx", scatter_dimension=0, tiled=True)
+    other = feed_forward_back(*units[1], dy[1], w_pair, after(wd, down_term))
+    same = feed_forward_back(*units[0], after(dy[0], other[0]), w_pair, wd)
+    grad_pair = same[0], other[0]
+    back, *sends = add_blocks(same[1], swap(other[1], 1), n // 2)
+    forth = swap(after(other[2], sends), 1)
+    pair_term = transposed_dot(after(second_in, forth), grad_pair)
+    forth, *forth_sends = add_blocks(same[2], forth, n // 2)
+    sent, pair_term, forth_sends, grad_down = together(
+        [swap(v, 2 * j) for j, v in enumerate(sends, 1)], pair_term, forth_sends, grad_down
+    )
+    pair_sum = lax.psum_scatter(pair_term, "ctx", scatter_dimension=0, tiled=True)
     grad_resid, branch = second_norm_back(resid, back, sent, gain2, dy_local, n, c)
 
-    same, grad_down, pair_term = together(dp_same(branch, n), grad_down, pair_term)
-    pair_sum = lax.psum_scatter(pair_term, "ctx", scatter_dimension=0, tiled=True)
+    same = together(*dp_same(branch, n))
     same = jnp.concatenate([branch, *same])
     grad_branch = same, swap(same, 1)
     grad_q, kept, sent = attend_back(
@@ -726,44 +804,39 @@
     grad_kv = sum_keys(where, own_kv, kv_parts, cosine, sine)
     unused = jnp.zeros((n * t, w_attn.shape[1] - used), BF16)
     grad_attn = jnp.concatenate([grad_q, grad_kv, unused], axis=1)
-    first_own, *sends = scatter_dp(grad_attn, w_attn, n, dot_nt)
     own_terms, *terms = attention_weight_terms(
         where, first_in, grad_attn, mixed, grad_branch, used, n, c
     )
-    sent, terms = together(
+    first_own, *sends = scatter_dp(after(grad_attn, terms), w_attn, n, dot_nt)
+    pair_sum = after(pair_sum, sends).reshape(n, block, 2 * f_cols)
+    sent, terms, pair_sum = together(
         [swap(v, 2 * j) for j, v in enumerate(sends, 1)],
         [shift(v, -j, c) for j, v in enumerate(terms, 1)],
-    )
-    pair_sum = after(pair_sum, terms).reshape(n, block, 2 * f_cols)
-    pair_sum = lax.all_to_all(pair_sum, every_dp, 0, 0)
-    terms = (own_terms.astype(F32) + sum(v.astype(F32) for v in terms)).reshape(n, block, -1)
-    grad_wout = terms[:, :, used : used + width // n].transpose(1, 0, 2).reshape(block, width)
-    attn_sum = lax.all_to_all(terms[:, :, :used].astype(BF16), every_dp, 0, 0).astype(F32)
+        lax.all_to_all(pair_sum, every_dp, 0, 0),
+    )
+    grad_wout, payload = gather_terms(own_terms, terms, n, used, width)
+    payload = lax.all_to_all(payload, every_dp, 0, 0)
+    grad_gate, grad_up, grad_query, grad_key, grad_value, grad_gains = weight_gradients(
+        pair_sum,
+        payload,
+        (w_gate, w_up, w_query, key_weight, value_weight),
+        jnp.stack([gain_attn, gain_mlp], axis=1),
+        q_cols,
+    )
     grad_first = first_own + sum(v.astype(F32) for v in sent)
-    grad_down = after(grad_down, attn_sum).astype(F32)
-
-    grad_gate, grad_up, grad_gain_mlp = columns_back(pair_sum, w_gate, w_up, gain_mlp, 1)
-    grad_query = attn_sum[:, :, :q_cols].transpose(1, 0, 2).reshape(block, -1)
-    kv_sum = attn_sum[:, :, q_cols:].reshape(KEY_VALUE_HEADS, -1, 2, block, HEAD_SIZE).sum(axis=1)
-    grad_key = kv_sum[:, 0].transpose(1, 0, 2).reshape(block, -1)
-    grad_value = kv_sum[:, 1].transpose(1, 0, 2).reshape(block, -1)
-    grad_gain_attn = (
-        jnp.sum(w_query.astype(F32) * grad_query, axis=1)
-        + jnp.sum(key_weight.astype(F32) * grad_key, axis=1)
-        + jnp.sum(value_weight.astype(F32) * grad_value, axis=1)
-    ) / gain_attn.astype(F32)
+    grad_down = after(grad_down, terms).astype(F32)
     x = x16.astype(F32)
     inverse1 = lax.rsqrt(jnp.mean(x * x, axis=-1, keepdims=True) + EPS)
     grad_input = grad_resid + norm_back(grad_first, x * inverse1, inverse1, gain1)
     return (
         result.astype(BF16)[None],
         grad_input[None],
-        grad_gain_attn,
+        grad_gains[:, 0],
         grad_query,
         grad_key,
         grad_value,
         grad_wout,
-        grad_gain_mlp,
+        grad_gains[:, 1],
         grad_gate,
         grad_up,
         grad_down,

time: 585 us -> 534 us (0.913)
  matrix products: 14.5 us -> 2.19 us
  starting transfers between devices: 89.8 us -> 78 us
  Pallas kernels: 109 us -> 99.8 us
  waiting for transfers between devices: 265 us -> 256 us
  other arithmetic: 22.5 us -> 15.8 us
    ppermute x12 -> x15, waiting for transfers between devices: 169 us -> 127 us  [shift(): lax.ppermute(value, 'ctx', [(i, (i - step) % size) for i in range(size)])]
    all_gather x1, waiting for transfers between devices: 0.01 us -> 24.8 us  [per_device(): w_pair = lax.all_gather(w_pair, 'ctx', axis=0, tiled=True)]
    ppermute x37, waiting for transfers between devices: 70.9 us -> 93.7 us  [swap(): lax.ppermute(value, ('plane', 'core'), [(i, i ^ rel) for i in range(size)])]
    ppermute x12 -> x15, starting transfers between devices: 42.2 us -> 28.1 us  [shift(): lax.ppermute(value, 'ctx', [(i, (i - step) % size) for i in range(size)])]
    all_to_all x2, waiting for transfers between devices: 15.4 us -> 2.39 us  [the longest x1 2.39 us: per_device(): payload = lax.all_to_all(payload, every_dp, 0, 0)]
    dot_general x3 -> x1, matrix products: 12.3 us -> 1.28 us  [dot_nt(): lax.dot_general(left, right, (((1,), (1,)), ((), ())), preferred_element_...]
    pallas_call x1, Pallas kernels: 17.8 us -> 26.1 us  [attend_back(): pl.pallas_call(body, grid=(sequences,), in_specs=[pl.BlockSpec(memory_spa...]
    all_to_all x1, waiting for transfers between devices: 8.29 us -> 0.01 us  [per_device(): w_attn = lax.all_to_all(w_attn, every_dp, 0, 0)]
  transfers between devices with their start and end apart: 58 -> 60, of which waited for: 26 -> 30; matrix products, arithmetic and copies ran while one was open for 10% -> 4% of each run, Pallas kernels for 15% -> 18%
where the time goes in v3:
time: 534 us; the launch traced here: 524 us
  waiting for transfers between devices  256 us (48%)
  Pallas kernels  99.8 us (19%)
  starting transfers between devices  78 us (15%)
  local copies, waits for them, and re-layouts  57 us (11%)
  other arithmetic  15.8 us (3%)
  between operations  15.3 us (3%)
    ppermute x15, waiting for transfers between devices, shift(): lax.ppermute(value, 'ctx', [(i, (i - step) % size) for i in range(size)])  127 us
    ppermute x37, waiting for transfers between devices, swap(): lax.ppermute(value, ('plane', 'core'), [(i, i ^ rel) for i in range(size)])  93.7 us
    unnamed x235, local copies, waits for them, and re-layouts  51.7 us
    ppermute x37, starting transfers between devices, swap(): lax.ppermute(value, ('plane', 'core'), [(i, i ^ rel) for i in range(size)])  33.8 us
    ppermute x15, starting transfers between devices, shift(): lax.ppermute(value, 'ctx', [(i, (i - step) % size) for i in range(size)])  28.1 us
    pallas_call x1, Pallas kernels, attend_back(): pl.pallas_call(body, grid=(sequences,), in_specs=[pl.BlockSpec(memory_spa...  26.1 us
    all_gather x1, waiting for transfers between devices, per_device(): w_pair = lax.all_gather(w_pair, 'ctx', axis=0, tiled=True)  24.8 us
    pallas_call x2, Pallas kernels, feed_forward_back(): pl.pallas_call(body, grid=(tokens // tile,), in_specs=[rows(2 * ff), rows...  16.9 us
  transfers between devices with their start and end apart: 60, of which 30 were waited for; matrix products, arithmetic and copies ran while one was open for 4% of the time, Pallas kernels for 18%

profile of v3, /device:TPU:24, one launch (start us, length us, event | category | flops | bytes accessed | tf_op | source)
XLA Modules:
  0.0 523.8 jit_solution(15743763227235907324)
XLA Ops:
  11.8 3.7 all-to-all-start
  16.4 3.0 collective-permute-start.2
  19.5 7.2 %collective-permute-done.refs_1_ = bf16[64,2048]{1,0:T(8,128)(2,1)S(1)} collective-permute-done((bf16[64,2048]{1,0:T(8,128)(2,1)S(1)}, bf16[64,2048]{1,0:T(8,128)(2,1)S(1)}, u32[]{:S(2)}, u32[]{:S(2)}) %collective-permute-start) | collective-permute-done | bytes 262176 | tf_op jit(solution)/shard_map/ppermute | solution.py:38
  26.7 10.7 %collective-permute-done.1.refs_2_ = bf16[64,2048]{1,0:T(8,128)(2,1)S(1)} collective-permute-done((bf16[64,2048]{1,0:T(8,128)(2,1)S(1)}, bf16[64,2048]{1,0:T(8,128)(2,1)S(1)}, u32[]{:S(2)}, u32[]{:S(2)}) %collective-permute-start.1) | collective-permute-done | bytes 262176 | tf_op jit(solution)/shard_map/ppermute | solution.py:38
  38.8 4.4 all-to-all-start.1
  43.4 1.9 collective-permute-start.6
  47.0 5.4 %collective-permute-start.3 = (bf16[8,64,384]{2,1,0:T(8,128)(2,1)S(1)}, bf16[8,64,384]{2,1,0:T(8,128)(2,1)S(1)}, u32[]{:S(2)}, u32[]{:S(2)}) collective-permute-start(bf16[8,64,384]{2,1,0:T(8,128)(2,1)S(1)} %all-to-all-done.refs_0_), channel_id=1, source_target_pairs={{0,3},{1,0},{2,1},{3,2},{4,7},{5,4},{6,5},{7,6},{8,11},{9,8},{10,9... | collective-permute-start | bytes 1179656 | tf_op jit(solution)/shard_map/ppermute | solution.py:38
  53.3 8.7 %collective-permute-done.3.refs_1_ = bf16[8,64,384]{2,1,0:T(8,128)(2,1)S(1)} collective-permute-done((bf16[8,64,384]{2,1,0:T(8,128)(2,1)S(1)}, bf16[8,64,384]{2,1,0:T(8,128)(2,1)S(1)}, u32[]{:S(2)}, u32[]{:S(2)}) %collective-permute-start.3) | collective-permute-done | bytes 393248 | tf_op jit(solution)/shard_map/ppermute | solution.py:38
  62.6 1.9 fusion.11
  65.5 12.2 %collective-permute-done.4.refs_2_ = bf16[8,64,384]{2,1,0:T(8,128)(2,1)S(1)} collective-permute-done((bf16[8,64,384]{2,1,0:T(8,128)(2,1)S(1)}, bf16[8,64,384]{2,1,0:T(8,128)(2,1)S(1)}, u32[]{:S(2)}, u32[]{:S(2)}) %collective-permute-start.4) | collective-permute-done | bytes 393248 | tf_op jit(solution)/shard_map/ppermute | solution.py:38
  79.2 6.2 %collective-permute-done.8 = bf16[128,2048]{1,0:T(8,128)(2,1)} collective-permute-done((bf16[128,2048]{1,0:T(8,128)(2,1)S(1)}, bf16[128,2048]{1,0:T(8,128)(2,1)}, u32[]{:S(2)}, u32[]{:S(2)}) %collective-permute-start.8) | collective-permute-done | bytes 524320 | tf_op jit(solution)/shard_map/ppermute | solution.py:34
  88.3 3.0 collective-permute-done.9.o
  91.3 5.7 %shard_map.214 = (bf16[1024,2048]{1,0:T(8,128)(2,1)S(1)}, bf16[1024,256]{1,0:T(8,128)(2,1)S(1)}, bf16[8,64,128]{2,1,0:T(8,128)(2,1)S(1)}) custom-call(s32[2]{0:T(128)S(1)} %pad_add_fusion.at, bf16[512,2048]{1,0:T(8,128)(2,1)S(1)} %pad_maximum_fusion.e, bf16[512,2048]{1,0:T(8,128)(2,1)S(1)} %collective-permute-done.9.o, f32[1,2048]{1,0:T(1,128)S(1)} %get-tuple-element.272.gn, ...), custom_call_target="tpu_custom_call" | custom-call | flops 1024 | bytes 1024 | tf_op jit(solution)/shard_map/pallas_call | solution.py:140
  97.0 2.0 copy-done.24
  99.9 2.6 collective-permute-start.15
  102.4 5.4 %collective-permute-start.10 = (bf16[8,64,128]{2,1,0:T(8,128)(2,1)S(1)}, bf16[8,64,128]{2,1,0:T(8,128)(2,1)S(1)}, u32[]{:S(2)}, u32[]{:S(2)}) collective-permute-start(bf16[8,64,128]{2,1,0:T(8,128)(2,1)S(1)} %get-tuple-element.147.refs_0_), channel_id=1, source_target_pairs={{0,3},{1,0},{2,1},{3,2},{4,7},{5,4},{6,5},{7,6},{8,11},{9,8},{10,9... | collective-permute-start | bytes 393224 | tf_op jit(solution)/shard_map/ppermute | solution.py:38
  108.0 6.5 %collective-permute-done.10.refs_1_ = bf16[8,64,128]{2,1,0:T(8,128)(2,1)S(1)} collective-permute-done((bf16[8,64,128]{2,1,0:T(8,128)(2,1)S(1)}, bf16[8,64,128]{2,1,0:T(8,128)(2,1)S(1)}, u32[]{:S(2)}, u32[]{:S(2)}) %collective-permute-start.10) | collective-permute-done | bytes 131104 | tf_op jit(solution)/shard_map/ppermute | solution.py:38
  114.5 3.6 collective-permute-start.12
  118.2 7.5 %collective-permute-done.11.refs_2_ = bf16[8,64,128]{2,1,0:T(8,128)(2,1)S(1)} collective-permute-done((bf16[8,64,128]{2,1,0:T(8,128)(2,1)S(1)}, bf16[8,64,128]{2,1,0:T(8,128)(2,1)S(1)}, u32[]{:S(2)}, u32[]{:S(2)}) %collective-permute-start.11) | collective-permute-done | bytes 131104 | tf_op jit(solution)/shard_map/ppermute | solution.py:38
  125.8 3.0 collective-permute-done.12.refs_3_
  134.2 9.9 %shard_map.215.a.m = bf16[1024,256]{1,0:T(8,128)(2,1)S(1)} custom-call(s32[2]{0:T(128)S(1)} %copy-done.83, bf16[1024,256]{1,0:T(8,128)(2,1)S(1)} %get-tuple-element.146.q, f32[8,128,1]{2,1,0:T(8,128)S(1)} %copy.72.m, f32[8,1,512]{2,1,0:T(1,128)S(1)} %broadcast_in_dim.34.th, bf16[8,64,128]{2,1,0:T(8,128)(2,1)S(1)} %get-tuple-element.147.refs_0_, ...), custom_call_target="tpu_custom_call" | custom-call | flops 1024 | bytes 1024 | tf_op jit(solution)/shard_map/pallas_call | solution.py:219
  145.0 4.1 collective-permute-done.20.c
  151.7 2.2 collective-permute-start.22
  153.9 10.8 %collective-permute-done.21.refs_0_ = bf16[128,2048]{1,0:T(8,128)(2,1)S(1)} collective-permute-done((bf16[128,2048]{1,0:T(8,128)(2,1)S(1)}, bf16[128,2048]{1,0:T(8,128)(2,1)S(1)}, u32[]{:S(2)}, u32[]{:S(2)}) %collective-permute-start.21) | collective-permute-done | bytes 524320 | tf_op jit(solution)/shard_map/ppermute | solution.py:34
  164.7 12.4 %collective-permute-done.22.refs_1_ = bf16[128,2048]{1,0:T(8,128)(2,1)S(1)} collective-permute-done((bf16[128,2048]{1,0:T(8,128)(2,1)S(1)}, bf16[128,2048]{1,0:T(8,128)(2,1)S(1)}, u32[]{:S(2)}, u32[]{:S(2)}) %collective-permute-start.22) | collective-permute-done | bytes 524320 | tf_op jit(solution)/shard_map/ppermute | solution.py:34
  178.7 24.8 %all-gather.3.cloned.1.call-done.w = bf16[2048,1408]{1,0:T(8,128)(2,1)} async-done(((bf16[512,1408]{1,0:T(8,128)(2,1)}), bf16[2048,1408]{1,0:T(8,128)(2,1)}) %all-gather.3.cloned.1.call-update) | async-done | bytes 5767184 | tf_op jit(solution)/shard_map/all_gather | solution.py:746
  211.8 11.2 %collective-permute-done.24 = bf16[128,2048]{1,0:T(8,128)(2,1)S(1)} collective-permute-done((bf16[128,2048]{1,0:T(8,128)(2,1)S(1)}, bf16[128,2048]{1,0:T(8,128)(2,1)S(1)}, u32[]{:S(2)}, u32[]{:S(2)}) %collective-permute-start.24) | collective-permute-done | bytes 524320 | tf_op jit(solution)/shard_map/ppermute | solution.py:34
  223.0 11.8 %collective-permute-done.25 = bf16[128,2048]{1,0:T(8,128)(2,1)S(1)} collective-permute-done((bf16[128,2048]{1,0:T(8,128)(2,1)S(1)}, bf16[128,2048]{1,0:T(8,128)(2,1)S(1)}, u32[]{:S(2)}, u32[]{:S(2)}) %collective-permute-start.25) | collective-permute-done | bytes 524320 | tf_op jit(solution)/shard_map/ppermute | solution.py:34
  236.3 2.0 copy-done
  238.3 3.9 shard_map.219
  243.8 3.9 shard_map.220
  249.3 4.3 shard_map.221
  257.4 5.4 %all-gather.5.cloned.1.call-done.wd = bf16[704,2048]{1,0:T(8,128)(2,1)} async-done(((bf16[176,2048]{1,0:T(8,128)(2,1)}), bf16[704,2048]{1,0:T(8,128)(2,1)}) %all-gather.5.cloned.1.call-update) | async-done | bytes 2883600 | tf_op jit(solution)/shard_map/all_gather | solution.py:770
  262.9 2.6 copy-done.1
  265.5 1.8 copy-done.7
  270.1 1.8 copy-done.35
  271.9 8.4 %shard_map.222 = (bf16[512,1408]{1,0:T(8,128)(2,1)S(1)}, bf16[512,2048]{1,0:T(8,128)(2,1)S(1)}, bf16[512,2048]{1,0:T(8,128)(2,1)S(1)}) custom-call(f32[512,1408]{1,0:T(8,128)S(1)} %copy-done.35, bf16[512,704]{1,0:T(8,128)(2,1)S(1)} %copy-done.31, bf16[512,2048]{1,0:T(8,128)(2,1)S(1)} %copy-done.15, bf16[2048,1408]{1,0:T(8,128)(2,1)S(1)} %copy-done.1, ...), custom_call_target="tpu_custom_call" | custom-call | flops 1024 | bytes 1024 | tf_op jit(solution)/shard_map/pallas_call | solution.py:429
  280.5 8.5 %shard_map.223 = (bf16[512,1408]{1,0:T(8,128)(2,1)S(1)}, bf16[512,2048]{1,0:T(8,128)(2,1)S(1)}, bf16[512,2048]{1,0:T(8,128)(2,1)S(1)}) custom-call(f32[512,1408]{1,0:T(8,128)S(1)} %copy-done.33, bf16[512,704]{1,0:T(8,128)(2,1)S(1)} %copy-done.29, bf16[512,2048]{1,0:T(8,128)(2,1)S(1)} %pad_maximum_fusion.1.refs_2_.dy, bf16[2048,1408]{1,0:T(8,128)(2,1)S(1)} %copy-done.1, ...), custom_call_target="tpu_custom_call" | custom-call | flops 1024 | bytes 1024 | tf_op jit(solution)/shard_map/pallas_call | solution.py:429
  297.3 8.7 %shard_map.226 = bf16[2048,1408]{1,0:T(8,128)(2,1)S(1)} custom-call(bf16[512,2048]{1,0:T(8,128)(2,1)S(1)} %copy-done.11, bf16[512,2048]{1,0:T(8,128)(2,1)S(1)} %copy-done.13, bf16[512,1408]{1,0:T(8,128)(2,1)S(1)} %get-tuple-element.194.refs_2_, bf16[512,1408]{1,0:T(8,128)(2,1)S(1)} %get-tuple-element.180.refs_3_), custom_call_target="tpu_custom_call" | custom-call | flops 1024 | bytes 1024 | tf_op jit(solution)/shard_map/pallas_call | solution.py:80
  306.1 2.5 copy-done.2
  314.0 5.1 collective-permute-done.32.refs_1_
  319.1 2.1 reduce-scatter.3.cloned.1.call-done
  323.8 2.2 shard_map.227
  330.7 11.2 %collective-permute-done.34 = bf16[128,2048]{1,0:T(8,128)(2,1)S(1)} collective-permute-done((bf16[128,2048]{1,0:T(8,128)(2,1)S(1)}, bf16[128,2048]{1,0:T(8,128)(2,1)S(1)}, u32[]{:S(2)}, u32[]{:S(2)}) %collective-permute-start.34) | collective-permute-done | bytes 524320 | tf_op jit(solution)/shard_map/ppermute | solution.py:34
  341.9 11.6 %collective-permute-done.35 = bf16[128,2048]{1,0:T(8,128)(2,1)S(1)} collective-permute-done((bf16[128,2048]{1,0:T(8,128)(2,1)S(1)}, bf16[128,2048]{1,0:T(8,128)(2,1)S(1)}, u32[]{:S(2)}, u32[]{:S(2)}) %collective-permute-start.35) | collective-permute-done | bytes 524320 | tf_op jit(solution)/shard_map/ppermute | solution.py:34
  357.9 26.1 %shard_map.228 = (bf16[1024,256]{1,0:T(8,128)(2,1)S(1)}, f32[8,4,64,128]{3,2,1,0:T(8,128)S(1)}, bf16[8,4,64,128]{3,2,1,0:T(8,128)(2,1)S(1)}) custom-call(s32[2]{0:T(128)S(1)} %copy-done.84, bf16[512,2048]{1,0:T(8,128)(2,1)S(1)} %constant_dynamic-update-slice_fusion.4.s.ba, bf16[512,2048]{1,0:T(8,128)(2,1)S(1)} %collective-permute-done.37.o.bb, ...), custom_call_target="tpu_custom_call" | custom-call | flops 1024 | bytes 1024 | tf_op jit(solution)/shard_map/pallas_call | solution.py:269
  389.4 9.6 %collective-permute-done.42.refs_0_ = bf16[8,64,128]{2,1,0:T(8,128)(2,1)S(1)} collective-permute-done((bf16[8,64,128]{2,1,0:T(8,128)(2,1)S(1)}, bf16[8,64,128]{2,1,0:T(8,128)(2,1)S(1)}, u32[]{:S(2)}, u32[]{:S(2)}) %collective-permute-start.42) | collective-permute-done | bytes 131104 | tf_op jit(solution)/shard_map/ppermute | solution.py:38
  399.1 19.5 %collective-permute-done.43.refs_1_ = bf16[8,64,128]{2,1,0:T(8,128)(2,1)S(1)} collective-permute-done((bf16[8,64,128]{2,1,0:T(8,128)(2,1)S(1)}, bf16[8,64,128]{2,1,0:T(8,128)(2,1)S(1)}, u32[]{:S(2)}, u32[]{:S(2)}) %collective-permute-start.43) | collective-permute-done | bytes 131104 | tf_op jit(solution)/shard_map/ppermute | solution.py:38
  420.0 4.8 shard_map.231
  426.3 4.1 collective-permute-done.45.c
  430.4 2.1 shard_map.232
  434.9 3.7 all-to-all-start.2
  439.7 3.4 collective-permute-start.50
  444.7 2.1 collective-permute-start.46
  448.3 7.4 %collective-permute-done.49.refs_0_ = bf16[256,1152]{1,0:T(8,128)(2,1)} collective-permute-done((bf16[256,1152]{1,0:T(8,128)(2,1)}, bf16[256,1152]{1,0:T(8,128)(2,1)}, u32[]{:S(2)}, u32[]{:S(2)}) %collective-permute-start.49) | collective-permute-done | bytes 589856 | tf_op jit(solution)/shard_map/ppermute | solution.py:38
  455.7 2.6 collective-permute-start.48
  458.3 3.2 fusion.8
  461.4 33.4 %collective-permute-done.50.refs_1_ = bf16[256,1152]{1,0:T(8,128)(2,1)} collective-permute-done((bf16[256,1152]{1,0:T(8,128)(2,1)}, bf16[256,1152]{1,0:T(8,128)(2,1)}, u32[]{:S(2)}, u32[]{:S(2)}) %collective-permute-start.50) | collective-permute-done | bytes 589856 | tf_op jit(solution)/shard_map/ppermute | solution.py:38
  497.5 2.6 shard_map.233
  500.8 3.8 all-to-all-start.3
  504.7 2.0 fusion.2
  506.7 2.6 fusion.6
  510.6 2.4 all-to-all-done.3.x
  514.0 2.3 shard_map.234
  (364 shorter events, 92.7 us)
Async XLA Ops:
  11.8 25.6 %all-to-all-start = ((bf16[8,64,384]{2,1,0:T(8,128)(2,1)}), bf16[8,64,384]{2,1,0:T(8,128)(2,1)S(1)}, u32[]{:S(2)}, u32[]{:S(2)}) async-start(bf16[8,64,384]{2,1,0:T(8,128)(2,1)} %bitcast.31), calls=%async_computation | async-start | bytes 786432 | tf_op jit(solution)/shard_map/all_to_all | solution.py:724
  15.6 11.1 %collective-permute-start = (bf16[64,2048]{1,0:T(8,128)(2,1)S(1)}, bf16[64,2048]{1,0:T(8,128)(2,1)S(1)}, u32[]{:S(2)}, u32[]{:S(2)}) collective-permute-start(bf16[64,2048]{1,0:T(8,128)(2,1)S(1)} %copy-done.70), channel_id=1, source_target_pairs={{0,3},{1,0},{2,1},{3,2},{4,7},{5,4},{6,5},{7,6},{8,11},{9,8},{10,9... | collective-permute-start | bytes 786440 | tf_op jit(solution)/shard_map/ppermute | solution.py:38
  16.1 21.3 %collective-permute-start.1 = (bf16[64,2048]{1,0:T(8,128)(2,1)S(1)}, bf16[64,2048]{1,0:T(8,128)(2,1)S(1)}, u32[]{:S(2)}, u32[]{:S(2)}) collective-permute-start(bf16[64,2048]{1,0:T(8,128)(2,1)S(1)} %copy-done.70), channel_id=1, source_target_pairs={{0,2},{1,3},{2,0},{3,1},{4,6},{5,7},{6,4},{7,5},{8,10},{9,11},{10,... | collective-permute-start | bytes 786440 | tf_op jit(solution)/shard_map/ppermute | solution.py:38
  16.4 21.0 %collective-permute-start.2 = (bf16[64,2048]{1,0:T(8,128)(2,1)S(1)}, bf16[64,2048]{1,0:T(8,128)(2,1)S(1)}, u32[]{:S(2)}, u32[]{:S(2)}) collective-permute-start(bf16[64,2048]{1,0:T(8,128)(2,1)S(1)} %copy-done.70), channel_id=1, source_target_pairs={{0,1},{1,2},{2,3},{3,0},{4,5},{5,6},{6,7},{7,4},{8,9},{9,10},{10,1... | collective-permute-start | bytes 786440 | tf_op jit(solution)/shard_map/ppermute | solution.py:38
  38.8 46.6 %all-to-all-start.1 = ((bf16[8,64,1408]{2,1,0:T(8,128)(2,1)}), bf16[8,64,1408]{2,1,0:T(8,128)(2,1)}, u32[]{:S(2)}, u32[]{:S(2)}) async-start(bf16[8,64,1408]{2,1,0:T(8,128)(2,1)} %shard_map.212), calls=%async_computation.1 | async-start | bytes 2883584 | tf_op jit(solution)/shard_map/all_to_all | solution.py:742
  43.2 160.2 %all-gather.3.cloned.1.call-start = ((), (), s32[]{:S(2)}) async-start(), calls=%async_computation.6 | async-start | bytes 7208960 | tf_op jit(solution)/shard_map/all_gather | solution.py:746
  43.4 35.8 %collective-permute-start.6 = (bf16[128,2048]{1,0:T(8,128)(2,1)S(1)}, bf16[128,2048]{1,0:T(8,128)(2,1)}, u32[]{:S(2)}, u32[]{:S(2)}) collective-permute-start(bf16[128,2048]{1,0:T(8,128)(2,1)S(1)} %bitcast.38), channel_id=1, source_target_pairs={{0,8},{4,12},{8,0},{12,4},{16,24},{20,28},{24,16},{28,20},{1,9},{5... | collective-permute-start | bytes 1572872 | tf_op jit(solution)/shard_map/ppermute | solution.py:34
  45.3 33.9 %collective-permute-start.7 = (bf16[128,2048]{1,0:T(8,128)(2,1)S(1)}, bf16[128,2048]{1,0:T(8,128)(2,1)}, u32[]{:S(2)}, u32[]{:S(2)}) collective-permute-start(bf16[128,2048]{1,0:T(8,128)(2,1)S(1)} %bitcast.39), channel_id=1, source_target_pairs={{0,16},{4,20},{8,24},{12,28},{16,0},{20,4},{24,8},{28,12},{1,17},{... | collective-permute-start | bytes 1572872 | tf_op jit(solution)/shard_map/ppermute | solution.py:34
  46.8 38.6 %collective-permute-start.8 = (bf16[128,2048]{1,0:T(8,128)(2,1)S(1)}, bf16[128,2048]{1,0:T(8,128)(2,1)}, u32[]{:S(2)}, u32[]{:S(2)}) collective-permute-start(bf16[128,2048]{1,0:T(8,128)(2,1)S(1)} %bitcast.40), channel_id=1, source_target_pairs={{0,24},{4,28},{8,16},{12,20},{16,8},{20,12},{24,0},{28,4},{1,25},{... | collective-permute-start | bytes 1572872 | tf_op jit(solution)/shard_map/ppermute | solution.py:34
  47.0 15.1 %collective-permute-start.3 = (bf16[8,64,384]{2,1,0:T(8,128)(2,1)S(1)}, bf16[8,64,384]{2,1,0:T(8,128)(2,1)S(1)}, u32[]{:S(2)}, u32[]{:S(2)}) collective-permute-start(bf16[8,64,384]{2,1,0:T(8,128)(2,1)S(1)} %all-to-all-done.refs_0_), channel_id=1, source_target_pairs={{0,3},{1,0},{2,1},{3,2},{4,7},{5,4},{6,5},{7,6},{8,11},{9,8},{10,9... | collective-permute-start | bytes 1179656 | tf_op jit(solution)/shard_map/ppermute | solution.py:38
  52.4 25.3 %collective-permute-start.4 = (bf16[8,64,384]{2,1,0:T(8,128)(2,1)S(1)}, bf16[8,64,384]{2,1,0:T(8,128)(2,1)S(1)}, u32[]{:S(2)}, u32[]{:S(2)}) collective-permute-start(bf16[8,64,384]{2,1,0:T(8,128)(2,1)S(1)} %all-to-all-done.refs_0_), channel_id=1, source_target_pairs={{0,2},{1,3},{2,0},{3,1},{4,6},{5,7},{6,4},{7,5},{8,10},{9,11},{10,... | collective-permute-start | bytes 1179656 | tf_op jit(solution)/shard_map/ppermute | solution.py:38
  62.1 17.1 %collective-permute-start.5 = (bf16[8,64,384]{2,1,0:T(8,128)(2,1)S(1)}, bf16[8,64,384]{2,1,0:T(8,128)(2,1)S(1)}, u32[]{:S(2)}, u32[]{:S(2)}) collective-permute-start(bf16[8,64,384]{2,1,0:T(8,128)(2,1)S(1)} %all-to-all-done.refs_0_), channel_id=1, source_target_pairs={{0,1},{1,2},{2,3},{3,0},{4,5},{5,6},{6,7},{7,4},{8,9},{9,10},{10,1... | collective-permute-start | bytes 1179656 | tf_op jit(solution)/shard_map/ppermute | solution.py:38
  85.4 177.4 %all-gather.5.cloned.1.call-start = ((), (), s32[]{:S(2)}) async-start(), calls=%async_computation.7 | async-start | bytes 3604480 | tf_op jit(solution)/shard_map/all_gather | solution.py:770
  87.0 4.2 collective-permute-start.9
  99.0 45.2 %copy-start.44 = (bf16[1024,256]{1,0:T(8,128)(2,1)}, bf16[1024,256]{1,0:T(8,128)(2,1)S(1)}, u32[]{:S(2)}) copy-start(bf16[1024,256]{1,0:T(8,128)(2,1)S(1)} %get-tuple-element.146.q) | copy-start | bytes 1572868
  99.0 29.9 %collective-permute-start.13 = (bf16[128,2048]{1,0:T(8,128)(2,1)S(1)}, bf16[128,2048]{1,0:T(8,128)(2,1)S(1)}, u32[]{:S(2)}, u32[]{:S(2)}) collective-permute-start(bf16[128,2048]{1,0:T(8,128)(2,1)S(1)} %bitcast.43), channel_id=1, source_target_pairs={{0,8},{4,12},{8,0},{12,4},{16,24},{20,28},{24,16},{28,20},{1,9},{5... | collective-permute-start | bytes 1572872 | tf_op jit(solution)/shard_map/ppermute | solution.py:34
  99.5 29.3 %collective-permute-start.14 = (bf16[128,2048]{1,0:T(8,128)(2,1)S(1)}, bf16[128,2048]{1,0:T(8,128)(2,1)S(1)}, u32[]{:S(2)}, u32[]{:S(2)}) collective-permute-start(bf16[128,2048]{1,0:T(8,128)(2,1)S(1)} %bitcast.44), channel_id=1, source_target_pairs={{0,16},{4,20},{8,24},{12,28},{16,0},{20,4},{24,8},{28,12},{1,17},{... | collective-permute-start | bytes 1572872 | tf_op jit(solution)/shard_map/ppermute | solution.py:34
  99.9 29.0 %collective-permute-start.15 = (bf16[128,2048]{1,0:T(8,128)(2,1)S(1)}, bf16[128,2048]{1,0:T(8,128)(2,1)S(1)}, u32[]{:S(2)}, u32[]{:S(2)}) collective-permute-start(bf16[128,2048]{1,0:T(8,128)(2,1)S(1)} %bitcast.45), channel_id=1, source_target_pairs={{0,24},{4,28},{8,16},{12,20},{16,8},{20,12},{24,0},{28,4},{1,25},{... | collective-permute-start | bytes 1572872 | tf_op jit(solution)/shard_map/ppermute | solution.py:34
  102.4 12.1 %collective-permute-start.10 = (bf16[8,64,128]{2,1,0:T(8,128)(2,1)S(1)}, bf16[8,64,128]{2,1,0:T(8,128)(2,1)S(1)}, u32[]{:S(2)}, u32[]{:S(2)}) collective-permute-start(bf16[8,64,128]{2,1,0:T(8,128)(2,1)S(1)} %get-tuple-element.147.refs_0_), channel_id=1, source_target_pairs={{0,3},{1,0},{2,1},{3,2},{4,7},{5,4},{6,5},{7,6},{8,11},{9,8},{10,9... | collective-permute-start | bytes 393224 | tf_op jit(solution)/shard_map/ppermute | solution.py:38
  107.9 17.8 %collective-permute-start.11 = (bf16[8,64,128]{2,1,0:T(8,128)(2,1)S(1)}, bf16[8,64,128]{2,1,0:T(8,128)(2,1)S(1)}, u32[]{:S(2)}, u32[]{:S(2)}) collective-permute-start(bf16[8,64,128]{2,1,0:T(8,128)(2,1)S(1)} %get-tuple-element.147.refs_0_), channel_id=1, source_target_pairs={{0,2},{1,3},{2,0},{3,1},{4,6},{5,7},{6,4},{7,5},{8,10},{9,11},{10,... | collective-permute-start | bytes 393224 | tf_op jit(solution)/shard_map/ppermute | solution.py:38
  114.5 14.3 %collective-permute-start.12 = (bf16[8,64,128]{2,1,0:T(8,128)(2,1)S(1)}, bf16[8,64,128]{2,1,0:T(8,128)(2,1)}, u32[]{:S(2)}, u32[]{:S(2)}) collective-permute-start(bf16[8,64,128]{2,1,0:T(8,128)(2,1)S(1)} %get-tuple-element.147.refs_0_), channel_id=1, source_target_pairs={{0,1},{1,2},{2,3},{3,0},{4,5},{5,6},{6,7},{7,4},{8,9},{9,10},{10,1... | collective-permute-start | bytes 393224 | tf_op jit(solution)/shard_map/ppermute | solution.py:38
  125.6 8.5 %collective-permute-start.16 = (bf16[8,64,128]{2,1,0:T(8,128)(2,1)S(1)}, bf16[8,64,128]{2,1,0:T(8,128)(2,1)}, u32[]{:S(2)}, u32[]{:S(2)}) collective-permute-start(bf16[8,64,128]{2,1,0:T(8,128)(2,1)S(1)} %get-tuple-element.147.refs_0_), channel_id=1, source_target_pairs={{0,4},{4,0},{8,12},{12,8},{16,20},{20,16},{24,28},{28,24},{1,5},{5... | collective-permute-start | bytes 393224 | tf_op jit(solution)/shard_map/ppermute | solution.py:34
  128.9 5.3 %collective-permute-start.17 = (bf16[8,64,128]{2,1,0:T(8,128)(2,1)S(1)}, bf16[8,64,128]{2,1,0:T(8,128)(2,1)S(1)}, u32[]{:S(2)}, u32[]{:S(2)}) collective-permute-start(bf16[8,64,128]{2,1,0:T(8,128)(2,1)S(1)} %collective-permute-done.10.refs_1_), channel_id=1, source_target_pairs={{0,4},{4,0},{8,12},{12,8},{16,20},{20,16},{24,28},{28,24},{1,5},{5... | collective-permute-start | bytes 393224 | tf_op jit(solution)/shard_map/ppermute | solution.py:34
  129.0 5.2 collective-permute-start.18
  129.5 4.7 collective-permute-start.19
  144.9 4.2 collective-permute-start.20
  149.9 14.8 %collective-permute-start.21 = (bf16[128,2048]{1,0:T(8,128)(2,1)S(1)}, bf16[128,2048]{1,0:T(8,128)(2,1)S(1)}, u32[]{:S(2)}, u32[]{:S(2)}) collective-permute-start(bf16[128,2048]{1,0:T(8,128)(2,1)S(1)} %get-tuple-element.157), channel_id=1, source_target_pairs={{0,8},{4,12},{8,0},{12,4},{16,24},{20,28},{24,16},{28,20},{1,9},{5... | collective-permute-start | bytes 1572872 | tf_op jit(solution)/shard_map/ppermute | solution.py:34
  151.7 25.4 %collective-permute-start.22 = (bf16[128,2048]{1,0:T(8,128)(2,1)S(1)}, bf16[128,2048]{1,0:T(8,128)(2,1)S(1)}, u32[]{:S(2)}, u32[]{:S(2)}) collective-permute-start(bf16[128,2048]{1,0:T(8,128)(2,1)S(1)} %get-tuple-element.158), channel_id=1, source_target_pairs={{0,16},{4,20},{8,24},{12,28},{16,0},{20,4},{24,8},{28,12},{1,17},{... | collective-permute-start | bytes 1572872 | tf_op jit(solution)/shard_map/ppermute | solution.py:34
  153.9 24.0 %collective-permute-start.23 = (bf16[128,2048]{1,0:T(8,128)(2,1)S(1)}, bf16[128,2048]{1,0:T(8,128)(2,1)S(1)}, u32[]{:S(2)}, u32[]{:S(2)}) collective-permute-start(bf16[128,2048]{1,0:T(8,128)(2,1)S(1)} %get-tuple-element.159), channel_id=1, source_target_pairs={{0,24},{4,28},{8,16},{12,20},{16,8},{20,12},{24,0},{28,4},{1,25},{... | collective-permute-start | bytes 1572872 | tf_op jit(solution)/shard_map/ppermute | solution.py:34
  203.5 117.7 %reduce-scatter.3.cloned.1.call-start = ((), (), s32[]{:S(2)}) async-start(), calls=%async_computation.8 | async-start | bytes 3604480 | tf_op jit(solution)/shard_map/reduce_scatter | solution.py:779
  208.2 14.8 %collective-permute-start.24 = (bf16[128,2048]{1,0:T(8,128)(2,1)S(1)}, bf16[128,2048]{1,0:T(8,128)(2,1)S(1)}, u32[]{:S(2)}, u32[]{:S(2)}) collective-permute-start(bf16[128,2048]{1,0:T(8,128)(2,1)S(1)} %get-tuple-element.165), channel_id=1, source_target_pairs={{0,8},{4,12},{8,0},{12,4},{16,24},{20,28},{24,16},{28,20},{1,9},{5... | collective-permute-start | bytes 1572872 | tf_op jit(solution)/shard_map/ppermute | solution.py:34
  210.0 24.8 %collective-permute-start.25 = (bf16[128,2048]{1,0:T(8,128)(2,1)S(1)}, bf16[128,2048]{1,0:T(8,128)(2,1)S(1)}, u32[]{:S(2)}, u32[]{:S(2)}) collective-permute-start(bf16[128,2048]{1,0:T(8,128)(2,1)S(1)} %get-tuple-element.165), channel_id=1, source_target_pairs={{0,16},{4,20},{8,24},{12,28},{16,0},{20,4},{24,8},{28,12},{1,17},{... | collective-permute-start | bytes 1572872 | tf_op jit(solution)/shard_map/ppermute | solution.py:34
  211.4 23.4 %collective-permute-start.26 = (bf16[128,2048]{1,0:T(8,128)(2,1)S(1)}, bf16[128,2048]{1,0:T(8,128)(2,1)S(1)}, u32[]{:S(2)}, u32[]{:S(2)}) collective-permute-start(bf16[128,2048]{1,0:T(8,128)(2,1)S(1)} %get-tuple-element.165), channel_id=1, source_target_pairs={{0,24},{4,28},{8,16},{12,20},{16,8},{20,12},{24,0},{28,4},{1,25},{... | collective-permute-start | bytes 1572872 | tf_op jit(solution)/shard_map/ppermute | solution.py:34
  235.0 8.8 %collective-permute-start.27 = (bf16[512,2048]{1,0:T(8,128)(2,1)S(1)}, bf16[512,2048]{1,0:T(8,128)(2,1)S(1)}, u32[]{:S(2)}, u32[]{:S(2)}) collective-permute-start(bf16[512,2048]{1,0:T(8,128)(2,1)S(1)} %constant_dynamic-update-slice_fusion.x.refs_0_), channel_id=1, source_target_pairs={{0,4},{4,0},{8,12},{12,8},{16,20},{20,16},{24,28},{28,24},{1,5},{5... | collective-permute-start | bytes 6291464 | tf_op jit(solution)/shard_map/ppermute | solution.py:34
  235.2 14.0 %collective-permute-start.28 = (bf16[512,2048]{1,0:T(8,128)(2,1)S(1)}, bf16[512,2048]{1,0:T(8,128)(2,1)S(1)}, u32[]{:S(2)}, u32[]{:S(2)}) collective-permute-start(bf16[512,2048]{1,0:T(8,128)(2,1)S(1)} %pad_maximum_fusion.1.refs_2_.dy), channel_id=1, source_target_pairs={{0,4},{4,0},{8,12},{12,8},{16,20},{20,16},{24,28},{28,24},{1,5},{5... | collective-permute-start | bytes 6291464 | tf_op jit(solution)/shard_map/ppermute | solution.py:34
  262.8 172.1 %reduce-scatter.5.cloned.1.call-start = ((), (), s32[]{:S(2)}) async-start(), calls=%async_computation.9 | async-start | bytes 7208960 | tf_op jit(solution)/shard_map/reduce_scatter | solution.py:790
  280.3 8.6 %collective-permute-start.29 = (bf16[512,2048]{1,0:T(8,128)(2,1)S(1)}, bf16[512,2048]{1,0:T(8,128)(2,1)S(1)}, u32[]{:S(2)}, u32[]{:S(2)}) collective-permute-start(bf16[512,2048]{1,0:T(8,128)(2,1)S(1)} %get-tuple-element.185), channel_id=1, source_target_pairs={{0,4},{4,0},{8,12},{12,8},{16,20},{20,16},{24,28},{28,24},{1,5},{5... | collective-permute-start | bytes 6291464 | tf_op jit(solution)/shard_map/ppermute | solution.py:34
  291.8 4.2 collective-permute-start.30
  292.2 21.7 %collective-permute-start.31 = (bf16[128,2048]{1,0:T(8,128)(2,1)}, bf16[128,2048]{1,0:T(8,128)(2,1)}, u32[]{:S(2)}, u32[]{:S(2)}) collective-permute-start(bf16[128,2048]{1,0:T(8,128)(2,1)} %get-tuple-element.186), channel_id=1, source_target_pairs={{0,8},{4,12},{8,0},{12,4},{16,24},{20,28},{24,16},{28,20},{1,9},{5... | collective-permute-start | bytes 1572872 | tf_op jit(solution)/shard_map/ppermute | solution.py:34
  293.9 25.2 %collective-permute-start.32 = (bf16[128,2048]{1,0:T(8,128)(2,1)}, bf16[128,2048]{1,0:T(8,128)(2,1)}, u32[]{:S(2)}, u32[]{:S(2)}) collective-permute-start(bf16[128,2048]{1,0:T(8,128)(2,1)} %get-tuple-element.187), channel_id=1, source_target_pairs={{0,16},{4,20},{8,24},{12,28},{16,0},{20,4},{24,8},{28,12},{1,17},{... | collective-permute-start | bytes 1572872 | tf_op jit(solution)/shard_map/ppermute | solution.py:34
  295.4 23.7 %collective-permute-start.33 = (bf16[128,2048]{1,0:T(8,128)(2,1)}, bf16[128,2048]{1,0:T(8,128)(2,1)}, u32[]{:S(2)}, u32[]{:S(2)}) collective-permute-start(bf16[128,2048]{1,0:T(8,128)(2,1)} %get-tuple-element.188), channel_id=1, source_target_pairs={{0,24},{4,28},{8,16},{12,20},{16,8},{20,12},{24,0},{28,4},{1,25},{... | collective-permute-start | bytes 1572872 | tf_op jit(solution)/shard_map/ppermute | solution.py:34
  327.1 14.8 %collective-permute-start.34 = (bf16[128,2048]{1,0:T(8,128)(2,1)S(1)}, bf16[128,2048]{1,0:T(8,128)(2,1)S(1)}, u32[]{:S(2)}, u32[]{:S(2)}) collective-permute-start(bf16[128,2048]{1,0:T(8,128)(2,1)S(1)} %get-tuple-element.202), channel_id=1, source_target_pairs={{0,8},{4,12},{8,0},{12,4},{16,24},{20,28},{24,16},{28,20},{1,9},{5... | collective-permute-start | bytes 1572872 | tf_op jit(solution)/shard_map/ppermute | solution.py:34
  328.8 24.7 %collective-permute-start.35 = (bf16[128,2048]{1,0:T(8,128)(2,1)S(1)}, bf16[128,2048]{1,0:T(8,128)(2,1)S(1)}, u32[]{:S(2)}, u32[]{:S(2)}) collective-permute-start(bf16[128,2048]{1,0:T(8,128)(2,1)S(1)} %get-tuple-element.202), channel_id=1, source_target_pairs={{0,16},{4,20},{8,24},{12,28},{16,0},{20,4},{24,8},{28,12},{1,17},{... | collective-permute-start | bytes 1572872 | tf_op jit(solution)/shard_map/ppermute | solution.py:34
  330.3 23.2 %collective-permute-start.36 = (bf16[128,2048]{1,0:T(8,128)(2,1)S(1)}, bf16[128,2048]{1,0:T(8,128)(2,1)S(1)}, u32[]{:S(2)}, u32[]{:S(2)}) collective-permute-start(bf16[128,2048]{1,0:T(8,128)(2,1)S(1)} %get-tuple-element.202), channel_id=1, source_target_pairs={{0,24},{4,28},{8,16},{12,20},{16,8},{20,12},{24,0},{28,4},{1,25},{... | collective-permute-start | bytes 1572872 | tf_op jit(solution)/shard_map/ppermute | solution.py:34
  353.7 4.2 collective-permute-start.37
  353.8 30.3 %collective-permute-start.38 = (bf16[128,2048]{1,0:T(8,128)(2,1)S(1)}, bf16[128,2048]{1,0:T(8,128)(2,1)S(1)}, u32[]{:S(2)}, u32[]{:S(2)}) collective-permute-start(bf16[128,2048]{1,0:T(8,128)(2,1)S(1)} %copy-done.93), channel_id=1, source_target_pairs={{0,8},{4,12},{8,0},{12,4},{16,24},{20,28},{24,16},{28,20},{1,9},{5... | collective-permute-start | bytes 1572872 | tf_op jit(solution)/shard_map/ppermute | solution.py:34
  355.0 29.1 %collective-permute-start.39 = (bf16[128,2048]{1,0:T(8,128)(2,1)S(1)}, bf16[128,2048]{1,0:T(8,128)(2,1)S(1)}, u32[]{:S(2)}, u32[]{:S(2)}) collective-permute-start(bf16[128,2048]{1,0:T(8,128)(2,1)S(1)} %copy-done.91), channel_id=1, source_target_pairs={{0,16},{4,20},{8,24},{12,28},{16,0},{20,4},{24,8},{28,12},{1,17},{... | collective-permute-start | bytes 1572872 | tf_op jit(solution)/shard_map/ppermute | solution.py:34
  355.9 28.3 %collective-permute-start.40 = (bf16[128,2048]{1,0:T(8,128)(2,1)S(1)}, bf16[128,2048]{1,0:T(8,128)(2,1)S(1)}, u32[]{:S(2)}, u32[]{:S(2)}) collective-permute-start(bf16[128,2048]{1,0:T(8,128)(2,1)S(1)} %copy-done.89), channel_id=1, source_target_pairs={{0,24},{4,28},{8,16},{12,20},{16,8},{20,12},{24,0},{28,4},{1,25},{... | collective-permute-start | bytes 1572872 | tf_op jit(solution)/shard_map/ppermute | solution.py:34
  384.1 35.8 %copy-start.108 = (bf16[128,2048]{1,0:T(8,128)(2,1)}, bf16[128,2048]{1,0:T(8,128)(2,1)S(1)}, u32[]{:S(2)}) copy-start(bf16[128,2048]{1,0:T(8,128)(2,1)S(1)} %collective-permute-done.38) | copy-start | bytes 1572868
  384.1 35.8 %copy-start.109 = (bf16[128,2048]{1,0:T(8,128)(2,1)}, bf16[128,2048]{1,0:T(8,128)(2,1)S(1)}, u32[]{:S(2)}) copy-start(bf16[128,2048]{1,0:T(8,128)(2,1)S(1)} %collective-permute-done.39) | copy-start | bytes 1572868
  384.2 2.0 collective-permute-start.41
  386.2 12.8 %collective-permute-start.42 = (bf16[8,64,128]{2,1,0:T(8,128)(2,1)S(1)}, bf16[8,64,128]{2,1,0:T(8,128)(2,1)S(1)}, u32[]{:S(2)}, u32[]{:S(2)}) collective-permute-start(bf16[8,64,128]{2,1,0:T(8,128)(2,1)S(1)} %get-tuple-element.219), channel_id=1, source_target_pairs={{0,1},{1,2},{2,3},{3,0},{4,5},{5,6},{6,7},{7,4},{8,9},{9,10},{10,1... | collective-permute-start | bytes 393224 | tf_op jit(solution)/shard_map/ppermute | solution.py:38
  387.7 30.8 %collective-permute-start.43 = (bf16[8,64,128]{2,1,0:T(8,128)(2,1)S(1)}, bf16[8,64,128]{2,1,0:T(8,128)(2,1)S(1)}, u32[]{:S(2)}, u32[]{:S(2)}) collective-permute-start(bf16[8,64,128]{2,1,0:T(8,128)(2,1)S(1)} %get-tuple-element.220), channel_id=1, source_target_pairs={{0,2},{1,3},{2,0},{3,1},{4,6},{5,7},{6,4},{7,5},{8,10},{9,11},{10,... | collective-permute-start | bytes 393224 | tf_op jit(solution)/shard_map/ppermute | solution.py:38
  389.3 29.2 %collective-permute-start.44 = (bf16[8,64,128]{2,1,0:T(8,128)(2,1)S(1)}, bf16[8,64,128]{2,1,0:T(8,128)(2,1)S(1)}, u32[]{:S(2)}, u32[]{:S(2)}) collective-permute-start(bf16[8,64,128]{2,1,0:T(8,128)(2,1)S(1)} %get-tuple-element.221), channel_id=1, source_target_pairs={{0,3},{1,0},{2,1},{3,2},{4,7},{5,4},{6,5},{7,6},{8,11},{9,8},{10,9... | collective-permute-start | bytes 393224 | tf_op jit(solution)/shard_map/ppermute | solution.py:38
  426.2 4.2 collective-permute-start.45
  434.9 61.5 %all-to-all-start.2 = ((bf16[8,64,1408]{2,1,0:T(8,128)(2,1)}), bf16[8,64,1408]{2,1,0:T(8,128)(2,1)S(1)}, u32[]{:S(2)}, u32[]{:S(2)}) async-start(bf16[8,64,1408]{2,1,0:T(8,128)(2,1)} %bitcast.51), calls=%async_computation.4 | async-start | bytes 2883584 | tf_op jit(solution)/shard_map/all_to_all | solution.py:815
  438.6 17.1 %collective-permute-start.49 = (bf16[256,1152]{1,0:T(8,128)(2,1)}, bf16[256,1152]{1,0:T(8,128)(2,1)}, u32[]{:S(2)}, u32[]{:S(2)}) collective-permute-start(bf16[256,1152]{1,0:T(8,128)(2,1)} %copy-done.87), channel_id=1, source_target_pairs={{0,1},{1,2},{2,3},{3,0},{4,5},{5,6},{6,7},{7,4},{8,9},{9,10},{10,1... | collective-permute-start | bytes 1769480 | tf_op jit(solution)/shard_map/ppermute | solution.py:38
  439.7 55.1 %collective-permute-start.50 = (bf16[256,1152]{1,0:T(8,128)(2,1)}, bf16[256,1152]{1,0:T(8,128)(2,1)}, u32[]{:S(2)}, u32[]{:S(2)}) collective-permute-start(bf16[256,1152]{1,0:T(8,128)(2,1)} %copy-done.86), channel_id=1, source_target_pairs={{0,2},{1,3},{2,0},{3,1},{4,6},{5,7},{6,4},{7,5},{8,10},{9,11},{10,... | collective-permute-start | bytes 1769480 | tf_op jit(solution)/shard_map/ppermute | solution.py:38
  443.1 51.7 %collective-permute-start.51 = (bf16[256,1152]{1,0:T(8,128)(2,1)}, bf16[256,1152]{1,0:T(8,128)(2,1)}, u32[]{:S(2)}, u32[]{:S(2)}) collective-permute-start(bf16[256,1152]{1,0:T(8,128)(2,1)} %copy-done.85), channel_id=1, source_target_pairs={{0,3},{1,0},{2,1},{3,2},{4,7},{5,4},{6,5},{7,6},{8,11},{9,8},{10,9... | collective-permute-start | bytes 1769480 | tf_op jit(solution)/shard_map/ppermute | solution.py:38
  444.7 50.1 %collective-permute-start.46 = (bf16[128,2048]{1,0:T(8,128)(2,1)}, bf16[128,2048]{1,0:T(8,128)(2,1)S(1)}, u32[]{:S(2)}, u32[]{:S(2)}) collective-permute-start(bf16[128,2048]{1,0:T(8,128)(2,1)} %copy-done.96), channel_id=1, source_target_pairs={{0,8},{4,12},{8,0},{12,4},{16,24},{20,28},{24,16},{28,20},{1,9},{5... | collective-permute-start | bytes 1572872 | tf_op jit(solution)/shard_map/ppermute | solution.py:34
  446.8 48.0 %collective-permute-start.47 = (bf16[128,2048]{1,0:T(8,128)(2,1)}, bf16[128,2048]{1,0:T(8,128)(2,1)S(1)}, u32[]{:S(2)}, u32[]{:S(2)}) collective-permute-start(bf16[128,2048]{1,0:T(8,128)(2,1)} %copy-done.95), channel_id=1, source_target_pairs={{0,16},{4,20},{8,24},{12,28},{16,0},{20,4},{24,8},{28,12},{1,17},{... | collective-permute-start | bytes 1572872 | tf_op jit(solution)/shard_map/ppermute | solution.py:34
  455.7 40.7 %collective-permute-start.48 = (bf16[128,2048]{1,0:T(8,128)(2,1)}, bf16[128,2048]{1,0:T(8,128)(2,1)}, u32[]{:S(2)}, u32[]{:S(2)}) collective-permute-start(bf16[128,2048]{1,0:T(8,128)(2,1)} %copy-done.94), channel_id=1, source_target_pairs={{0,24},{4,28},{8,16},{12,20},{16,8},{20,12},{24,0},{28,4},{1,25},{... | collective-permute-start | bytes 1572872 | tf_op jit(solution)/shard_map/ppermute | solution.py:34
  458.3 46.4 %copy-start.79 = (f32[1,2048]{1,0:T(1,128)S(1)}, f32[1,2048]{1,0:T(1,128)}, u32[]{:S(2)}) copy-start(f32[1,2048]{1,0:T(1,128)} %copy-done.78) | copy-start | bytes 24580
  500.8 12.2 %all-to-all-start.3 = ((bf16[8,64,320]{2,1,0:T(8,128)(2,1)}), bf16[8,64,320]{2,1,0:T(8,128)(2,1)S(1)}, u32[]{:S(2)}, u32[]{:S(2)}) async-start(bf16[8,64,320]{2,1,0:T(8,128)(2,1)} %copy-done.67), calls=%async_computation.5 | async-start | bytes 786432 | tf_op jit(solution)/shard_map/all_to_all | solution.py:818
  (110 other events, 945.7 us)
Sparse Core Ops, SparseCore 0:
  85.5 117.8 all-gather.2
  205.0 57.7 all-gather.4
  265.1 56.0 reduce-scatter.2
  323.4 111.2 reduce-scatter.4

commit v4 on v3

--- a/solution.py
+++ b/solution.py
@@ -723,7 +723,8 @@
     w_attn = jnp.concatenate(pieces, axis=1).reshape(block, n, -1).transpose(1, 0, 2)
     w_attn = lax.all_to_all(w_attn, every_dp, 0, 0)
     x16, dy_local = tokens[0], out_grad[0]
-    w_attn, wo_parts = together(w_attn, shifts(w_out, c))
+    wd = lax.all_gather(w_down, "ctx", axis=0, tiled=True)
+    w_attn, wo_parts, same = together(w_attn, shifts(w_out, c), dp_same(x16, n))
     seg_rows = w_attn[:, :, used + 2 : used + 2 + length // block].reshape(n, length)
 
     order = me ^ jnp.array([*range(0, n, 2), *range(1, n, 2)], jnp.int32)
@@ -740,12 +741,12 @@
     sine = jnp.concatenate([-sine, sine] * 2, axis=1)
     w_pair = columns_out(*after((w_gate, w_up), w_attn), 1, n)
     w_pair = lax.all_to_all(w_pair, every_dp, 0, 0).reshape(n * block, 2 * f_cols)
-    w_parts, same, cosine, sine, w_pair = together(
-        shifts(w_attn, c), dp_same(after(x16, w_attn), n), cosine, sine, w_pair
-    )
-    w_pair = lax.all_gather(w_pair, "ctx", axis=0, tiled=True)
     even = jnp.concatenate([x16, *same])
     odd = swap(even, 1)
+    w_parts, cosine, sine, w_pair, wd = together(
+        shifts(w_attn, c), cosine, sine, w_pair, wd
+    )
+    w_pair = lax.all_gather(w_pair, "ctx", axis=0, tiled=True)
 
     w_attn, gains = attention_weights([w_attn, *w_parts], place_z, used)
     w_attn = w_attn.reshape(width, -1)
@@ -766,8 +767,7 @@
     kv_other = [swap(v, 1) for v in kv_all]
     mixed = attend(where, queries, kv_all, kv_other, *sides)
     attn_own, *sends = scatter_dp(mixed, wo, n, dot)
-    sent, w_pair = together([swap(v, 2 * j) for j, v in enumerate(sends, 1)], w_pair)
-    wd = lax.all_gather(after(w_down, w_pair), "ctx", axis=0, tiled=True)
+    sent = together(*[swap(v, 2 * j) for j, v in enumerate(sends, 1)])
     resid, second_in = second_norm(x16, attn_own, sent, gain2, n, c)
 
     second_in = jnp.concatenate([second_in, *together(*dp_same(second_in, n))])

time: 534 us -> 523 us (0.979)
  waiting for transfers between devices: 256 us -> 229 us
  starting transfers between devices: 78 us -> 99.3 us
    all_gather x1, waiting for transfers between devices: 24.8 us -> 1.8 us  [per_device(): w_pair = lax.all_gather(w_pair, 'ctx', axis=0, tiled=True)]
    ppermute x15, starting transfers between devices: 28.1 us -> 49.4 us  [shift(): lax.ppermute(value, 'ctx', [(i, (i - step) % size) for i in range(size)])]
    pallas_call x1, Pallas kernels: 26.1 us -> 17 us  [attend_back(): pl.pallas_call(body, grid=(sequences,), in_specs=[pl.BlockSpec(memory_spa...]
    ppermute x15, waiting for transfers between devices: 127 us -> 120 us  [shift(): lax.ppermute(value, 'ctx', [(i, (i - step) % size) for i in range(size)])]
    ppermute x37, waiting for transfers between devices: 93.7 us -> 86.7 us  [swap(): lax.ppermute(value, ('plane', 'core'), [(i, i ^ rel) for i in range(size)])]
    reduce_scatter x1, waiting for transfers between devices: 0.01 us -> 7.02 us  [per_device(): lax.psum_scatter(pair_term, 'ctx', scatter_dimension=0, tiled=True)]
    unnamed x235 -> x213, local copies, waits for them, and re-layouts: 51.7 us -> 45.8 us
  transfers between devices with their start and end apart: 60 -> 60, of which waited for: 30 -> 29; matrix products, arithmetic and copies ran while one was open for 4% -> 6% of each run, Pallas kernels for 18% -> 17%
where the time goes in v4:
time: 523 us; the launch traced here: 516 us
  waiting for transfers between devices  229 us (44%)
  starting transfers between devices  99.3 us (19%)
  Pallas kernels  98.2 us (19%)
  local copies, waits for them, and re-layouts  53 us (10%)
  other arithmetic  19.2 us (4%)
  between operations  15.4 us (3%)
    ppermute x15, waiting for transfers between devices, shift(): lax.ppermute(value, 'ctx', [(i, (i - step) % size) for i in range(size)])  120 us
    ppermute x37, waiting for transfers between devices, swap(): lax.ppermute(value, ('plane', 'core'), [(i, i ^ rel) for i in range(size)])  86.7 us
    ppermute x15, starting transfers between devices, shift(): lax.ppermute(value, 'ctx', [(i, (i - step) % size) for i in range(size)])  49.4 us
    unnamed x213, local copies, waits for them, and re-layouts  45.8 us
    ppermute x37, starting transfers between devices, swap(): lax.ppermute(value, ('plane', 'core'), [(i, i ^ rel) for i in range(size)])  33.3 us
    pallas_call x2, Pallas kernels, feed_forward_back(): pl.pallas_call(body, grid=(tokens // tile,), in_specs=[rows(2 * ff), rows...  18.3 us
    pallas_call x1, Pallas kernels, attend_back(): pl.pallas_call(body, grid=(sequences,), in_specs=[pl.BlockSpec(memory_spa...  17 us
    pallas_call x2, Pallas kernels, transposed_dot(): pl.pallas_call(body, grid=(rows // row_tile if by_rows else columns // co...  14.5 us
  transfers between devices with their start and end apart: 60, of which 29 were waited for; matrix products, arithmetic and copies ran while one was open for 6% of the time, Pallas kernels for 17%

profile of v4, /device:TPU:24, one launch (start us, length us, event | category | flops | bytes accessed | tf_op | source)
XLA Modules:
  0.0 515.8 jit_solution(16449331224124443950)
XLA Ops:
  8.5 1.8 collective-permute-start.3
  16.4 4.1 all-to-all-start
  21.2 3.1 collective-permute-start.2
  24.9 15.9 %collective-permute-done.1.refs_2_ = bf16[64,2048]{1,0:T(8,128)(2,1)S(1)} collective-permute-done((bf16[64,2048]{1,0:T(8,128)(2,1)}, bf16[64,2048]{1,0:T(8,128)(2,1)S(1)}, u32[]{:S(2)}, u32[]{:S(2)}) %collective-permute-start.1) | collective-permute-done | bytes 262176 | tf_op jit(solution)/shard_map/ppermute | solution.py:38
  41.5 7.0 %collective-permute-done.2.refs_3_ = bf16[64,2048]{1,0:T(8,128)(2,1)S(1)} collective-permute-done((bf16[64,2048]{1,0:T(8,128)(2,1)S(1)}, bf16[64,2048]{1,0:T(8,128)(2,1)S(1)}, u32[]{:S(2)}, u32[]{:S(2)}) %collective-permute-start.2) | collective-permute-done | bytes 262176 | tf_op jit(solution)/shard_map/ppermute | solution.py:38
  49.2 24.7 %collective-permute-start.7 = (bf16[8,64,384]{2,1,0:T(8,128)(2,1)S(1)}, bf16[8,64,384]{2,1,0:T(8,128)(2,1)S(1)}, u32[]{:S(2)}, u32[]{:S(2)}) collective-permute-start(bf16[8,64,384]{2,1,0:T(8,128)(2,1)S(1)} %all-to-all-done.refs_0_), channel_id=1, source_target_pairs={{0,3},{1,0},{2,1},{3,2},{4,7},{5,4},{6,5},{7,6},{8,11},{9,8},{10,9... | collective-permute-start | bytes 1179656 | tf_op jit(solution)/shard_map/ppermute | solution.py:38
  74.0 3.1 collective-permute-start.9
  78.4 4.4 all-to-all-start.1
  82.9 2.8 pad_maximum_fusion.e
  87.0 1.9 fusion.11
  89.9 15.1 %collective-permute-done.8.refs_2_ = bf16[8,64,384]{2,1,0:T(8,128)(2,1)S(1)} collective-permute-done((bf16[8,64,384]{2,1,0:T(8,128)(2,1)S(1)}, bf16[8,64,384]{2,1,0:T(8,128)(2,1)S(1)}, u32[]{:S(2)}, u32[]{:S(2)}) %collective-permute-start.8) | collective-permute-done | bytes 393248 | tf_op jit(solution)/shard_map/ppermute | solution.py:38
  104.9 4.8 all-gather.3.cloned.1.call-done.wd
  111.0 6.7 %shard_map.214 = (bf16[1024,2048]{1,0:T(8,128)(2,1)S(1)}, bf16[1024,256]{1,0:T(8,128)(2,1)S(1)}, bf16[8,64,128]{2,1,0:T(8,128)(2,1)S(1)}) custom-call(s32[2]{0:T(128)S(1)} %pad_add_fusion.at, bf16[512,2048]{1,0:T(8,128)(2,1)} %pad_maximum_fusion.e, bf16[512,2048]{1,0:T(8,128)(2,1)} %collective-permute-done.6.o, f32[1,2048]{1,0:T(1,128)S(1)} %get-tuple-element.268.gn, ...), custom_call_target="tpu_custom_call" | custom-call | flops 1024 | bytes 1024 | tf_op jit(solution)/shard_map/pallas_call | solution.py:140
  117.7 2.0 copy-done.19
  123.2 5.1 collective-permute-start.10
  128.8 6.5 %collective-permute-done.10.refs_1_ = bf16[8,64,128]{2,1,0:T(8,128)(2,1)S(1)} collective-permute-done((bf16[8,64,128]{2,1,0:T(8,128)(2,1)S(1)}, bf16[8,64,128]{2,1,0:T(8,128)(2,1)S(1)}, u32[]{:S(2)}, u32[]{:S(2)}) %collective-permute-start.10) | collective-permute-done | bytes 131104 | tf_op jit(solution)/shard_map/ppermute | solution.py:38
  135.3 3.5 collective-permute-start.12
  138.8 6.5 %collective-permute-done.11.refs_2_ = bf16[8,64,128]{2,1,0:T(8,128)(2,1)S(1)} collective-permute-done((bf16[8,64,128]{2,1,0:T(8,128)(2,1)S(1)}, bf16[8,64,128]{2,1,0:T(8,128)(2,1)S(1)}, u32[]{:S(2)}, u32[]{:S(2)}) %collective-permute-start.11) | collective-permute-done | bytes 131104 | tf_op jit(solution)/shard_map/ppermute | solution.py:38
  145.3 2.6 collective-permute-done.12.refs_3_
  155.2 9.7 %shard_map.215.a.m = bf16[1024,256]{1,0:T(8,128)(2,1)S(1)} custom-call(s32[2]{0:T(128)S(1)} %copy-done.75, bf16[1024,256]{1,0:T(8,128)(2,1)S(1)} %get-tuple-element.143.q, f32[8,128,1]{2,1,0:T(8,128)S(1)} %copy.72.m, f32[8,1,512]{2,1,0:T(1,128)S(1)} %broadcast_in_dim.34.th, bf16[8,64,128]{2,1,0:T(8,128)(2,1)S(1)} %get-tuple-element.144.refs_0_, ...), custom_call_target="tpu_custom_call" | custom-call | flops 1024 | bytes 1024 | tf_op jit(solution)/shard_map/pallas_call | solution.py:219
  165.9 4.0 collective-permute-done.20.c
  174.3 11.3 %collective-permute-done.21.refs_0_ = bf16[128,2048]{1,0:T(8,128)(2,1)S(1)} collective-permute-done((bf16[128,2048]{1,0:T(8,128)(2,1)S(1)}, bf16[128,2048]{1,0:T(8,128)(2,1)S(1)}, u32[]{:S(2)}, u32[]{:S(2)}) %collective-permute-start.21) | collective-permute-done | bytes 524320 | tf_op jit(solution)/shard_map/ppermute | solution.py:34
  185.5 11.5 %collective-permute-done.22.refs_1_ = bf16[128,2048]{1,0:T(8,128)(2,1)S(1)} collective-permute-done((bf16[128,2048]{1,0:T(8,128)(2,1)S(1)}, bf16[128,2048]{1,0:T(8,128)(2,1)S(1)}, u32[]{:S(2)}, u32[]{:S(2)}) %collective-permute-start.22) | collective-permute-done | bytes 524320 | tf_op jit(solution)/shard_map/ppermute | solution.py:34
  202.1 10.5 %collective-permute-done.24 = bf16[128,2048]{1,0:T(8,128)(2,1)S(1)} collective-permute-done((bf16[128,2048]{1,0:T(8,128)(2,1)S(1)}, bf16[128,2048]{1,0:T(8,128)(2,1)S(1)}, u32[]{:S(2)}, u32[]{:S(2)}) %collective-permute-start.24) | collective-permute-done | bytes 524320 | tf_op jit(solution)/shard_map/ppermute | solution.py:34
  212.6 10.6 %collective-permute-done.25 = bf16[128,2048]{1,0:T(8,128)(2,1)S(1)} collective-permute-done((bf16[128,2048]{1,0:T(8,128)(2,1)S(1)}, bf16[128,2048]{1,0:T(8,128)(2,1)S(1)}, u32[]{:S(2)}, u32[]{:S(2)}) %collective-permute-start.25) | collective-permute-done | bytes 524320 | tf_op jit(solution)/shard_map/ppermute | solution.py:34
  227.5 1.8 all-gather.5.cloned.1.call-done.w
  229.3 2.6 copy-done
  232.0 5.3 %shard_map.219 = (f32[512,1408]{1,0:T(8,128)S(1)}, bf16[512,704]{1,0:T(8,128)(2,1)S(1)}) custom-call(bf16[512,2048]{1,0:T(8,128)(2,1)} %constant_dynamic-update-slice_fusion.x.refs_0_, bf16[2048,1408]{1,0:T(8,128)(2,1)S(1)} %copy-done), custom_call_target="tpu_custom_call" | custom-call | flops 1024 | bytes 1024 | tf_op jit(solution)/shard_map/pallas_call | solution.py:393
  237.3 5.9 %shard_map.220 = (f32[512,1408]{1,0:T(8,128)S(1)}, bf16[512,704]{1,0:T(8,128)(2,1)S(1)}) custom-call(bf16[512,2048]{1,0:T(8,128)(2,1)} %collective-permute-done.27.x.refs_1_, bf16[2048,1408]{1,0:T(8,128)(2,1)S(1)} %copy-done.1), custom_call_target="tpu_custom_call" | custom-call | flops 1024 | bytes 1024 | tf_op jit(solution)/shard_map/pallas_call | solution.py:393
  244.8 5.2 %shard_map.221 = bf16[704,2048]{1,0:T(8,128)(2,1)S(1)} custom-call(bf16[512,704]{1,0:T(8,128)(2,1)S(1)} %get-tuple-element.167.refs_0_.h, bf16[512,704]{1,0:T(8,128)(2,1)S(1)} %get-tuple-element.173.refs_1_.h, bf16[512,2048]{1,0:T(8,128)(2,1)S(1)} %pad_maximum_fusion.1.refs_2_.dy, bf16[512,2048]{1,0:T(8,128)(2,1)} %collective-permute-done.28.refs_3_.dy), custom_call_target="tpu_custom_call" | custom-call | flops 1024 | bytes 1024 | tf_op jit(solution)/shard_map/pallas_call | solution.py:80
  252.8 2.6 copy-done.2
  255.4 1.8 copy-done.8
  258.3 1.8 copy-done.30
  260.2 9.8 %shard_map.222 = (bf16[512,1408]{1,0:T(8,128)(2,1)S(1)}, bf16[512,2048]{1,0:T(8,128)(2,1)S(1)}, bf16[512,2048]{1,0:T(8,128)(2,1)S(1)}) custom-call(f32[512,1408]{1,0:T(8,128)S(1)} %copy-done.30, bf16[512,704]{1,0:T(8,128)(2,1)S(1)} %copy-done.26, bf16[512,2048]{1,0:T(8,128)(2,1)} %collective-permute-done.28.refs_3_.dy, bf16[2048,1408]{1,0:T(8,128)(2,1)S(1)} %copy-done.2, ...), custom_call_target="tpu_custom_call" | custom-call | flops 1024 | bytes 1024 | tf_op jit(solution)/shard_map/pallas_call | solution.py:429
  270.1 8.5 %shard_map.223 = (bf16[512,1408]{1,0:T(8,128)(2,1)S(1)}, bf16[512,2048]{1,0:T(8,128)(2,1)S(1)}, bf16[512,2048]{1,0:T(8,128)(2,1)S(1)}) custom-call(f32[512,1408]{1,0:T(8,128)S(1)} %copy-done.28, bf16[512,704]{1,0:T(8,128)(2,1)S(1)} %copy-done.24, bf16[512,2048]{1,0:T(8,128)(2,1)S(1)} %pad_maximum_fusion.1.refs_2_.dy, bf16[2048,1408]{1,0:T(8,128)(2,1)S(1)} %copy-done.2, ...), custom_call_target="tpu_custom_call" | custom-call | flops 1024 | bytes 1024 | tf_op jit(solution)/shard_map/pallas_call | solution.py:429
  287.0 9.4 %shard_map.226 = bf16[2048,1408]{1,0:T(8,128)(2,1)S(1)} custom-call(bf16[512,2048]{1,0:T(8,128)(2,1)} %constant_dynamic-update-slice_fusion.x.refs_0_, bf16[512,2048]{1,0:T(8,128)(2,1)} %collective-permute-done.27.x.refs_1_, bf16[512,1408]{1,0:T(8,128)(2,1)S(1)} %get-tuple-element.190.refs_2_, bf16[512,1408]{1,0:T(8,128)(2,1)S(1)} %get-tuple-element.176.refs_3_), custom_call_target="tpu_custom_call" | custom-call | flops 1024 | bytes 1024 | tf_op jit(solution)/shard_map/pallas_call | solution.py:80
  296.4 2.4 copy-done.3
  304.2 4.5 collective-permute-done.32.refs_1_
  308.7 3.5 reduce-scatter.3.cloned.1.call-done
  314.8 2.2 shard_map.227
  321.7 11.2 %collective-permute-done.34 = bf16[128,2048]{1,0:T(8,128)(2,1)S(1)} collective-permute-done((bf16[128,2048]{1,0:T(8,128)(2,1)S(1)}, bf16[128,2048]{1,0:T(8,128)(2,1)S(1)}, u32[]{:S(2)}, u32[]{:S(2)}) %collective-permute-start.34) | collective-permute-done | bytes 524320 | tf_op jit(solution)/shard_map/ppermute | solution.py:34
  332.9 11.6 %collective-permute-done.35 = bf16[128,2048]{1,0:T(8,128)(2,1)S(1)} collective-permute-done((bf16[128,2048]{1,0:T(8,128)(2,1)S(1)}, bf16[128,2048]{1,0:T(8,128)(2,1)S(1)}, u32[]{:S(2)}, u32[]{:S(2)}) %collective-permute-start.35) | collective-permute-done | bytes 524320 | tf_op jit(solution)/shard_map/ppermute | solution.py:34
  349.0 17.0 %shard_map.228 = (bf16[1024,256]{1,0:T(8,128)(2,1)S(1)}, f32[8,4,64,128]{3,2,1,0:T(8,128)S(1)}, bf16[8,4,64,128]{3,2,1,0:T(8,128)(2,1)S(1)}) custom-call(s32[2]{0:T(128)S(1)} %copy-done.76, bf16[512,2048]{1,0:T(8,128)(2,1)S(1)} %constant_dynamic-update-slice_fusion.4.s.ba, bf16[512,2048]{1,0:T(8,128)(2,1)S(1)} %collective-permute-done.37.o.bb, ...), custom_call_target="tpu_custom_call" | custom-call | flops 1024 | bytes 1024 | tf_op jit(solution)/shard_map/pallas_call | solution.py:269
  366.0 3.6 collective-permute-done.39
  373.3 2.0 collective-permute-start.42
  376.4 6.2 %collective-permute-done.42.refs_0_ = bf16[8,64,128]{2,1,0:T(8,128)(2,1)S(1)} collective-permute-done((bf16[8,64,128]{2,1,0:T(8,128)(2,1)S(1)}, bf16[8,64,128]{2,1,0:T(8,128)(2,1)S(1)}, u32[]{:S(2)}, u32[]{:S(2)}) %collective-permute-start.42) | collective-permute-done | bytes 131104 | tf_op jit(solution)/shard_map/ppermute | solution.py:38
  382.6 19.6 %collective-permute-done.43.refs_1_ = bf16[8,64,128]{2,1,0:T(8,128)(2,1)S(1)} collective-permute-done((bf16[8,64,128]{2,1,0:T(8,128)(2,1)S(1)}, bf16[8,64,128]{2,1,0:T(8,128)(2,1)S(1)}, u32[]{:S(2)}, u32[]{:S(2)}) %collective-permute-start.43) | collective-permute-done | bytes 131104 | tf_op jit(solution)/shard_map/ppermute | solution.py:38
  403.7 4.8 shard_map.231
  410.0 4.1 collective-permute-done.45.c
  414.1 2.1 shard_map.232
  418.6 7.0 %reduce-scatter.5.cloned.1.call-done = bf16[512,1408]{1,0:T(8,128)(2,1)} async-done(((bf16[2048,1408]{1,0:T(8,128)(2,1)}), bf16[512,1408]{1,0:T(8,128)(2,1)}) %reduce-scatter.5.cloned.1.call-update) | async-done | bytes 1441808 | tf_op jit(solution)/shard_map/reduce_scatter | solution.py:790
  425.6 3.9 all-to-all-start.2
  430.7 3.4 collective-permute-start.50
  435.7 2.1 collective-permute-start.46
  439.3 7.4 %collective-permute-done.49.refs_0_ = bf16[256,1152]{1,0:T(8,128)(2,1)} collective-permute-done((bf16[256,1152]{1,0:T(8,128)(2,1)}, bf16[256,1152]{1,0:T(8,128)(2,1)}, u32[]{:S(2)}, u32[]{:S(2)}) %collective-permute-start.49) | collective-permute-done | bytes 589856 | tf_op jit(solution)/shard_map/ppermute | solution.py:38
  446.7 2.6 collective-permute-start.48
  449.3 3.2 fusion.8
  452.4 33.4 %collective-permute-done.50.refs_1_ = bf16[256,1152]{1,0:T(8,128)(2,1)} collective-permute-done((bf16[256,1152]{1,0:T(8,128)(2,1)}, bf16[256,1152]{1,0:T(8,128)(2,1)}, u32[]{:S(2)}, u32[]{:S(2)}) %collective-permute-start.50) | collective-permute-done | bytes 589856 | tf_op jit(solution)/shard_map/ppermute | solution.py:38
  487.4 1.9 fusion.2
  489.3 2.6 shard_map.233
  492.7 3.8 all-to-all-start.3
  496.5 3.2 fusion.6
  501.0 3.8 all-to-all-done.3.x
  505.8 2.3 shard_map.234
  (342 shorter events, 90.9 us)
Async XLA Ops:
  7.2 69.8 %copy-start.31 = (bf16[64,5632]{1,0:T(8,128)(2,1)S(1)}, bf16[64,5632]{1,0:T(8,128)(2,1)}, u32[]{:S(2)}) copy-start(bf16[64,5632]{1,0:T(8,128)(2,1)} %g.2) | copy-start | bytes 2162692
  7.2 69.8 %copy-start.33 = (bf16[64,5632]{1,0:T(8,128)(2,1)S(1)}, bf16[64,5632]{1,0:T(8,128)(2,1)}, u32[]{:S(2)}) copy-start(bf16[64,5632]{1,0:T(8,128)(2,1)} %u.2) | copy-start | bytes 2162692
  7.2 102.5 %all-gather.3.cloned.1.call-start = ((), (), s32[]{:S(2)}) async-start(), calls=%async_computation.6 | async-start | bytes 3604480 | tf_op jit(solution)/shard_map/all_gather | solution.py:726
  7.9 12.5 %collective-permute-start = (bf16[64,2048]{1,0:T(8,128)(2,1)}, bf16[64,2048]{1,0:T(8,128)(2,1)S(1)}, u32[]{:S(2)}, u32[]{:S(2)}) collective-permute-start(bf16[64,2048]{1,0:T(8,128)(2,1)} %refs_0_.1), channel_id=1, source_target_pairs={{0,3},{1,0},{2,1},{3,2},{4,7},{5,4},{6,5},{7,6},{8,11},{9,8},{10,9... | collective-permute-start | bytes 786440 | tf_op jit(solution)/shard_map/ppermute | solution.py:38
  8.4 32.4 %collective-permute-start.1 = (bf16[64,2048]{1,0:T(8,128)(2,1)}, bf16[64,2048]{1,0:T(8,128)(2,1)S(1)}, u32[]{:S(2)}, u32[]{:S(2)}) collective-permute-start(bf16[64,2048]{1,0:T(8,128)(2,1)} %refs_0_.1), channel_id=1, source_target_pairs={{0,2},{1,3},{2,0},{3,1},{4,6},{5,7},{6,4},{7,5},{8,10},{9,11},{10,... | collective-permute-start | bytes 786440 | tf_op jit(solution)/shard_map/ppermute | solution.py:38
  8.5 40.8 %collective-permute-start.3 = (bf16[128,2048]{1,0:T(8,128)(2,1)}, bf16[128,2048]{1,0:T(8,128)(2,1)S(1)}, u32[]{:S(2)}, u32[]{:S(2)}) collective-permute-start(bf16[128,2048]{1,0:T(8,128)(2,1)} %bitcast.38), channel_id=1, source_target_pairs={{0,8},{4,12},{8,0},{12,4},{16,24},{20,28},{24,16},{28,20},{1,9},{5... | collective-permute-start | bytes 1572872 | tf_op jit(solution)/shard_map/ppermute | solution.py:34
  10.3 38.9 %collective-permute-start.4 = (bf16[128,2048]{1,0:T(8,128)(2,1)}, bf16[128,2048]{1,0:T(8,128)(2,1)}, u32[]{:S(2)}, u32[]{:S(2)}) collective-permute-start(bf16[128,2048]{1,0:T(8,128)(2,1)} %bitcast.39), channel_id=1, source_target_pairs={{0,16},{4,20},{8,24},{12,28},{16,0},{20,4},{24,8},{28,12},{1,17},{... | collective-permute-start | bytes 1572872 | tf_op jit(solution)/shard_map/ppermute | solution.py:34
  11.8 37.4 %collective-permute-start.5 = (bf16[128,2048]{1,0:T(8,128)(2,1)}, bf16[128,2048]{1,0:T(8,128)(2,1)}, u32[]{:S(2)}, u32[]{:S(2)}) collective-permute-start(bf16[128,2048]{1,0:T(8,128)(2,1)} %bitcast.40), channel_id=1, source_target_pairs={{0,24},{4,28},{8,16},{12,20},{16,8},{20,12},{24,0},{28,4},{1,25},{... | collective-permute-start | bytes 1572872 | tf_op jit(solution)/shard_map/ppermute | solution.py:34
  16.4 32.8 %all-to-all-start = ((bf16[8,64,384]{2,1,0:T(8,128)(2,1)}), bf16[8,64,384]{2,1,0:T(8,128)(2,1)S(1)}, u32[]{:S(2)}, u32[]{:S(2)}) async-start(bf16[8,64,384]{2,1,0:T(8,128)(2,1)} %bitcast.31), calls=%async_computation | async-start | bytes 786432 | tf_op jit(solution)/shard_map/all_to_all | solution.py:724
  21.2 27.3 %collective-permute-start.2 = (bf16[64,2048]{1,0:T(8,128)(2,1)S(1)}, bf16[64,2048]{1,0:T(8,128)(2,1)S(1)}, u32[]{:S(2)}, u32[]{:S(2)}) collective-permute-start(bf16[64,2048]{1,0:T(8,128)(2,1)S(1)} %copy-done.62), channel_id=1, source_target_pairs={{0,1},{1,2},{2,3},{3,0},{4,5},{5,6},{6,7},{7,4},{8,9},{9,10},{10,1... | collective-permute-start | bytes 786440 | tf_op jit(solution)/shard_map/ppermute | solution.py:38
  49.2 40.6 %collective-permute-start.7 = (bf16[8,64,384]{2,1,0:T(8,128)(2,1)S(1)}, bf16[8,64,384]{2,1,0:T(8,128)(2,1)S(1)}, u32[]{:S(2)}, u32[]{:S(2)}) collective-permute-start(bf16[8,64,384]{2,1,0:T(8,128)(2,1)S(1)} %all-to-all-done.refs_0_), channel_id=1, source_target_pairs={{0,3},{1,0},{2,1},{3,2},{4,7},{5,4},{6,5},{7,6},{8,11},{9,8},{10,9... | collective-permute-start | bytes 1179656 | tf_op jit(solution)/shard_map/ppermute | solution.py:38
  74.0 31.0 %collective-permute-start.8 = (bf16[8,64,384]{2,1,0:T(8,128)(2,1)S(1)}, bf16[8,64,384]{2,1,0:T(8,128)(2,1)S(1)}, u32[]{:S(2)}, u32[]{:S(2)}) collective-permute-start(bf16[8,64,384]{2,1,0:T(8,128)(2,1)S(1)} %all-to-all-done.refs_0_), channel_id=1, source_target_pairs={{0,2},{1,3},{2,0},{3,1},{4,6},{5,7},{6,4},{7,5},{8,10},{9,11},{10,... | collective-permute-start | bytes 1179656 | tf_op jit(solution)/shard_map/ppermute | solution.py:38
  74.0 31.0 %collective-permute-start.9 = (bf16[8,64,384]{2,1,0:T(8,128)(2,1)S(1)}, bf16[8,64,384]{2,1,0:T(8,128)(2,1)S(1)}, u32[]{:S(2)}, u32[]{:S(2)}) collective-permute-start(bf16[8,64,384]{2,1,0:T(8,128)(2,1)S(1)} %all-to-all-done.refs_0_), channel_id=1, source_target_pairs={{0,1},{1,2},{2,3},{3,0},{4,5},{5,6},{6,7},{7,4},{8,9},{9,10},{10,1... | collective-permute-start | bytes 1179656 | tf_op jit(solution)/shard_map/ppermute | solution.py:38
  78.4 26.5 %all-to-all-start.1 = ((bf16[8,64,1408]{2,1,0:T(8,128)(2,1)}), bf16[8,64,1408]{2,1,0:T(8,128)(2,1)}, u32[]{:S(2)}, u32[]{:S(2)}) async-start(bf16[8,64,1408]{2,1,0:T(8,128)(2,1)} %shard_map.212), calls=%async_computation.1 | async-start | bytes 2883584 | tf_op jit(solution)/shard_map/all_to_all | solution.py:743
  82.8 146.5 %all-gather.5.cloned.1.call-start = ((), (), s32[]{:S(2)}) async-start(), calls=%async_computation.7 | async-start | bytes 7208960 | tf_op jit(solution)/shard_map/all_gather | solution.py:749
  85.8 25.2 %collective-permute-start.6 = (bf16[512,2048]{1,0:T(8,128)(2,1)}, bf16[512,2048]{1,0:T(8,128)(2,1)}, u32[]{:S(2)}, u32[]{:S(2)}) collective-permute-start(bf16[512,2048]{1,0:T(8,128)(2,1)} %pad_maximum_fusion.e), channel_id=1, source_target_pairs={{0,4},{4,0},{8,12},{12,8},{16,20},{20,16},{24,28},{28,24},{1,5},{5... | collective-permute-start | bytes 6291464 | tf_op jit(solution)/shard_map/ppermute | solution.py:34
  109.8 202.4 %reduce-scatter.3.cloned.1.call-start = ((), (), s32[]{:S(2)}) async-start(), calls=%async_computation.8 | async-start | bytes 3604480 | tf_op jit(solution)/shard_map/reduce_scatter | solution.py:779
  119.7 45.2 %copy-start.39 = (bf16[1024,256]{1,0:T(8,128)(2,1)}, bf16[1024,256]{1,0:T(8,128)(2,1)S(1)}, u32[]{:S(2)}) copy-start(bf16[1024,256]{1,0:T(8,128)(2,1)S(1)} %get-tuple-element.143.q) | copy-start | bytes 1572868
  119.7 28.3 %collective-permute-start.13 = (bf16[128,2048]{1,0:T(8,128)(2,1)S(1)}, bf16[128,2048]{1,0:T(8,128)(2,1)S(1)}, u32[]{:S(2)}, u32[]{:S(2)}) collective-permute-start(bf16[128,2048]{1,0:T(8,128)(2,1)S(1)} %bitcast.43), channel_id=1, source_target_pairs={{0,8},{4,12},{8,0},{12,4},{16,24},{20,28},{24,16},{28,20},{1,9},{5... | collective-permute-start | bytes 1572872 | tf_op jit(solution)/shard_map/ppermute | solution.py:34
  121.2 26.8 %collective-permute-start.14 = (bf16[128,2048]{1,0:T(8,128)(2,1)S(1)}, bf16[128,2048]{1,0:T(8,128)(2,1)S(1)}, u32[]{:S(2)}, u32[]{:S(2)}) collective-permute-start(bf16[128,2048]{1,0:T(8,128)(2,1)S(1)} %bitcast.44), channel_id=1, source_target_pairs={{0,16},{4,20},{8,24},{12,28},{16,0},{20,4},{24,8},{28,12},{1,17},{... | collective-permute-start | bytes 1572872 | tf_op jit(solution)/shard_map/ppermute | solution.py:34
  122.7 25.3 %collective-permute-start.15 = (bf16[128,2048]{1,0:T(8,128)(2,1)S(1)}, bf16[128,2048]{1,0:T(8,128)(2,1)}, u32[]{:S(2)}, u32[]{:S(2)}) collective-permute-start(bf16[128,2048]{1,0:T(8,128)(2,1)S(1)} %bitcast.45), channel_id=1, source_target_pairs={{0,24},{4,28},{8,16},{12,20},{16,8},{20,12},{24,0},{28,4},{1,25},{... | collective-permute-start | bytes 1572872 | tf_op jit(solution)/shard_map/ppermute | solution.py:34
  123.2 12.1 %collective-permute-start.10 = (bf16[8,64,128]{2,1,0:T(8,128)(2,1)S(1)}, bf16[8,64,128]{2,1,0:T(8,128)(2,1)S(1)}, u32[]{:S(2)}, u32[]{:S(2)}) collective-permute-start(bf16[8,64,128]{2,1,0:T(8,128)(2,1)S(1)} %get-tuple-element.144.refs_0_), channel_id=1, source_target_pairs={{0,3},{1,0},{2,1},{3,2},{4,7},{5,4},{6,5},{7,6},{8,11},{9,8},{10,9... | collective-permute-start | bytes 393224 | tf_op jit(solution)/shard_map/ppermute | solution.py:38
  128.3 17.1 %collective-permute-start.11 = (bf16[8,64,128]{2,1,0:T(8,128)(2,1)S(1)}, bf16[8,64,128]{2,1,0:T(8,128)(2,1)S(1)}, u32[]{:S(2)}, u32[]{:S(2)}) collective-permute-start(bf16[8,64,128]{2,1,0:T(8,128)(2,1)S(1)} %get-tuple-element.144.refs_0_), channel_id=1, source_target_pairs={{0,2},{1,3},{2,0},{3,1},{4,6},{5,7},{6,4},{7,5},{8,10},{9,11},{10,... | collective-permute-start | bytes 393224 | tf_op jit(solution)/shard_map/ppermute | solution.py:38
  135.3 12.7 %collective-permute-start.12 = (bf16[8,64,128]{2,1,0:T(8,128)(2,1)S(1)}, bf16[8,64,128]{2,1,0:T(8,128)(2,1)S(1)}, u32[]{:S(2)}, u32[]{:S(2)}) collective-permute-start(bf16[8,64,128]{2,1,0:T(8,128)(2,1)S(1)} %get-tuple-element.144.refs_0_), channel_id=1, source_target_pairs={{0,1},{1,2},{2,3},{3,0},{4,5},{5,6},{6,7},{7,4},{8,9},{9,10},{10,1... | collective-permute-start | bytes 393224 | tf_op jit(solution)/shard_map/ppermute | solution.py:38
  145.3 9.1 %collective-permute-start.16 = (bf16[8,64,128]{2,1,0:T(8,128)(2,1)S(1)}, bf16[8,64,128]{2,1,0:T(8,128)(2,1)S(1)}, u32[]{:S(2)}, u32[]{:S(2)}) collective-permute-start(bf16[8,64,128]{2,1,0:T(8,128)(2,1)S(1)} %get-tuple-element.144.refs_0_), channel_id=1, source_target_pairs={{0,4},{4,0},{8,12},{12,8},{16,20},{20,16},{24,28},{28,24},{1,5},{5... | collective-permute-start | bytes 393224 | tf_op jit(solution)/shard_map/ppermute | solution.py:34
  148.0 6.4 %collective-permute-start.17 = (bf16[8,64,128]{2,1,0:T(8,128)(2,1)S(1)}, bf16[8,64,128]{2,1,0:T(8,128)(2,1)S(1)}, u32[]{:S(2)}, u32[]{:S(2)}) collective-permute-start(bf16[8,64,128]{2,1,0:T(8,128)(2,1)S(1)} %collective-permute-done.10.refs_1_), channel_id=1, source_target_pairs={{0,4},{4,0},{8,12},{12,8},{16,20},{20,16},{24,28},{28,24},{1,5},{5... | collective-permute-start | bytes 393224 | tf_op jit(solution)/shard_map/ppermute | solution.py:34
  148.1 6.4 %collective-permute-start.18 = (bf16[8,64,128]{2,1,0:T(8,128)(2,1)S(1)}, bf16[8,64,128]{2,1,0:T(8,128)(2,1)S(1)}, u32[]{:S(2)}, u32[]{:S(2)}) collective-permute-start(bf16[8,64,128]{2,1,0:T(8,128)(2,1)S(1)} %collective-permute-done.11.refs_2_), channel_id=1, source_target_pairs={{0,4},{4,0},{8,12},{12,8},{16,20},{20,16},{24,28},{28,24},{1,5},{5... | collective-permute-start | bytes 393224 | tf_op jit(solution)/shard_map/ppermute | solution.py:34
  148.6 5.9 %collective-permute-start.19 = (bf16[8,64,128]{2,1,0:T(8,128)(2,1)S(1)}, bf16[8,64,128]{2,1,0:T(8,128)(2,1)}, u32[]{:S(2)}, u32[]{:S(2)}) collective-permute-start(bf16[8,64,128]{2,1,0:T(8,128)(2,1)S(1)} %collective-permute-done.12.refs_3_), channel_id=1, source_target_pairs={{0,4},{4,0},{8,12},{12,8},{16,20},{20,16},{24,28},{28,24},{1,5},{5... | collective-permute-start | bytes 393224 | tf_op jit(solution)/shard_map/ppermute | solution.py:34
  165.7 4.2 collective-permute-start.20
  170.7 14.8 %collective-permute-start.21 = (bf16[128,2048]{1,0:T(8,128)(2,1)S(1)}, bf16[128,2048]{1,0:T(8,128)(2,1)S(1)}, u32[]{:S(2)}, u32[]{:S(2)}) collective-permute-start(bf16[128,2048]{1,0:T(8,128)(2,1)S(1)} %get-tuple-element.154), channel_id=1, source_target_pairs={{0,8},{4,12},{8,0},{12,4},{16,24},{20,28},{24,16},{28,20},{1,9},{5... | collective-permute-start | bytes 1572872 | tf_op jit(solution)/shard_map/ppermute | solution.py:34
  172.1 24.9 %collective-permute-start.22 = (bf16[128,2048]{1,0:T(8,128)(2,1)S(1)}, bf16[128,2048]{1,0:T(8,128)(2,1)S(1)}, u32[]{:S(2)}, u32[]{:S(2)}) collective-permute-start(bf16[128,2048]{1,0:T(8,128)(2,1)S(1)} %get-tuple-element.155), channel_id=1, source_target_pairs={{0,16},{4,20},{8,24},{12,28},{16,0},{20,4},{24,8},{28,12},{1,17},{... | collective-permute-start | bytes 1572872 | tf_op jit(solution)/shard_map/ppermute | solution.py:34
  173.7 23.4 %collective-permute-start.23 = (bf16[128,2048]{1,0:T(8,128)(2,1)S(1)}, bf16[128,2048]{1,0:T(8,128)(2,1)S(1)}, u32[]{:S(2)}, u32[]{:S(2)}) collective-permute-start(bf16[128,2048]{1,0:T(8,128)(2,1)S(1)} %get-tuple-element.156), channel_id=1, source_target_pairs={{0,24},{4,28},{8,16},{12,20},{16,8},{20,12},{24,0},{28,4},{1,25},{... | collective-permute-start | bytes 1572872 | tf_op jit(solution)/shard_map/ppermute | solution.py:34
  197.7 14.9 %collective-permute-start.24 = (bf16[128,2048]{1,0:T(8,128)(2,1)S(1)}, bf16[128,2048]{1,0:T(8,128)(2,1)S(1)}, u32[]{:S(2)}, u32[]{:S(2)}) collective-permute-start(bf16[128,2048]{1,0:T(8,128)(2,1)S(1)} %get-tuple-element.161), channel_id=1, source_target_pairs={{0,8},{4,12},{8,0},{12,4},{16,24},{20,28},{24,16},{28,20},{1,9},{5... | collective-permute-start | bytes 1572872 | tf_op jit(solution)/shard_map/ppermute | solution.py:34
  199.0 24.2 %collective-permute-start.25 = (bf16[128,2048]{1,0:T(8,128)(2,1)S(1)}, bf16[128,2048]{1,0:T(8,128)(2,1)S(1)}, u32[]{:S(2)}, u32[]{:S(2)}) collective-permute-start(bf16[128,2048]{1,0:T(8,128)(2,1)S(1)} %get-tuple-element.161), channel_id=1, source_target_pairs={{0,16},{4,20},{8,24},{12,28},{16,0},{20,4},{24,8},{28,12},{1,17},{... | collective-permute-start | bytes 1572872 | tf_op jit(solution)/shard_map/ppermute | solution.py:34
  199.8 23.4 %collective-permute-start.26 = (bf16[128,2048]{1,0:T(8,128)(2,1)S(1)}, bf16[128,2048]{1,0:T(8,128)(2,1)S(1)}, u32[]{:S(2)}, u32[]{:S(2)}) collective-permute-start(bf16[128,2048]{1,0:T(8,128)(2,1)S(1)} %get-tuple-element.161), channel_id=1, source_target_pairs={{0,24},{4,28},{8,16},{12,20},{16,8},{20,12},{24,0},{28,4},{1,25},{... | collective-permute-start | bytes 1572872 | tf_op jit(solution)/shard_map/ppermute | solution.py:34
  225.8 11.5 %collective-permute-start.27 = (bf16[512,2048]{1,0:T(8,128)(2,1)}, bf16[512,2048]{1,0:T(8,128)(2,1)}, u32[]{:S(2)}, u32[]{:S(2)}) collective-permute-start(bf16[512,2048]{1,0:T(8,128)(2,1)} %constant_dynamic-update-slice_fusion.x.refs_0_), channel_id=1, source_target_pairs={{0,4},{4,0},{8,12},{12,8},{16,20},{20,16},{24,28},{28,24},{1,5},{5... | collective-permute-start | bytes 6291464 | tf_op jit(solution)/shard_map/ppermute | solution.py:34
  227.0 17.8 %collective-permute-start.28 = (bf16[512,2048]{1,0:T(8,128)(2,1)S(1)}, bf16[512,2048]{1,0:T(8,128)(2,1)}, u32[]{:S(2)}, u32[]{:S(2)}) collective-permute-start(bf16[512,2048]{1,0:T(8,128)(2,1)S(1)} %pad_maximum_fusion.1.refs_2_.dy), channel_id=1, source_target_pairs={{0,4},{4,0},{8,12},{12,8},{16,20},{20,16},{24,28},{28,24},{1,5},{5... | collective-permute-start | bytes 6291464 | tf_op jit(solution)/shard_map/ppermute | solution.py:34
  252.5 173.1 %reduce-scatter.5.cloned.1.call-start = ((), (), s32[]{:S(2)}) async-start(), calls=%async_computation.9 | async-start | bytes 7208960 | tf_op jit(solution)/shard_map/reduce_scatter | solution.py:790
  270.0 8.6 %collective-permute-start.29 = (bf16[512,2048]{1,0:T(8,128)(2,1)S(1)}, bf16[512,2048]{1,0:T(8,128)(2,1)S(1)}, u32[]{:S(2)}, u32[]{:S(2)}) collective-permute-start(bf16[512,2048]{1,0:T(8,128)(2,1)S(1)} %get-tuple-element.181), channel_id=1, source_target_pairs={{0,4},{4,0},{8,12},{12,8},{16,20},{20,16},{24,28},{28,24},{1,5},{5... | collective-permute-start | bytes 6291464 | tf_op jit(solution)/shard_map/ppermute | solution.py:34
  281.4 4.2 collective-permute-start.30
  281.9 22.4 %collective-permute-start.31 = (bf16[128,2048]{1,0:T(8,128)(2,1)}, bf16[128,2048]{1,0:T(8,128)(2,1)}, u32[]{:S(2)}, u32[]{:S(2)}) collective-permute-start(bf16[128,2048]{1,0:T(8,128)(2,1)} %get-tuple-element.182), channel_id=1, source_target_pairs={{0,8},{4,12},{8,0},{12,4},{16,24},{20,28},{24,16},{28,20},{1,9},{5... | collective-permute-start | bytes 1572872 | tf_op jit(solution)/shard_map/ppermute | solution.py:34
  283.6 25.2 %collective-permute-start.32 = (bf16[128,2048]{1,0:T(8,128)(2,1)}, bf16[128,2048]{1,0:T(8,128)(2,1)}, u32[]{:S(2)}, u32[]{:S(2)}) collective-permute-start(bf16[128,2048]{1,0:T(8,128)(2,1)} %get-tuple-element.183), channel_id=1, source_target_pairs={{0,16},{4,20},{8,24},{12,28},{16,0},{20,4},{24,8},{28,12},{1,17},{... | collective-permute-start | bytes 1572872 | tf_op jit(solution)/shard_map/ppermute | solution.py:34
  285.0 23.7 %collective-permute-start.33 = (bf16[128,2048]{1,0:T(8,128)(2,1)}, bf16[128,2048]{1,0:T(8,128)(2,1)}, u32[]{:S(2)}, u32[]{:S(2)}) collective-permute-start(bf16[128,2048]{1,0:T(8,128)(2,1)} %get-tuple-element.184), channel_id=1, source_target_pairs={{0,24},{4,28},{8,16},{12,20},{16,8},{20,12},{24,0},{28,4},{1,25},{... | collective-permute-start | bytes 1572872 | tf_op jit(solution)/shard_map/ppermute | solution.py:34
  318.1 14.8 %collective-permute-start.34 = (bf16[128,2048]{1,0:T(8,128)(2,1)S(1)}, bf16[128,2048]{1,0:T(8,128)(2,1)S(1)}, u32[]{:S(2)}, u32[]{:S(2)}) collective-permute-start(bf16[128,2048]{1,0:T(8,128)(2,1)S(1)} %get-tuple-element.198), channel_id=1, source_target_pairs={{0,8},{4,12},{8,0},{12,4},{16,24},{20,28},{24,16},{28,20},{1,9},{5... | collective-permute-start | bytes 1572872 | tf_op jit(solution)/shard_map/ppermute | solution.py:34
  319.8 24.7 %collective-permute-start.35 = (bf16[128,2048]{1,0:T(8,128)(2,1)S(1)}, bf16[128,2048]{1,0:T(8,128)(2,1)S(1)}, u32[]{:S(2)}, u32[]{:S(2)}) collective-permute-start(bf16[128,2048]{1,0:T(8,128)(2,1)S(1)} %get-tuple-element.198), channel_id=1, source_target_pairs={{0,16},{4,20},{8,24},{12,28},{16,0},{20,4},{24,8},{28,12},{1,17},{... | collective-permute-start | bytes 1572872 | tf_op jit(solution)/shard_map/ppermute | solution.py:34
  321.3 23.2 %collective-permute-start.36 = (bf16[128,2048]{1,0:T(8,128)(2,1)S(1)}, bf16[128,2048]{1,0:T(8,128)(2,1)S(1)}, u32[]{:S(2)}, u32[]{:S(2)}) collective-permute-start(bf16[128,2048]{1,0:T(8,128)(2,1)S(1)} %get-tuple-element.198), channel_id=1, source_target_pairs={{0,24},{4,28},{8,16},{12,20},{16,8},{20,12},{24,0},{28,4},{1,25},{... | collective-permute-start | bytes 1572872 | tf_op jit(solution)/shard_map/ppermute | solution.py:34
  344.7 4.2 collective-permute-start.37
  344.8 21.3 %collective-permute-start.38 = (bf16[128,2048]{1,0:T(8,128)(2,1)S(1)}, bf16[128,2048]{1,0:T(8,128)(2,1)S(1)}, u32[]{:S(2)}, u32[]{:S(2)}) collective-permute-start(bf16[128,2048]{1,0:T(8,128)(2,1)S(1)} %copy-done.85), channel_id=1, source_target_pairs={{0,8},{4,12},{8,0},{12,4},{16,24},{20,28},{24,16},{28,20},{1,9},{5... | collective-permute-start | bytes 1572872 | tf_op jit(solution)/shard_map/ppermute | solution.py:34
  346.0 23.6 %collective-permute-start.39 = (bf16[128,2048]{1,0:T(8,128)(2,1)S(1)}, bf16[128,2048]{1,0:T(8,128)(2,1)S(1)}, u32[]{:S(2)}, u32[]{:S(2)}) collective-permute-start(bf16[128,2048]{1,0:T(8,128)(2,1)S(1)} %copy-done.83), channel_id=1, source_target_pairs={{0,16},{4,20},{8,24},{12,28},{16,0},{20,4},{24,8},{28,12},{1,17},{... | collective-permute-start | bytes 1572872 | tf_op jit(solution)/shard_map/ppermute | solution.py:34
  346.9 24.4 %collective-permute-start.40 = (bf16[128,2048]{1,0:T(8,128)(2,1)S(1)}, bf16[128,2048]{1,0:T(8,128)(2,1)S(1)}, u32[]{:S(2)}, u32[]{:S(2)}) collective-permute-start(bf16[128,2048]{1,0:T(8,128)(2,1)S(1)} %copy-done.81), channel_id=1, source_target_pairs={{0,24},{4,28},{8,16},{12,20},{16,8},{20,12},{24,0},{28,4},{1,25},{... | collective-permute-start | bytes 1572872 | tf_op jit(solution)/shard_map/ppermute | solution.py:34
  371.2 1.9 collective-permute-start.41
  373.3 9.4 %collective-permute-start.42 = (bf16[8,64,128]{2,1,0:T(8,128)(2,1)S(1)}, bf16[8,64,128]{2,1,0:T(8,128)(2,1)S(1)}, u32[]{:S(2)}, u32[]{:S(2)}) collective-permute-start(bf16[8,64,128]{2,1,0:T(8,128)(2,1)S(1)} %get-tuple-element.215), channel_id=1, source_target_pairs={{0,1},{1,2},{2,3},{3,0},{4,5},{5,6},{6,7},{7,4},{8,9},{9,10},{10,1... | collective-permute-start | bytes 393224 | tf_op jit(solution)/shard_map/ppermute | solution.py:38
  375.3 27.0 %collective-permute-start.43 = (bf16[8,64,128]{2,1,0:T(8,128)(2,1)S(1)}, bf16[8,64,128]{2,1,0:T(8,128)(2,1)S(1)}, u32[]{:S(2)}, u32[]{:S(2)}) collective-permute-start(bf16[8,64,128]{2,1,0:T(8,128)(2,1)S(1)} %get-tuple-element.216), channel_id=1, source_target_pairs={{0,2},{1,3},{2,0},{3,1},{4,6},{5,7},{6,4},{7,5},{8,10},{9,11},{10,... | collective-permute-start | bytes 393224 | tf_op jit(solution)/shard_map/ppermute | solution.py:38
  376.3 25.9 %collective-permute-start.44 = (bf16[8,64,128]{2,1,0:T(8,128)(2,1)S(1)}, bf16[8,64,128]{2,1,0:T(8,128)(2,1)S(1)}, u32[]{:S(2)}, u32[]{:S(2)}) collective-permute-start(bf16[8,64,128]{2,1,0:T(8,128)(2,1)S(1)} %get-tuple-element.217), channel_id=1, source_target_pairs={{0,3},{1,0},{2,1},{3,2},{4,7},{5,4},{6,5},{7,6},{8,11},{9,8},{10,9... | collective-permute-start | bytes 393224 | tf_op jit(solution)/shard_map/ppermute | solution.py:38
  409.9 4.2 collective-permute-start.45
  425.6 61.8 %all-to-all-start.2 = ((bf16[8,64,1408]{2,1,0:T(8,128)(2,1)}), bf16[8,64,1408]{2,1,0:T(8,128)(2,1)S(1)}, u32[]{:S(2)}, u32[]{:S(2)}) async-start(bf16[8,64,1408]{2,1,0:T(8,128)(2,1)} %bitcast.51), calls=%async_computation.4 | async-start | bytes 2883584 | tf_op jit(solution)/shard_map/all_to_all | solution.py:815
  429.5 17.2 %collective-permute-start.49 = (bf16[256,1152]{1,0:T(8,128)(2,1)}, bf16[256,1152]{1,0:T(8,128)(2,1)}, u32[]{:S(2)}, u32[]{:S(2)}) collective-permute-start(bf16[256,1152]{1,0:T(8,128)(2,1)} %copy-done.79), channel_id=1, source_target_pairs={{0,1},{1,2},{2,3},{3,0},{4,5},{5,6},{6,7},{7,4},{8,9},{9,10},{10,1... | collective-permute-start | bytes 1769480 | tf_op jit(solution)/shard_map/ppermute | solution.py:38
  430.7 55.1 %collective-permute-start.50 = (bf16[256,1152]{1,0:T(8,128)(2,1)}, bf16[256,1152]{1,0:T(8,128)(2,1)}, u32[]{:S(2)}, u32[]{:S(2)}) collective-permute-start(bf16[256,1152]{1,0:T(8,128)(2,1)} %copy-done.78), channel_id=1, source_target_pairs={{0,2},{1,3},{2,0},{3,1},{4,6},{5,7},{6,4},{7,5},{8,10},{9,11},{10,... | collective-permute-start | bytes 1769480 | tf_op jit(solution)/shard_map/ppermute | solution.py:38
  434.1 51.7 %collective-permute-start.51 = (bf16[256,1152]{1,0:T(8,128)(2,1)}, bf16[256,1152]{1,0:T(8,128)(2,1)}, u32[]{:S(2)}, u32[]{:S(2)}) collective-permute-start(bf16[256,1152]{1,0:T(8,128)(2,1)} %copy-done.77), channel_id=1, source_target_pairs={{0,3},{1,0},{2,1},{3,2},{4,7},{5,4},{6,5},{7,6},{8,11},{9,8},{10,9... | collective-permute-start | bytes 1769480 | tf_op jit(solution)/shard_map/ppermute | solution.py:38
  435.7 50.1 %collective-permute-start.46 = (bf16[128,2048]{1,0:T(8,128)(2,1)}, bf16[128,2048]{1,0:T(8,128)(2,1)S(1)}, u32[]{:S(2)}, u32[]{:S(2)}) collective-permute-start(bf16[128,2048]{1,0:T(8,128)(2,1)} %copy-done.88), channel_id=1, source_target_pairs={{0,8},{4,12},{8,0},{12,4},{16,24},{20,28},{24,16},{28,20},{1,9},{5... | collective-permute-start | bytes 1572872 | tf_op jit(solution)/shard_map/ppermute | solution.py:34
  437.8 48.0 %collective-permute-start.47 = (bf16[128,2048]{1,0:T(8,128)(2,1)}, bf16[128,2048]{1,0:T(8,128)(2,1)S(1)}, u32[]{:S(2)}, u32[]{:S(2)}) collective-permute-start(bf16[128,2048]{1,0:T(8,128)(2,1)} %copy-done.87), channel_id=1, source_target_pairs={{0,16},{4,20},{8,24},{12,28},{16,0},{20,4},{24,8},{28,12},{1,17},{... | collective-permute-start | bytes 1572872 | tf_op jit(solution)/shard_map/ppermute | solution.py:34
  446.7 40.7 %collective-permute-start.48 = (bf16[128,2048]{1,0:T(8,128)(2,1)}, bf16[128,2048]{1,0:T(8,128)(2,1)}, u32[]{:S(2)}, u32[]{:S(2)}) collective-permute-start(bf16[128,2048]{1,0:T(8,128)(2,1)} %copy-done.86), channel_id=1, source_target_pairs={{0,24},{4,28},{8,16},{12,20},{16,8},{20,12},{24,0},{28,4},{1,25},{... | collective-permute-start | bytes 1572872 | tf_op jit(solution)/shard_map/ppermute | solution.py:34
  449.3 38.1 %copy-start.71 = (f32[1,2048]{1,0:T(1,128)S(1)}, f32[1,2048]{1,0:T(1,128)}, u32[]{:S(2)}) copy-start(f32[1,2048]{1,0:T(1,128)} %copy-done.70) | copy-start | bytes 24580
  492.7 12.2 %all-to-all-start.3 = ((bf16[8,64,320]{2,1,0:T(8,128)(2,1)}), bf16[8,64,320]{2,1,0:T(8,128)(2,1)S(1)}, u32[]{:S(2)}, u32[]{:S(2)}) async-start(bf16[8,64,320]{2,1,0:T(8,128)(2,1)} %copy-done.59), calls=%async_computation.5 | async-start | bytes 786432 | tf_op jit(solution)/shard_map/all_to_all | solution.py:818
  (99 other events, 1041.6 us)
Sparse Core Ops, SparseCore 0:
  9.6 100.0 all-gather.2
  111.3 117.9 all-gather.4
  252.6 59.5 reduce-scatter.2
  314.3 111.2 reduce-scatter.4

commit v5 on v4

--- a/solution.py
+++ b/solution.py
@@ -621,6 +621,21 @@
         compiler_params=kernel_params(),
         cost_estimate=LIGHT,
     )(pairs, blocks, *weights, gains)
+
+
+def stack_rows(parts):
+    rows, columns = parts[0].shape
+
+    def body(*refs):
+        for j, ref in enumerate(refs[:-1]):
+            refs[-1][j * rows : (j + 1) * rows, :] = ref[...]
+
+    return pl.pallas_call(
+        body,
+        out_shape=jax.ShapeDtypeStruct((len(parts) * rows, columns), parts[0].dtype),
+        compiler_params=kernel_params(),
+        cost_estimate=LIGHT,
+    )(*parts)
 
 
 def scatter_dp(left, right, size, product):
@@ -743,15 +758,15 @@
     w_pair = lax.all_to_all(w_pair, every_dp, 0, 0).reshape(n * block, 2 * f_cols)
     even = jnp.concatenate([x16, *same])
     odd = swap(even, 1)
-    w_parts, cosine, sine, w_pair, wd = together(
-        shifts(w_attn, c), cosine, sine, w_pair, wd
+    wo = in_order([w_out, *wo_parts], place_z)
+    w_parts, cosine, sine, w_pair, wd, wo = together(
+        shifts(w_attn, c), cosine, sine, w_pair, wd, wo
     )
     w_pair = lax.all_gather(w_pair, "ctx", axis=0, tiled=True)
 
     w_attn, gains = attention_weights([w_attn, *w_parts], place_z, used)
     w_attn = w_attn.reshape(width, -1)
     gain1, gain2 = gains[:1], gains[1:]
-    wo = in_order([w_out, *wo_parts], place_z)
     where = jnp.stack([place_z, core]).astype(jnp.int32)
     key_seg = lax.dynamic_slice_in_dim(
         jnp.concatenate([segs, segs], axis=1), place_z * t, length, axis=1
@@ -770,7 +785,7 @@
     sent = together(*[swap(v, 2 * j) for j, v in enumerate(sends, 1)])
     resid, second_in = second_norm(x16, attn_own, sent, gain2, n, c)
 
-    second_in = jnp.concatenate([second_in, *together(*dp_same(second_in, n))])
+    second_in = stack_rows([second_in, *together(*dp_same(second_in, n))])
     second_in = second_in, swap(second_in, 1)
     units = hidden_units(second_in[0], w_pair)
     units = units, hidden_units(after(second_in[1], units), w_pair)
@@ -791,7 +806,7 @@
     grad_resid, branch = second_norm_back(resid, back, sent, gain2, dy_local, n, c)
 
     same = together(*dp_same(branch, n))
-    same = jnp.concatenate([branch, *same])
+    same = stack_rows([branch, *same])
     grad_branch = same, swap(same, 1)
     grad_q, kept, sent = attend_back(
         where, *grad_branch, wo, queries, kv_all, kv_other, *sides, cosine, sine

time: 523 us -> 519 us (level)
  local copies, waits for them, and re-layouts: 53 us -> 46.3 us
    unnamed x213 -> x203, local copies, waits for them, and re-layouts: 45.8 us -> 40 us
  transfers between devices with their start and end apart: 60 -> 60, of which waited for: 29 -> 28; matrix products, arithmetic and copies ran while one was open for 6% -> 6% of each run, Pallas kernels for 17% -> 18%
where the time goes in v5:
time: 519 us; the launch traced here: 512 us
  waiting for transfers between devices  225 us (43%)
  starting transfers between devices  100 us (19%)
  Pallas kernels  100 us (19%)
  local copies, waits for them, and re-layouts  46.3 us (9%)
  other arithmetic  22.5 us (4%)
  between operations  15.4 us (3%)
    ppermute x15, waiting for transfers between devices, shift(): lax.ppermute(value, 'ctx', [(i, (i - step) % size) for i in range(size)])  119 us
    ppermute x37, waiting for transfers between devices, swap(): lax.ppermute(value, ('plane', 'core'), [(i, i ^ rel) for i in range(size)])  85.2 us
    ppermute x15, starting transfers between devices, shift(): lax.ppermute(value, 'ctx', [(i, (i - step) % size) for i in range(size)])  50 us
    unnamed x203, local copies, waits for them, and re-layouts  40 us
    ppermute x37, starting transfers between devices, swap(): lax.ppermute(value, ('plane', 'core'), [(i, i ^ rel) for i in range(size)])  33.4 us
    pallas_call x2, Pallas kernels, feed_forward_back(): pl.pallas_call(body, grid=(tokens // tile,), in_specs=[rows(2 * ff), rows...  19.8 us
    pallas_call x1, Pallas kernels, attend_back(): pl.pallas_call(body, grid=(sequences,), in_specs=[pl.BlockSpec(memory_spa...  17 us
    pallas_call x2, Pallas kernels, transposed_dot(): pl.pallas_call(body, grid=(rows // row_tile if by_rows else columns // co...  14.8 us
  transfers between devices with their start and end apart: 60, of which 28 were waited for; matrix products, arithmetic and copies ran while one was open for 6% of the time, Pallas kernels for 18%

profile of v5, /device:TPU:24, one launch (start us, length us, event | category | flops | bytes accessed | tf_op | source)
XLA Modules:
  0.0 511.7 jit_solution(13742073950260110581)
XLA Ops:
  8.5 1.8 collective-permute-start.3
  16.4 4.1 all-to-all-start
  21.0 3.1 collective-permute-start.2
  25.8 15.1 %collective-permute-done.1.refs_2_ = bf16[64,2048]{1,0:T(8,128)(2,1)S(1)} collective-permute-done((bf16[64,2048]{1,0:T(8,128)(2,1)}, bf16[64,2048]{1,0:T(8,128)(2,1)S(1)}, u32[]{:S(2)}, u32[]{:S(2)}) %collective-permute-start.1) | collective-permute-done | bytes 262176 | tf_op jit(solution)/shard_map/ppermute | solution.py:38
  40.8 7.6 %collective-permute-done.2.refs_3_ = bf16[64,2048]{1,0:T(8,128)(2,1)S(1)} collective-permute-done((bf16[64,2048]{1,0:T(8,128)(2,1)S(1)}, bf16[64,2048]{1,0:T(8,128)(2,1)S(1)}, u32[]{:S(2)}, u32[]{:S(2)}) %collective-permute-start.2) | collective-permute-done | bytes 262176 | tf_op jit(solution)/shard_map/ppermute | solution.py:38
  49.2 24.8 %collective-permute-start.7 = (bf16[8,64,384]{2,1,0:T(8,128)(2,1)S(1)}, bf16[8,64,384]{2,1,0:T(8,128)(2,1)S(1)}, u32[]{:S(2)}, u32[]{:S(2)}) collective-permute-start(bf16[8,64,384]{2,1,0:T(8,128)(2,1)S(1)} %all-to-all-done.refs_0_), channel_id=1, source_target_pairs={{0,3},{1,0},{2,1},{3,2},{4,7},{5,4},{6,5},{7,6},{8,11},{9,8},{10,9... | collective-permute-start | bytes 1179656 | tf_op jit(solution)/shard_map/ppermute | solution.py:38
  74.0 2.4 collective-permute-start.9
  77.8 4.4 all-to-all-start.1
  82.3 2.8 pad_maximum_fusion.e
  86.5 1.9 fusion.11
  89.5 15.4 %collective-permute-done.8.refs_2_ = bf16[8,64,384]{2,1,0:T(8,128)(2,1)} collective-permute-done((bf16[8,64,384]{2,1,0:T(8,128)(2,1)S(1)}, bf16[8,64,384]{2,1,0:T(8,128)(2,1)}, u32[]{:S(2)}, u32[]{:S(2)}) %collective-permute-start.8) | collective-permute-done | bytes 393248 | tf_op jit(solution)/shard_map/ppermute | solution.py:38
  105.0 4.8 all-gather.3.cloned.1.call-done.wd
  112.1 6.7 %shard_map.215 = (bf16[1024,2048]{1,0:T(8,128)(2,1)S(1)}, bf16[1024,256]{1,0:T(8,128)(2,1)S(1)}, bf16[8,64,128]{2,1,0:T(8,128)(2,1)S(1)}) custom-call(s32[2]{0:T(128)S(1)} %pad_add_fusion.at, bf16[512,2048]{1,0:T(8,128)(2,1)} %pad_maximum_fusion.e, bf16[512,2048]{1,0:T(8,128)(2,1)} %collective-permute-done.6.o, f32[1,2048]{1,0:T(1,128)S(1)} %get-tuple-element.270.gn, ...), custom_call_target="tpu_custom_call" | custom-call | flops 1024 | bytes 1024 | tf_op jit(solution)/shard_map/pallas_call | solution.py:140
  118.8 2.0 copy-done.19
  124.3 5.2 %collective-permute-start.10 = (bf16[8,64,128]{2,1,0:T(8,128)(2,1)S(1)}, bf16[8,64,128]{2,1,0:T(8,128)(2,1)S(1)}, u32[]{:S(2)}, u32[]{:S(2)}) collective-permute-start(bf16[8,64,128]{2,1,0:T(8,128)(2,1)S(1)} %get-tuple-element.148.refs_0_), channel_id=1, source_target_pairs={{0,3},{1,0},{2,1},{3,2},{4,7},{5,4},{6,5},{7,6},{8,11},{9,8},{10,9... | collective-permute-start | bytes 393224 | tf_op jit(solution)/shard_map/ppermute | solution.py:38
  130.0 6.6 %collective-permute-done.10.refs_1_ = bf16[8,64,128]{2,1,0:T(8,128)(2,1)S(1)} collective-permute-done((bf16[8,64,128]{2,1,0:T(8,128)(2,1)S(1)}, bf16[8,64,128]{2,1,0:T(8,128)(2,1)S(1)}, u32[]{:S(2)}, u32[]{:S(2)}) %collective-permute-start.10) | collective-permute-done | bytes 131104 | tf_op jit(solution)/shard_map/ppermute | solution.py:38
  136.5 4.3 collective-permute-start.12
  140.9 5.6 %collective-permute-done.11.refs_2_ = bf16[8,64,128]{2,1,0:T(8,128)(2,1)S(1)} collective-permute-done((bf16[8,64,128]{2,1,0:T(8,128)(2,1)S(1)}, bf16[8,64,128]{2,1,0:T(8,128)(2,1)S(1)}, u32[]{:S(2)}, u32[]{:S(2)}) %collective-permute-start.11) | collective-permute-done | bytes 131104 | tf_op jit(solution)/shard_map/ppermute | solution.py:38
  146.5 2.4 collective-permute-done.12.refs_3_
  152.0 9.7 %shard_map.216.a.m = bf16[1024,256]{1,0:T(8,128)(2,1)S(1)} custom-call(s32[2]{0:T(128)S(1)} %copy-done.72, bf16[1024,256]{1,0:T(8,128)(2,1)S(1)} %get-tuple-element.147.q, f32[8,128,1]{2,1,0:T(8,128)S(1)} %copy.72.m, f32[8,1,512]{2,1,0:T(1,128)S(1)} %broadcast_in_dim.34.th, bf16[8,64,128]{2,1,0:T(8,128)(2,1)S(1)} %get-tuple-element.148.refs_0_, ...), custom_call_target="tpu_custom_call" | custom-call | flops 1024 | bytes 1024 | tf_op jit(solution)/shard_map/pallas_call | solution.py:219
  162.9 3.9 collective-permute-done.20.c
  171.0 11.3 %collective-permute-done.21.refs_0_ = bf16[128,2048]{1,0:T(8,128)(2,1)S(1)} collective-permute-done((bf16[128,2048]{1,0:T(8,128)(2,1)S(1)}, bf16[128,2048]{1,0:T(8,128)(2,1)S(1)}, u32[]{:S(2)}, u32[]{:S(2)}) %collective-permute-start.21) | collective-permute-done | bytes 524320 | tf_op jit(solution)/shard_map/ppermute | solution.py:34
  182.3 11.8 %collective-permute-done.22.refs_1_ = bf16[128,2048]{1,0:T(8,128)(2,1)S(1)} collective-permute-done((bf16[128,2048]{1,0:T(8,128)(2,1)S(1)}, bf16[128,2048]{1,0:T(8,128)(2,1)S(1)}, u32[]{:S(2)}, u32[]{:S(2)}) %collective-permute-start.22) | collective-permute-done | bytes 524320 | tf_op jit(solution)/shard_map/ppermute | solution.py:34
  199.2 11.4 %collective-permute-done.24.refs_1_ = bf16[128,2048]{1,0:T(8,128)(2,1)S(1)} collective-permute-done((bf16[128,2048]{1,0:T(8,128)(2,1)S(1)}, bf16[128,2048]{1,0:T(8,128)(2,1)S(1)}, u32[]{:S(2)}, u32[]{:S(2)}) %collective-permute-start.24) | collective-permute-done | bytes 524320 | tf_op jit(solution)/shard_map/ppermute | solution.py:34
  210.6 10.7 %collective-permute-done.25.refs_2_ = bf16[128,2048]{1,0:T(8,128)(2,1)S(1)} collective-permute-done((bf16[128,2048]{1,0:T(8,128)(2,1)S(1)}, bf16[128,2048]{1,0:T(8,128)(2,1)S(1)}, u32[]{:S(2)}, u32[]{:S(2)}) %collective-permute-start.25) | collective-permute-done | bytes 524320 | tf_op jit(solution)/shard_map/ppermute | solution.py:34
  221.5 2.9 pad_maximum_fusion.1.refs_2_.dy
  224.9 4.5 all-gather.5.cloned.1.call-done.w
  229.5 2.6 copy-done
  232.1 3.9 shard_map.220
  236.0 5.9 %shard_map.221 = (f32[512,1408]{1,0:T(8,128)S(1)}, bf16[512,704]{1,0:T(8,128)(2,1)S(1)}) custom-call(bf16[512,2048]{1,0:T(8,128)(2,1)} %collective-permute-done.27.x.refs_1_, bf16[2048,1408]{1,0:T(8,128)(2,1)S(1)} %copy-done.1), custom_call_target="tpu_custom_call" | custom-call | flops 1024 | bytes 1024 | tf_op jit(solution)/shard_map/pallas_call | solution.py:393
  243.5 5.4 %shard_map.222 = bf16[704,2048]{1,0:T(8,128)(2,1)S(1)} custom-call(bf16[512,704]{1,0:T(8,128)(2,1)S(1)} %get-tuple-element.169.refs_0_.h, bf16[512,704]{1,0:T(8,128)(2,1)S(1)} %get-tuple-element.175.refs_1_.h, bf16[512,2048]{1,0:T(8,128)(2,1)} %pad_maximum_fusion.1.refs_2_.dy, bf16[512,2048]{1,0:T(8,128)(2,1)} %collective-permute-done.28.refs_3_.dy), custom_call_target="tpu_custom_call" | custom-call | flops 1024 | bytes 1024 | tf_op jit(solution)/shard_map/pallas_call | solution.py:80
  251.7 2.6 copy-done.2
  254.4 1.8 copy-done.8
  257.3 1.8 copy-done.30
  259.1 10.1 %shard_map.223 = (bf16[512,1408]{1,0:T(8,128)(2,1)S(1)}, bf16[512,2048]{1,0:T(8,128)(2,1)S(1)}, bf16[512,2048]{1,0:T(8,128)(2,1)S(1)}) custom-call(f32[512,1408]{1,0:T(8,128)S(1)} %copy-done.30, bf16[512,704]{1,0:T(8,128)(2,1)S(1)} %copy-done.26, bf16[512,2048]{1,0:T(8,128)(2,1)} %collective-permute-done.28.refs_3_.dy, bf16[2048,1408]{1,0:T(8,128)(2,1)S(1)} %copy-done.2, ...), custom_call_target="tpu_custom_call" | custom-call | flops 1024 | bytes 1024 | tf_op jit(solution)/shard_map/pallas_call | solution.py:429
  269.3 9.7 %shard_map.224 = (bf16[512,1408]{1,0:T(8,128)(2,1)S(1)}, bf16[512,2048]{1,0:T(8,128)(2,1)S(1)}, bf16[512,2048]{1,0:T(8,128)(2,1)S(1)}) custom-call(f32[512,1408]{1,0:T(8,128)S(1)} %copy-done.28, bf16[512,704]{1,0:T(8,128)(2,1)S(1)} %copy-done.24, bf16[512,2048]{1,0:T(8,128)(2,1)} %pad_maximum_fusion.1.refs_2_.dy, bf16[2048,1408]{1,0:T(8,128)(2,1)S(1)} %copy-done.2, ...), custom_call_target="tpu_custom_call" | custom-call | flops 1024 | bytes 1024 | tf_op jit(solution)/shard_map/pallas_call | solution.py:429
  287.4 9.3 %shard_map.227 = bf16[2048,1408]{1,0:T(8,128)(2,1)S(1)} custom-call(bf16[512,2048]{1,0:T(8,128)(2,1)S(1)} %shard_map.219.x.refs_0_, bf16[512,2048]{1,0:T(8,128)(2,1)} %collective-permute-done.27.x.refs_1_, bf16[512,1408]{1,0:T(8,128)(2,1)S(1)} %get-tuple-element.192.refs_2_, bf16[512,1408]{1,0:T(8,128)(2,1)S(1)} %get-tuple-element.178.refs_3_), custom_call_target="tpu_custom_call" | custom-call | flops 1024 | bytes 1024 | tf_op jit(solution)/shard_map/pallas_call | solution.py:80
  296.8 2.4 copy-done.3
  306.2 2.9 collective-permute-done.32.refs_1_
  311.4 2.4 shard_map.228
  318.4 11.4 %collective-permute-done.34.refs_1_ = bf16[128,2048]{1,0:T(8,128)(2,1)S(1)} collective-permute-done((bf16[128,2048]{1,0:T(8,128)(2,1)S(1)}, bf16[128,2048]{1,0:T(8,128)(2,1)S(1)}, u32[]{:S(2)}, u32[]{:S(2)}) %collective-permute-start.34) | collective-permute-done | bytes 524320 | tf_op jit(solution)/shard_map/ppermute | solution.py:34
  329.7 10.5 %collective-permute-done.35.refs_2_ = bf16[128,2048]{1,0:T(8,128)(2,1)S(1)} collective-permute-done((bf16[128,2048]{1,0:T(8,128)(2,1)S(1)}, bf16[128,2048]{1,0:T(8,128)(2,1)S(1)}, u32[]{:S(2)}, u32[]{:S(2)}) %collective-permute-start.35) | collective-permute-done | bytes 524320 | tf_op jit(solution)/shard_map/ppermute | solution.py:34
  344.6 17.0 %shard_map.230 = (bf16[1024,256]{1,0:T(8,128)(2,1)S(1)}, f32[8,4,64,128]{3,2,1,0:T(8,128)S(1)}, bf16[8,4,64,128]{3,2,1,0:T(8,128)(2,1)S(1)}) custom-call(s32[2]{0:T(128)S(1)} %copy-done.73, bf16[512,2048]{1,0:T(8,128)(2,1)S(1)} %shard_map.229.s.ba, bf16[512,2048]{1,0:T(8,128)(2,1)S(1)} %collective-permute-done.37.o.bb, bf16[256,2048]{1,0:T(8,128)(2,1)S(1)} %bitcast.34, ...), custom_call_target="tpu_custom_call" | custom-call | flops 1024 | bytes 1024 | tf_op jit(solution)/shard_map/pallas_call | solution.py:269
  361.7 3.6 collective-permute-done.39
  368.9 2.7 collective-permute-start.42
  372.4 6.2 %collective-permute-done.42.refs_0_ = bf16[8,64,128]{2,1,0:T(8,128)(2,1)S(1)} collective-permute-done((bf16[8,64,128]{2,1,0:T(8,128)(2,1)S(1)}, bf16[8,64,128]{2,1,0:T(8,128)(2,1)S(1)}, u32[]{:S(2)}, u32[]{:S(2)}) %collective-permute-start.42) | collective-permute-done | bytes 131104 | tf_op jit(solution)/shard_map/ppermute | solution.py:38
  378.6 19.4 %collective-permute-done.43.refs_1_ = bf16[8,64,128]{2,1,0:T(8,128)(2,1)S(1)} collective-permute-done((bf16[8,64,128]{2,1,0:T(8,128)(2,1)S(1)}, bf16[8,64,128]{2,1,0:T(8,128)(2,1)S(1)}, u32[]{:S(2)}, u32[]{:S(2)}) %collective-permute-start.43) | collective-permute-done | bytes 131104 | tf_op jit(solution)/shard_map/ppermute | solution.py:38
  399.4 4.8 shard_map.233
  405.7 4.1 collective-permute-done.45.c
  409.9 2.1 shard_map.234
  414.3 7.2 %reduce-scatter.5.cloned.1.call-done = bf16[512,1408]{1,0:T(8,128)(2,1)} async-done(((bf16[2048,1408]{1,0:T(8,128)(2,1)}), bf16[512,1408]{1,0:T(8,128)(2,1)}) %reduce-scatter.5.cloned.1.call-update) | async-done | bytes 1441808 | tf_op jit(solution)/shard_map/reduce_scatter | solution.py:805
  421.5 3.9 all-to-all-start.2
  426.6 3.4 collective-permute-start.50
  431.6 2.1 collective-permute-start.46
  435.2 7.4 %collective-permute-done.49.refs_0_ = bf16[256,1152]{1,0:T(8,128)(2,1)} collective-permute-done((bf16[256,1152]{1,0:T(8,128)(2,1)}, bf16[256,1152]{1,0:T(8,128)(2,1)}, u32[]{:S(2)}, u32[]{:S(2)}) %collective-permute-start.49) | collective-permute-done | bytes 589856 | tf_op jit(solution)/shard_map/ppermute | solution.py:38
  442.6 2.6 collective-permute-start.48
  445.2 3.2 fusion.8
  448.3 33.4 %collective-permute-done.50.refs_1_ = bf16[256,1152]{1,0:T(8,128)(2,1)} collective-permute-done((bf16[256,1152]{1,0:T(8,128)(2,1)}, bf16[256,1152]{1,0:T(8,128)(2,1)}, u32[]{:S(2)}, u32[]{:S(2)}) %collective-permute-start.50) | collective-permute-done | bytes 589856 | tf_op jit(solution)/shard_map/ppermute | solution.py:38
  483.3 1.9 fusion.2
  485.2 2.6 shard_map.235
  488.5 3.8 all-to-all-start.3
  492.4 3.2 fusion.6
  496.9 3.8 all-to-all-done.3.x
  501.7 2.3 shard_map.236
  (332 shorter events, 85.8 us)
Async XLA Ops:
  7.2 69.2 %copy-start.31 = (bf16[64,5632]{1,0:T(8,128)(2,1)S(1)}, bf16[64,5632]{1,0:T(8,128)(2,1)}, u32[]{:S(2)}) copy-start(bf16[64,5632]{1,0:T(8,128)(2,1)} %g.2) | copy-start | bytes 2162692
  7.2 69.2 %copy-start.33 = (bf16[64,5632]{1,0:T(8,128)(2,1)S(1)}, bf16[64,5632]{1,0:T(8,128)(2,1)}, u32[]{:S(2)}) copy-start(bf16[64,5632]{1,0:T(8,128)(2,1)} %u.2) | copy-start | bytes 2162692
  7.2 102.6 %all-gather.3.cloned.1.call-start = ((), (), s32[]{:S(2)}) async-start(), calls=%async_computation.6 | async-start | bytes 3604480 | tf_op jit(solution)/shard_map/all_gather | solution.py:741
  7.9 13.1 %collective-permute-start = (bf16[64,2048]{1,0:T(8,128)(2,1)}, bf16[64,2048]{1,0:T(8,128)(2,1)S(1)}, u32[]{:S(2)}, u32[]{:S(2)}) collective-permute-start(bf16[64,2048]{1,0:T(8,128)(2,1)} %refs_0_.1), channel_id=1, source_target_pairs={{0,3},{1,0},{2,1},{3,2},{4,7},{5,4},{6,5},{7,6},{8,11},{9,8},{10,9... | collective-permute-start | bytes 786440 | tf_op jit(solution)/shard_map/ppermute | solution.py:38
  8.4 32.4 %collective-permute-start.1 = (bf16[64,2048]{1,0:T(8,128)(2,1)}, bf16[64,2048]{1,0:T(8,128)(2,1)S(1)}, u32[]{:S(2)}, u32[]{:S(2)}) collective-permute-start(bf16[64,2048]{1,0:T(8,128)(2,1)} %refs_0_.1), channel_id=1, source_target_pairs={{0,2},{1,3},{2,0},{3,1},{4,6},{5,7},{6,4},{7,5},{8,10},{9,11},{10,... | collective-permute-start | bytes 786440 | tf_op jit(solution)/shard_map/ppermute | solution.py:38
  8.5 40.0 %collective-permute-start.3 = (bf16[128,2048]{1,0:T(8,128)(2,1)}, bf16[128,2048]{1,0:T(8,128)(2,1)S(1)}, u32[]{:S(2)}, u32[]{:S(2)}) collective-permute-start(bf16[128,2048]{1,0:T(8,128)(2,1)} %bitcast.38), channel_id=1, source_target_pairs={{0,8},{4,12},{8,0},{12,4},{16,24},{20,28},{24,16},{28,20},{1,9},{5... | collective-permute-start | bytes 1572872 | tf_op jit(solution)/shard_map/ppermute | solution.py:34
  10.3 38.2 %collective-permute-start.4 = (bf16[128,2048]{1,0:T(8,128)(2,1)}, bf16[128,2048]{1,0:T(8,128)(2,1)}, u32[]{:S(2)}, u32[]{:S(2)}) collective-permute-start(bf16[128,2048]{1,0:T(8,128)(2,1)} %bitcast.39), channel_id=1, source_target_pairs={{0,16},{4,20},{8,24},{12,28},{16,0},{20,4},{24,8},{28,12},{1,17},{... | collective-permute-start | bytes 1572872 | tf_op jit(solution)/shard_map/ppermute | solution.py:34
  11.8 37.5 %collective-permute-start.5 = (bf16[128,2048]{1,0:T(8,128)(2,1)}, bf16[128,2048]{1,0:T(8,128)(2,1)}, u32[]{:S(2)}, u32[]{:S(2)}) collective-permute-start(bf16[128,2048]{1,0:T(8,128)(2,1)} %bitcast.40), channel_id=1, source_target_pairs={{0,24},{4,28},{8,16},{12,20},{16,8},{20,12},{24,0},{28,4},{1,25},{... | collective-permute-start | bytes 1572872 | tf_op jit(solution)/shard_map/ppermute | solution.py:34
  16.4 32.0 %all-to-all-start = ((bf16[8,64,384]{2,1,0:T(8,128)(2,1)}), bf16[8,64,384]{2,1,0:T(8,128)(2,1)S(1)}, u32[]{:S(2)}, u32[]{:S(2)}) async-start(bf16[8,64,384]{2,1,0:T(8,128)(2,1)} %bitcast.31), calls=%async_computation | async-start | bytes 786432 | tf_op jit(solution)/shard_map/all_to_all | solution.py:739
  21.0 56.8 %copy-start.61 = (bf16[64,2048]{1,0:T(8,128)(2,1)}, bf16[64,2048]{1,0:T(8,128)(2,1)S(1)}, u32[]{:S(2)}) copy-start(bf16[64,2048]{1,0:T(8,128)(2,1)S(1)} %collective-permute-done.refs_1_) | copy-start | bytes 786436
  21.0 27.4 %collective-permute-start.2 = (bf16[64,2048]{1,0:T(8,128)(2,1)S(1)}, bf16[64,2048]{1,0:T(8,128)(2,1)S(1)}, u32[]{:S(2)}, u32[]{:S(2)}) collective-permute-start(bf16[64,2048]{1,0:T(8,128)(2,1)S(1)} %copy-done.59), channel_id=1, source_target_pairs={{0,1},{1,2},{2,3},{3,0},{4,5},{5,6},{6,7},{7,4},{8,9},{9,10},{10,1... | collective-permute-start | bytes 786440 | tf_op jit(solution)/shard_map/ppermute | solution.py:38
  49.2 40.3 %collective-permute-start.7 = (bf16[8,64,384]{2,1,0:T(8,128)(2,1)S(1)}, bf16[8,64,384]{2,1,0:T(8,128)(2,1)S(1)}, u32[]{:S(2)}, u32[]{:S(2)}) collective-permute-start(bf16[8,64,384]{2,1,0:T(8,128)(2,1)S(1)} %all-to-all-done.refs_0_), channel_id=1, source_target_pairs={{0,3},{1,0},{2,1},{3,2},{4,7},{5,4},{6,5},{7,6},{8,11},{9,8},{10,9... | collective-permute-start | bytes 1179656 | tf_op jit(solution)/shard_map/ppermute | solution.py:38
  74.0 30.9 %collective-permute-start.8 = (bf16[8,64,384]{2,1,0:T(8,128)(2,1)S(1)}, bf16[8,64,384]{2,1,0:T(8,128)(2,1)}, u32[]{:S(2)}, u32[]{:S(2)}) collective-permute-start(bf16[8,64,384]{2,1,0:T(8,128)(2,1)S(1)} %all-to-all-done.refs_0_), channel_id=1, source_target_pairs={{0,2},{1,3},{2,0},{3,1},{4,6},{5,7},{6,4},{7,5},{8,10},{9,11},{10,... | collective-permute-start | bytes 1179656 | tf_op jit(solution)/shard_map/ppermute | solution.py:38
  74.0 30.9 %collective-permute-start.9 = (bf16[8,64,384]{2,1,0:T(8,128)(2,1)S(1)}, bf16[8,64,384]{2,1,0:T(8,128)(2,1)}, u32[]{:S(2)}, u32[]{:S(2)}) collective-permute-start(bf16[8,64,384]{2,1,0:T(8,128)(2,1)S(1)} %all-to-all-done.refs_0_), channel_id=1, source_target_pairs={{0,1},{1,2},{2,3},{3,0},{4,5},{5,6},{6,7},{7,4},{8,9},{9,10},{10,1... | collective-permute-start | bytes 1179656 | tf_op jit(solution)/shard_map/ppermute | solution.py:38
  77.8 27.2 %all-to-all-start.1 = ((bf16[8,64,1408]{2,1,0:T(8,128)(2,1)}), bf16[8,64,1408]{2,1,0:T(8,128)(2,1)}, u32[]{:S(2)}, u32[]{:S(2)}) async-start(bf16[8,64,1408]{2,1,0:T(8,128)(2,1)} %shard_map.212), calls=%async_computation.1 | async-start | bytes 2883584 | tf_op jit(solution)/shard_map/all_to_all | solution.py:758
  82.3 147.2 %all-gather.5.cloned.1.call-start = ((), (), s32[]{:S(2)}) async-start(), calls=%async_computation.7 | async-start | bytes 7208960 | tf_op jit(solution)/shard_map/all_gather | solution.py:765
  85.2 26.9 %collective-permute-start.6 = (bf16[512,2048]{1,0:T(8,128)(2,1)}, bf16[512,2048]{1,0:T(8,128)(2,1)}, u32[]{:S(2)}, u32[]{:S(2)}) collective-permute-start(bf16[512,2048]{1,0:T(8,128)(2,1)} %pad_maximum_fusion.e), channel_id=1, source_target_pairs={{0,4},{4,0},{8,12},{12,8},{16,20},{20,16},{24,28},{28,24},{1,5},{5... | collective-permute-start | bytes 6291464 | tf_op jit(solution)/shard_map/ppermute | solution.py:34
  109.8 199.3 %reduce-scatter.3.cloned.1.call-start = ((), (), s32[]{:S(2)}) async-start(), calls=%async_computation.8 | async-start | bytes 3604480 | tf_op jit(solution)/shard_map/reduce_scatter | solution.py:794
  120.8 41.7 %copy-start.39 = (bf16[1024,256]{1,0:T(8,128)(2,1)}, bf16[1024,256]{1,0:T(8,128)(2,1)S(1)}, u32[]{:S(2)}) copy-start(bf16[1024,256]{1,0:T(8,128)(2,1)S(1)} %get-tuple-element.147.q) | copy-start | bytes 1572868
  120.8 28.0 %collective-permute-start.13 = (bf16[128,2048]{1,0:T(8,128)(2,1)}, bf16[128,2048]{1,0:T(8,128)(2,1)S(1)}, u32[]{:S(2)}, u32[]{:S(2)}) collective-permute-start(bf16[128,2048]{1,0:T(8,128)(2,1)} %bitcast.11.grad_out), channel_id=1, source_target_pairs={{0,8},{4,12},{8,0},{12,4},{16,24},{20,28},{24,16},{28,20},{1,9},{5... | collective-permute-start | bytes 1572872 | tf_op jit(solution)/shard_map/ppermute | solution.py:34
  122.3 26.5 %collective-permute-start.14 = (bf16[128,2048]{1,0:T(8,128)(2,1)}, bf16[128,2048]{1,0:T(8,128)(2,1)}, u32[]{:S(2)}, u32[]{:S(2)}) collective-permute-start(bf16[128,2048]{1,0:T(8,128)(2,1)} %bitcast.11.grad_out), channel_id=1, source_target_pairs={{0,16},{4,20},{8,24},{12,28},{16,0},{20,4},{24,8},{28,12},{1,17},{... | collective-permute-start | bytes 1572872 | tf_op jit(solution)/shard_map/ppermute | solution.py:34
  123.8 25.0 %collective-permute-start.15 = (bf16[128,2048]{1,0:T(8,128)(2,1)}, bf16[128,2048]{1,0:T(8,128)(2,1)}, u32[]{:S(2)}, u32[]{:S(2)}) collective-permute-start(bf16[128,2048]{1,0:T(8,128)(2,1)} %bitcast.11.grad_out), channel_id=1, source_target_pairs={{0,24},{4,28},{8,16},{12,20},{16,8},{20,12},{24,0},{28,4},{1,25},{... | collective-permute-start | bytes 1572872 | tf_op jit(solution)/shard_map/ppermute | solution.py:34
  124.3 12.3 %collective-permute-start.10 = (bf16[8,64,128]{2,1,0:T(8,128)(2,1)S(1)}, bf16[8,64,128]{2,1,0:T(8,128)(2,1)S(1)}, u32[]{:S(2)}, u32[]{:S(2)}) collective-permute-start(bf16[8,64,128]{2,1,0:T(8,128)(2,1)S(1)} %get-tuple-element.148.refs_0_), channel_id=1, source_target_pairs={{0,3},{1,0},{2,1},{3,2},{4,7},{5,4},{6,5},{7,6},{8,11},{9,8},{10,9... | collective-permute-start | bytes 393224 | tf_op jit(solution)/shard_map/ppermute | solution.py:38
  129.5 17.0 %collective-permute-start.11 = (bf16[8,64,128]{2,1,0:T(8,128)(2,1)S(1)}, bf16[8,64,128]{2,1,0:T(8,128)(2,1)S(1)}, u32[]{:S(2)}, u32[]{:S(2)}) collective-permute-start(bf16[8,64,128]{2,1,0:T(8,128)(2,1)S(1)} %get-tuple-element.148.refs_0_), channel_id=1, source_target_pairs={{0,2},{1,3},{2,0},{3,1},{4,6},{5,7},{6,4},{7,5},{8,10},{9,11},{10,... | collective-permute-start | bytes 393224 | tf_op jit(solution)/shard_map/ppermute | solution.py:38
  136.5 12.3 %collective-permute-start.12 = (bf16[8,64,128]{2,1,0:T(8,128)(2,1)S(1)}, bf16[8,64,128]{2,1,0:T(8,128)(2,1)S(1)}, u32[]{:S(2)}, u32[]{:S(2)}) collective-permute-start(bf16[8,64,128]{2,1,0:T(8,128)(2,1)S(1)} %get-tuple-element.148.refs_0_), channel_id=1, source_target_pairs={{0,1},{1,2},{2,3},{3,0},{4,5},{5,6},{6,7},{7,4},{8,9},{9,10},{10,1... | collective-permute-start | bytes 393224 | tf_op jit(solution)/shard_map/ppermute | solution.py:38
  146.5 4.7 collective-permute-start.16
  148.8 2.4 collective-permute-start.17
  148.9 2.3 collective-permute-start.18
  149.4 1.9 collective-permute-start.19
  162.5 4.2 collective-permute-start.20
  167.5 14.8 %collective-permute-start.21 = (bf16[128,2048]{1,0:T(8,128)(2,1)S(1)}, bf16[128,2048]{1,0:T(8,128)(2,1)S(1)}, u32[]{:S(2)}, u32[]{:S(2)}) collective-permute-start(bf16[128,2048]{1,0:T(8,128)(2,1)S(1)} %get-tuple-element.156), channel_id=1, source_target_pairs={{0,8},{4,12},{8,0},{12,4},{16,24},{20,28},{24,16},{28,20},{1,9},{5... | collective-permute-start | bytes 1572872 | tf_op jit(solution)/shard_map/ppermute | solution.py:34
  169.0 25.1 %collective-permute-start.22 = (bf16[128,2048]{1,0:T(8,128)(2,1)S(1)}, bf16[128,2048]{1,0:T(8,128)(2,1)S(1)}, u32[]{:S(2)}, u32[]{:S(2)}) collective-permute-start(bf16[128,2048]{1,0:T(8,128)(2,1)S(1)} %get-tuple-element.157), channel_id=1, source_target_pairs={{0,16},{4,20},{8,24},{12,28},{16,0},{20,4},{24,8},{28,12},{1,17},{... | collective-permute-start | bytes 1572872 | tf_op jit(solution)/shard_map/ppermute | solution.py:34
  170.5 23.5 %collective-permute-start.23 = (bf16[128,2048]{1,0:T(8,128)(2,1)S(1)}, bf16[128,2048]{1,0:T(8,128)(2,1)S(1)}, u32[]{:S(2)}, u32[]{:S(2)}) collective-permute-start(bf16[128,2048]{1,0:T(8,128)(2,1)S(1)} %get-tuple-element.158), channel_id=1, source_target_pairs={{0,24},{4,28},{8,16},{12,20},{16,8},{20,12},{24,0},{28,4},{1,25},{... | collective-permute-start | bytes 1572872 | tf_op jit(solution)/shard_map/ppermute | solution.py:34
  195.7 14.9 %collective-permute-start.24 = (bf16[128,2048]{1,0:T(8,128)(2,1)S(1)}, bf16[128,2048]{1,0:T(8,128)(2,1)S(1)}, u32[]{:S(2)}, u32[]{:S(2)}) collective-permute-start(bf16[128,2048]{1,0:T(8,128)(2,1)S(1)} %get-tuple-element.163.refs_0_), channel_id=1, source_target_pairs={{0,8},{4,12},{8,0},{12,4},{16,24},{20,28},{24,16},{28,20},{1,9},{5... | collective-permute-start | bytes 1572872 | tf_op jit(solution)/shard_map/ppermute | solution.py:34
  196.9 24.4 %collective-permute-start.25 = (bf16[128,2048]{1,0:T(8,128)(2,1)S(1)}, bf16[128,2048]{1,0:T(8,128)(2,1)S(1)}, u32[]{:S(2)}, u32[]{:S(2)}) collective-permute-start(bf16[128,2048]{1,0:T(8,128)(2,1)S(1)} %get-tuple-element.163.refs_0_), channel_id=1, source_target_pairs={{0,16},{4,20},{8,24},{12,28},{16,0},{20,4},{24,8},{28,12},{1,17},{... | collective-permute-start | bytes 1572872 | tf_op jit(solution)/shard_map/ppermute | solution.py:34
  197.7 23.6 %collective-permute-start.26 = (bf16[128,2048]{1,0:T(8,128)(2,1)S(1)}, bf16[128,2048]{1,0:T(8,128)(2,1)S(1)}, u32[]{:S(2)}, u32[]{:S(2)}) collective-permute-start(bf16[128,2048]{1,0:T(8,128)(2,1)S(1)} %get-tuple-element.163.refs_0_), channel_id=1, source_target_pairs={{0,24},{4,28},{8,16},{12,20},{16,8},{20,12},{24,0},{28,4},{1,25},{... | collective-permute-start | bytes 1572872 | tf_op jit(solution)/shard_map/ppermute | solution.py:34
  221.4 14.6 %collective-permute-start.27 = (bf16[512,2048]{1,0:T(8,128)(2,1)S(1)}, bf16[512,2048]{1,0:T(8,128)(2,1)}, u32[]{:S(2)}, u32[]{:S(2)}) collective-permute-start(bf16[512,2048]{1,0:T(8,128)(2,1)S(1)} %shard_map.219.x.refs_0_), channel_id=1, source_target_pairs={{0,4},{4,0},{8,12},{12,8},{16,20},{20,16},{24,28},{28,24},{1,5},{5... | collective-permute-start | bytes 6291464 | tf_op jit(solution)/shard_map/ppermute | solution.py:34
  224.4 19.1 %collective-permute-start.28 = (bf16[512,2048]{1,0:T(8,128)(2,1)}, bf16[512,2048]{1,0:T(8,128)(2,1)}, u32[]{:S(2)}, u32[]{:S(2)}) collective-permute-start(bf16[512,2048]{1,0:T(8,128)(2,1)} %pad_maximum_fusion.1.refs_2_.dy), channel_id=1, source_target_pairs={{0,4},{4,0},{8,12},{12,8},{16,20},{20,16},{24,28},{28,24},{1,5},{5... | collective-permute-start | bytes 6291464 | tf_op jit(solution)/shard_map/ppermute | solution.py:34
  251.5 170.1 %reduce-scatter.5.cloned.1.call-start = ((), (), s32[]{:S(2)}) async-start(), calls=%async_computation.9 | async-start | bytes 7208960 | tf_op jit(solution)/shard_map/reduce_scatter | solution.py:805
  269.2 9.9 %collective-permute-start.29 = (bf16[512,2048]{1,0:T(8,128)(2,1)S(1)}, bf16[512,2048]{1,0:T(8,128)(2,1)S(1)}, u32[]{:S(2)}, u32[]{:S(2)}) collective-permute-start(bf16[512,2048]{1,0:T(8,128)(2,1)S(1)} %get-tuple-element.183), channel_id=1, source_target_pairs={{0,4},{4,0},{8,12},{12,8},{16,20},{20,16},{24,28},{28,24},{1,5},{5... | collective-permute-start | bytes 6291464 | tf_op jit(solution)/shard_map/ppermute | solution.py:34
  281.9 4.2 collective-permute-start.30
  282.3 23.9 %collective-permute-start.31 = (bf16[128,2048]{1,0:T(8,128)(2,1)}, bf16[128,2048]{1,0:T(8,128)(2,1)}, u32[]{:S(2)}, u32[]{:S(2)}) collective-permute-start(bf16[128,2048]{1,0:T(8,128)(2,1)} %get-tuple-element.184), channel_id=1, source_target_pairs={{0,8},{4,12},{8,0},{12,4},{16,24},{20,28},{24,16},{28,20},{1,9},{5... | collective-permute-start | bytes 1572872 | tf_op jit(solution)/shard_map/ppermute | solution.py:34
  283.9 25.2 %collective-permute-start.32 = (bf16[128,2048]{1,0:T(8,128)(2,1)}, bf16[128,2048]{1,0:T(8,128)(2,1)}, u32[]{:S(2)}, u32[]{:S(2)}) collective-permute-start(bf16[128,2048]{1,0:T(8,128)(2,1)} %get-tuple-element.185), channel_id=1, source_target_pairs={{0,16},{4,20},{8,24},{12,28},{16,0},{20,4},{24,8},{28,12},{1,17},{... | collective-permute-start | bytes 1572872 | tf_op jit(solution)/shard_map/ppermute | solution.py:34
  285.4 23.8 %collective-permute-start.33 = (bf16[128,2048]{1,0:T(8,128)(2,1)}, bf16[128,2048]{1,0:T(8,128)(2,1)}, u32[]{:S(2)}, u32[]{:S(2)}) collective-permute-start(bf16[128,2048]{1,0:T(8,128)(2,1)} %get-tuple-element.186), channel_id=1, source_target_pairs={{0,24},{4,28},{8,16},{12,20},{16,8},{20,12},{24,0},{28,4},{1,25},{... | collective-permute-start | bytes 1572872 | tf_op jit(solution)/shard_map/ppermute | solution.py:34
  314.8 14.9 %collective-permute-start.34 = (bf16[128,2048]{1,0:T(8,128)(2,1)S(1)}, bf16[128,2048]{1,0:T(8,128)(2,1)S(1)}, u32[]{:S(2)}, u32[]{:S(2)}) collective-permute-start(bf16[128,2048]{1,0:T(8,128)(2,1)S(1)} %get-tuple-element.200.refs_0_), channel_id=1, source_target_pairs={{0,8},{4,12},{8,0},{12,4},{16,24},{20,28},{24,16},{28,20},{1,9},{5... | collective-permute-start | bytes 1572872 | tf_op jit(solution)/shard_map/ppermute | solution.py:34
  316.1 24.1 %collective-permute-start.35 = (bf16[128,2048]{1,0:T(8,128)(2,1)S(1)}, bf16[128,2048]{1,0:T(8,128)(2,1)S(1)}, u32[]{:S(2)}, u32[]{:S(2)}) collective-permute-start(bf16[128,2048]{1,0:T(8,128)(2,1)S(1)} %get-tuple-element.200.refs_0_), channel_id=1, source_target_pairs={{0,16},{4,20},{8,24},{12,28},{16,0},{20,4},{24,8},{28,12},{1,17},{... | collective-permute-start | bytes 1572872 | tf_op jit(solution)/shard_map/ppermute | solution.py:34
  317.0 23.2 %collective-permute-start.36 = (bf16[128,2048]{1,0:T(8,128)(2,1)S(1)}, bf16[128,2048]{1,0:T(8,128)(2,1)S(1)}, u32[]{:S(2)}, u32[]{:S(2)}) collective-permute-start(bf16[128,2048]{1,0:T(8,128)(2,1)S(1)} %get-tuple-element.200.refs_0_), channel_id=1, source_target_pairs={{0,24},{4,28},{8,16},{12,20},{16,8},{20,12},{24,0},{28,4},{1,25},{... | collective-permute-start | bytes 1572872 | tf_op jit(solution)/shard_map/ppermute | solution.py:34
  340.3 4.2 collective-permute-start.37
  340.4 21.3 %collective-permute-start.38 = (bf16[128,2048]{1,0:T(8,128)(2,1)S(1)}, bf16[128,2048]{1,0:T(8,128)(2,1)S(1)}, u32[]{:S(2)}, u32[]{:S(2)}) collective-permute-start(bf16[128,2048]{1,0:T(8,128)(2,1)S(1)} %copy-done.82), channel_id=1, source_target_pairs={{0,8},{4,12},{8,0},{12,4},{16,24},{20,28},{24,16},{28,20},{1,9},{5... | collective-permute-start | bytes 1572872 | tf_op jit(solution)/shard_map/ppermute | solution.py:34
  341.7 23.6 %collective-permute-start.39 = (bf16[128,2048]{1,0:T(8,128)(2,1)S(1)}, bf16[128,2048]{1,0:T(8,128)(2,1)S(1)}, u32[]{:S(2)}, u32[]{:S(2)}) collective-permute-start(bf16[128,2048]{1,0:T(8,128)(2,1)S(1)} %copy-done.80), channel_id=1, source_target_pairs={{0,16},{4,20},{8,24},{12,28},{16,0},{20,4},{24,8},{28,12},{1,17},{... | collective-permute-start | bytes 1572872 | tf_op jit(solution)/shard_map/ppermute | solution.py:34
  342.5 24.4 %collective-permute-start.40 = (bf16[128,2048]{1,0:T(8,128)(2,1)S(1)}, bf16[128,2048]{1,0:T(8,128)(2,1)S(1)}, u32[]{:S(2)}, u32[]{:S(2)}) collective-permute-start(bf16[128,2048]{1,0:T(8,128)(2,1)S(1)} %copy-done.78), channel_id=1, source_target_pairs={{0,24},{4,28},{8,16},{12,20},{16,8},{20,12},{24,0},{28,4},{1,25},{... | collective-permute-start | bytes 1572872 | tf_op jit(solution)/shard_map/ppermute | solution.py:34
  366.9 1.9 collective-permute-start.41
  368.9 9.6 %collective-permute-start.42 = (bf16[8,64,128]{2,1,0:T(8,128)(2,1)S(1)}, bf16[8,64,128]{2,1,0:T(8,128)(2,1)S(1)}, u32[]{:S(2)}, u32[]{:S(2)}) collective-permute-start(bf16[8,64,128]{2,1,0:T(8,128)(2,1)S(1)} %get-tuple-element.217), channel_id=1, source_target_pairs={{0,1},{1,2},{2,3},{3,0},{4,5},{5,6},{6,7},{7,4},{8,9},{9,10},{10,1... | collective-permute-start | bytes 393224 | tf_op jit(solution)/shard_map/ppermute | solution.py:38
  371.7 26.3 %collective-permute-start.43 = (bf16[8,64,128]{2,1,0:T(8,128)(2,1)S(1)}, bf16[8,64,128]{2,1,0:T(8,128)(2,1)S(1)}, u32[]{:S(2)}, u32[]{:S(2)}) collective-permute-start(bf16[8,64,128]{2,1,0:T(8,128)(2,1)S(1)} %get-tuple-element.218), channel_id=1, source_target_pairs={{0,2},{1,3},{2,0},{3,1},{4,6},{5,7},{6,4},{7,5},{8,10},{9,11},{10,... | collective-permute-start | bytes 393224 | tf_op jit(solution)/shard_map/ppermute | solution.py:38
  372.1 25.9 %collective-permute-start.44 = (bf16[8,64,128]{2,1,0:T(8,128)(2,1)S(1)}, bf16[8,64,128]{2,1,0:T(8,128)(2,1)S(1)}, u32[]{:S(2)}, u32[]{:S(2)}) collective-permute-start(bf16[8,64,128]{2,1,0:T(8,128)(2,1)S(1)} %get-tuple-element.219), channel_id=1, source_target_pairs={{0,3},{1,0},{2,1},{3,2},{4,7},{5,4},{6,5},{7,6},{8,11},{9,8},{10,9... | collective-permute-start | bytes 393224 | tf_op jit(solution)/shard_map/ppermute | solution.py:38
  405.6 4.2 collective-permute-start.45
  421.5 61.8 %all-to-all-start.2 = ((bf16[8,64,1408]{2,1,0:T(8,128)(2,1)}), bf16[8,64,1408]{2,1,0:T(8,128)(2,1)S(1)}, u32[]{:S(2)}, u32[]{:S(2)}) async-start(bf16[8,64,1408]{2,1,0:T(8,128)(2,1)} %bitcast.46), calls=%async_computation.4 | async-start | bytes 2883584 | tf_op jit(solution)/shard_map/all_to_all | solution.py:830
  425.4 17.2 %collective-permute-start.49 = (bf16[256,1152]{1,0:T(8,128)(2,1)}, bf16[256,1152]{1,0:T(8,128)(2,1)}, u32[]{:S(2)}, u32[]{:S(2)}) collective-permute-start(bf16[256,1152]{1,0:T(8,128)(2,1)} %copy-done.76), channel_id=1, source_target_pairs={{0,1},{1,2},{2,3},{3,0},{4,5},{5,6},{6,7},{7,4},{8,9},{9,10},{10,1... | collective-permute-start | bytes 1769480 | tf_op jit(solution)/shard_map/ppermute | solution.py:38
  426.6 55.1 %collective-permute-start.50 = (bf16[256,1152]{1,0:T(8,128)(2,1)}, bf16[256,1152]{1,0:T(8,128)(2,1)}, u32[]{:S(2)}, u32[]{:S(2)}) collective-permute-start(bf16[256,1152]{1,0:T(8,128)(2,1)} %copy-done.75), channel_id=1, source_target_pairs={{0,2},{1,3},{2,0},{3,1},{4,6},{5,7},{6,4},{7,5},{8,10},{9,11},{10,... | collective-permute-start | bytes 1769480 | tf_op jit(solution)/shard_map/ppermute | solution.py:38
  430.0 51.7 %collective-permute-start.51 = (bf16[256,1152]{1,0:T(8,128)(2,1)}, bf16[256,1152]{1,0:T(8,128)(2,1)}, u32[]{:S(2)}, u32[]{:S(2)}) collective-permute-start(bf16[256,1152]{1,0:T(8,128)(2,1)} %copy-done.74), channel_id=1, source_target_pairs={{0,3},{1,0},{2,1},{3,2},{4,7},{5,4},{6,5},{7,6},{8,11},{9,8},{10,9... | collective-permute-start | bytes 1769480 | tf_op jit(solution)/shard_map/ppermute | solution.py:38
  431.6 50.1 %collective-permute-start.46 = (bf16[128,2048]{1,0:T(8,128)(2,1)}, bf16[128,2048]{1,0:T(8,128)(2,1)S(1)}, u32[]{:S(2)}, u32[]{:S(2)}) collective-permute-start(bf16[128,2048]{1,0:T(8,128)(2,1)} %copy-done.85), channel_id=1, source_target_pairs={{0,8},{4,12},{8,0},{12,4},{16,24},{20,28},{24,16},{28,20},{1,9},{5... | collective-permute-start | bytes 1572872 | tf_op jit(solution)/shard_map/ppermute | solution.py:34
  433.7 48.0 %collective-permute-start.47 = (bf16[128,2048]{1,0:T(8,128)(2,1)}, bf16[128,2048]{1,0:T(8,128)(2,1)S(1)}, u32[]{:S(2)}, u32[]{:S(2)}) collective-permute-start(bf16[128,2048]{1,0:T(8,128)(2,1)} %copy-done.84), channel_id=1, source_target_pairs={{0,16},{4,20},{8,24},{12,28},{16,0},{20,4},{24,8},{28,12},{1,17},{... | collective-permute-start | bytes 1572872 | tf_op jit(solution)/shard_map/ppermute | solution.py:34
  442.6 40.7 %collective-permute-start.48 = (bf16[128,2048]{1,0:T(8,128)(2,1)}, bf16[128,2048]{1,0:T(8,128)(2,1)}, u32[]{:S(2)}, u32[]{:S(2)}) collective-permute-start(bf16[128,2048]{1,0:T(8,128)(2,1)} %copy-done.83), channel_id=1, source_target_pairs={{0,24},{4,28},{8,16},{12,20},{16,8},{20,12},{24,0},{28,4},{1,25},{... | collective-permute-start | bytes 1572872 | tf_op jit(solution)/shard_map/ppermute | solution.py:34
  488.5 12.2 %all-to-all-start.3 = ((bf16[8,64,320]{2,1,0:T(8,128)(2,1)}), bf16[8,64,320]{2,1,0:T(8,128)(2,1)S(1)}, u32[]{:S(2)}, u32[]{:S(2)}) async-start(bf16[8,64,320]{2,1,0:T(8,128)(2,1)} %copy-done.56), calls=%async_computation.5 | async-start | bytes 786432 | tf_op jit(solution)/shard_map/all_to_all | solution.py:833
  (97 other events, 949.3 us)
Sparse Core Ops, SparseCore 0:
  9.6 100.1 all-gather.2
  111.3 118.0 all-gather.4
  251.6 56.4 reduce-scatter.2
  310.2 111.2 reduce-scatter.4

commit v6 on v5

--- a/solution.py
+++ b/solution.py
@@ -384,7 +384,7 @@
     def body(x, w, both, hidden):
         product = dot(x[...], w[...])
         gate, up = product[:, :ff], product[:, ff:]
-        both[...] = product
+        both[...] = product.astype(BF16)
         hidden[...] = (gate * jax.nn.sigmoid(gate) * up).astype(BF16)
 
     def rows(columns):
@@ -396,7 +396,7 @@
         in_specs=[rows(width), pl.BlockSpec(w_pair.shape, lambda i: (0, 0), pipeline_mode=pl.Buffered(1))],
         out_specs=(rows(2 * ff), rows(ff)),
         out_shape=(
-            jax.ShapeDtypeStruct((tokens, 2 * ff), F32),
+            jax.ShapeDtypeStruct((tokens, 2 * ff), BF16),
             jax.ShapeDtypeStruct((tokens, ff), BF16),
         ),
         compiler_params=kernel_params(),
@@ -410,7 +410,7 @@
     tile = 256
 
     def body(both, h, dy, w, wd, grads, back, forth):
-        gate, up = both[:, :ff], both[:, ff:]
+        gate, up = both[:, :ff].astype(F32), both[:, ff:].astype(F32)
         sig = jax.nn.sigmoid(gate)
         forth[...] = dot(h[...], wd[...]).astype(BF16)
         dh_sig = dot_nt(dy[...], wd[...]) * sig
@@ -558,6 +558,18 @@
         compiler_params=kernel_params(),
         cost_estimate=LIGHT,
     )(gate, up)
+
+
+def sum_terms(*terms):
+    def body(*refs):
+        refs[-1][...] = sum(ref[...].astype(F32) for ref in refs[:-1])
+
+    return pl.pallas_call(
+        body,
+        out_shape=jax.ShapeDtypeStruct(terms[0].shape, F32),
+        compiler_params=kernel_params(),
+        cost_estimate=LIGHT,
+    )(*terms)
 
 
 def gather_terms(own, sums, members, used, width):
@@ -823,12 +835,18 @@
         where, first_in, grad_attn, mixed, grad_branch, used, n, c
     )
     first_own, *sends = scatter_dp(after(grad_attn, terms), w_attn, n, dot_nt)
-    pair_sum = after(pair_sum, sends).reshape(n, block, 2 * f_cols)
-    sent, terms, pair_sum = together(
+    sent, near, last, far = together(
         [swap(v, 2 * j) for j, v in enumerate(sends, 1)],
-        [shift(v, -j, c) for j, v in enumerate(terms, 1)],
-        lax.all_to_all(pair_sum, every_dp, 0, 0),
-    )
+        shift(terms[0], -1, c),
+        shift(terms[-1], 1, c),
+        terms[1:-1],
+    )
+    pair_sum = after(pair_sum, near)
+    far, pair_sum = together(
+        [shift(v, -j, c) for j, v in enumerate(far, 2)],
+        lax.all_to_all(pair_sum.reshape(n, block, 2 * f_cols), every_dp, 0, 0),
+    )
+    own_terms, terms = sum_terms(own_terms, near, last), far
     grad_wout, payload = gather_terms(own_terms, terms, n, used, width)
     payload = lax.all_to_all(payload, every_dp, 0, 0)
     grad_gate, grad_up, grad_query, grad_key, grad_value, grad_gains = weight_gradients(

time: 519 us -> 519 us (level)
  the two profiles are of different devices: /device:TPU:24 before, /device:TPU:0 now
where the time goes in v6:
time: 519 us; the launch traced here: 512 us
  waiting for transfers between devices  200 us (39%)
  starting transfers between devices  124 us (24%)
  Pallas kernels  101 us (19%)
  local copies, waits for them, and re-layouts  47.3 us (9%)
  other arithmetic  21.6 us (4%)
  between operations  15.4 us (3%)
    ppermute x15, waiting for transfers between devices, shift(): lax.ppermute(value, 'ctx', [(i, (i - step) % size) for i in range(size)])  111 us
    ppermute x37, waiting for transfers between devices, swap(): lax.ppermute(value, ('plane', 'core'), [(i, i ^ rel) for i in range(size)])  81.4 us
    ppermute x15, starting transfers between devices, shift(): lax.ppermute(value, 'ctx', [(i, (i - step) % size) for i in range(size)])  76.7 us
    unnamed x201, local copies, waits for them, and re-layouts  40.3 us
    ppermute x37, starting transfers between devices, swap(): lax.ppermute(value, ('plane', 'core'), [(i, i ^ rel) for i in range(size)])  31.1 us
    pallas_call x2, Pallas kernels, feed_forward_back(): pl.pallas_call(body, grid=(tokens // tile,), in_specs=[rows(2 * ff), rows...  19.7 us
    pallas_call x1, Pallas kernels, attend_back(): pl.pallas_call(body, grid=(sequences,), in_specs=[pl.BlockSpec(memory_spa...  17 us
    pallas_call x2, Pallas kernels, transposed_dot(): pl.pallas_call(body, grid=(rows // row_tile if by_rows else columns // co...  14.8 us
  transfers between devices with their start and end apart: 60, of which 26 were waited for; matrix products, arithmetic and copies ran while one was open for 6% of the time, Pallas kernels for 18%

profile of v6, /device:TPU:0, one launch (start us, length us, event | category | flops | bytes accessed | tf_op | source)
XLA Modules:
  0.0 511.6 jit_solution(15541171507060382733)
XLA Ops:
  7.9 4.1 collective-permute-start.1
  13.4 2.4 collective-permute-start.5
  21.4 3.7 all-to-all-start
  25.6 2.0 collective-permute-done.1.refs_2_
  27.6 20.4 %collective-permute-start.2 = (bf16[64,2048]{1,0:T(8,128)(2,1)S(1)}, bf16[64,2048]{1,0:T(8,128)(2,1)S(1)}, u32[]{:S(2)}, u32[]{:S(2)}) collective-permute-start(bf16[64,2048]{1,0:T(8,128)(2,1)S(1)} %copy-done.66), channel_id=1, source_target_pairs={{0,1},{1,2},{2,3},{3,0},{4,5},{5,6},{6,7},{7,4},{8,9},{9,10},{10,1... | collective-permute-start | bytes 786440 | tf_op jit(solution)/shard_map/ppermute | solution.py:38
  48.7 14.1 %collective-permute-done.2.refs_3_ = bf16[64,2048]{1,0:T(8,128)(2,1)S(1)} collective-permute-done((bf16[64,2048]{1,0:T(8,128)(2,1)S(1)}, bf16[64,2048]{1,0:T(8,128)(2,1)S(1)}, u32[]{:S(2)}, u32[]{:S(2)}) %collective-permute-start.2) | collective-permute-done | bytes 262176 | tf_op jit(solution)/shard_map/ppermute | solution.py:38
  63.6 2.6 collective-permute-start.9
  66.2 8.4 %collective-permute-start.8 = (bf16[8,64,384]{2,1,0:T(8,128)(2,1)S(1)}, bf16[8,64,384]{2,1,0:T(8,128)(2,1)}, u32[]{:S(2)}, u32[]{:S(2)}) collective-permute-start(bf16[8,64,384]{2,1,0:T(8,128)(2,1)S(1)} %all-to-all-done.refs_0_), channel_id=1, source_target_pairs={{0,2},{1,3},{2,0},{3,1},{4,6},{5,7},{6,4},{7,5},{8,10},{9,11},{10,... | collective-permute-start | bytes 1179656 | tf_op jit(solution)/shard_map/ppermute | solution.py:38
  76.0 4.4 all-to-all-start.1
  80.5 2.8 pad_maximum_fusion.e
  84.6 1.9 fusion.11
  88.8 18.9 %collective-permute-done.8.refs_2_ = bf16[8,64,384]{2,1,0:T(8,128)(2,1)} collective-permute-done((bf16[8,64,384]{2,1,0:T(8,128)(2,1)S(1)}, bf16[8,64,384]{2,1,0:T(8,128)(2,1)}, u32[]{:S(2)}, u32[]{:S(2)}) %collective-permute-start.8) | collective-permute-done | bytes 393248 | tf_op jit(solution)/shard_map/ppermute | solution.py:38
  111.7 6.4 %shard_map.215 = (bf16[1024,2048]{1,0:T(8,128)(2,1)S(1)}, bf16[1024,256]{1,0:T(8,128)(2,1)S(1)}, bf16[8,64,128]{2,1,0:T(8,128)(2,1)S(1)}) custom-call(s32[2]{0:T(128)S(1)} %pad_add_fusion.at, bf16[512,2048]{1,0:T(8,128)(2,1)S(1)} %copy-done.14, bf16[512,2048]{1,0:T(8,128)(2,1)} %collective-permute-done.6.o, f32[1,2048]{1,0:T(1,128)S(1)} %get-tuple-element.272.gn, ...), custom_call_target="tpu_custom_call" | custom-call | flops 1024 | bytes 1024 | tf_op jit(solution)/shard_map/pallas_call | solution.py:140
  118.1 2.0 copy-done.19
  120.0 2.5 collective-permute-start.15
  123.5 8.7 %collective-permute-start.12 = (bf16[8,64,128]{2,1,0:T(8,128)(2,1)S(1)}, bf16[8,64,128]{2,1,0:T(8,128)(2,1)S(1)}, u32[]{:S(2)}, u32[]{:S(2)}) collective-permute-start(bf16[8,64,128]{2,1,0:T(8,128)(2,1)S(1)} %get-tuple-element.149.refs_0_), channel_id=1, source_target_pairs={{0,1},{1,2},{2,3},{3,0},{4,5},{5,6},{6,7},{7,4},{8,9},{9,10},{10,1... | collective-permute-start | bytes 393224 | tf_op jit(solution)/shard_map/ppermute | solution.py:38
  132.3 3.6 collective-permute-start.11
  135.8 6.6 %collective-permute-done.12.refs_3_ = bf16[8,64,128]{2,1,0:T(8,128)(2,1)S(1)} collective-permute-done((bf16[8,64,128]{2,1,0:T(8,128)(2,1)S(1)}, bf16[8,64,128]{2,1,0:T(8,128)(2,1)S(1)}, u32[]{:S(2)}, u32[]{:S(2)}) %collective-permute-start.12) | collective-permute-done | bytes 131104 | tf_op jit(solution)/shard_map/ppermute | solution.py:38
  142.4 3.5 collective-permute-start.10
  145.8 5.7 %collective-permute-done.11.refs_2_ = bf16[8,64,128]{2,1,0:T(8,128)(2,1)S(1)} collective-permute-done((bf16[8,64,128]{2,1,0:T(8,128)(2,1)S(1)}, bf16[8,64,128]{2,1,0:T(8,128)(2,1)S(1)}, u32[]{:S(2)}, u32[]{:S(2)}) %collective-permute-start.11) | collective-permute-done | bytes 131104 | tf_op jit(solution)/shard_map/ppermute | solution.py:38
  151.5 3.8 collective-permute-done.10.refs_1_
  159.1 9.7 %shard_map.216.a.m = bf16[1024,256]{1,0:T(8,128)(2,1)S(1)} custom-call(s32[2]{0:T(128)S(1)} %copy-done.79, bf16[1024,256]{1,0:T(8,128)(2,1)S(1)} %get-tuple-element.148.q, f32[8,128,1]{2,1,0:T(8,128)S(1)} %copy.72.m, f32[8,1,512]{2,1,0:T(1,128)S(1)} %broadcast_in_dim.34.th, bf16[8,64,128]{2,1,0:T(8,128)(2,1)S(1)} %get-tuple-element.149.refs_0_, ...), custom_call_target="tpu_custom_call" | custom-call | flops 1024 | bytes 1024 | tf_op jit(solution)/shard_map/pallas_call | solution.py:219
  170.0 3.8 collective-permute-done.20.c
  178.2 11.3 %collective-permute-done.21.refs_0_ = bf16[128,2048]{1,0:T(8,128)(2,1)S(1)} collective-permute-done((bf16[128,2048]{1,0:T(8,128)(2,1)S(1)}, bf16[128,2048]{1,0:T(8,128)(2,1)S(1)}, u32[]{:S(2)}, u32[]{:S(2)}) %collective-permute-start.21) | collective-permute-done | bytes 524320 | tf_op jit(solution)/shard_map/ppermute | solution.py:34
  189.4 11.9 %collective-permute-done.22.refs_1_ = bf16[128,2048]{1,0:T(8,128)(2,1)S(1)} collective-permute-done((bf16[128,2048]{1,0:T(8,128)(2,1)S(1)}, bf16[128,2048]{1,0:T(8,128)(2,1)S(1)}, u32[]{:S(2)}, u32[]{:S(2)}) %collective-permute-start.22) | collective-permute-done | bytes 524320 | tf_op jit(solution)/shard_map/ppermute | solution.py:34
  206.4 12.3 %collective-permute-done.26.refs_3_ = bf16[128,2048]{1,0:T(8,128)(2,1)S(1)} collective-permute-done((bf16[128,2048]{1,0:T(8,128)(2,1)S(1)}, bf16[128,2048]{1,0:T(8,128)(2,1)S(1)}, u32[]{:S(2)}, u32[]{:S(2)}) %collective-permute-start.26) | collective-permute-done | bytes 524320 | tf_op jit(solution)/shard_map/ppermute | solution.py:34
  218.7 9.6 %collective-permute-done.25.refs_2_ = bf16[128,2048]{1,0:T(8,128)(2,1)S(1)} collective-permute-done((bf16[128,2048]{1,0:T(8,128)(2,1)S(1)}, bf16[128,2048]{1,0:T(8,128)(2,1)S(1)}, u32[]{:S(2)}, u32[]{:S(2)}) %collective-permute-start.25) | collective-permute-done | bytes 524320 | tf_op jit(solution)/shard_map/ppermute | solution.py:34
  228.7 2.9 pad_maximum_fusion.1.refs_2_.dy
  232.0 3.0 all-gather.5.cloned.1.call-done.w
  235.0 2.6 copy-done
  237.7 3.9 shard_map.220
  241.6 5.9 %shard_map.221 = (bf16[512,1408]{1,0:T(8,128)(2,1)S(1)}, bf16[512,704]{1,0:T(8,128)(2,1)S(1)}) custom-call(bf16[512,2048]{1,0:T(8,128)(2,1)} %collective-permute-done.27.x.refs_1_, bf16[2048,1408]{1,0:T(8,128)(2,1)S(1)} %copy-done.1), custom_call_target="tpu_custom_call" | custom-call | flops 1024 | bytes 1024 | tf_op jit(solution)/shard_map/pallas_call | solution.py:393
  248.6 5.4 %shard_map.222 = bf16[704,2048]{1,0:T(8,128)(2,1)S(1)} custom-call(bf16[512,704]{1,0:T(8,128)(2,1)S(1)} %get-tuple-element.170.refs_0_.h, bf16[512,704]{1,0:T(8,128)(2,1)S(1)} %get-tuple-element.176.refs_1_.h, bf16[512,2048]{1,0:T(8,128)(2,1)} %pad_maximum_fusion.1.refs_2_.dy, bf16[512,2048]{1,0:T(8,128)(2,1)} %collective-permute-done.28.refs_3_.dy), custom_call_target="tpu_custom_call" | custom-call | flops 1024 | bytes 1024 | tf_op jit(solution)/shard_map/pallas_call | solution.py:80
  256.8 2.6 copy-done.2
  259.4 1.8 copy-done.9
  264.0 9.9 %shard_map.223 = (bf16[512,1408]{1,0:T(8,128)(2,1)S(1)}, bf16[512,2048]{1,0:T(8,128)(2,1)S(1)}, bf16[512,2048]{1,0:T(8,128)(2,1)S(1)}) custom-call(bf16[512,1408]{1,0:T(8,128)(2,1)S(1)} %copy-done.42, bf16[512,704]{1,0:T(8,128)(2,1)S(1)} %copy-done.28, bf16[512,2048]{1,0:T(8,128)(2,1)} %collective-permute-done.28.refs_3_.dy, ...), custom_call_target="tpu_custom_call" | custom-call | flops 1024 | bytes 1024 | tf_op jit(solution)/shard_map/pallas_call | solution.py:429
  274.0 9.8 %shard_map.224 = (bf16[512,1408]{1,0:T(8,128)(2,1)S(1)}, bf16[512,2048]{1,0:T(8,128)(2,1)S(1)}, bf16[512,2048]{1,0:T(8,128)(2,1)S(1)}) custom-call(bf16[512,1408]{1,0:T(8,128)(2,1)S(1)} %copy-done.40, bf16[512,704]{1,0:T(8,128)(2,1)S(1)} %copy-done.26, bf16[512,2048]{1,0:T(8,128)(2,1)} %pad_maximum_fusion.1.refs_2_.dy, bf16[2048,1408]{1,0:T(8,128)(2,1)S(1)} %copy-done.2, ...), custom_call_target="tpu_custom_call" | custom-call | flops 1024 | bytes 1024 | tf_op jit(solution)/shard_map/pallas_call | solution.py:429
  292.2 9.3 %shard_map.227 = bf16[2048,1408]{1,0:T(8,128)(2,1)S(1)} custom-call(bf16[512,2048]{1,0:T(8,128)(2,1)S(1)} %shard_map.219.x.refs_0_, bf16[512,2048]{1,0:T(8,128)(2,1)} %collective-permute-done.27.x.refs_1_, bf16[512,1408]{1,0:T(8,128)(2,1)S(1)} %get-tuple-element.193.refs_2_, bf16[512,1408]{1,0:T(8,128)(2,1)S(1)} %get-tuple-element.179.refs_3_), custom_call_target="tpu_custom_call" | custom-call | flops 1024 | bytes 1024 | tf_op jit(solution)/shard_map/pallas_call | solution.py:80
  301.6 2.4 copy-done.3
  310.2 3.4 collective-permute-done.32.refs_1_
  316.1 2.4 shard_map.228
  323.1 12.3 %collective-permute-done.36.refs_3_ = bf16[128,2048]{1,0:T(8,128)(2,1)S(1)} collective-permute-done((bf16[128,2048]{1,0:T(8,128)(2,1)S(1)}, bf16[128,2048]{1,0:T(8,128)(2,1)S(1)}, u32[]{:S(2)}, u32[]{:S(2)}) %collective-permute-start.36) | collective-permute-done | bytes 524320 | tf_op jit(solution)/shard_map/ppermute | solution.py:34
  335.4 9.2 %collective-permute-done.35.refs_2_ = bf16[128,2048]{1,0:T(8,128)(2,1)S(1)} collective-permute-done((bf16[128,2048]{1,0:T(8,128)(2,1)S(1)}, bf16[128,2048]{1,0:T(8,128)(2,1)S(1)}, u32[]{:S(2)}, u32[]{:S(2)}) %collective-permute-start.35) | collective-permute-done | bytes 524320 | tf_op jit(solution)/shard_map/ppermute | solution.py:34
  349.0 17.0 %shard_map.230 = (bf16[1024,256]{1,0:T(8,128)(2,1)S(1)}, f32[8,4,64,128]{3,2,1,0:T(8,128)S(1)}, bf16[8,4,64,128]{3,2,1,0:T(8,128)(2,1)S(1)}) custom-call(s32[2]{0:T(128)S(1)} %copy-done.80, bf16[512,2048]{1,0:T(8,128)(2,1)S(1)} %shard_map.229.s.ba, bf16[512,2048]{1,0:T(8,128)(2,1)S(1)} %collective-permute-done.37.o.bb, bf16[256,2048]{1,0:T(8,128)(2,1)S(1)} %bitcast.34, ...), custom_call_target="tpu_custom_call" | custom-call | flops 1024 | bytes 1024 | tf_op jit(solution)/shard_map/pallas_call | solution.py:269
  366.1 5.0 collective-permute-done.39
  372.1 1.7 collective-permute-done.41.b
  373.9 2.3 collective-permute-start.42
  376.7 2.5 collective-permute-start.44
  379.2 5.8 %collective-permute-done.42.refs_0_ = bf16[8,64,128]{2,1,0:T(8,128)(2,1)S(1)} collective-permute-done((bf16[8,64,128]{2,1,0:T(8,128)(2,1)S(1)}, bf16[8,64,128]{2,1,0:T(8,128)(2,1)S(1)}, u32[]{:S(2)}, u32[]{:S(2)}) %collective-permute-start.42) | collective-permute-done | bytes 131104 | tf_op jit(solution)/shard_map/ppermute | solution.py:38
  385.1 9.0 %collective-permute-done.43.refs_1_ = bf16[8,64,128]{2,1,0:T(8,128)(2,1)S(1)} collective-permute-done((bf16[8,64,128]{2,1,0:T(8,128)(2,1)S(1)}, bf16[8,64,128]{2,1,0:T(8,128)(2,1)S(1)}, u32[]{:S(2)}, u32[]{:S(2)}) %collective-permute-start.43) | collective-permute-done | bytes 131104 | tf_op jit(solution)/shard_map/ppermute | solution.py:38
  395.5 5.9 %shard_map.233 = (bf16[256,1152]{1,0:T(8,128)(2,1)S(1)}, bf16[256,1152]{1,0:T(8,128)(2,1)}, bf16[256,1152]{1,0:T(8,128)(2,1)S(1)}, bf16[256,1152]{1,0:T(8,128)(2,1)}) custom-call(s32[2]{0:T(128)S(1)} %copy-done.80, bf16[1024,2048]{1,0:T(8,128)(2,1)S(1)} %copy-done.20, bf16[1024,384]{1,0:T(8,128)(2,1)S(1)} %maximum_maximum_fusion.g.a, ...), custom_call_target="tpu_custom_call" | custom-call | flops 1024 | bytes 1024 | tf_op jit(solution)/shard_map/pallas_call | solution.py:366
  403.0 13.7 %collective-permute-start.49 = (bf16[256,1152]{1,0:T(8,128)(2,1)}, bf16[256,1152]{1,0:T(8,128)(2,1)S(1)}, u32[]{:S(2)}, u32[]{:S(2)}) collective-permute-start(bf16[256,1152]{1,0:T(8,128)(2,1)} %get-tuple-element.224), channel_id=1, source_target_pairs={{0,1},{1,2},{2,3},{3,0},{4,5},{5,6},{6,7},{7,4},{8,9},{9,10},{10,1... | collective-permute-start | bytes 1769480 | tf_op jit(solution)/shard_map/ppermute | solution.py:38
  416.7 2.8 shard_map.234
  424.3 14.1 %collective-permute-done.49.refs_1_ = bf16[256,1152]{1,0:T(8,128)(2,1)S(1)} collective-permute-done((bf16[256,1152]{1,0:T(8,128)(2,1)}, bf16[256,1152]{1,0:T(8,128)(2,1)S(1)}, u32[]{:S(2)}, u32[]{:S(2)}) %collective-permute-start.49) | collective-permute-done | bytes 589856 | tf_op jit(solution)/shard_map/ppermute | solution.py:38
  439.2 9.4 %collective-permute-done.50.refs_2_ = bf16[256,1152]{1,0:T(8,128)(2,1)S(1)} collective-permute-done((bf16[256,1152]{1,0:T(8,128)(2,1)}, bf16[256,1152]{1,0:T(8,128)(2,1)S(1)}, u32[]{:S(2)}, u32[]{:S(2)}) %collective-permute-start.50) | collective-permute-done | bytes 589856 | tf_op jit(solution)/shard_map/ppermute | solution.py:38
  449.5 3.7 all-to-all-start.2
  453.2 5.2 %collective-permute-start.51 = (bf16[256,1152]{1,0:T(8,128)(2,1)}, bf16[256,1152]{1,0:T(8,128)(2,1)S(1)}, u32[]{:S(2)}, u32[]{:S(2)}) collective-permute-start(bf16[256,1152]{1,0:T(8,128)(2,1)} %copy-done.81), channel_id=1, source_target_pairs={{0,2},{1,3},{2,0},{3,1},{4,6},{5,7},{6,4},{7,5},{8,10},{9,11},{10,... | collective-permute-start | bytes 1769480 | tf_op jit(solution)/shard_map/ppermute | solution.py:38
  458.4 2.9 fusion.8
  462.5 1.8 fusion.2
  464.3 20.8 %collective-permute-done.51.refs_0_ = bf16[256,1152]{1,0:T(8,128)(2,1)S(1)} collective-permute-done((bf16[256,1152]{1,0:T(8,128)(2,1)}, bf16[256,1152]{1,0:T(8,128)(2,1)S(1)}, u32[]{:S(2)}, u32[]{:S(2)}) %collective-permute-start.51) | collective-permute-done | bytes 589856 | tf_op jit(solution)/shard_map/ppermute | solution.py:38
  488.2 4.1 all-to-all-start.3
  492.3 3.5 fusion.6
  497.1 3.5 all-to-all-done.3.x
  500.6 3.3 shard_map.237
  (331 shorter events, 84.3 us)
Async XLA Ops:
  7.2 67.4 %copy-start.31 = (bf16[64,5632]{1,0:T(8,128)(2,1)S(1)}, bf16[64,5632]{1,0:T(8,128)(2,1)}, u32[]{:S(2)}) copy-start(bf16[64,5632]{1,0:T(8,128)(2,1)} %u.2) | copy-start | bytes 2162692
  7.2 67.4 %copy-start.29 = (bf16[64,5632]{1,0:T(8,128)(2,1)S(1)}, bf16[64,5632]{1,0:T(8,128)(2,1)}, u32[]{:S(2)}) copy-start(bf16[64,5632]{1,0:T(8,128)(2,1)} %g.2) | copy-start | bytes 2162692
  7.2 100.5 %all-gather.3.cloned.1.call-start = ((), (), s32[]{:S(2)}) async-start(), calls=%async_computation.6 | async-start | bytes 3604480 | tf_op jit(solution)/shard_map/all_gather | solution.py:753
  7.9 19.7 %collective-permute-start.1 = (bf16[64,2048]{1,0:T(8,128)(2,1)}, bf16[64,2048]{1,0:T(8,128)(2,1)S(1)}, u32[]{:S(2)}, u32[]{:S(2)}) collective-permute-start(bf16[64,2048]{1,0:T(8,128)(2,1)} %refs_0_.1), channel_id=1, source_target_pairs={{0,2},{1,3},{2,0},{3,1},{4,6},{5,7},{6,4},{7,5},{8,10},{9,11},{10,... | collective-permute-start | bytes 786440 | tf_op jit(solution)/shard_map/ppermute | solution.py:38
  12.0 36.7 %collective-permute-start = (bf16[64,2048]{1,0:T(8,128)(2,1)}, bf16[64,2048]{1,0:T(8,128)(2,1)S(1)}, u32[]{:S(2)}, u32[]{:S(2)}) collective-permute-start(bf16[64,2048]{1,0:T(8,128)(2,1)} %refs_0_.1), channel_id=1, source_target_pairs={{0,3},{1,0},{2,1},{3,2},{4,7},{5,4},{6,5},{7,6},{8,11},{9,8},{10,9... | collective-permute-start | bytes 786440 | tf_op jit(solution)/shard_map/ppermute | solution.py:38
  13.4 49.4 %collective-permute-start.5 = (bf16[128,2048]{1,0:T(8,128)(2,1)}, bf16[128,2048]{1,0:T(8,128)(2,1)S(1)}, u32[]{:S(2)}, u32[]{:S(2)}) collective-permute-start(bf16[128,2048]{1,0:T(8,128)(2,1)} %bitcast.38), channel_id=1, source_target_pairs={{0,24},{4,28},{8,16},{12,20},{16,8},{20,12},{24,0},{28,4},{1,25},{... | collective-permute-start | bytes 1572872 | tf_op jit(solution)/shard_map/ppermute | solution.py:34
  15.8 47.0 %collective-permute-start.4 = (bf16[128,2048]{1,0:T(8,128)(2,1)}, bf16[128,2048]{1,0:T(8,128)(2,1)}, u32[]{:S(2)}, u32[]{:S(2)}) collective-permute-start(bf16[128,2048]{1,0:T(8,128)(2,1)} %bitcast.39), channel_id=1, source_target_pairs={{0,16},{4,20},{8,24},{12,28},{16,0},{20,4},{24,8},{28,12},{1,17},{... | collective-permute-start | bytes 1572872 | tf_op jit(solution)/shard_map/ppermute | solution.py:34
  16.4 47.3 %collective-permute-start.3 = (bf16[128,2048]{1,0:T(8,128)(2,1)}, bf16[128,2048]{1,0:T(8,128)(2,1)}, u32[]{:S(2)}, u32[]{:S(2)}) collective-permute-start(bf16[128,2048]{1,0:T(8,128)(2,1)} %bitcast.40), channel_id=1, source_target_pairs={{0,8},{4,12},{8,0},{12,4},{16,24},{20,28},{24,16},{28,20},{1,9},{5... | collective-permute-start | bytes 1572872 | tf_op jit(solution)/shard_map/ppermute | solution.py:34
  21.4 41.4 %all-to-all-start = ((bf16[8,64,384]{2,1,0:T(8,128)(2,1)}), bf16[8,64,384]{2,1,0:T(8,128)(2,1)S(1)}, u32[]{:S(2)}, u32[]{:S(2)}) async-start(bf16[8,64,384]{2,1,0:T(8,128)(2,1)} %bitcast.31), calls=%async_computation | async-start | bytes 786432 | tf_op jit(solution)/shard_map/all_to_all | solution.py:751
  27.6 35.2 %collective-permute-start.2 = (bf16[64,2048]{1,0:T(8,128)(2,1)S(1)}, bf16[64,2048]{1,0:T(8,128)(2,1)S(1)}, u32[]{:S(2)}, u32[]{:S(2)}) collective-permute-start(bf16[64,2048]{1,0:T(8,128)(2,1)S(1)} %copy-done.66), channel_id=1, source_target_pairs={{0,1},{1,2},{2,3},{3,0},{4,5},{5,6},{6,7},{7,4},{8,9},{9,10},{10,1... | collective-permute-start | bytes 786440 | tf_op jit(solution)/shard_map/ppermute | solution.py:38
  63.6 25.1 %collective-permute-start.9 = (bf16[8,64,384]{2,1,0:T(8,128)(2,1)S(1)}, bf16[8,64,384]{2,1,0:T(8,128)(2,1)S(1)}, u32[]{:S(2)}, u32[]{:S(2)}) collective-permute-start(bf16[8,64,384]{2,1,0:T(8,128)(2,1)S(1)} %all-to-all-done.refs_0_), channel_id=1, source_target_pairs={{0,1},{1,2},{2,3},{3,0},{4,5},{5,6},{6,7},{7,4},{8,9},{9,10},{10,1... | collective-permute-start | bytes 1179656 | tf_op jit(solution)/shard_map/ppermute | solution.py:38
  66.2 41.5 %collective-permute-start.8 = (bf16[8,64,384]{2,1,0:T(8,128)(2,1)S(1)}, bf16[8,64,384]{2,1,0:T(8,128)(2,1)}, u32[]{:S(2)}, u32[]{:S(2)}) collective-permute-start(bf16[8,64,384]{2,1,0:T(8,128)(2,1)S(1)} %all-to-all-done.refs_0_), channel_id=1, source_target_pairs={{0,2},{1,3},{2,0},{3,1},{4,6},{5,7},{6,4},{7,5},{8,10},{9,11},{10,... | collective-permute-start | bytes 1179656 | tf_op jit(solution)/shard_map/ppermute | solution.py:38
  74.6 33.1 %collective-permute-start.7 = (bf16[8,64,384]{2,1,0:T(8,128)(2,1)S(1)}, bf16[8,64,384]{2,1,0:T(8,128)(2,1)}, u32[]{:S(2)}, u32[]{:S(2)}) collective-permute-start(bf16[8,64,384]{2,1,0:T(8,128)(2,1)S(1)} %all-to-all-done.refs_0_), channel_id=1, source_target_pairs={{0,3},{1,0},{2,1},{3,2},{4,7},{5,4},{6,5},{7,6},{8,11},{9,8},{10,9... | collective-permute-start | bytes 1179656 | tf_op jit(solution)/shard_map/ppermute | solution.py:38
  76.0 31.7 %all-to-all-start.1 = ((bf16[8,64,1408]{2,1,0:T(8,128)(2,1)}), bf16[8,64,1408]{2,1,0:T(8,128)(2,1)}, u32[]{:S(2)}, u32[]{:S(2)}) async-start(bf16[8,64,1408]{2,1,0:T(8,128)(2,1)} %shard_map.212), calls=%async_computation.1 | async-start | bytes 2883584 | tf_op jit(solution)/shard_map/all_to_all | solution.py:770
  80.5 154.6 %all-gather.5.cloned.1.call-start = ((), (), s32[]{:S(2)}) async-start(), calls=%async_computation.7 | async-start | bytes 7208960 | tf_op jit(solution)/shard_map/all_gather | solution.py:777
  83.6 26.5 %collective-permute-start.6 = (bf16[512,2048]{1,0:T(8,128)(2,1)}, bf16[512,2048]{1,0:T(8,128)(2,1)}, u32[]{:S(2)}, u32[]{:S(2)}) collective-permute-start(bf16[512,2048]{1,0:T(8,128)(2,1)} %pad_maximum_fusion.e), channel_id=1, source_target_pairs={{0,4},{4,0},{8,12},{12,8},{16,20},{20,16},{24,28},{28,24},{1,5},{5... | collective-permute-start | bytes 6291464 | tf_op jit(solution)/shard_map/ppermute | solution.py:34
  84.2 71.8 %copy-start.96 = (f32[8,512]{1,0:T(8,128)}, f32[8,512]{1,0:T(8,128)S(1)}, u32[]{:S(2)}) copy-start(f32[8,512]{1,0:T(8,128)S(1)} %fusion.13) | copy-start | bytes 49156
  107.7 205.9 %reduce-scatter.3.cloned.1.call-start = ((), (), s32[]{:S(2)}) async-start(), calls=%async_computation.8 | async-start | bytes 3604480 | tf_op jit(solution)/shard_map/reduce_scatter | solution.py:806
  120.0 49.5 %copy-start.37 = (bf16[1024,256]{1,0:T(8,128)(2,1)}, bf16[1024,256]{1,0:T(8,128)(2,1)S(1)}, u32[]{:S(2)}) copy-start(bf16[1024,256]{1,0:T(8,128)(2,1)S(1)} %get-tuple-element.148.q) | copy-start | bytes 1572868
  120.0 35.3 %collective-permute-start.15 = (bf16[128,2048]{1,0:T(8,128)(2,1)}, bf16[128,2048]{1,0:T(8,128)(2,1)S(1)}, u32[]{:S(2)}, u32[]{:S(2)}) collective-permute-start(bf16[128,2048]{1,0:T(8,128)(2,1)} %bitcast.11.grad_out), channel_id=1, source_target_pairs={{0,24},{4,28},{8,16},{12,20},{16,8},{20,12},{24,0},{28,4},{1,25},{... | collective-permute-start | bytes 1572872 | tf_op jit(solution)/shard_map/ppermute | solution.py:34
  122.5 32.8 %collective-permute-start.14 = (bf16[128,2048]{1,0:T(8,128)(2,1)}, bf16[128,2048]{1,0:T(8,128)(2,1)}, u32[]{:S(2)}, u32[]{:S(2)}) collective-permute-start(bf16[128,2048]{1,0:T(8,128)(2,1)} %bitcast.11.grad_out), channel_id=1, source_target_pairs={{0,16},{4,20},{8,24},{12,28},{16,0},{20,4},{24,8},{28,12},{1,17},{... | collective-permute-start | bytes 1572872 | tf_op jit(solution)/shard_map/ppermute | solution.py:34
  123.0 32.3 %collective-permute-start.13 = (bf16[128,2048]{1,0:T(8,128)(2,1)}, bf16[128,2048]{1,0:T(8,128)(2,1)}, u32[]{:S(2)}, u32[]{:S(2)}) collective-permute-start(bf16[128,2048]{1,0:T(8,128)(2,1)} %bitcast.11.grad_out), channel_id=1, source_target_pairs={{0,8},{4,12},{8,0},{12,4},{16,24},{20,28},{24,16},{28,20},{1,9},{5... | collective-permute-start | bytes 1572872 | tf_op jit(solution)/shard_map/ppermute | solution.py:34
  123.5 18.8 %collective-permute-start.12 = (bf16[8,64,128]{2,1,0:T(8,128)(2,1)S(1)}, bf16[8,64,128]{2,1,0:T(8,128)(2,1)S(1)}, u32[]{:S(2)}, u32[]{:S(2)}) collective-permute-start(bf16[8,64,128]{2,1,0:T(8,128)(2,1)S(1)} %get-tuple-element.149.refs_0_), channel_id=1, source_target_pairs={{0,1},{1,2},{2,3},{3,0},{4,5},{5,6},{6,7},{7,4},{8,9},{9,10},{10,1... | collective-permute-start | bytes 393224 | tf_op jit(solution)/shard_map/ppermute | solution.py:38
  132.3 19.3 %collective-permute-start.11 = (bf16[8,64,128]{2,1,0:T(8,128)(2,1)S(1)}, bf16[8,64,128]{2,1,0:T(8,128)(2,1)S(1)}, u32[]{:S(2)}, u32[]{:S(2)}) collective-permute-start(bf16[8,64,128]{2,1,0:T(8,128)(2,1)S(1)} %get-tuple-element.149.refs_0_), channel_id=1, source_target_pairs={{0,2},{1,3},{2,0},{3,1},{4,6},{5,7},{6,4},{7,5},{8,10},{9,11},{10,... | collective-permute-start | bytes 393224 | tf_op jit(solution)/shard_map/ppermute | solution.py:38
  142.4 12.9 %collective-permute-start.10 = (bf16[8,64,128]{2,1,0:T(8,128)(2,1)S(1)}, bf16[8,64,128]{2,1,0:T(8,128)(2,1)S(1)}, u32[]{:S(2)}, u32[]{:S(2)}) collective-permute-start(bf16[8,64,128]{2,1,0:T(8,128)(2,1)S(1)} %get-tuple-element.149.refs_0_), channel_id=1, source_target_pairs={{0,3},{1,0},{2,1},{3,2},{4,7},{5,4},{6,5},{7,6},{8,11},{9,8},{10,9... | collective-permute-start | bytes 393224 | tf_op jit(solution)/shard_map/ppermute | solution.py:38
  151.5 6.8 %collective-permute-start.16 = (bf16[8,64,128]{2,1,0:T(8,128)(2,1)S(1)}, bf16[8,64,128]{2,1,0:T(8,128)(2,1)S(1)}, u32[]{:S(2)}, u32[]{:S(2)}) collective-permute-start(bf16[8,64,128]{2,1,0:T(8,128)(2,1)S(1)} %get-tuple-element.149.refs_0_), channel_id=1, source_target_pairs={{0,4},{4,0},{8,12},{12,8},{16,20},{20,16},{24,28},{28,24},{1,5},{5... | collective-permute-start | bytes 393224 | tf_op jit(solution)/shard_map/ppermute | solution.py:34
  155.3 3.0 collective-permute-start.17
  155.4 3.0 collective-permute-start.18
  155.9 2.5 collective-permute-start.19
  169.6 4.2 collective-permute-start.20
  174.6 14.8 %collective-permute-start.21 = (bf16[128,2048]{1,0:T(8,128)(2,1)S(1)}, bf16[128,2048]{1,0:T(8,128)(2,1)S(1)}, u32[]{:S(2)}, u32[]{:S(2)}) collective-permute-start(bf16[128,2048]{1,0:T(8,128)(2,1)S(1)} %get-tuple-element.157), channel_id=1, source_target_pairs={{0,8},{4,12},{8,0},{12,4},{16,24},{20,28},{24,16},{28,20},{1,9},{5... | collective-permute-start | bytes 1572872 | tf_op jit(solution)/shard_map/ppermute | solution.py:34
  176.2 25.1 %collective-permute-start.22 = (bf16[128,2048]{1,0:T(8,128)(2,1)S(1)}, bf16[128,2048]{1,0:T(8,128)(2,1)S(1)}, u32[]{:S(2)}, u32[]{:S(2)}) collective-permute-start(bf16[128,2048]{1,0:T(8,128)(2,1)S(1)} %get-tuple-element.158), channel_id=1, source_target_pairs={{0,16},{4,20},{8,24},{12,28},{16,0},{20,4},{24,8},{28,12},{1,17},{... | collective-permute-start | bytes 1572872 | tf_op jit(solution)/shard_map/ppermute | solution.py:34
  177.7 23.6 %collective-permute-start.23 = (bf16[128,2048]{1,0:T(8,128)(2,1)S(1)}, bf16[128,2048]{1,0:T(8,128)(2,1)S(1)}, u32[]{:S(2)}, u32[]{:S(2)}) collective-permute-start(bf16[128,2048]{1,0:T(8,128)(2,1)S(1)} %get-tuple-element.159), channel_id=1, source_target_pairs={{0,24},{4,28},{8,16},{12,20},{16,8},{20,12},{24,0},{28,4},{1,25},{... | collective-permute-start | bytes 1572872 | tf_op jit(solution)/shard_map/ppermute | solution.py:34
  202.9 15.8 %collective-permute-start.26 = (bf16[128,2048]{1,0:T(8,128)(2,1)S(1)}, bf16[128,2048]{1,0:T(8,128)(2,1)S(1)}, u32[]{:S(2)}, u32[]{:S(2)}) collective-permute-start(bf16[128,2048]{1,0:T(8,128)(2,1)S(1)} %get-tuple-element.164.refs_0_), channel_id=1, source_target_pairs={{0,24},{4,28},{8,16},{12,20},{16,8},{20,12},{24,0},{28,4},{1,25},{... | collective-permute-start | bytes 1572872 | tf_op jit(solution)/shard_map/ppermute | solution.py:34
  204.4 23.9 %collective-permute-start.25 = (bf16[128,2048]{1,0:T(8,128)(2,1)S(1)}, bf16[128,2048]{1,0:T(8,128)(2,1)S(1)}, u32[]{:S(2)}, u32[]{:S(2)}) collective-permute-start(bf16[128,2048]{1,0:T(8,128)(2,1)S(1)} %get-tuple-element.164.refs_0_), channel_id=1, source_target_pairs={{0,16},{4,20},{8,24},{12,28},{16,0},{20,4},{24,8},{28,12},{1,17},{... | collective-permute-start | bytes 1572872 | tf_op jit(solution)/shard_map/ppermute | solution.py:34
  205.6 22.7 %collective-permute-start.24 = (bf16[128,2048]{1,0:T(8,128)(2,1)S(1)}, bf16[128,2048]{1,0:T(8,128)(2,1)S(1)}, u32[]{:S(2)}, u32[]{:S(2)}) collective-permute-start(bf16[128,2048]{1,0:T(8,128)(2,1)S(1)} %get-tuple-element.164.refs_0_), channel_id=1, source_target_pairs={{0,8},{4,12},{8,0},{12,4},{16,24},{20,28},{24,16},{28,20},{1,9},{5... | collective-permute-start | bytes 1572872 | tf_op jit(solution)/shard_map/ppermute | solution.py:34
  228.5 13.1 %collective-permute-start.27 = (bf16[512,2048]{1,0:T(8,128)(2,1)S(1)}, bf16[512,2048]{1,0:T(8,128)(2,1)}, u32[]{:S(2)}, u32[]{:S(2)}) collective-permute-start(bf16[512,2048]{1,0:T(8,128)(2,1)S(1)} %shard_map.219.x.refs_0_), channel_id=1, source_target_pairs={{0,4},{4,0},{8,12},{12,8},{16,20},{20,16},{24,28},{28,24},{1,5},{5... | collective-permute-start | bytes 6291464 | tf_op jit(solution)/shard_map/ppermute | solution.py:34
  231.6 17.0 %collective-permute-start.28 = (bf16[512,2048]{1,0:T(8,128)(2,1)}, bf16[512,2048]{1,0:T(8,128)(2,1)}, u32[]{:S(2)}, u32[]{:S(2)}) collective-permute-start(bf16[512,2048]{1,0:T(8,128)(2,1)} %pad_maximum_fusion.1.refs_2_.dy), channel_id=1, source_target_pairs={{0,4},{4,0},{8,12},{12,8},{16,20},{20,16},{24,28},{28,24},{1,5},{5... | collective-permute-start | bytes 6291464 | tf_op jit(solution)/shard_map/ppermute | solution.py:34
  256.5 193.0 %reduce-scatter.5.cloned.1.call-start = ((), (), s32[]{:S(2)}) async-start(), calls=%async_computation.9 | async-start | bytes 7208960 | tf_op jit(solution)/shard_map/reduce_scatter | solution.py:817
  273.9 9.9 %collective-permute-start.29 = (bf16[512,2048]{1,0:T(8,128)(2,1)S(1)}, bf16[512,2048]{1,0:T(8,128)(2,1)S(1)}, u32[]{:S(2)}, u32[]{:S(2)}) collective-permute-start(bf16[512,2048]{1,0:T(8,128)(2,1)S(1)} %get-tuple-element.184), channel_id=1, source_target_pairs={{0,4},{4,0},{8,12},{12,8},{16,20},{20,16},{24,28},{28,24},{1,5},{5... | collective-permute-start | bytes 6291464 | tf_op jit(solution)/shard_map/ppermute | solution.py:34
  286.6 4.3 collective-permute-start.30
  287.1 23.1 %collective-permute-start.31 = (bf16[128,2048]{1,0:T(8,128)(2,1)}, bf16[128,2048]{1,0:T(8,128)(2,1)}, u32[]{:S(2)}, u32[]{:S(2)}) collective-permute-start(bf16[128,2048]{1,0:T(8,128)(2,1)} %get-tuple-element.185), channel_id=1, source_target_pairs={{0,8},{4,12},{8,0},{12,4},{16,24},{20,28},{24,16},{28,20},{1,9},{5... | collective-permute-start | bytes 1572872 | tf_op jit(solution)/shard_map/ppermute | solution.py:34
  288.5 25.1 %collective-permute-start.32 = (bf16[128,2048]{1,0:T(8,128)(2,1)}, bf16[128,2048]{1,0:T(8,128)(2,1)}, u32[]{:S(2)}, u32[]{:S(2)}) collective-permute-start(bf16[128,2048]{1,0:T(8,128)(2,1)} %get-tuple-element.186), channel_id=1, source_target_pairs={{0,16},{4,20},{8,24},{12,28},{16,0},{20,4},{24,8},{28,12},{1,17},{... | collective-permute-start | bytes 1572872 | tf_op jit(solution)/shard_map/ppermute | solution.py:34
  289.9 23.7 %collective-permute-start.33 = (bf16[128,2048]{1,0:T(8,128)(2,1)}, bf16[128,2048]{1,0:T(8,128)(2,1)}, u32[]{:S(2)}, u32[]{:S(2)}) collective-permute-start(bf16[128,2048]{1,0:T(8,128)(2,1)} %get-tuple-element.187), channel_id=1, source_target_pairs={{0,24},{4,28},{8,16},{12,20},{16,8},{20,12},{24,0},{28,4},{1,25},{... | collective-permute-start | bytes 1572872 | tf_op jit(solution)/shard_map/ppermute | solution.py:34
  319.5 15.9 %collective-permute-start.36 = (bf16[128,2048]{1,0:T(8,128)(2,1)S(1)}, bf16[128,2048]{1,0:T(8,128)(2,1)S(1)}, u32[]{:S(2)}, u32[]{:S(2)}) collective-permute-start(bf16[128,2048]{1,0:T(8,128)(2,1)S(1)} %get-tuple-element.201.refs_0_), channel_id=1, source_target_pairs={{0,24},{4,28},{8,16},{12,20},{16,8},{20,12},{24,0},{28,4},{1,25},{... | collective-permute-start | bytes 1572872 | tf_op jit(solution)/shard_map/ppermute | solution.py:34
  321.1 23.5 %collective-permute-start.35 = (bf16[128,2048]{1,0:T(8,128)(2,1)S(1)}, bf16[128,2048]{1,0:T(8,128)(2,1)S(1)}, u32[]{:S(2)}, u32[]{:S(2)}) collective-permute-start(bf16[128,2048]{1,0:T(8,128)(2,1)S(1)} %get-tuple-element.201.refs_0_), channel_id=1, source_target_pairs={{0,16},{4,20},{8,24},{12,28},{16,0},{20,4},{24,8},{28,12},{1,17},{... | collective-permute-start | bytes 1572872 | tf_op jit(solution)/shard_map/ppermute | solution.py:34
  322.3 22.3 %collective-permute-start.34 = (bf16[128,2048]{1,0:T(8,128)(2,1)S(1)}, bf16[128,2048]{1,0:T(8,128)(2,1)S(1)}, u32[]{:S(2)}, u32[]{:S(2)}) collective-permute-start(bf16[128,2048]{1,0:T(8,128)(2,1)S(1)} %get-tuple-element.201.refs_0_), channel_id=1, source_target_pairs={{0,8},{4,12},{8,0},{12,4},{16,24},{20,28},{24,16},{28,20},{1,9},{5... | collective-permute-start | bytes 1572872 | tf_op jit(solution)/shard_map/ppermute | solution.py:34
  344.7 4.2 collective-permute-start.37
  344.9 21.2 %collective-permute-start.38 = (bf16[128,2048]{1,0:T(8,128)(2,1)S(1)}, bf16[128,2048]{1,0:T(8,128)(2,1)S(1)}, u32[]{:S(2)}, u32[]{:S(2)}) collective-permute-start(bf16[128,2048]{1,0:T(8,128)(2,1)S(1)} %copy-done.87), channel_id=1, source_target_pairs={{0,8},{4,12},{8,0},{12,4},{16,24},{20,28},{24,16},{28,20},{1,9},{5... | collective-permute-start | bytes 1572872 | tf_op jit(solution)/shard_map/ppermute | solution.py:34
  345.9 25.2 %collective-permute-start.39 = (bf16[128,2048]{1,0:T(8,128)(2,1)S(1)}, bf16[128,2048]{1,0:T(8,128)(2,1)S(1)}, u32[]{:S(2)}, u32[]{:S(2)}) collective-permute-start(bf16[128,2048]{1,0:T(8,128)(2,1)S(1)} %copy-done.85), channel_id=1, source_target_pairs={{0,16},{4,20},{8,24},{12,28},{16,0},{20,4},{24,8},{28,12},{1,17},{... | collective-permute-start | bytes 1572872 | tf_op jit(solution)/shard_map/ppermute | solution.py:34
  347.1 24.0 %collective-permute-start.40 = (bf16[128,2048]{1,0:T(8,128)(2,1)S(1)}, bf16[128,2048]{1,0:T(8,128)(2,1)S(1)}, u32[]{:S(2)}, u32[]{:S(2)}) collective-permute-start(bf16[128,2048]{1,0:T(8,128)(2,1)S(1)} %copy-done.83), channel_id=1, source_target_pairs={{0,24},{4,28},{8,16},{12,20},{16,8},{20,12},{24,0},{28,4},{1,25},{... | collective-permute-start | bytes 1572872 | tf_op jit(solution)/shard_map/ppermute | solution.py:34
  371.9 1.9 collective-permute-start.41
  373.9 11.1 %collective-permute-start.42 = (bf16[8,64,128]{2,1,0:T(8,128)(2,1)S(1)}, bf16[8,64,128]{2,1,0:T(8,128)(2,1)S(1)}, u32[]{:S(2)}, u32[]{:S(2)}) collective-permute-start(bf16[8,64,128]{2,1,0:T(8,128)(2,1)S(1)} %get-tuple-element.218), channel_id=1, source_target_pairs={{0,1},{1,2},{2,3},{3,0},{4,5},{5,6},{6,7},{7,4},{8,9},{9,10},{10,1... | collective-permute-start | bytes 393224 | tf_op jit(solution)/shard_map/ppermute | solution.py:38
  376.2 17.9 %collective-permute-start.43 = (bf16[8,64,128]{2,1,0:T(8,128)(2,1)S(1)}, bf16[8,64,128]{2,1,0:T(8,128)(2,1)S(1)}, u32[]{:S(2)}, u32[]{:S(2)}) collective-permute-start(bf16[8,64,128]{2,1,0:T(8,128)(2,1)S(1)} %get-tuple-element.219), channel_id=1, source_target_pairs={{0,2},{1,3},{2,0},{3,1},{4,6},{5,7},{6,4},{7,5},{8,10},{9,11},{10,... | collective-permute-start | bytes 393224 | tf_op jit(solution)/shard_map/ppermute | solution.py:38
  376.7 17.4 %collective-permute-start.44 = (bf16[8,64,128]{2,1,0:T(8,128)(2,1)S(1)}, bf16[8,64,128]{2,1,0:T(8,128)(2,1)S(1)}, u32[]{:S(2)}, u32[]{:S(2)}) collective-permute-start(bf16[8,64,128]{2,1,0:T(8,128)(2,1)S(1)} %get-tuple-element.220), channel_id=1, source_target_pairs={{0,3},{1,0},{2,1},{3,2},{4,7},{5,4},{6,5},{7,6},{8,11},{9,8},{10,9... | collective-permute-start | bytes 393224 | tf_op jit(solution)/shard_map/ppermute | solution.py:38
  402.7 14.0 %collective-permute-start.45 = (bf16[512,2048]{1,0:T(8,128)(2,1)S(1)}, bf16[512,2048]{1,0:T(8,128)(2,1)S(1)}, u32[]{:S(2)}, u32[]{:S(2)}) collective-permute-start(bf16[512,2048]{1,0:T(8,128)(2,1)S(1)} %convolution_convert_fusion.1), channel_id=1, source_target_pairs={{0,4},{4,0},{8,12},{12,8},{16,20},{20,16},{24,28},{28,24},{1,5},{5... | collective-permute-start | bytes 6291464 | tf_op jit(solution)/shard_map/ppermute | solution.py:34
  403.0 35.4 %collective-permute-start.49 = (bf16[256,1152]{1,0:T(8,128)(2,1)}, bf16[256,1152]{1,0:T(8,128)(2,1)S(1)}, u32[]{:S(2)}, u32[]{:S(2)}) collective-permute-start(bf16[256,1152]{1,0:T(8,128)(2,1)} %get-tuple-element.224), channel_id=1, source_target_pairs={{0,1},{1,2},{2,3},{3,0},{4,5},{5,6},{6,7},{7,4},{8,9},{9,10},{10,1... | collective-permute-start | bytes 1769480 | tf_op jit(solution)/shard_map/ppermute | solution.py:38
  416.7 32.0 %collective-permute-start.50 = (bf16[256,1152]{1,0:T(8,128)(2,1)}, bf16[256,1152]{1,0:T(8,128)(2,1)S(1)}, u32[]{:S(2)}, u32[]{:S(2)}) collective-permute-start(bf16[256,1152]{1,0:T(8,128)(2,1)} %get-tuple-element.226), channel_id=1, source_target_pairs={{0,3},{1,0},{2,1},{3,2},{4,7},{5,4},{6,5},{7,6},{8,11},{9,8},{10,9... | collective-permute-start | bytes 1769480 | tf_op jit(solution)/shard_map/ppermute | solution.py:38
  420.5 29.0 %collective-permute-start.46 = (bf16[128,2048]{1,0:T(8,128)(2,1)}, bf16[128,2048]{1,0:T(8,128)(2,1)}, u32[]{:S(2)}, u32[]{:S(2)}) collective-permute-start(bf16[128,2048]{1,0:T(8,128)(2,1)} %get-tuple-element.229), channel_id=1, source_target_pairs={{0,8},{4,12},{8,0},{12,4},{16,24},{20,28},{24,16},{28,20},{1,9},{5... | collective-permute-start | bytes 1572872 | tf_op jit(solution)/shard_map/ppermute | solution.py:34
  421.9 27.6 %collective-permute-start.47 = (bf16[128,2048]{1,0:T(8,128)(2,1)}, bf16[128,2048]{1,0:T(8,128)(2,1)}, u32[]{:S(2)}, u32[]{:S(2)}) collective-permute-start(bf16[128,2048]{1,0:T(8,128)(2,1)} %get-tuple-element.230), channel_id=1, source_target_pairs={{0,16},{4,20},{8,24},{12,28},{16,0},{20,4},{24,8},{28,12},{1,17},{... | collective-permute-start | bytes 1572872 | tf_op jit(solution)/shard_map/ppermute | solution.py:34
  422.7 26.8 %collective-permute-start.48 = (bf16[128,2048]{1,0:T(8,128)(2,1)}, bf16[128,2048]{1,0:T(8,128)(2,1)}, u32[]{:S(2)}, u32[]{:S(2)}) collective-permute-start(bf16[128,2048]{1,0:T(8,128)(2,1)} %get-tuple-element.231), channel_id=1, source_target_pairs={{0,24},{4,28},{8,16},{12,20},{16,8},{20,12},{24,0},{28,4},{1,25},{... | collective-permute-start | bytes 1572872 | tf_op jit(solution)/shard_map/ppermute | solution.py:34
  449.5 36.4 %all-to-all-start.2 = ((bf16[8,64,1408]{2,1,0:T(8,128)(2,1)}), bf16[8,64,1408]{2,1,0:T(8,128)(2,1)S(1)}, u32[]{:S(2)}, u32[]{:S(2)}) async-start(bf16[8,64,1408]{2,1,0:T(8,128)(2,1)} %bitcast.46), calls=%async_computation.4 | async-start | bytes 2883584 | tf_op jit(solution)/shard_map/all_to_all | solution.py:847
  453.2 31.9 %collective-permute-start.51 = (bf16[256,1152]{1,0:T(8,128)(2,1)}, bf16[256,1152]{1,0:T(8,128)(2,1)S(1)}, u32[]{:S(2)}, u32[]{:S(2)}) collective-permute-start(bf16[256,1152]{1,0:T(8,128)(2,1)} %copy-done.81), channel_id=1, source_target_pairs={{0,2},{1,3},{2,0},{3,1},{4,6},{5,7},{6,4},{7,5},{8,10},{9,11},{10,... | collective-permute-start | bytes 1769480 | tf_op jit(solution)/shard_map/ppermute | solution.py:38
  488.2 12.5 %all-to-all-start.3 = ((bf16[8,64,320]{2,1,0:T(8,128)(2,1)}), bf16[8,64,320]{2,1,0:T(8,128)(2,1)}, u32[]{:S(2)}, u32[]{:S(2)}) async-start(bf16[8,64,320]{2,1,0:T(8,128)(2,1)} %get-tuple-element.243), calls=%async_computation.5 | async-start | bytes 786432 | tf_op jit(solution)/shard_map/all_to_all | solution.py:851
  (96 other events, 952.2 us)
Sparse Core Ops, SparseCore 0:
  9.6 95.6 all-gather.2
  107.9 127.1 all-gather.4
  256.7 55.5 reduce-scatter.2
  314.4 122.2 reduce-scatter.4
